TPU v7x, 32 devices: a whole 2x2x4 slice. The times are simulated.
32 devices in a mesh: row: 2 (over core), col: 2 (over x), layer: 8 (over z, y).
Axes of the slice: x: 2, y: 2, z: 4, core: 2. Of those that a mesh axis runs over, the one named last changes fastest.
Arguments:
- a_tiles: bfloat16 [2, 2, 8, 64, 128, 128], P('row', 'col', 'layer'), may hold values from -6 to 6
- p_tiles: bfloat16 [2, 2, 8, 16, 128, 128], P('row', 'col', 'layer'), may hold values from -0.03125 to 0.03125
- pair_a: int32 [2, 2, 8, 2, 32, 16], P('row', 'col', 'layer'), may hold values from 0 to 63
- pair_p: int32 [2, 2, 8, 2, 32, 16], P('row', 'col', 'layer'), may hold values from 0 to 31
Outputs:
- c_tiles: bfloat16 [2, 2, 32, 128, 128], P('row', 'col', 'layer')
All inputs are finite; a program needn't handle non-finite values.
Results may differ from a plain program's by a relative error of at most 0.0014.
Values may be sent and summed in bfloat16 or wider, within the bound.
No kernel may reach another device: no remote copies, remote signals or barrier semaphores. Data moves between devices by JAX's collectives and lax.ppermute only.
A program may use at most 128 MiB of HBM per device.

v0:
```python
import math

import jax
import jax.numpy as jnp
from jax import lax
from jax.sharding import PartitionSpec as P


def products(source_a, source_p, index_a, index_p):
    slot_count = index_a.shape[0]
    fan_count = index_a.shape[1]
    width = source_a.shape[-1]
    group_size = math.gcd(slot_count, 16)

    def one_group(chosen):
        left = jnp.take(source_a, chosen[0], axis=0)
        right = jnp.take(source_p, chosen[1], axis=0)
        return jnp.einsum("sfij,sfjk->sik", left, right, preferred_element_type=jnp.float32)

    shaped_a = index_a.reshape(slot_count // group_size, group_size, fan_count)
    shaped_p = index_p.reshape(slot_count // group_size, group_size, fan_count)
    results = lax.map(one_group, (shaped_a, shaped_p))
    return results.reshape(slot_count, width, width)


def on_device(a_tiles, p_tiles, pair_a, pair_p):
    local_a = a_tiles[0, 0, 0]
    local_p = p_tiles[0, 0, 0]
    pairs_a = pair_a[0, 0, 0]
    pairs_p = pair_p[0, 0, 0]
    columns = pairs_a.shape[0]
    slots = pairs_a.shape[1]
    per_col = pairs_a.shape[2]
    held = local_a.shape[0]
    gathered_p = lax.all_gather(local_p, "row", axis=0, tiled=True)
    offsets = (jnp.arange(columns, dtype=jnp.int32) * held)[:, None, None]
    glob_a = jnp.transpose(pairs_a + offsets, (1, 0, 2)).reshape(slots, columns * per_col)
    glob_p = jnp.transpose(pairs_p, (1, 0, 2)).reshape(slots, columns * per_col)
    gathered_a = lax.all_gather(local_a, "col", axis=0, tiled=True)
    partial_value = products(gathered_a, gathered_p, glob_a, glob_p)
    merged = lax.psum_scatter(partial_value, "layer", scatter_dimension=0, tiled=True)
    return merged.astype(jnp.bfloat16)[None, None]


def solution(mesh):
    in_specs = (
        P("row", "col", "layer", None, None, None),
        P("row", "col", "layer", None, None, None),
        P("row", "col", "layer", None, None, None),
        P("row", "col", "layer", None, None, None),
    )
    out_specs = P("row", "col", "layer", None, None)
    return jax.shard_map(
        on_device, mesh=mesh, in_specs=in_specs, out_specs=out_specs, check_vma=False
    )
```

profile of v0, /device:TPU:0, one launch (start us, length us, event | category | flops | bytes accessed | tf_op | source)
XLA Modules:
  0.0 246.4 jit_solution(4031097484055626964)
XLA Ops:
  6.5 0.7 all-gather.7.cloned.1.call-update
  7.3 0.7 all-gather.5.cloned.1.call-update
  8.0 0.0 reduce-scatter.2.cloned.1.call-start
  8.1 0.8 fusion.17
  8.9 0.1 reshape.97
  9.0 0.1 copy.14
  9.0 0.8 reshape.98
  9.8 0.1 copy.15
  9.9 10.8 %all-gather.7.cloned.1.call-done = bf16[1,1,1,32,128,128]{5,4,2,1,0,3:T(8,128)(2,1)} async-done(((bf16[1,1,1,16,128,128]{5,4,2,1,0,3:T(8,128)(2,1)}), bf16[1,1,1,32,128,128]{5,4,2,1,0,3:T(8,128)(2,1)}) %all-gather.7.cloned.1.call-update) | async-done | bytes 1048592 | tf_op jit(solution)/shard_map/all_gather | solution.py:35
  20.7 59.5 %all-gather.5.cloned.1.call-done = bf16[1,1,1,128,128,128]{5,4,2,1,0,3:T(8,128)(2,1)} async-done(((bf16[1,1,1,64,128,128]{5,4,2,1,0,3:T(8,128)(2,1)}), bf16[1,1,1,128,128,128]{5,4,2,1,0,3:T(8,128)(2,1)}) %all-gather.5.cloned.1.call-update) | async-done | bytes 4194320 | tf_op jit(solution)/shard_map/all_gather | solution.py:39
  80.2 89.0 %while.10 = (s32[]{:T(128)}, f32[2,16,128,128]{3,2,1,0:T(8,128)S(1)}, s32[2,16,32]{2,1,0:T(8,128)S(1)}, bf16[128,128,128]{2,1,0:T(8,128)(2,1)}, s32[2,16,32]{2,1...) while((s32[]{:T(128)}, f32[2,16,128,128]{3,2,1,0:T(8,128)S(1)}, s32[2,16,32]{2,1,0:T(8,128)S(1)}, ...), condition=%wide.region_1.2_spmd, body=%wide.region_0.1_spmd.sunk | while | flops 2164272128 | bytes 101753936 | solution.py:22
  80.2 0.1 reshape.109
  80.2 15.1 %gather_fusion = bf16[512,128,128]{2,1,0:T(8,128)(2,1)} fusion(bf16[32,128,128]{2,1,0:T(8,128)(2,1)} %get-tuple-element.118, s32[1024]{0:T(1024)S(1)} %pad_clamp_fusion.4), kind=kCustom, calls=%fused_computation.1.clone.1 | custom fusion | bytes 33556480 | tf_op jit(solution)/shard_map/while/body/eval_jaxpr/jit(_take)/gather | solution.py:17
  95.4 0.1 reshape.110
  95.4 16.1 %gather_fusion.1 = bf16[512,128,128]{2,1,0:T(8,128)(2,1)} fusion(bf16[128,128,128]{2,1,0:T(8,128)(2,1)} %get-tuple-element.116, s32[1024]{0:T(1024)S(1)} %pad_clamp_fusion.5), kind=kCustom, calls=%fused_computation.clone.1 | custom fusion | bytes 33556480 | tf_op jit(solution)/shard_map/while/body/eval_jaxpr/jit(_take)/gather | solution.py:16
  111.6 13.1 %fusion.23 = f32[2,16,128,128]{3,2,1,0:T(8,128)S(1)} fusion(f32[2,16,128,128]{3,2,1,0:T(8,128)S(1)} %get-tuple-element.107, s32[]{:T(128)} %get-tuple-element.106, bf16[16,32,128,128]{3,2,1,0:T(8,128)(2,1)} %bitcast.56, pred[16,32]{1,0:T(8,128)(4,1)S(1)} %get-tuple-element.96, bf16[16,32,128,128]{3,2,1,0:T(8,128)(2,1)} %bitcast.57, ...), kind=kOutput, calls=%fused_computation.9.clone.1 | convolution fusion | flops 2164260864 | bytes 34607108 | tf_op jit(solution)/shard_map/while/body/eval_jaxpr/sfij,sfjk->sik/dot_general | solution.py:18
  124.7 0.1 reshape.109
  124.8 15.1 %gather_fusion = bf16[512,128,128]{2,1,0:T(8,128)(2,1)} fusion(bf16[32,128,128]{2,1,0:T(8,128)(2,1)} %get-tuple-element.118, s32[1024]{0:T(1024)S(1)} %pad_clamp_fusion.4), kind=kCustom, calls=%fused_computation.1.clone.1 | custom fusion | bytes 33556480 | tf_op jit(solution)/shard_map/while/body/eval_jaxpr/jit(_take)/gather | solution.py:17
  139.9 0.1 reshape.110
  140.0 16.1 %gather_fusion.1 = bf16[512,128,128]{2,1,0:T(8,128)(2,1)} fusion(bf16[128,128,128]{2,1,0:T(8,128)(2,1)} %get-tuple-element.116, s32[1024]{0:T(1024)S(1)} %pad_clamp_fusion.5), kind=kCustom, calls=%fused_computation.clone.1 | custom fusion | bytes 33556480 | tf_op jit(solution)/shard_map/while/body/eval_jaxpr/jit(_take)/gather | solution.py:16
  156.1 13.1 %fusion.23 = f32[2,16,128,128]{3,2,1,0:T(8,128)S(1)} fusion(f32[2,16,128,128]{3,2,1,0:T(8,128)S(1)} %get-tuple-element.107, s32[]{:T(128)} %get-tuple-element.106, bf16[16,32,128,128]{3,2,1,0:T(8,128)(2,1)} %bitcast.56, pred[16,32]{1,0:T(8,128)(4,1)S(1)} %get-tuple-element.96, bf16[16,32,128,128]{3,2,1,0:T(8,128)(2,1)} %bitcast.57, ...), kind=kOutput, calls=%fused_computation.9.clone.1 | convolution fusion | flops 2164260864 | bytes 34607108 | tf_op jit(solution)/shard_map/while/body/eval_jaxpr/sfij,sfjk->sik/dot_general | solution.py:18
  169.2 1.3 copy-done
  170.5 67.8 %reduce-scatter.2.cloned.1.call-done = f32[4,128,128]{2,1,0:T(8,128)} async-done(((f32[32,128,128]{2,1,0:T(8,128)}), f32[4,128,128]{2,1,0:T(8,128)}) %reduce-scatter.2.cloned.1.call-update) | async-done | bytes 262160 | tf_op jit(solution)/shard_map/reduce_scatter | solution.py:41
  238.3 1.6 convert_bitcast_fusion
  (14 shorter events, 0.1 us)
Async XLA Ops:
  6.5 14.1 %all-gather.7.cloned.1.call-start = ((), (), s32[]{:S(2)}) async-start(), calls=%async_computation.3 | async-start | bytes 1572864 | tf_op jit(solution)/shard_map/all_gather | solution.py:35
  7.3 72.9 %all-gather.5.cloned.1.call-start = ((), (), s32[]{:S(2)}) async-start(), calls=%async_computation.2 | async-start | bytes 6291456 | tf_op jit(solution)/shard_map/all_gather | solution.py:39
  8.0 230.3 %reduce-scatter.2.cloned.1.call-start = ((), (), s32[]{:S(2)}) async-start(), calls=%async_computation.1 | async-start | bytes 2359296 | tf_op jit(solution)/shard_map/reduce_scatter | solution.py:41
  169.1 1.3 copy-start
Sparse Core Ops, SparseCore 0:
  8.9 11.7 all-gather.6
  22.2 57.8 all-gather.4
  170.6 67.6 reduce-scatter.1
where the time goes:
time: 247 us; the launch traced here: 246 us
  waiting for transfers between devices  139 us (56%)
  local copies, waits for them, and re-layouts  65.1 us (26%)
  matrix products  26.1 us (11%)
  between operations  13.1 us (5%)
  other arithmetic  2.48 us (1%)
    reduce_scatter x1, waiting for transfers between devices, on_device(): lax.psum_scatter(partial_value, 'layer', scatter_dimension=0, tiled=True)  67.8 us
    all_gather x1, waiting for transfers between devices, on_device(): gathered_a = lax.all_gather(local_a, 'col', axis=0, tiled=True)  59.5 us
    gather x2, local copies, waits for them, and re-layouts, one_group(): left = jnp.take(source_a, chosen[0], axis=0)  32.2 us
    gather x2, local copies, waits for them, and re-layouts, one_group(): right = jnp.take(source_p, chosen[1], axis=0)  30.2 us
    dot_general x2, matrix products, one_group(): jnp.einsum('sfij,sfjk->sik', left, right, preferred_element_type=jnp.floa...  26.1 us
    all_gather x1, waiting for transfers between devices, on_device(): gathered_p = lax.all_gather(local_p, 'row', axis=0, tiled=True)  10.8 us
  transfers between devices with their start and end apart: 3, of which 3 were waited for; matrix products, arithmetic and copies ran while one was open for 1% of the time, Pallas kernels for 0%

commit v1 on v0

v1 whole, which is shorter than its diff:
```python
import jax
import jax.numpy as jnp
from jax import lax
from jax.experimental import pallas as pl
from jax.experimental.pallas import tpu as pltpu
from jax.sharding import PartitionSpec as P

PEAK = 32766.0
HEAD = 16
SMEM = pltpu.MemorySpace.SMEM
VMEM = pltpu.MemorySpace.VMEM


def encode(tile):
    top = jnp.max(jnp.abs(tile), axis=0, keepdims=True)
    power = jnp.floor(jnp.log2(jnp.maximum(top, 2.0**-100)) + 0.001) + 1.0
    scaled = jnp.round(tile * (jnp.exp2(-power) * PEAK))
    return scaled.astype(jnp.int32).astype(jnp.int16), power.astype(jnp.int32)


def decode(coded, power):
    return coded.astype(jnp.int32).astype(jnp.float32) * (jnp.exp2(power.astype(jnp.float32)) * (1.0 / PEAK))


def store_unit(out_ref, unit, tiles):
    width = tiles[0].shape[0]
    count = len(tiles)
    rows = lax.broadcasted_iota(jnp.int32, (HEAD, width), 0)
    head = jnp.zeros((HEAD, width), jnp.int32)
    for i, tile in enumerate(tiles):
        coded, power = encode(tile)
        out_ref[unit, pl.ds(i * width, width), :] = coded
        head = jnp.where(rows == i, power, head)
    out_ref[unit, pl.ds(count * width, HEAD), :] = head.astype(jnp.int16)


def load_unit(in_ref, unit, count):
    width = in_ref.shape[-1]
    head = in_ref[unit, pl.ds(count * width, HEAD), :].astype(jnp.int32)
    return [decode(in_ref[unit, pl.ds(i * width, width), :], head[i : i + 1]) for i in range(count)]


def one_tile(a_ref, p_refs, look, fan):
    held = p_refs[0].shape[0]
    lefts, rights = [], []
    for f in range(fan):
        pa, pp = look(f)
        lefts.append(a_ref[pa])
        rights.append(p_refs[0][pp])
    left = jnp.concatenate(lefts, axis=1)
    right = jnp.concatenate(rights, axis=0)
    return jnp.dot(left, right, preferred_element_type=jnp.float32)


def own_kernel(me_ref, ia_ref, ip_ref, a_ref, p0_ref, p1_ref, out_ref, p_ref):
    held = p0_ref.shape[0]
    row = me_ref[0]
    col = me_ref[1]
    p_ref[pl.ds(row * held, held)] = p0_ref[...]
    p_ref[pl.ds((1 - row) * held, held)] = p1_ref[...]
    fan = ia_ref.shape[-1]

    def body(t, _):
        out_ref[t] = one_tile(a_ref, (p_ref,), lambda f: (ia_ref[col, t, f], ip_ref[col, t, f]), fan)
        return 0

    lax.fori_loop(0, out_ref.shape[0], body, 0)


def other_kernel(me_ref, ia_ref, ip_ref, a_ref, p0_ref, p1_ref, out_ref, p_ref):
    held = p0_ref.shape[0]
    row = me_ref[0]
    col = me_ref[1]
    p_ref[pl.ds(row * held, held)] = p0_ref[...]
    p_ref[pl.ds((1 - row) * held, held)] = p1_ref[...]
    fan = ia_ref.shape[-1]
    units = out_ref.shape[0]
    width = out_ref.shape[-1]
    count = (out_ref.shape[1] - HEAD) // width

    def body(unit, _):
        tiles = []
        for i in range(count):
            t = unit * count + i
            tiles.append(one_tile(a_ref, (p_ref,), lambda f: (ia_ref[col, t, f], ip_ref[col, t, f]), fan))
        store_unit(out_ref, unit, tiles)
        return 0

    lax.fori_loop(0, units, body, 0)


def add_kernel(own_ref, in_ref, out_ref):
    units = out_ref.shape[0]
    width = out_ref.shape[-1]
    count = (out_ref.shape[1] - HEAD) // width

    def body(unit, _):
        got = load_unit(in_ref, unit, count)
        tiles = [own_ref[unit * count + i] + got[i] for i in range(count)]
        store_unit(out_ref, unit, tiles)
        return 0

    lax.fori_loop(0, units, body, 0)


def last_kernel(in_ref, out_ref):
    units = in_ref.shape[0]
    width = out_ref.shape[-1]
    count = out_ref.shape[0]
    for i in range(count):
        total = jnp.zeros((width, width), jnp.float32)
        for unit in range(units):
            power = in_ref[unit, pl.ds(count * width, HEAD), :].astype(jnp.int32)[i : i + 1]
            total += decode(in_ref[unit, pl.ds(i * width, width), :], power)
        out_ref[i] = total.astype(out_ref.dtype)


def call(kernel, out_shape, smem, vmem, scratch=(), flops=0):
    moved = sum(x.size * x.dtype.itemsize for x in vmem) + out_shape.size * out_shape.dtype.itemsize
    return pl.pallas_call(
        kernel,
        out_shape=out_shape,
        in_specs=[pl.BlockSpec(memory_space=SMEM)] * len(smem) + [pl.BlockSpec(memory_space=VMEM)] * len(vmem),
        out_specs=pl.BlockSpec(memory_space=VMEM),
        scratch_shapes=list(scratch),
        compiler_params=pltpu.CompilerParams(vmem_limit_bytes=40 * 2**20),
        cost_estimate=pl.CostEstimate(flops=flops, bytes_accessed=moved, transcendentals=0),
    )(*smem, *vmem)


def on_device(a_tiles, p_tiles, pair_a, pair_p):
    a, p, ia, ip = a_tiles[0, 0, 0], p_tiles[0, 0, 0], pair_a[0, 0, 0], pair_p[0, 0, 0]
    slots, fan = ia.shape[1:]
    held, width = p.shape[0], p.shape[-1]
    layers = lax.axis_size("layer")
    count = slots // layers
    swap = [(0, 1), (1, 0)]
    me = jnp.stack([lax.axis_index("row"), lax.axis_index("col")]).astype(jnp.int32)

    p_x = lax.ppermute(p, "col", swap)
    p_r = lax.ppermute(p, "row", swap)
    ia_x = lax.ppermute(ia, "col", swap)
    ip_x = lax.ppermute(ip, "col", swap)
    p_xr = lax.ppermute(p_x, "row", swap)

    flops = 2 * slots * fan * width**3
    both = pltpu.VMEM((2 * held, width, width), jnp.bfloat16)
    whole = jax.ShapeDtypeStruct((slots, width, width), jnp.float32)
    coded = jax.ShapeDtypeStruct((layers, count * width + HEAD, width), jnp.int16)
    own = call(own_kernel, whole, (me, ia, ip), (a, p, p_r), (both,), flops)
    other = call(other_kernel, coded, (me, ia_x, ip_x), (a, p_x, p_xr), (both,), flops)
    came = lax.ppermute(other, "col", swap)
    sums = call(add_kernel, coded, (), (own, came))
    spread = lax.all_to_all(sums, "layer", split_axis=0, concat_axis=0, tiled=True)
    out = call(last_kernel, jax.ShapeDtypeStruct((count, width, width), jnp.bfloat16), (), (spread,))
    return out[None, None]


def solution(mesh):
    spec = P("row", "col", "layer", None, None, None)
    return jax.shard_map(
        on_device,
        mesh=mesh,
        in_specs=(spec,) * 4,
        out_specs=P("row", "col", "layer", None, None),
        check_vma=False,
    )
```

time: 247 us -> 89.7 us (0.36)
  waiting for transfers between devices: 139 us -> 29.3 us
  local copies, waits for them, and re-layouts: 65.1 us -> 3.18 us
  blocking collectives: 0 us -> 31.2 us
  matrix products: 26.1 us -> 0 us
  Pallas kernels: 0 us -> 20.3 us
  between operations: 13.1 us -> 0.03 us
  starting transfers between devices: 0.08 us -> 5.32 us
    all_gather x2 -> x0, waiting for transfers between devices: 70.2 us -> none  [the longest x1 59.5 us: on_device(): gathered_a = lax.all_gather(local_a, 'col', axis=0, tiled=True)]
    reduce_scatter x1 -> x0, waiting for transfers between devices: 67.8 us -> none  [on_device(): lax.psum_scatter(partial_value, 'layer', scatter_dimension=0, tiled=True)]
    gather x4 -> x0, local copies, waits for them, and re-layouts: 62.4 us -> none  [the longest x2 32.2 us: one_group(): left = jnp.take(source_a, chosen[0], axis=0)]
    all_to_all x0 -> x1, blocking collectives: none -> 31.2 us  [on_device(): lax.all_to_all(sums, 'layer', split_axis=0, concat_axis=0, tiled=True)]
    ppermute x0 -> x6, waiting for transfers between devices: none -> 29.3 us  [the longest x1 12.1 us: on_device(): p_x = lax.ppermute(p, 'col', swap)]
    dot_general x2 -> x0, matrix products: 26.1 us -> none  [one_group(): jnp.einsum('sfij,sfjk->sik', left, right, preferred_element_type=jnp.floa...]
    pallas_call x0 -> x4, Pallas kernels: none -> 20.3 us  [call(): pl.pallas_call(kernel, out_shape=out_shape, in_specs=[pl.BlockSpec(memory...]
    ppermute x0 -> x6, starting transfers between devices: none -> 5.32 us  [the longest x1 2.94 us: on_device(): p_x = lax.ppermute(p, 'col', swap)]
  transfers between devices with their start and end apart: 3 -> 6, of which waited for: 3 -> 5; matrix products, arithmetic and copies ran while one was open for 1% -> 2% of each run, Pallas kernels for 0% -> 12%
where the time goes in v1:
time: 89.7 us; the launch traced here: 89.3 us
  blocking collectives  31.2 us (35%)
  waiting for transfers between devices  29.3 us (33%)
  Pallas kernels  20.3 us (23%)
  starting transfers between devices  5.32 us (6%)
  local copies, waits for them, and re-layouts  3.18 us (4%)
    all_to_all x1, blocking collectives, on_device(): lax.all_to_all(sums, 'layer', split_axis=0, concat_axis=0, tiled=True)  31.2 us
    pallas_call x4, Pallas kernels, call(): pl.pallas_call(kernel, out_shape=out_shape, in_specs=[pl.BlockSpec(memory...  20.3 us
    ppermute x1, waiting for transfers between devices, on_device(): p_x = lax.ppermute(p, 'col', swap)  12.1 us
    ppermute x1, waiting for transfers between devices, on_device(): came = lax.ppermute(other, 'col', swap)  11.7 us
    unnamed x6, local copies, waits for them, and re-layouts  3.18 us
    ppermute x1, starting transfers between devices, on_device(): p_x = lax.ppermute(p, 'col', swap)  2.94 us
    ppermute x1, waiting for transfers between devices, on_device(): ia_x = lax.ppermute(ia, 'col', swap)  2.53 us
    ppermute x1, waiting for transfers between devices, on_device(): p_r = lax.ppermute(p, 'row', swap)  1.91 us
  transfers between devices with their start and end apart: 6, of which 5 were waited for; matrix products, arithmetic and copies ran while one was open for 2% of the time, Pallas kernels for 12%

profile of v1, /device:TPU:0, one launch (start us, length us, event | category | flops | bytes accessed | tf_op | source)
XLA Modules:
  0.0 89.3 jit_solution(9960377348865272208)
XLA Ops:
  0.0 2.9 %collective-permute-start.3 = (bf16[16,128,128]{2,1,0:T(8,128)(2,1)}, bf16[16,128,128]{2,1,0:T(8,128)(2,1)S(1)}, u32[]{:S(2)}, u32[]{:S(2)}) collective-permute-start(bf16[16,128,128]{2,1,0:T(8,128)(2,1)} %bitcast.13), channel_id=1, source_target_pairs={{0,8},{8,0},{1,9},{9,1},{2,10},{10,2},{3,11},{11,3},{4,12},{12,4},... | collective-permute-start | bytes 1572872 | tf_op jit(solution)/shard_map/ppermute | solution.py:140
  2.9 12.1 %collective-permute-done.3.p0_ref = bf16[16,128,128]{2,1,0:T(8,128)(2,1)S(1)} collective-permute-done((bf16[16,128,128]{2,1,0:T(8,128)(2,1)}, bf16[16,128,128]{2,1,0:T(8,128)(2,1)S(1)}, u32[]{:S(2)}, u32[]{:S(2)}) %collective-permute-start.3) | collective-permute-done | bytes 524320 | tf_op jit(solution)/shard_map/ppermute | solution.py:140
  15.1 0.0 collective-permute-start.4
  15.1 0.8 copy.6
  15.9 1.7 %collective-permute-start.2 = (s32[2,32,16]{2,1,0:T(8,128)S(1)}, s32[2,32,16]{2,1,0:T(8,128)S(1)}, u32[]{:S(2)}, u32[]{:S(2)}) collective-permute-start(s32[2,32,16]{2,1,0:T(8,128)S(1)} %bitcast.7), channel_id=1, source_target_pairs={{0,8},{8,0},{1,9},{9,1},{2,10},{10,2},{3,11},{11,3},{4,12},{12,4},... | collective-permute-start | bytes 12296 | tf_op jit(solution)/shard_map/ppermute | solution.py:143
  17.6 0.8 copy.5
  18.4 0.3 collective-permute-start.1
  18.7 0.1 pad_add_fusion.me_ref
  18.8 1.0 %collective-permute-done.2.ip_ref = s32[2,32,16]{2,1,0:T(8,128)S(1)} collective-permute-done((s32[2,32,16]{2,1,0:T(8,128)S(1)}, s32[2,32,16]{2,1,0:T(8,128)S(1)}, u32[]{:S(2)}, u32[]{:S(2)}) %collective-permute-start.2) | collective-permute-done | bytes 4128 | tf_op jit(solution)/shard_map/ppermute | solution.py:143
  19.8 2.5 %collective-permute-done.1.ia_ref = s32[2,32,16]{2,1,0:T(8,128)S(1)} collective-permute-done((s32[2,32,16]{2,1,0:T(8,128)S(1)}, s32[2,32,16]{2,1,0:T(8,128)S(1)}, u32[]{:S(2)}, u32[]{:S(2)}) %collective-permute-start.1) | collective-permute-done | bytes 4128 | tf_op jit(solution)/shard_map/ppermute | solution.py:142
  22.3 0.0 collective-permute-done.4.p1_ref
  22.3 0.0 copy-start
  22.3 1.6 %copy-done = bf16[1,1,1,64,128,128]{5,4,3,2,1,0:T(8,128)(2,1)S(1)} copy-done((bf16[1,1,1,64,128,128]{5,4,3,2,1,0:T(8,128)(2,1)S(1)}, bf16[1,1,1,64,128,128]{5,4,3,2,1,0:T(8,128)(2,1)}, u32[]{:S(2)}) %copy-start) | copy-done | bytes 2097176
  23.9 0.0 copy-start.1
  23.9 7.6 %shard_map.47 = s16[8,528,128]{2,1,0:T(8,128)(2,1)S(1)} custom-call(s32[2]{0:T(128)S(1)} %pad_add_fusion.me_ref, s32[2,32,16]{2,1,0:T(8,128)S(1)} %collective-permute-done.1.ia_ref, s32[2,32,16]{2,1,0:T(8,128)S(1)} %collective-permute-done.2.ip_ref, bf16[64,128,128]{2,1,0:T(8,128)(2,1)S(1)} %bitcast.11, ...), custom_call_target="tpu_custom_call" | custom-call | flops 2147483648 | bytes 4227072 | tf_op jit(solution)/shard_map/pallas_call | solution.py:120
  31.5 0.3 collective-permute-start.5
  31.9 0.0 copy-done.1
  31.9 0.0 collective-permute-start
  31.9 1.9 %collective-permute-done.p1_ref = bf16[16,128,128]{2,1,0:T(8,128)(2,1)S(1)} collective-permute-done((bf16[16,128,128]{2,1,0:T(8,128)(2,1)S(1)}, bf16[16,128,128]{2,1,0:T(8,128)(2,1)S(1)}, u32[]{:S(2)}, u32[]{:S(2)}) %collective-permute-start) | collective-permute-done | bytes 524320 | tf_op jit(solution)/shard_map/ppermute | solution.py:141
  33.8 10.9 %shard_map.46.own_ref = f32[32,128,128]{2,1,0:T(8,128)S(1)} custom-call(s32[2]{0:T(128)S(1)} %pad_add_fusion.me_ref, s32[2,32,16]{2,1,0:T(8,128)S(1)} %bitcast.10, s32[2,32,16]{2,1,0:T(8,128)S(1)} %bitcast.8, bf16[64,128,128]{2,1,0:T(8,128)(2,1)S(1)} %bitcast.12, bf16[16,128,128]{2,1,0:T(8,128)(2,1)S(1)} %bitcast.15, ...), custom_call_target="tpu_custom_call" | custom-call | flops 2147483648 | bytes 5242880 | tf_op jit(solution)/shard_map/pallas_call | solution.py:120
  44.7 11.7 %collective-permute-done.5.in_ref = s16[8,528,128]{2,1,0:T(8,128)(2,1)S(1)} collective-permute-done((s16[8,528,128]{2,1,0:T(8,128)(2,1)S(1)}, s16[8,528,128]{2,1,0:T(8,128)(2,1)S(1)}, u32[]{:S(2)}, u32[]{:S(2)}) %collective-permute-start.5) | collective-permute-done | bytes 1081376 | tf_op jit(solution)/shard_map/ppermute | solution.py:152
  56.4 0.8 shard_map.48
  57.2 31.2 %all_to_all.5.in_ref = s16[8,528,128]{2,1,0:T(8,128)(2,1)S(1)} all-to-all(s16[8,528,128]{2,1,0:T(8,128)(2,1)S(1)} %shard_map.48), channel_id=1, replica_groups=mesh['row'=2,'col'=2,'layer'=8] {'layer'}, dimensions={0} | all-to-all | bytes 2162688 | tf_op jit(solution)/shard_map/all_to_all | solution.py:154
  88.4 0.9 %shard_map.49 = bf16[4,128,128]{2,1,0:T(8,128)(2,1)} custom-call(s16[8,528,128]{2,1,0:T(8,128)(2,1)S(1)} %all_to_all.5.in_ref), custom_call_target="tpu_custom_call" | custom-call | bytes 1212416 | tf_op jit(solution)/shard_map/pallas_call | solution.py:120
Async XLA Ops:
  0.0 15.1 %collective-permute-start.3 = (bf16[16,128,128]{2,1,0:T(8,128)(2,1)}, bf16[16,128,128]{2,1,0:T(8,128)(2,1)S(1)}, u32[]{:S(2)}, u32[]{:S(2)}) collective-permute-start(bf16[16,128,128]{2,1,0:T(8,128)(2,1)} %bitcast.13), channel_id=1, source_target_pairs={{0,8},{8,0},{1,9},{9,1},{2,10},{10,2},{3,11},{11,3},{4,12},{12,4},... | collective-permute-start | bytes 1572872 | tf_op jit(solution)/shard_map/ppermute | solution.py:140
  15.1 7.2 %collective-permute-start.4 = (bf16[16,128,128]{2,1,0:T(8,128)(2,1)S(1)}, bf16[16,128,128]{2,1,0:T(8,128)(2,1)S(1)}, u32[]{:S(2)}, u32[]{:S(2)}) collective-permute-start(bf16[16,128,128]{2,1,0:T(8,128)(2,1)S(1)} %collective-permute-done.3.p0_ref), channel_id=1, source_target_pairs={{0,16},{16,0},{1,17},{17,1},{2,18},{18,2},{3,19},{19,3},{4,20},{20... | collective-permute-start | bytes 1572872 | tf_op jit(solution)/shard_map/ppermute | solution.py:144
  15.9 3.9 %collective-permute-start.2 = (s32[2,32,16]{2,1,0:T(8,128)S(1)}, s32[2,32,16]{2,1,0:T(8,128)S(1)}, u32[]{:S(2)}, u32[]{:S(2)}) collective-permute-start(s32[2,32,16]{2,1,0:T(8,128)S(1)} %bitcast.7), channel_id=1, source_target_pairs={{0,8},{8,0},{1,9},{9,1},{2,10},{10,2},{3,11},{11,3},{4,12},{12,4},... | collective-permute-start | bytes 12296 | tf_op jit(solution)/shard_map/ppermute | solution.py:143
  18.4 3.9 %collective-permute-start.1 = (s32[2,32,16]{2,1,0:T(8,128)S(1)}, s32[2,32,16]{2,1,0:T(8,128)S(1)}, u32[]{:S(2)}, u32[]{:S(2)}) collective-permute-start(s32[2,32,16]{2,1,0:T(8,128)S(1)} %bitcast.9), channel_id=1, source_target_pairs={{0,8},{8,0},{1,9},{9,1},{2,10},{10,2},{3,11},{11,3},{4,12},{12,4},... | collective-permute-start | bytes 12296 | tf_op jit(solution)/shard_map/ppermute | solution.py:142
  22.3 1.6 %copy-start = (bf16[1,1,1,64,128,128]{5,4,3,2,1,0:T(8,128)(2,1)S(1)}, bf16[1,1,1,64,128,128]{5,4,3,2,1,0:T(8,128)(2,1)}, u32[]{:S(2)}) copy-start(bf16[1,1,1,64,128,128]{5,4,3,2,1,0:T(8,128)(2,1)} %param.4) | copy-start | bytes 6291460
  23.9 8.0 %copy-start.1 = (bf16[1,1,1,16,128,128]{5,4,3,2,1,0:T(8,128)(2,1)S(1)}, bf16[1,1,1,16,128,128]{5,4,3,2,1,0:T(8,128)(2,1)}, u32[]{:S(2)}) copy-start(bf16[1,1,1,16,128,128]{5,4,3,2,1,0:T(8,128)(2,1)} %param.5) | copy-start | bytes 1572868
  31.5 24.9 %collective-permute-start.5 = (s16[8,528,128]{2,1,0:T(8,128)(2,1)S(1)}, s16[8,528,128]{2,1,0:T(8,128)(2,1)S(1)}, u32[]{:S(2)}, u32[]{:S(2)}) collective-permute-start(s16[8,528,128]{2,1,0:T(8,128)(2,1)S(1)} %shard_map.47), channel_id=1, source_target_pairs={{0,8},{8,0},{1,9},{9,1},{2,10},{10,2},{3,11},{11,3},{4,12},{12,4},... | collective-permute-start | bytes 3244040 | tf_op jit(solution)/shard_map/ppermute | solution.py:152
  31.9 1.9 %collective-permute-start = (bf16[16,128,128]{2,1,0:T(8,128)(2,1)S(1)}, bf16[16,128,128]{2,1,0:T(8,128)(2,1)S(1)}, u32[]{:S(2)}, u32[]{:S(2)}) collective-permute-start(bf16[16,128,128]{2,1,0:T(8,128)(2,1)S(1)} %bitcast.14), channel_id=1, source_target_pairs={{0,16},{16,0},{1,17},{17,1},{2,18},{18,2},{3,19},{19,3},{4,20},{20... | collective-permute-start | bytes 1572872 | tf_op jit(solution)/shard_map/ppermute | solution.py:141

commit v2 on v0

v2 whole, which is shorter than its diff:
```python
import jax
import jax.numpy as jnp
from jax import lax
from jax.experimental import pallas as pl
from jax.experimental.pallas import tpu as pltpu
from jax.sharding import PartitionSpec as P

PEAK = 32766.0
ROWS = 16
GROUP = 4
SMEM = pltpu.MemorySpace.SMEM
VMEM = pltpu.MemorySpace.VMEM


def head_rows(count):
    return -(-count // ROWS) * ROWS


def message(count, width):
    return jax.ShapeDtypeStruct((count * width + head_rows(count), width), jnp.int16)


def encode(tile):
    top = jnp.max(jnp.abs(tile), axis=0, keepdims=True)
    power = jnp.floor(jnp.log2(jnp.maximum(top, 2.0**-100)) + 0.001) + 1.0
    scaled = jnp.round(tile * (jnp.exp2(-power) * PEAK))
    return scaled.astype(jnp.int32).astype(jnp.int16), power.astype(jnp.int32)


def new_head(count, width):
    return jnp.zeros((head_rows(count), width), jnp.int32)


def put_tile(ref, slot, tile, head):
    width = tile.shape[0]
    coded, power = encode(tile)
    ref[pl.ds(pl.multiple_of(slot * width, width), width), :] = coded
    rows = lax.broadcasted_iota(jnp.int32, head.shape, 0)
    return jnp.where(rows == slot, power, head)


def put_head(ref, head):
    ref[pl.ds(ref.shape[0] - head.shape[0], head.shape[0]), :] = head.astype(jnp.int16)


def get_head(ref, count):
    rows = head_rows(count)
    return ref[pl.ds(ref.shape[0] - rows, rows), :].astype(jnp.int32)


def get_tile(ref, slot, head):
    width = ref.shape[-1]
    rows = lax.broadcasted_iota(jnp.int32, head.shape, 0)
    power = jnp.sum(jnp.where(rows == slot, head, 0), axis=0, keepdims=True)
    coded = ref[pl.ds(pl.multiple_of(slot * width, width), width), :]
    return coded.astype(jnp.int32).astype(jnp.float32) * (jnp.exp2(power.astype(jnp.float32)) * (1.0 / PEAK))


def product(a_ref, p_ref, look, fan):
    chosen = [look(f) for f in range(fan)]
    left = jnp.concatenate([a_ref[pa] for pa, _ in chosen], axis=1)
    right = jnp.concatenate([p_ref[pp] for _, pp in chosen], axis=0)
    return jnp.dot(left, right, preferred_element_type=jnp.float32)


def join(me_ref, p0_ref, p1_ref, p_ref):
    held = p0_ref.shape[0]
    p_ref[pl.ds(me_ref[0] * held, held)] = p0_ref[...]
    p_ref[pl.ds((1 - me_ref[0]) * held, held)] = p1_ref[...]


def finder(me_ref, index_refs, fan):
    if len(index_refs) == 2:
        ia_ref, ip_ref = index_refs
        col = me_ref[1]
        return lambda t: lambda f: (ia_ref[col, f, t], ip_ref[col, f, t])
    (both_ref,) = index_refs
    return lambda t: lambda f: (both_ref[f, t], both_ref[fan + f, t])


def send_kernel(n_index, fan, count, chunk):
    first, size = chunk

    def kernel(me_ref, *refs):
        index_refs = refs[:n_index]
        a_ref, p0_ref, p1_ref = refs[n_index : n_index + 3]
        out_ref, p_ref = refs[-2:]
        width = out_ref.shape[-1]
        join(me_ref, p0_ref, p1_ref, p_ref)
        find = finder(me_ref, index_refs, fan)
        side = 1 - (me_ref[2] & 1)
        places = out_ref.shape[0] // (width * size)

        def body(step, head):
            for k in range(GROUP):
                slot = step * GROUP + k
                place, i = slot // size, slot % size
                tile = product(a_ref, p_ref, find((place * 2 + side) * count + first + i), fan)
                head = put_tile(out_ref, slot, tile, head)
            return head

        head = lax.fori_loop(0, places * size // GROUP, body, new_head(places * size, width))
        put_head(out_ref, head)

    return kernel


def keep_kernel(n_index, fan, count, chunks):
    def kernel(me_ref, *refs):
        index_refs = refs[:n_index]
        a_ref, p0_ref, p1_ref = refs[n_index : n_index + 3]
        out_refs, p_ref = refs[-1 - len(chunks) : -1], refs[-1]
        join(me_ref, p0_ref, p1_ref, p_ref)
        find = finder(me_ref, index_refs, fan)
        side = me_ref[2] & 1
        for (first, size), out_ref in zip(chunks, out_refs):

            def body(step, _):
                for k in range(GROUP):
                    slot = step * GROUP + k
                    place, i = slot // size, slot % size
                    out_ref[slot] = product(a_ref, p_ref, find((place * 2 + side) * count + first + i), fan)
                return 0

            lax.fori_loop(0, out_ref.shape[0] // GROUP, body, 0)

    return kernel


def add_kernel(size, keeps_own):
    def kernel(me_ref, kept_ref, in_ref, *refs):
        total = kept_ref.shape[0]
        places = total // size
        out_refs = refs[-places:]
        head_in = get_head(in_ref, total)
        mine = me_ref[2] >> 1
        for d, out_ref in enumerate(out_refs):
            place = mine ^ d
            sums = [kept_ref[place * size + i] + get_tile(in_ref, place * size + i, head_in) for i in range(size)]
            if d == 0 and keeps_own:
                for i in range(size):
                    out_ref[i] = sums[i]
            else:
                head = new_head(size, kept_ref.shape[-1])
                for i in range(size):
                    head = put_tile(out_ref, i, sums[i], head)
                put_head(out_ref, head)

    return kernel


def last_kernel(size, n_messages, n_before):
    def kernel(*refs):
        own_ref, in_refs, before_refs = refs[0], refs[1 : 1 + n_messages], refs[1 + n_messages : 1 + n_messages + n_before]
        out_ref = refs[-1]
        at = 0
        for ref in before_refs:
            out_ref[pl.ds(at, ref.shape[0])] = ref[...]
            at += ref.shape[0]
        heads = [get_head(ref, size) for ref in in_refs]
        for i in range(size):
            total = own_ref[i]
            for ref, head in zip(in_refs, heads):
                total += get_tile(ref, i, head)
            out_ref[at + i] = total.astype(out_ref.dtype)

    return kernel


def call(kernel, out_shape, smem, vmem, after=(), scratch=(), flops=0):
    outs = out_shape if isinstance(out_shape, (list, tuple)) else [out_shape]
    moved = sum(x.size * x.dtype.itemsize for x in (*vmem, *outs))
    n_real = len(smem) + len(vmem)

    def wrapped(*refs):
        kernel(*refs[:n_real], *refs[n_real + len(after) :])

    return pl.pallas_call(
        wrapped,
        out_shape=out_shape,
        in_specs=[pl.BlockSpec(memory_space=SMEM)] * len(smem)
        + [pl.BlockSpec(memory_space=VMEM)] * len(vmem)
        + [pl.BlockSpec(memory_space=pl.ANY)] * len(after),
        out_specs=jax.tree.map(lambda _: pl.BlockSpec(memory_space=VMEM), out_shape),
        scratch_shapes=list(scratch),
        compiler_params=pltpu.CompilerParams(vmem_limit_bytes=40 * 2**20),
        cost_estimate=pl.CostEstimate(flops=flops, bytes_accessed=moved, transcendentals=0),
    )(*smem, *vmem, *after)


def on_device(a_tiles, p_tiles, pair_a, pair_p):
    a, p = a_tiles[0, 0, 0], p_tiles[0, 0, 0]
    ia, ip = jnp.swapaxes(pair_a[0, 0, 0], 1, 2), jnp.swapaxes(pair_p[0, 0, 0], 1, 2)
    fan, slots = ia.shape[1:]
    held, width = p.shape[0], p.shape[-1]
    layers = lax.axis_size("layer")
    count, places = slots // layers, layers // 2
    swap = [(0, 1), (1, 0)]
    me = jnp.stack([lax.axis_index("row"), lax.axis_index("col"), lax.axis_index("layer")]).astype(jnp.int32)

    p_x = lax.ppermute(p, "col", swap)
    p_r = lax.ppermute(p, "row", swap)
    far = 1 - lax.axis_index("col")
    lists = jnp.concatenate([ia[far], ip[far]], axis=0)
    lists_x = lax.ppermute(lists, "col", swap)
    p_xr = lax.ppermute(p_x, "row", swap)

    both = (pltpu.VMEM((2 * held, width, width), jnp.bfloat16),)
    half = count // 2
    chunks = [(0, half), (half, count - half)]
    flops = 2 * places * half * fan * width**3
    pairs = [(i, i ^ 1) for i in range(layers)]

    def floats(size):
        return jax.ShapeDtypeStruct((size, width, width), jnp.float32)

    def send(smem, vmem, chunk, after):
        shape = message(places * chunk[1], width)
        kernel = send_kernel(len(smem) - 1, fan, count, chunk)
        return call(kernel, shape, smem, vmem, after, both, flops)

    def keep(smem, vmem, after):
        shapes = [floats(places * size) for _, size in chunks]
        kernel = keep_kernel(len(smem) - 1, fan, count, chunks)
        return call(kernel, shapes, smem, vmem, after, both, 2 * flops)

    def add(kept, came, size, keeps_own, after):
        shapes = [floats(size) if d == 0 and keeps_own else message(size, width) for d in range(places)]
        return call(add_kernel(size, keeps_own), shapes, (me,), (kept, came), after)

    own_in = ((me, ia, ip), (a, p, p_r))
    own_sent, after = [], ()
    for chunk in chunks:
        made = send(*own_in, chunk, after)
        after = (made,)
        own_sent.append(lax.ppermute(made, "layer", pairs))
    own_kept = keep(*own_in, after)
    after = (own_kept[0],)

    def own_second(n, after):
        out = add(own_kept[n], own_sent[n], chunks[n][1], True, after)
        moved = [
            lax.ppermute(out[d], "layer", [(i, i ^ (2 * d)) for i in range(layers)]) for d in range(1, places)
        ]
        return out[0], moved

    other_in = ((me, lists_x), (a, p_x, p_xr))
    owns, other_sent = [], []
    owns.append(own_second(0, after))
    after = (owns[0][0],)
    for n, chunk in enumerate(chunks):
        made = send(*other_in, chunk, after)
        after = (made,)
        other_sent.append(lax.ppermute(made, "layer", pairs))
    owns.append(own_second(1, after))
    after = (owns[1][0],)
    other_kept = keep(*other_in, after)
    results = []
    for n, (first, size) in enumerate(chunks):
        out = add(other_kept[n], other_sent[n], size, False, ())
        moved = []
        for d in reversed(range(places)):
            perm = [(c * layers + i, (1 - c) * layers + (i ^ (2 * d))) for c in range(2) for i in range(layers)]
            moved.append(lax.ppermute(out[d], ("col", "layer"), perm))
        mine, came = owns[n]
        final = n == len(chunks) - 1
        shape = jax.ShapeDtypeStruct((count if final else size, width, width), jnp.bfloat16)
        before = tuple(results) if final else ()
        kernel = last_kernel(size, len(came) + len(moved), len(before))
        results.append(call(kernel, shape, (), (mine, *came, *moved, *before)))
    return results[-1][None, None]


def solution(mesh):
    spec = P("row", "col", "layer", None, None, None)
    return jax.shard_map(
        on_device,
        mesh=mesh,
        in_specs=(spec,) * 4,
        out_specs=P("row", "col", "layer", None, None),
        check_vma=False,
    )
```

time: 247 us -> 73.7 us (0.30)
  waiting for transfers between devices: 139 us -> 15.4 us
  local copies, waits for them, and re-layouts: 65.1 us -> 4.08 us
  starting transfers between devices: 0.08 us -> 31.8 us
  matrix products: 26.1 us -> 0 us
  Pallas kernels: 0 us -> 21.9 us
  between operations: 13.1 us -> 0.17 us
    all_gather x2 -> x0, waiting for transfers between devices: 70.2 us -> none  [the longest x1 59.5 us: on_device(): gathered_a = lax.all_gather(local_a, 'col', axis=0, tiled=True)]
    reduce_scatter x1 -> x0, waiting for transfers between devices: 67.8 us -> none  [on_device(): lax.psum_scatter(partial_value, 'layer', scatter_dimension=0, tiled=True)]
    gather x4 -> x0, local copies, waits for them, and re-layouts: 62.4 us -> none  [the longest x2 32.2 us: one_group(): left = jnp.take(source_a, chosen[0], axis=0)]
    ppermute x0 -> x22, starting transfers between devices: none -> 31.8 us  [the longest x8 13.8 us: on_device(): moved.append(lax.ppermute(out[d], ('col', 'layer'), perm))]
    dot_general x2 -> x0, matrix products: 26.1 us -> none  [one_group(): jnp.einsum('sfij,sfjk->sik', left, right, preferred_element_type=jnp.floa...]
    pallas_call x0 -> x12, Pallas kernels: none -> 21.9 us  [call(): pl.pallas_call(wrapped, out_shape=out_shape, in_specs=[pl.BlockSpec(memor...]
    ppermute x0 -> x22, waiting for transfers between devices: none -> 15.4 us  [the longest x1 12.1 us: on_device(): p_x = lax.ppermute(p, 'col', swap)]
    unnamed x2 -> x10, local copies, waits for them, and re-layouts: 1.33 us -> 4.08 us
  transfers between devices with their start and end apart: 3 -> 22, of which waited for: 3 -> 4; matrix products, arithmetic and copies ran while one was open for 1% -> 0% of each run, Pallas kernels for 0% -> 29%
where the time goes in v2:
time: 73.7 us; the launch traced here: 73.4 us
  starting transfers between devices  31.8 us (43%)
  Pallas kernels  21.9 us (30%)
  waiting for transfers between devices  15.4 us (21%)
  local copies, waits for them, and re-layouts  4.08 us (6%)
    pallas_call x12, Pallas kernels, call(): pl.pallas_call(wrapped, out_shape=out_shape, in_specs=[pl.BlockSpec(memor...  21.9 us
    ppermute x8, starting transfers between devices, on_device(): moved.append(lax.ppermute(out[d], ('col', 'layer'), perm))  13.8 us
    ppermute x1, waiting for transfers between devices, on_device(): p_x = lax.ppermute(p, 'col', swap)  12.1 us
    ppermute x6, starting transfers between devices, own_second(): lax.ppermute(out[d], 'layer', [(i, i ^ 2 * d) for i in range(layers)])  8.97 us
    unnamed x10, local copies, waits for them, and re-layouts  4.08 us
    ppermute x8, waiting for transfers between devices, on_device(): moved.append(lax.ppermute(out[d], ('col', 'layer'), perm))  3.22 us
    ppermute x1, starting transfers between devices, on_device(): p_x = lax.ppermute(p, 'col', swap)  2.94 us
    ppermute x2, starting transfers between devices, on_device(): own_sent.append(lax.ppermute(made, 'layer', pairs))  2.41 us
  transfers between devices with their start and end apart: 22, of which 4 were waited for; matrix products, arithmetic and copies ran while one was open for 0% of the time, Pallas kernels for 29%

profile of v2, /device:TPU:0, one launch (start us, length us, event | category | flops | bytes accessed | tf_op | source)
XLA Modules:
  0.0 73.4 jit_solution(3068133036049410842)
XLA Ops:
  0.0 2.9 %collective-permute-start.3 = (bf16[16,128,128]{2,1,0:T(8,128)(2,1)}, bf16[16,128,128]{2,1,0:T(8,128)(2,1)S(1)}, u32[]{:S(2)}, u32[]{:S(2)}) collective-permute-start(bf16[16,128,128]{2,1,0:T(8,128)(2,1)} %bitcast.30), channel_id=1, source_target_pairs={{0,8},{8,0},{1,9},{9,1},{2,10},{10,2},{3,11},{11,3},{4,12},{12,4},... | collective-permute-start | bytes 1572872 | tf_op jit(solution)/shard_map/ppermute | solution.py:201
  2.9 12.1 %collective-permute-done.3.refs_3_ = bf16[16,128,128]{2,1,0:T(8,128)(2,1)S(1)} collective-permute-done((bf16[16,128,128]{2,1,0:T(8,128)(2,1)}, bf16[16,128,128]{2,1,0:T(8,128)(2,1)S(1)}, u32[]{:S(2)}, u32[]{:S(2)}) %collective-permute-start.3) | collective-permute-done | bytes 524320 | tf_op jit(solution)/shard_map/ppermute | solution.py:201
  15.2 1.6 %copy-done = bf16[1,1,1,64,128,128]{5,4,3,2,1,0:T(8,128)(2,1)S(1)} copy-done((bf16[1,1,1,64,128,128]{5,4,3,2,1,0:T(8,128)(2,1)S(1)}, bf16[1,1,1,64,128,128]{5,4,3,2,1,0:T(8,128)(2,1)}, u32[]{:S(2)}) %copy-start) | copy-done | bytes 2097176
  16.8 1.0 %copy-done.2 = bf16[1,1,1,16,128,128]{5,4,3,2,1,0:T(8,128)(2,1)S(1)} copy-done((bf16[1,1,1,16,128,128]{5,4,3,2,1,0:T(8,128)(2,1)S(1)}, bf16[1,1,1,16,128,128]{5,4,3,2,1,0:T(8,128)(2,1)}, u32[]{:S(2)}) %copy-start.2) | copy-done | bytes 524312
  19.2 2.7 %shard_map.46.refs_6_ = s16[1040,128]{1,0:T(8,128)(2,1)S(1)} custom-call(s32[3]{0:T(128)S(1)} %pad_add_fusion.1.refs_0_, s32[2,16,32]{2,1,0:T(8,128)S(1)} %bitcast.35, s32[2,16,32]{2,1,0:T(8,128)S(1)} %bitcast.38, bf16[64,128,128]{2,1,0:T(8,128)(2,1)S(1)} %bitcast.24, bf16[16,128,128]{2,1,0:T(8,128)(2,1)S(1)} %bitcast.32, ...), custom_call_target="tpu_custom_call" | custom-call | flops 536870912 | bytes 3411968 | tf_op jit(solution)/shard_map/pallas_call | solution.py:178
  21.9 1.8 %collective-permute-start.5 = (s16[1040,128]{1,0:T(8,128)(2,1)S(1)}, s16[1040,128]{1,0:T(8,128)(2,1)S(1)}, u32[]{:S(2)}, u32[]{:S(2)}) collective-permute-start(s16[1040,128]{1,0:T(8,128)(2,1)S(1)} %shard_map.46.refs_6_), channel_id=1, source_target_pairs={{0,1},{1,0},{2,3},{3,2},{4,5},{5,4},{6,7},{7,6},{8,9},{9,8},{10,11... | collective-permute-start | bytes 798728 | tf_op jit(solution)/shard_map/ppermute | solution.py:236
  23.8 1.5 %collective-permute-start.2 = (s32[32,32]{1,0:T(8,128)S(1)}, s32[32,32]{1,0:T(8,128)S(1)}, u32[]{:S(2)}, u32[]{:S(2)}) collective-permute-start(s32[32,32]{1,0:T(8,128)S(1)} %pad_add_fusion), channel_id=1, source_target_pairs={{0,8},{8,0},{1,9},{9,1},{2,10},{10,2},{3,11},{11,3},{4,12},{12,4},... | collective-permute-start | bytes 12296 | tf_op jit(solution)/shard_map/ppermute | solution.py:205
  25.2 2.7 %shard_map.47.refs_6_ = s16[1040,128]{1,0:T(8,128)(2,1)S(1)} custom-call(s32[3]{0:T(128)S(1)} %pad_add_fusion.1.refs_0_, s32[2,16,32]{2,1,0:T(8,128)S(1)} %bitcast.36, s32[2,16,32]{2,1,0:T(8,128)S(1)} %bitcast.39, bf16[64,128,128]{2,1,0:T(8,128)(2,1)S(1)} %bitcast.25, bf16[16,128,128]{2,1,0:T(8,128)(2,1)S(1)} %bitcast.33, ...), custom_call_target="tpu_custom_call" | custom-call | flops 536870912 | bytes 3411968 | tf_op jit(solution)/shard_map/pallas_call | solution.py:178
  28.5 4.1 %shard_map.48 = (f32[8,128,128]{2,1,0:T(8,128)S(1)}, f32[8,128,128]{2,1,0:T(8,128)S(1)}) custom-call(s32[3]{0:T(128)S(1)} %pad_add_fusion.1.refs_0_, s32[2,16,32]{2,1,0:T(8,128)S(1)} %bitcast.37, s32[2,16,32]{2,1,0:T(8,128)S(1)} %bitcast.40, bf16[64,128,128]{2,1,0:T(8,128)(2,1)S(1)} %bitcast.26, bf16[16,128,128]{2,1,0:T(8,128)(2,1)S(1)} %bitcast.34, ...), custom_call_target="tpu_custom_call" | custom-call | flops 1073741824 | bytes 4194304 | tf_op jit(solution)/shard_map/pallas_call | solution.py:178
  33.4 2.4 %shard_map.50.refs_5_ = s16[1040,128]{1,0:T(8,128)(2,1)S(1)} custom-call(s32[3]{0:T(128)S(1)} %pad_add_fusion.1.refs_0_, s32[32,32]{1,0:T(8,128)S(1)} %collective-permute-done.2.refs_1_, bf16[64,128,128]{2,1,0:T(8,128)(2,1)S(1)} %bitcast.27, bf16[16,128,128]{2,1,0:T(8,128)(2,1)S(1)} %collective-permute-done.3.refs_3_, ...), custom_call_target="tpu_custom_call" | custom-call | flops 536870912 | bytes 3411968 | tf_op jit(solution)/shard_map/pallas_call | solution.py:178
  35.8 1.6 %collective-permute-start.17 = (s16[1040,128]{1,0:T(8,128)(2,1)S(1)}, s16[1040,128]{1,0:T(8,128)(2,1)S(1)}, u32[]{:S(2)}, u32[]{:S(2)}) collective-permute-start(s16[1040,128]{1,0:T(8,128)(2,1)S(1)} %shard_map.50.refs_5_), channel_id=1, source_target_pairs={{0,1},{1,0},{2,3},{3,2},{4,5},{5,4},{6,7},{7,6},{8,9},{9,8},{10,11... | collective-permute-start | bytes 798728 | tf_op jit(solution)/shard_map/ppermute | solution.py:254
  37.4 2.4 %shard_map.51.refs_3_ = s16[1040,128]{1,0:T(8,128)(2,1)S(1)} custom-call(s32[3]{0:T(128)S(1)} %pad_add_fusion.1.refs_0_, s32[32,32]{1,0:T(8,128)S(1)} %collective-permute-done.2.refs_1_, bf16[64,128,128]{2,1,0:T(8,128)(2,1)S(1)} %bitcast.28, bf16[16,128,128]{2,1,0:T(8,128)(2,1)S(1)} %collective-permute-done.3.refs_3_, ...), custom_call_target="tpu_custom_call" | custom-call | flops 536870912 | bytes 3411968 | tf_op jit(solution)/shard_map/pallas_call | solution.py:178
  40.3 1.6 %collective-permute-start.14 = (s16[272,128]{1,0:T(8,128)(2,1)S(1)}, s16[272,128]{1,0:T(8,128)(2,1)S(1)}, u32[]{:S(2)}, u32[]{:S(2)}) collective-permute-start(s16[272,128]{1,0:T(8,128)(2,1)S(1)} %get-tuple-element.37), channel_id=1, source_target_pairs={{0,2},{1,3},{2,0},{3,1},{4,6},{5,7},{6,4},{7,5},{8,10},{9,11},{10,... | collective-permute-start | bytes 208904 | tf_op jit(solution)/shard_map/ppermute | solution.py:243
  41.9 2.6 %collective-permute-start.15 = (s16[272,128]{1,0:T(8,128)(2,1)S(1)}, s16[272,128]{1,0:T(8,128)(2,1)S(1)}, u32[]{:S(2)}, u32[]{:S(2)}) collective-permute-start(s16[272,128]{1,0:T(8,128)(2,1)S(1)} %get-tuple-element.38), channel_id=1, source_target_pairs={{0,4},{1,5},{2,6},{3,7},{4,0},{5,1},{6,2},{7,3},{8,12},{9,13},{10,... | collective-permute-start | bytes 208904 | tf_op jit(solution)/shard_map/ppermute | solution.py:243
  45.5 1.2 %collective-permute-start.6 = (s16[272,128]{1,0:T(8,128)(2,1)S(1)}, s16[272,128]{1,0:T(8,128)(2,1)S(1)}, u32[]{:S(2)}, u32[]{:S(2)}) collective-permute-start(s16[272,128]{1,0:T(8,128)(2,1)S(1)} %get-tuple-element.29), channel_id=1, source_target_pairs={{0,2},{1,3},{2,0},{3,1},{4,6},{5,7},{6,4},{7,5},{8,10},{9,11},{10,... | collective-permute-start | bytes 208904 | tf_op jit(solution)/shard_map/ppermute | solution.py:243
  46.7 3.8 %shard_map.53 = (f32[8,128,128]{2,1,0:T(8,128)S(1)}, f32[8,128,128]{2,1,0:T(8,128)S(1)}) custom-call(s32[3]{0:T(128)S(1)} %pad_add_fusion.1.refs_0_, s32[32,32]{1,0:T(8,128)S(1)} %collective-permute-done.2.refs_1_, bf16[64,128,128]{2,1,0:T(8,128)(2,1)S(1)} %bitcast.29, bf16[16,128,128]{2,1,0:T(8,128)(2,1)S(1)} %collective-permute-done.3.refs_3_, ...), custom_call_target="tpu_custom_call" | custom-call | flops 1073741824 | bytes 4194304 | tf_op jit(solution)/shard_map/pallas_call | solution.py:178
  51.3 3.1 %collective-permute-start.7 = (s16[272,128]{1,0:T(8,128)(2,1)S(1)}, s16[272,128]{1,0:T(8,128)(2,1)S(1)}, u32[]{:S(2)}, u32[]{:S(2)}) collective-permute-start(s16[272,128]{1,0:T(8,128)(2,1)S(1)} %get-tuple-element.30), channel_id=1, source_target_pairs={{0,4},{1,5},{2,6},{3,7},{4,0},{5,1},{6,2},{7,3},{8,12},{9,13},{10,... | collective-permute-start | bytes 208904 | tf_op jit(solution)/shard_map/ppermute | solution.py:243
  54.3 2.4 %collective-permute-start.19 = (s16[272,128]{1,0:T(8,128)(2,1)S(1)}, s16[272,128]{1,0:T(8,128)(2,1)S(1)}, u32[]{:S(2)}, u32[]{:S(2)}) collective-permute-start(s16[272,128]{1,0:T(8,128)(2,1)S(1)} %get-tuple-element.42), channel_id=1, source_target_pairs={{0,12},{1,13},{2,14},{3,15},{4,8},{5,9},{6,10},{7,11},{8,4},{9,5},... | collective-permute-start | bytes 208904 | tf_op jit(solution)/shard_map/ppermute | solution.py:264
  56.7 2.8 %collective-permute-start.20 = (s16[272,128]{1,0:T(8,128)(2,1)S(1)}, s16[272,128]{1,0:T(8,128)(2,1)S(1)}, u32[]{:S(2)}, u32[]{:S(2)}) collective-permute-start(s16[272,128]{1,0:T(8,128)(2,1)S(1)} %get-tuple-element.43), channel_id=1, source_target_pairs={{0,10},{1,11},{2,8},{3,9},{4,14},{5,15},{6,12},{7,13},{8,2},{9,3},... | collective-permute-start | bytes 208904 | tf_op jit(solution)/shard_map/ppermute | solution.py:264
  59.6 1.5 %collective-permute-start.21 = (s16[272,128]{1,0:T(8,128)(2,1)S(1)}, s16[272,128]{1,0:T(8,128)(2,1)S(1)}, u32[]{:S(2)}, u32[]{:S(2)}) collective-permute-start(s16[272,128]{1,0:T(8,128)(2,1)S(1)} %get-tuple-element.44), channel_id=1, source_target_pairs={{0,8},{1,9},{2,10},{3,11},{4,12},{5,13},{6,14},{7,15},{8,0},{9,1},... | collective-permute-start | bytes 208904 | tf_op jit(solution)/shard_map/ppermute | solution.py:264
  62.1 3.6 %collective-permute-start.10 = (s16[272,128]{1,0:T(8,128)(2,1)S(1)}, s16[272,128]{1,0:T(8,128)(2,1)S(1)}, u32[]{:S(2)}, u32[]{:S(2)}) collective-permute-start(s16[272,128]{1,0:T(8,128)(2,1)S(1)} %get-tuple-element.33), channel_id=1, source_target_pairs={{0,14},{1,15},{2,12},{3,13},{4,10},{5,11},{6,8},{7,9},{8,6},{9,7},... | collective-permute-start | bytes 208904 | tf_op jit(solution)/shard_map/ppermute | solution.py:264
  65.7 2.3 %collective-permute-start.12 = (s16[272,128]{1,0:T(8,128)(2,1)S(1)}, s16[272,128]{1,0:T(8,128)(2,1)S(1)}, u32[]{:S(2)}, u32[]{:S(2)}) collective-permute-start(s16[272,128]{1,0:T(8,128)(2,1)S(1)} %get-tuple-element.35), channel_id=1, source_target_pairs={{0,10},{1,11},{2,8},{3,9},{4,14},{5,15},{6,12},{7,13},{8,2},{9,3},... | collective-permute-start | bytes 208904 | tf_op jit(solution)/shard_map/ppermute | solution.py:264
  68.0 1.2 %collective-permute-start.13 = (s16[272,128]{1,0:T(8,128)(2,1)S(1)}, s16[272,128]{1,0:T(8,128)(2,1)S(1)}, u32[]{:S(2)}, u32[]{:S(2)}) collective-permute-start(s16[272,128]{1,0:T(8,128)(2,1)S(1)} %get-tuple-element.36), channel_id=1, source_target_pairs={{0,8},{1,9},{2,10},{3,11},{4,12},{5,13},{6,14},{7,15},{8,0},{9,1},... | collective-permute-start | bytes 208904 | tf_op jit(solution)/shard_map/ppermute | solution.py:264
  69.8 2.1 %collective-permute-done.11.refs_5_ = s16[272,128]{1,0:T(8,128)(2,1)S(1)} collective-permute-done((s16[272,128]{1,0:T(8,128)(2,1)S(1)}, s16[272,128]{1,0:T(8,128)(2,1)S(1)}, u32[]{:S(2)}, u32[]{:S(2)}) %collective-permute-start.11) | collective-permute-done | bytes 69664 | tf_op jit(solution)/shard_map/ppermute | solution.py:264
  (45 shorter events, 8.2 us)
Async XLA Ops:
  0.0 15.1 %collective-permute-start.3 = (bf16[16,128,128]{2,1,0:T(8,128)(2,1)}, bf16[16,128,128]{2,1,0:T(8,128)(2,1)S(1)}, u32[]{:S(2)}, u32[]{:S(2)}) collective-permute-start(bf16[16,128,128]{2,1,0:T(8,128)(2,1)} %bitcast.30), channel_id=1, source_target_pairs={{0,8},{8,0},{1,9},{9,1},{2,10},{10,2},{3,11},{11,3},{4,12},{12,4},... | collective-permute-start | bytes 1572872 | tf_op jit(solution)/shard_map/ppermute | solution.py:201
  2.9 12.2 %collective-permute-start = (bf16[16,128,128]{2,1,0:T(8,128)(2,1)}, bf16[16,128,128]{2,1,0:T(8,128)(2,1)S(1)}, u32[]{:S(2)}, u32[]{:S(2)}) collective-permute-start(bf16[16,128,128]{2,1,0:T(8,128)(2,1)} %bitcast.31), channel_id=1, source_target_pairs={{0,16},{16,0},{1,17},{17,1},{2,18},{18,2},{3,19},{19,3},{4,20},{20... | collective-permute-start | bytes 1572872 | tf_op jit(solution)/shard_map/ppermute | solution.py:202
  15.1 18.3 %collective-permute-start.4 = (bf16[16,128,128]{2,1,0:T(8,128)(2,1)S(1)}, bf16[16,128,128]{2,1,0:T(8,128)(2,1)S(1)}, u32[]{:S(2)}, u32[]{:S(2)}) collective-permute-start(bf16[16,128,128]{2,1,0:T(8,128)(2,1)S(1)} %collective-permute-done.3.refs_3_), channel_id=1, source_target_pairs={{0,16},{16,0},{1,17},{17,1},{2,18},{18,2},{3,19},{19,3},{4,20},{20... | collective-permute-start | bytes 1572872 | tf_op jit(solution)/shard_map/ppermute | solution.py:206
  15.2 1.6 %copy-start = (bf16[1,1,1,64,128,128]{5,4,3,2,1,0:T(8,128)(2,1)S(1)}, bf16[1,1,1,64,128,128]{5,4,3,2,1,0:T(8,128)(2,1)}, u32[]{:S(2)}) copy-start(bf16[1,1,1,64,128,128]{5,4,3,2,1,0:T(8,128)(2,1)} %param.4) | copy-start | bytes 6291460
  21.9 10.7 %collective-permute-start.5 = (s16[1040,128]{1,0:T(8,128)(2,1)S(1)}, s16[1040,128]{1,0:T(8,128)(2,1)S(1)}, u32[]{:S(2)}, u32[]{:S(2)}) collective-permute-start(s16[1040,128]{1,0:T(8,128)(2,1)S(1)} %shard_map.46.refs_6_), channel_id=1, source_target_pairs={{0,1},{1,0},{2,3},{3,2},{4,5},{5,4},{6,7},{7,6},{8,9},{9,8},{10,11... | collective-permute-start | bytes 798728 | tf_op jit(solution)/shard_map/ppermute | solution.py:236
  23.8 9.6 %collective-permute-start.2 = (s32[32,32]{1,0:T(8,128)S(1)}, s32[32,32]{1,0:T(8,128)S(1)}, u32[]{:S(2)}, u32[]{:S(2)}) collective-permute-start(s32[32,32]{1,0:T(8,128)S(1)} %pad_add_fusion), channel_id=1, source_target_pairs={{0,8},{8,0},{1,9},{9,1},{2,10},{10,2},{3,11},{11,3},{4,12},{12,4},... | collective-permute-start | bytes 12296 | tf_op jit(solution)/shard_map/ppermute | solution.py:205
  27.9 5.4 %copy-start.1 = (bf16[1,1,1,64,128,128]{5,4,3,2,1,0:T(8,128)(2,1)S(1)}, bf16[1,1,1,64,128,128]{5,4,3,2,1,0:T(8,128)(2,1)}, u32[]{:S(2)}) copy-start(bf16[1,1,1,64,128,128]{5,4,3,2,1,0:T(8,128)(2,1)} %param.4) | copy-start | bytes 6291460
  27.9 16.6 %collective-permute-start.1 = (s16[1040,128]{1,0:T(8,128)(2,1)S(1)}, s16[1040,128]{1,0:T(8,128)(2,1)S(1)}, u32[]{:S(2)}, u32[]{:S(2)}) collective-permute-start(s16[1040,128]{1,0:T(8,128)(2,1)S(1)} %shard_map.47.refs_6_), channel_id=1, source_target_pairs={{0,1},{1,0},{2,3},{3,2},{4,5},{5,4},{6,7},{7,6},{8,9},{9,8},{10,11... | collective-permute-start | bytes 798728 | tf_op jit(solution)/shard_map/ppermute | solution.py:236
  35.8 9.7 %collective-permute-start.17 = (s16[1040,128]{1,0:T(8,128)(2,1)S(1)}, s16[1040,128]{1,0:T(8,128)(2,1)S(1)}, u32[]{:S(2)}, u32[]{:S(2)}) collective-permute-start(s16[1040,128]{1,0:T(8,128)(2,1)S(1)} %shard_map.50.refs_5_), channel_id=1, source_target_pairs={{0,1},{1,0},{2,3},{3,2},{4,5},{5,4},{6,7},{7,6},{8,9},{9,8},{10,11... | collective-permute-start | bytes 798728 | tf_op jit(solution)/shard_map/ppermute | solution.py:254
  39.8 19.8 %collective-permute-start.9 = (s16[1040,128]{1,0:T(8,128)(2,1)S(1)}, s16[1040,128]{1,0:T(8,128)(2,1)S(1)}, u32[]{:S(2)}, u32[]{:S(2)}) collective-permute-start(s16[1040,128]{1,0:T(8,128)(2,1)S(1)} %shard_map.51.refs_3_), channel_id=1, source_target_pairs={{0,1},{1,0},{2,3},{3,2},{4,5},{5,4},{6,7},{7,6},{8,9},{9,8},{10,11... | collective-permute-start | bytes 798728 | tf_op jit(solution)/shard_map/ppermute | solution.py:254
  40.3 10.9 %collective-permute-start.14 = (s16[272,128]{1,0:T(8,128)(2,1)S(1)}, s16[272,128]{1,0:T(8,128)(2,1)S(1)}, u32[]{:S(2)}, u32[]{:S(2)}) collective-permute-start(s16[272,128]{1,0:T(8,128)(2,1)S(1)} %get-tuple-element.37), channel_id=1, source_target_pairs={{0,2},{1,3},{2,0},{3,1},{4,6},{5,7},{6,4},{7,5},{8,10},{9,11},{10,... | collective-permute-start | bytes 208904 | tf_op jit(solution)/shard_map/ppermute | solution.py:243
  41.9 12.4 %collective-permute-start.15 = (s16[272,128]{1,0:T(8,128)(2,1)S(1)}, s16[272,128]{1,0:T(8,128)(2,1)S(1)}, u32[]{:S(2)}, u32[]{:S(2)}) collective-permute-start(s16[272,128]{1,0:T(8,128)(2,1)S(1)} %get-tuple-element.38), channel_id=1, source_target_pairs={{0,4},{1,5},{2,6},{3,7},{4,0},{5,1},{6,2},{7,3},{8,12},{9,13},{10,... | collective-permute-start | bytes 208904 | tf_op jit(solution)/shard_map/ppermute | solution.py:243
  44.5 9.8 %collective-permute-start.16 = (s16[272,128]{1,0:T(8,128)(2,1)S(1)}, s16[272,128]{1,0:T(8,128)(2,1)S(1)}, u32[]{:S(2)}, u32[]{:S(2)}) collective-permute-start(s16[272,128]{1,0:T(8,128)(2,1)S(1)} %get-tuple-element.39), channel_id=1, source_target_pairs={{0,6},{1,7},{2,4},{3,5},{4,2},{5,3},{6,0},{7,1},{8,14},{9,15},{10,... | collective-permute-start | bytes 208904 | tf_op jit(solution)/shard_map/ppermute | solution.py:243
  45.5 11.3 %collective-permute-start.6 = (s16[272,128]{1,0:T(8,128)(2,1)S(1)}, s16[272,128]{1,0:T(8,128)(2,1)S(1)}, u32[]{:S(2)}, u32[]{:S(2)}) collective-permute-start(s16[272,128]{1,0:T(8,128)(2,1)S(1)} %get-tuple-element.29), channel_id=1, source_target_pairs={{0,2},{1,3},{2,0},{3,1},{4,6},{5,7},{6,4},{7,5},{8,10},{9,11},{10,... | collective-permute-start | bytes 208904 | tf_op jit(solution)/shard_map/ppermute | solution.py:243
  51.3 10.6 %collective-permute-start.7 = (s16[272,128]{1,0:T(8,128)(2,1)S(1)}, s16[272,128]{1,0:T(8,128)(2,1)S(1)}, u32[]{:S(2)}, u32[]{:S(2)}) collective-permute-start(s16[272,128]{1,0:T(8,128)(2,1)S(1)} %get-tuple-element.30), channel_id=1, source_target_pairs={{0,4},{1,5},{2,6},{3,7},{4,0},{5,1},{6,2},{7,3},{8,12},{9,13},{10,... | collective-permute-start | bytes 208904 | tf_op jit(solution)/shard_map/ppermute | solution.py:243
  54.3 7.8 %collective-permute-start.18 = (s16[272,128]{1,0:T(8,128)(2,1)S(1)}, s16[272,128]{1,0:T(8,128)(2,1)S(1)}, u32[]{:S(2)}, u32[]{:S(2)}) collective-permute-start(s16[272,128]{1,0:T(8,128)(2,1)S(1)} %get-tuple-element.41), channel_id=1, source_target_pairs={{0,14},{1,15},{2,12},{3,13},{4,10},{5,11},{6,8},{7,9},{8,6},{9,7},... | collective-permute-start | bytes 208904 | tf_op jit(solution)/shard_map/ppermute | solution.py:264
  54.3 11.4 %collective-permute-start.19 = (s16[272,128]{1,0:T(8,128)(2,1)S(1)}, s16[272,128]{1,0:T(8,128)(2,1)S(1)}, u32[]{:S(2)}, u32[]{:S(2)}) collective-permute-start(s16[272,128]{1,0:T(8,128)(2,1)S(1)} %get-tuple-element.42), channel_id=1, source_target_pairs={{0,12},{1,13},{2,14},{3,15},{4,8},{5,9},{6,10},{7,11},{8,4},{9,5},... | collective-permute-start | bytes 208904 | tf_op jit(solution)/shard_map/ppermute | solution.py:264
  56.7 9.0 %collective-permute-start.20 = (s16[272,128]{1,0:T(8,128)(2,1)S(1)}, s16[272,128]{1,0:T(8,128)(2,1)S(1)}, u32[]{:S(2)}, u32[]{:S(2)}) collective-permute-start(s16[272,128]{1,0:T(8,128)(2,1)S(1)} %get-tuple-element.43), channel_id=1, source_target_pairs={{0,10},{1,11},{2,8},{3,9},{4,14},{5,15},{6,12},{7,13},{8,2},{9,3},... | collective-permute-start | bytes 208904 | tf_op jit(solution)/shard_map/ppermute | solution.py:264
  59.6 8.4 %collective-permute-start.21 = (s16[272,128]{1,0:T(8,128)(2,1)S(1)}, s16[272,128]{1,0:T(8,128)(2,1)S(1)}, u32[]{:S(2)}, u32[]{:S(2)}) collective-permute-start(s16[272,128]{1,0:T(8,128)(2,1)S(1)} %get-tuple-element.44), channel_id=1, source_target_pairs={{0,8},{1,9},{2,10},{3,11},{4,12},{5,13},{6,14},{7,15},{8,0},{9,1},... | collective-permute-start | bytes 208904 | tf_op jit(solution)/shard_map/ppermute | solution.py:264
  61.8 7.5 %collective-permute-start.8 = (s16[272,128]{1,0:T(8,128)(2,1)S(1)}, s16[272,128]{1,0:T(8,128)(2,1)S(1)}, u32[]{:S(2)}, u32[]{:S(2)}) collective-permute-start(s16[272,128]{1,0:T(8,128)(2,1)S(1)} %get-tuple-element.31), channel_id=1, source_target_pairs={{0,6},{1,7},{2,4},{3,5},{4,2},{5,3},{6,0},{7,1},{8,14},{9,15},{10,... | collective-permute-start | bytes 208904 | tf_op jit(solution)/shard_map/ppermute | solution.py:243
  62.1 7.6 %collective-permute-start.10 = (s16[272,128]{1,0:T(8,128)(2,1)S(1)}, s16[272,128]{1,0:T(8,128)(2,1)S(1)}, u32[]{:S(2)}, u32[]{:S(2)}) collective-permute-start(s16[272,128]{1,0:T(8,128)(2,1)S(1)} %get-tuple-element.33), channel_id=1, source_target_pairs={{0,14},{1,15},{2,12},{3,13},{4,10},{5,11},{6,8},{7,9},{8,6},{9,7},... | collective-permute-start | bytes 208904 | tf_op jit(solution)/shard_map/ppermute | solution.py:264
  65.7 6.1 %collective-permute-start.11 = (s16[272,128]{1,0:T(8,128)(2,1)S(1)}, s16[272,128]{1,0:T(8,128)(2,1)S(1)}, u32[]{:S(2)}, u32[]{:S(2)}) collective-permute-start(s16[272,128]{1,0:T(8,128)(2,1)S(1)} %get-tuple-element.34), channel_id=1, source_target_pairs={{0,12},{1,13},{2,14},{3,15},{4,8},{5,9},{6,10},{7,11},{8,4},{9,5},... | collective-permute-start | bytes 208904 | tf_op jit(solution)/shard_map/ppermute | solution.py:264
  65.7 6.1 %collective-permute-start.12 = (s16[272,128]{1,0:T(8,128)(2,1)S(1)}, s16[272,128]{1,0:T(8,128)(2,1)S(1)}, u32[]{:S(2)}, u32[]{:S(2)}) collective-permute-start(s16[272,128]{1,0:T(8,128)(2,1)S(1)} %get-tuple-element.35), channel_id=1, source_target_pairs={{0,10},{1,11},{2,8},{3,9},{4,14},{5,15},{6,12},{7,13},{8,2},{9,3},... | collective-permute-start | bytes 208904 | tf_op jit(solution)/shard_map/ppermute | solution.py:264
  68.0 4.5 %collective-permute-start.13 = (s16[272,128]{1,0:T(8,128)(2,1)S(1)}, s16[272,128]{1,0:T(8,128)(2,1)S(1)}, u32[]{:S(2)}, u32[]{:S(2)}) collective-permute-start(s16[272,128]{1,0:T(8,128)(2,1)S(1)} %get-tuple-element.36), channel_id=1, source_target_pairs={{0,8},{1,9},{2,10},{3,11},{4,12},{5,13},{6,14},{7,15},{8,0},{9,1},... | collective-permute-start | bytes 208904 | tf_op jit(solution)/shard_map/ppermute | solution.py:264
  (3 other events, 2.5 us)

commit v3 on v2

v3 whole, which is shorter than its diff:
```python
import jax
import jax.numpy as jnp
from jax import lax
from jax.experimental import pallas as pl
from jax.experimental.pallas import tpu as pltpu
from jax.sharding import PartitionSpec as P

PEAK = 32766.0
ROWS = 16
GROUP = 4
SMEM = pltpu.MemorySpace.SMEM
VMEM = pltpu.MemorySpace.VMEM


def head_rows(count):
    return -(-count // ROWS) * ROWS


def message(count, width):
    return jax.ShapeDtypeStruct((count * width + head_rows(count), width), jnp.int16)


def encode(tile):
    top = jnp.max(jnp.abs(tile), axis=0, keepdims=True)
    power = jnp.floor(jnp.log2(jnp.maximum(top, 2.0**-100)) + 0.001) + 1.0
    scaled = jnp.round(tile * (jnp.exp2(-power) * PEAK))
    return scaled.astype(jnp.int32).astype(jnp.int16), power.astype(jnp.int32)


def new_head(count, width):
    return jnp.zeros((head_rows(count), width), jnp.int32)


def rows_at(slot, width):
    start = slot * width
    return pl.ds(start if isinstance(start, int) else pl.multiple_of(start, width), width)


def put_tile(ref, slot, tile, head):
    coded, power = encode(tile)
    ref[rows_at(slot, tile.shape[0]), :] = coded
    rows = lax.broadcasted_iota(jnp.int32, head.shape, 0)
    return jnp.where(rows == slot, power, head)


def put_head(ref, head):
    ref[pl.ds(ref.shape[0] - head.shape[0], head.shape[0]), :] = head.astype(jnp.int16)


def get_head(ref, count):
    rows = head_rows(count)
    return ref[pl.ds(ref.shape[0] - rows, rows), :].astype(jnp.int32)


def get_tile(ref, slot, head):
    rows = lax.broadcasted_iota(jnp.int32, head.shape, 0)
    power = jnp.sum(jnp.where(rows == slot, head, 0), axis=0, keepdims=True)
    coded = ref[rows_at(slot, ref.shape[-1]), :]
    return coded.astype(jnp.int32).astype(jnp.float32) * (jnp.exp2(power.astype(jnp.float32)) * (1.0 / PEAK))


def product(a_ref, p_ref, look, fan):
    chosen = [look(f) for f in range(fan)]
    left = jnp.concatenate([a_ref[pa] for pa, _ in chosen], axis=1)
    right = jnp.concatenate([p_ref[pp] for _, pp in chosen], axis=0)
    return jnp.dot(left, right, preferred_element_type=jnp.float32)


def insert(rest, at, bit):
    low = rest & ((1 << at) - 1)
    return ((rest >> at) << (at + 1)) | (bit << at) | low


def finder(me_ref, index_refs, fan):
    if len(index_refs) == 2:
        ia_ref, ip_ref = index_refs
        col = me_ref[1]
        return lambda t: lambda f: (ia_ref[col, f, t], ip_ref[col, f, t])
    (both_ref,) = index_refs
    return lambda t: lambda f: (both_ref[f, t], both_ref[fan + f, t])


def send_kernel(n_index, n_p, fan, count, chunk, bit):
    first, size = chunk

    def kernel(me_ref, *refs):
        find = finder(me_ref, refs[:n_index], fan)
        a_ref = refs[n_index]
        p_refs = refs[n_index + 1 : n_index + 1 + n_p]
        out_ref = refs[n_index + 1 + n_p]
        width = out_ref.shape[-1]
        if n_p == 2:
            p_ref = refs[-1]
            held = p_refs[0].shape[0]
            p_ref[pl.ds(me_ref[0] * held, held)] = p_refs[0][...]
            p_ref[pl.ds((1 - me_ref[0]) * held, held)] = p_refs[1][...]
        else:
            (p_ref,) = p_refs
        side = 1 - ((me_ref[2] >> bit) & 1)
        total = out_ref.shape[0] // width

        def body(step, head):
            for k in range(GROUP):
                slot = step * GROUP + k
                layer = insert(slot // size, bit, side)
                tile = product(a_ref, p_ref, find(layer * count + first + slot % size), fan)
                head = put_tile(out_ref, slot, tile, head)
            return head

        put_head(out_ref, lax.fori_loop(0, total // GROUP, body, new_head(total, width)))

    return kernel


def keep_kernel(n_index, fan, count, chunks, bit):
    def kernel(me_ref, *refs):
        find = finder(me_ref, refs[:n_index], fan)
        a_ref, p_ref = refs[n_index : n_index + 2]
        side = (me_ref[2] >> bit) & 1
        for (first, size), out_ref in zip(chunks, refs[n_index + 2 :]):

            def body(step, _):
                for k in range(GROUP):
                    slot = step * GROUP + k
                    layer = insert(slot // size, bit, side)
                    out_ref[slot] = product(a_ref, p_ref, find(layer * count + first + slot % size), fan)
                return 0

            lax.fori_loop(0, out_ref.shape[0] // GROUP, body, 0)

    return kernel


def add_kernel(sizes, rest, bit, keeps):
    at = rest.index(bit)
    full = sum(sizes)
    halves = 1 << (len(rest) - 1)

    def kernel(me_ref, *refs):
        n = len(sizes)
        kept_refs, in_refs, (sent_ref, stay_ref) = refs[:n], refs[n : 2 * n], refs[2 * n : 2 * n + 2]
        width = sent_ref.shape[-1]
        mine = (me_ref[2] >> bit) & 1
        heads = [get_head(ref, ref.shape[0] // width) for ref in in_refs]

        def sums(place):
            for size, kept_ref, in_ref, head in zip(sizes, kept_refs, in_refs, heads):
                for i in range(size):
                    slot = place * size + i
                    yield kept_ref[slot] + get_tile(in_ref, slot, head)

        def send(ref, side):
            def body(half, head):
                for i, tile in enumerate(sums(insert(half, at, side))):
                    head = put_tile(ref, half * full + i, tile, head)
                return head

            put_head(ref, lax.fori_loop(0, halves, body, new_head(halves * full, width), unroll=halves <= 4))

        send(sent_ref, 1 - mine)
        if keeps:

            def body(half, _):
                for i, tile in enumerate(sums(insert(half, at, mine))):
                    stay_ref[half * full + i] = tile
                return 0

            lax.fori_loop(0, halves, body, 0, unroll=halves <= 4)
        else:
            send(stay_ref, mine)

    return kernel


def last_kernel(first, size, n_own, n_messages, n_before):
    def kernel(own_ref, own_in_ref, *refs):
        in_refs, before_refs, out_ref = refs[:n_messages], refs[n_messages:-1], refs[-1]
        at = 0
        for ref in before_refs:
            out_ref[pl.ds(at, ref.shape[0])] = ref[...]
            at += ref.shape[0]
        own_head = get_head(own_in_ref, n_own)
        heads = [get_head(ref, size) for ref in in_refs]
        for i in range(size):
            total = own_ref[first + i] + get_tile(own_in_ref, first + i, own_head)
            for ref, head in zip(in_refs, heads):
                total += get_tile(ref, i, head)
            out_ref[at + i] = total.astype(out_ref.dtype)

    return kernel


def call(kernel, out_shape, smem, vmem, after=(), scratch=(), flops=0):
    n_real = len(smem) + len(vmem)

    def wrapped(*refs):
        kernel(*refs[:n_real], *refs[n_real + len(after) :])

    return pl.pallas_call(
        wrapped,
        out_shape=out_shape,
        in_specs=[pl.BlockSpec(memory_space=SMEM)] * len(smem)
        + [pl.BlockSpec(memory_space=VMEM)] * len(vmem)
        + [pl.BlockSpec(memory_space=pl.ANY)] * len(after),
        out_specs=jax.tree.map(lambda _: pl.BlockSpec(memory_space=VMEM), out_shape),
        scratch_shapes=list(scratch),
        compiler_params=pltpu.CompilerParams(vmem_limit_bytes=40 * 2**20),
        cost_estimate=pl.CostEstimate(flops=1, bytes_accessed=1, transcendentals=0),
    )(*smem, *vmem, *after)


def hold(x, after):
    def kernel(*refs):
        pass

    return pl.pallas_call(
        kernel,
        out_shape=jax.ShapeDtypeStruct(x.shape, x.dtype),
        in_specs=[pl.BlockSpec(memory_space=pl.ANY)] * (1 + len(after)),
        out_specs=pl.BlockSpec(memory_space=pl.ANY),
        input_output_aliases={0: 0},
    )(x, *after)


def on_device(a_tiles, p_tiles, pair_a, pair_p):
    a, p = a_tiles[0, 0, 0], p_tiles[0, 0, 0]
    ia, ip = jnp.swapaxes(pair_a[0, 0, 0], 1, 2), jnp.swapaxes(pair_p[0, 0, 0], 1, 2)
    fan, slots = ia.shape[1:]
    held, width = p.shape[0], p.shape[-1]
    layers = lax.axis_size("layer")
    bits = layers.bit_length() - 1
    count = slots // layers
    swap = [(0, 1), (1, 0)]
    me = jnp.stack([lax.axis_index("row"), lax.axis_index("col"), lax.axis_index("layer")]).astype(jnp.int32)

    half = count // 2
    chunks = [(0, half), (half, count - half)]
    flops = layers * half * fan * width**3

    def floats(size):
        return jax.ShapeDtypeStruct((size, width, width), jnp.float32)

    def exchange(x, bit):
        return lax.ppermute(x, "layer", [(i, i ^ (1 << bit)) for i in range(layers)])

    def cross(x, bit):
        flip = 0 if bit is None else 1 << bit
        perm = [(c * layers + i, (1 - c) * layers + (i ^ flip)) for c in range(2) for i in range(layers)]
        return lax.ppermute(x, ("col", "layer"), perm)

    def start(smem, vmem, chunk, bit, after):
        shapes = [message(layers // 2 * chunk[1], width), jax.ShapeDtypeStruct((2 * held, width, width), p.dtype)]
        return call(send_kernel(len(smem) - 1, 2, fan, count, chunk, bit), shapes, smem, vmem, after, (), flops)

    def send(smem, vmem, chunk, bit, after):
        shape = message(layers // 2 * chunk[1], width)
        return call(send_kernel(len(smem) - 1, 1, fan, count, chunk, bit), shape, smem, vmem, after, (), flops)

    def keep(smem, vmem, bit, after):
        shapes = [floats(layers // 2 * size) for _, size in chunks]
        return call(keep_kernel(len(smem) - 1, fan, count, chunks, bit), shapes, smem, vmem, after, (), 2 * flops)

    def add(kept, came, sizes, rest, bit, keeps, after):
        n = sum(sizes) << (len(rest) - 1)
        shapes = [message(n, width), floats(n) if keeps else message(n, width)]
        return call(add_kernel(sizes, rest, bit, keeps), shapes, (me,), (*kept, *came), after)

    p_x = lax.ppermute(p, "col", swap)
    p_r = lax.ppermute(p, "row", swap)
    far = 1 - lax.axis_index("col")
    lists_x = lax.ppermute(jnp.concatenate([ia[far], ip[far]], axis=0), "col", swap)
    own_bits = [*range(1, bits), 0]
    gate = call(lambda *refs: None, jax.ShapeDtypeStruct((8, width), jnp.float32), (ia, ip), (a, p))
    smem, bit = (me, ia, ip), own_bits[0]
    made, joined = start(smem, (a, p, p_r), chunks[0], bit, (gate,))
    own_sent = [exchange(made, bit)]
    made = send(smem, (a, joined), chunks[1], bit, (made,))
    own_sent.append(exchange(made, bit))
    own_kept = keep(smem, (a, joined), bit, (made,))

    p_x = hold(p_x, (own_kept[0], own_sent[0], lists_x))
    p_xr = lax.ppermute(p_x, "row", swap)

    smem, bit = (me, lists_x), 0
    made, joined = start(smem, (a, p_x, p_xr), chunks[0], bit, ())
    other_sent = [exchange(made, bit)]
    made = send(smem, (a, joined), chunks[1], bit, (made,))
    other_sent.append(exchange(made, bit))
    rest = sorted(own_bits[1:])
    sent, own_kept = add(own_kept, own_sent, [s for _, s in chunks], rest, own_bits[1], True, (made,))
    own_sent = exchange(sent, own_bits[1])
    other_kept = keep(smem, (a, joined), bit, (sent,))

    streams = [(other_kept[n], other_sent[n]) for n in range(len(chunks))]
    rest = list(range(1, bits))
    after = ()
    for b in range(1, bits - 1):
        for n, (kept, came) in enumerate(streams):
            sent, kept = add((kept,), (came,), [chunks[n][1]], rest, b, True, after)
            after = (sent,)
            streams[n] = (kept, exchange(sent, b))
            if n == 0 and len(own_bits) > 2:
                own_rest = sorted(own_bits[2:])
                sent, own_kept = add((own_kept,), (own_sent,), [count], own_rest, own_bits[2], True, after)
                own_sent = exchange(sent, own_bits[2])
                own_bits = own_bits[:2] + own_bits[3:]
                after = (sent,)
        rest.remove(b)
    for b in own_bits[2:]:
        own_rest = sorted(own_bits[own_bits.index(b) :])
        sent, own_kept = add((own_kept,), (own_sent,), [count], own_rest, b, True, after)
        own_sent = exchange(sent, b)
        after = (sent,)

    moved = []
    for n, (kept, came) in enumerate(streams):
        sent, stay = add((kept,), (came,), [chunks[n][1]], rest, rest[0], False, after)
        after = (sent,)
        moved.append((cross(sent, rest[0]), cross(stay, None)))
    result = ()
    for n, (first, size) in enumerate(chunks):
        final = n == len(chunks) - 1
        shape = jax.ShapeDtypeStruct((count if final else size, width, width), jnp.bfloat16)
        kernel = last_kernel(first, size, count, len(moved[n]), len(result))
        result = (call(kernel, shape, (), (own_kept, own_sent, *moved[n], *result)),)
    return result[0][None, None]


def solution(mesh):
    spec = P("row", "col", "layer", None, None, None)
    return jax.shard_map(
        on_device,
        mesh=mesh,
        in_specs=(spec,) * 4,
        out_specs=P("row", "col", "layer", None, None),
        check_vma=False,
    )
```

time: 73.7 us -> 67.3 us (0.913)
  starting transfers between devices: 31.8 us -> 17.5 us
  local copies, waits for them, and re-layouts: 4.08 us -> 9.9 us
  Pallas kernels: 21.9 us -> 25.2 us
  waiting for transfers between devices: 15.4 us -> 13.9 us
    ppermute x19 -> x13, starting transfers between devices: 28.8 us -> 14.6 us  [the longest x8 8.06 us: exchange(): return lax.ppermute(x, 'layer', [(i, i ^ 1 << bit) for i in range(layers)])]
    ppermute x1, waiting for transfers between devices: 12.1 us -> 0.01 us  [on_device(): p_x = lax.ppermute(p, 'col', swap)]
    ppermute x19 -> x13, waiting for transfers between devices: 3.25 us -> 11.9 us  [the longest x8 6.92 us: exchange(): return lax.ppermute(x, 'layer', [(i, i ^ 1 << bit) for i in range(layers)])]
    unnamed x10 -> x34, local copies, waits for them, and re-layouts: 4.08 us -> 9.9 us
    pallas_call x12 -> x15, Pallas kernels: 21.9 us -> 25.2 us  [call(): pl.pallas_call(wrapped, out_shape=out_shape, in_specs=[pl.BlockSpec(memor...]
    ppermute x1, waiting for transfers between devices: 0.01 us -> 2.05 us  [on_device(): p_xr = lax.ppermute(p_x, 'row', swap)]
  transfers between devices with their start and end apart: 22 -> 16, of which waited for: 4 -> 5; matrix products, arithmetic and copies ran while one was open for 0% -> 0% of each run, Pallas kernels for 29% -> 37%
where the time goes in v3:
time: 67.3 us; the launch traced here: 66.8 us
  Pallas kernels  25.2 us (37%)
  starting transfers between devices  17.5 us (26%)
  waiting for transfers between devices  13.9 us (21%)
  local copies, waits for them, and re-layouts  9.9 us (15%)
    pallas_call x15, Pallas kernels, call(): pl.pallas_call(wrapped, out_shape=out_shape, in_specs=[pl.BlockSpec(memor...  25.2 us
    unnamed x34, local copies, waits for them, and re-layouts  9.9 us
    ppermute x8, starting transfers between devices, exchange(): return lax.ppermute(x, 'layer', [(i, i ^ 1 << bit) for i in range(layers)])  8.06 us
    ppermute x8, waiting for transfers between devices, exchange(): return lax.ppermute(x, 'layer', [(i, i ^ 1 << bit) for i in range(layers)])  6.92 us
    ppermute x4, starting transfers between devices, cross(): return lax.ppermute(x, ('col', 'layer'), perm)  5.98 us
    ppermute x4, waiting for transfers between devices, cross(): return lax.ppermute(x, ('col', 'layer'), perm)  4.94 us
    ppermute x1, starting transfers between devices, on_device(): p_x = lax.ppermute(p, 'col', swap)  2.49 us
    ppermute x1, waiting for transfers between devices, on_device(): p_xr = lax.ppermute(p_x, 'row', swap)  2.05 us
  transfers between devices with their start and end apart: 16, of which 5 were waited for; matrix products, arithmetic and copies ran while one was open for 0% of the time, Pallas kernels for 37%

profile of v3, /device:TPU:0, one launch (start us, length us, event | category | flops | bytes accessed | tf_op | source)
XLA Modules:
  0.0 66.8 jit_solution(7978919236455770146)
XLA Ops:
  0.5 2.5 %collective-permute-start.4 = (bf16[16,128,128]{2,1,0:T(8,128)(2,1)}, bf16[16,128,128]{2,1,0:T(8,128)(2,1)}, u32[]{:S(2)}, u32[]{:S(2)}) collective-permute-start(bf16[16,128,128]{2,1,0:T(8,128)(2,1)} %bitcast.32), channel_id=1, source_target_pairs={{0,8},{8,0},{1,9},{9,1},{2,10},{10,2},{3,11},{11,3},{4,12},{12,4},... | collective-permute-start | bytes 1572872 | tf_op jit(solution)/shard_map/ppermute | solution.py:268
  2.9 1.6 %copy-done = bf16[1,1,1,64,128,128]{5,4,3,2,1,0:T(8,128)(2,1)S(1)} copy-done((bf16[1,1,1,64,128,128]{5,4,3,2,1,0:T(8,128)(2,1)S(1)}, bf16[1,1,1,64,128,128]{5,4,3,2,1,0:T(8,128)(2,1)}, u32[]{:S(2)}) %copy-start) | copy-done | bytes 2097176
  4.5 1.0 %copy-done.4 = bf16[1,1,1,16,128,128]{5,4,3,2,1,0:T(8,128)(2,1)S(1)} copy-done((bf16[1,1,1,16,128,128]{5,4,3,2,1,0:T(8,128)(2,1)S(1)}, bf16[1,1,1,16,128,128]{5,4,3,2,1,0:T(8,128)(2,1)}, u32[]{:S(2)}) %copy-start.4) | copy-done | bytes 524312
  7.0 1.1 %shard_map.46.refs_6_ = f32[8,128]{1,0:T(8,128)S(1)} custom-call(s32[2,16,32]{2,1,0:T(8,128)S(1)} %bitcast.35, s32[2,16,32]{2,1,0:T(8,128)S(1)} %bitcast.39, bf16[64,128,128]{2,1,0:T(8,128)(2,1)S(1)} %bitcast.24, bf16[16,128,128]{2,1,0:T(8,128)(2,1)S(1)} %bitcast.33), custom_call_target="tpu_custom_call" | custom-call | flops 1 | bytes 1 | tf_op jit(solution)/shard_map/pallas_call | solution.py:199
  9.0 1.0 %copy-done.5 = bf16[1,1,1,16,128,128]{5,4,3,2,1,0:T(8,128)(2,1)S(1)} copy-done((bf16[1,1,1,16,128,128]{5,4,3,2,1,0:T(8,128)(2,1)S(1)}, bf16[1,1,1,16,128,128]{5,4,3,2,1,0:T(8,128)(2,1)}, u32[]{:S(2)}) %copy-start.5) | copy-done | bytes 524312
  10.1 1.0 %copy-done.9 = bf16[16,128,128]{2,1,0:T(8,128)(2,1)S(1)} copy-done((bf16[16,128,128]{2,1,0:T(8,128)(2,1)S(1)}, bf16[16,128,128]{2,1,0:T(8,128)(2,1)}, u32[]{:S(2)}) %copy-start.9) | copy-done | bytes 524312
  11.1 3.4 %shard_map.47 = (s16[1040,128]{1,0:T(8,128)(2,1)}, bf16[32,128,128]{2,1,0:T(8,128)(2,1)S(1)}) custom-call(s32[3]{0:T(128)S(1)} %pad_add_fusion.1.refs_0_, s32[2,16,32]{2,1,0:T(8,128)S(1)} %bitcast.36, s32[2,16,32]{2,1,0:T(8,128)S(1)} %bitcast.40, bf16[64,128,128]{2,1,0:T(8,128)(2,1)S(1)} %bitcast.25, bf16[16,128,128]{2,1,0:T(8,128)(2,1)S(1)} %bitcast.34, ...), custom_call_target="tpu_custom_call" | custom-call | flops 1 | bytes 1 | tf_op jit(solution)/shard_map/pallas_call | solution.py:199
  14.4 1.6 %collective-permute-start.1 = (s16[1040,128]{1,0:T(8,128)(2,1)}, s16[1040,128]{1,0:T(8,128)(2,1)}, u32[]{:S(2)}, u32[]{:S(2)}) collective-permute-start(s16[1040,128]{1,0:T(8,128)(2,1)} %get-tuple-element.26.refs_5_), channel_id=1, source_target_pairs={{0,2},{1,3},{2,0},{3,1},{4,6},{5,7},{6,4},{7,5},{8,10},{9,11},{10,... | collective-permute-start | bytes 798728 | tf_op jit(solution)/shard_map/ppermute | solution.py:244
  16.6 2.6 %shard_map.48.refs_5_ = s16[1040,128]{1,0:T(8,128)(2,1)S(1)} custom-call(s32[3]{0:T(128)S(1)} %pad_add_fusion.1.refs_0_, s32[2,16,32]{2,1,0:T(8,128)S(1)} %bitcast.37, s32[2,16,32]{2,1,0:T(8,128)S(1)} %bitcast.41, bf16[64,128,128]{2,1,0:T(8,128)(2,1)S(1)} %bitcast.26, bf16[32,128,128]{2,1,0:T(8,128)(2,1)S(1)} %get-tuple-element.25.refs_4_, ...), custom_call_target="tpu_custom_call" | custom-call | flops 1 | bytes 1 | tf_op jit(solution)/shard_map/pallas_call | solution.py:199
  19.2 4.0 %shard_map.49 = (f32[8,128,128]{2,1,0:T(8,128)S(1)}, f32[8,128,128]{2,1,0:T(8,128)S(1)}) custom-call(s32[3]{0:T(128)S(1)} %pad_add_fusion.1.refs_0_, s32[2,16,32]{2,1,0:T(8,128)S(1)} %bitcast.38, s32[2,16,32]{2,1,0:T(8,128)S(1)} %bitcast.42, bf16[64,128,128]{2,1,0:T(8,128)(2,1)S(1)} %bitcast.27, bf16[32,128,128]{2,1,0:T(8,128)(2,1)S(1)} %get-tuple-element.25.refs_4_, ...), custom_call_target="tpu_custom_call" | custom-call | flops 1 | bytes 1 | tf_op jit(solution)/shard_map/pallas_call | solution.py:199
  25.4 2.1 %collective-permute-done.5.refs_4_ = bf16[16,128,128]{2,1,0:T(8,128)(2,1)S(1)} collective-permute-done((bf16[16,128,128]{2,1,0:T(8,128)(2,1)}, bf16[16,128,128]{2,1,0:T(8,128)(2,1)S(1)}, u32[]{:S(2)}, u32[]{:S(2)}) %collective-permute-start.5) | collective-permute-done | bytes 524320 | tf_op jit(solution)/shard_map/ppermute | solution.py:282
  28.2 2.7 %shard_map.51 = (s16[1040,128]{1,0:T(8,128)(2,1)S(1)}, bf16[32,128,128]{2,1,0:T(8,128)(2,1)S(1)}) custom-call(s32[3]{0:T(128)S(1)} %pad_add_fusion.1.refs_0_, s32[32,32]{1,0:T(8,128)S(1)} %copy-done.15, bf16[64,128,128]{2,1,0:T(8,128)(2,1)S(1)} %bitcast.28, bf16[16,128,128]{2,1,0:T(8,128)(2,1)} %shard_map.50.refs_3_, ...), custom_call_target="tpu_custom_call" | custom-call | flops 1 | bytes 1 | tf_op jit(solution)/shard_map/pallas_call | solution.py:199
  30.9 1.6 %collective-permute-start.7 = (s16[1040,128]{1,0:T(8,128)(2,1)S(1)}, s16[1040,128]{1,0:T(8,128)(2,1)S(1)}, u32[]{:S(2)}, u32[]{:S(2)}) collective-permute-start(s16[1040,128]{1,0:T(8,128)(2,1)S(1)} %get-tuple-element.30.refs_4_), channel_id=1, source_target_pairs={{0,1},{1,0},{2,3},{3,2},{4,5},{5,4},{6,7},{7,6},{8,9},{9,8},{10,11... | collective-permute-start | bytes 798728 | tf_op jit(solution)/shard_map/ppermute | solution.py:244
  32.5 2.3 %shard_map.52.refs_5_ = s16[1040,128]{1,0:T(8,128)(2,1)S(1)} custom-call(s32[3]{0:T(128)S(1)} %pad_add_fusion.1.refs_0_, s32[32,32]{1,0:T(8,128)S(1)} %copy-done.15, bf16[64,128,128]{2,1,0:T(8,128)(2,1)S(1)} %bitcast.29, bf16[32,128,128]{2,1,0:T(8,128)(2,1)S(1)} %get-tuple-element.29.refs_3_, s16[1040,128]{1,0:T(8,128)(2,1)S(1)} %get-tuple-element.30.refs_4_), custom_call_target="tpu_custom_call" | custom-call | flops 1 | bytes 1 | tf_op jit(solution)/shard_map/pallas_call | solution.py:199
  34.9 1.3 %shard_map.53 = (s16[1040,128]{1,0:T(8,128)(2,1)S(1)}, f32[8,128,128]{2,1,0:T(8,128)S(1)}) custom-call(s32[3]{0:T(128)S(1)} %pad_add_fusion.1.refs_0_, f32[8,128,128]{2,1,0:T(8,128)S(1)} %copy-done.3, f32[8,128,128]{2,1,0:T(8,128)S(1)} %copy-done.7, s16[1040,128]{1,0:T(8,128)(2,1)} %collective-permute-done.1.refs_2_.refs_3_, ...), custom_call_target="tpu_custom_call" | custom-call | flops 1 | bytes 1 | tf_op jit(solution)/shard_map/pallas_call | solution.py:199
  36.1 2.7 %collective-permute-start.6 = (s16[1040,128]{1,0:T(8,128)(2,1)S(1)}, s16[1040,128]{1,0:T(8,128)(2,1)S(1)}, u32[]{:S(2)}, u32[]{:S(2)}) collective-permute-start(s16[1040,128]{1,0:T(8,128)(2,1)S(1)} %get-tuple-element.32.refs_4_), channel_id=1, source_target_pairs={{0,4},{1,5},{2,6},{3,7},{4,0},{5,1},{6,2},{7,3},{8,12},{9,13},{10,... | collective-permute-start | bytes 798728 | tf_op jit(solution)/shard_map/ppermute | solution.py:244
  38.8 0.8 %collective-permute-start.9 = (s16[1040,128]{1,0:T(8,128)(2,1)S(1)}, s16[1040,128]{1,0:T(8,128)(2,1)S(1)}, u32[]{:S(2)}, u32[]{:S(2)}) collective-permute-start(s16[1040,128]{1,0:T(8,128)(2,1)S(1)} %shard_map.52.refs_5_), channel_id=1, source_target_pairs={{0,1},{1,0},{2,3},{3,2},{4,5},{5,4},{6,7},{7,6},{8,9},{9,8},{10,11... | collective-permute-start | bytes 798728 | tf_op jit(solution)/shard_map/ppermute | solution.py:244
  39.6 3.7 %shard_map.54 = (f32[8,128,128]{2,1,0:T(8,128)S(1)}, f32[8,128,128]{2,1,0:T(8,128)S(1)}) custom-call(s32[3]{0:T(128)S(1)} %pad_add_fusion.1.refs_0_, s32[32,32]{1,0:T(8,128)S(1)} %copy-done.16, bf16[64,128,128]{2,1,0:T(8,128)(2,1)S(1)} %bitcast.30, bf16[32,128,128]{2,1,0:T(8,128)(2,1)S(1)} %get-tuple-element.29.refs_3_, ...), custom_call_target="tpu_custom_call" | custom-call | flops 1 | bytes 1 | tf_op jit(solution)/shard_map/pallas_call | solution.py:199
  44.6 6.4 %collective-permute-done.6.refs_2_ = s16[1040,128]{1,0:T(8,128)(2,1)S(1)} collective-permute-done((s16[1040,128]{1,0:T(8,128)(2,1)S(1)}, s16[1040,128]{1,0:T(8,128)(2,1)S(1)}, u32[]{:S(2)}, u32[]{:S(2)}) %collective-permute-start.6) | collective-permute-done | bytes 266272 | tf_op jit(solution)/shard_map/ppermute | solution.py:244
  54.4 1.6 %collective-permute-start.15 = (s16[272,128]{1,0:T(8,128)(2,1)S(1)}, s16[272,128]{1,0:T(8,128)(2,1)S(1)}, u32[]{:S(2)}, u32[]{:S(2)}) collective-permute-start(s16[272,128]{1,0:T(8,128)(2,1)S(1)} %get-tuple-element.44), channel_id=1, source_target_pairs={{0,8},{1,9},{2,10},{3,11},{4,12},{5,13},{6,14},{7,15},{8,0},{9,1},... | collective-permute-start | bytes 208904 | tf_op jit(solution)/shard_map/ppermute | solution.py:249
  55.9 2.5 %collective-permute-start.14 = (s16[272,128]{1,0:T(8,128)(2,1)S(1)}, s16[272,128]{1,0:T(8,128)(2,1)S(1)}, u32[]{:S(2)}, u32[]{:S(2)}) collective-permute-start(s16[272,128]{1,0:T(8,128)(2,1)S(1)} %get-tuple-element.41.refs_3_), channel_id=1, source_target_pairs={{0,12},{1,13},{2,14},{3,15},{4,8},{5,9},{6,10},{7,11},{8,4},{9,5},... | collective-permute-start | bytes 208904 | tf_op jit(solution)/shard_map/ppermute | solution.py:249
  59.1 1.4 %collective-permute-start.12 = (s16[272,128]{1,0:T(8,128)(2,1)S(1)}, s16[272,128]{1,0:T(8,128)(2,1)S(1)}, u32[]{:S(2)}, u32[]{:S(2)}) collective-permute-start(s16[272,128]{1,0:T(8,128)(2,1)S(1)} %get-tuple-element.42), channel_id=1, source_target_pairs={{0,12},{1,13},{2,14},{3,15},{4,8},{5,9},{6,10},{7,11},{8,4},{9,5},... | collective-permute-start | bytes 208904 | tf_op jit(solution)/shard_map/ppermute | solution.py:249
  61.0 3.0 %collective-permute-done.14.refs_2_ = s16[272,128]{1,0:T(8,128)(2,1)S(1)} collective-permute-done((s16[272,128]{1,0:T(8,128)(2,1)S(1)}, s16[272,128]{1,0:T(8,128)(2,1)S(1)}, u32[]{:S(2)}, u32[]{:S(2)}) %collective-permute-start.14) | collective-permute-done | bytes 69664 | tf_op jit(solution)/shard_map/ppermute | solution.py:249
  64.1 1.9 %collective-permute-done.12.refs_2_ = s16[272,128]{1,0:T(8,128)(2,1)S(1)} collective-permute-done((s16[272,128]{1,0:T(8,128)(2,1)S(1)}, s16[272,128]{1,0:T(8,128)(2,1)S(1)}, u32[]{:S(2)}, u32[]{:S(2)}) %collective-permute-start.12) | collective-permute-done | bytes 69664 | tf_op jit(solution)/shard_map/ppermute | solution.py:249
  (61 shorter events, 13.0 us)
Async XLA Ops:
  0.0 8.2 %collective-permute-start = (bf16[16,128,128]{2,1,0:T(8,128)(2,1)}, bf16[16,128,128]{2,1,0:T(8,128)(2,1)S(1)}, u32[]{:S(2)}, u32[]{:S(2)}) collective-permute-start(bf16[16,128,128]{2,1,0:T(8,128)(2,1)} %bitcast.31), channel_id=1, source_target_pairs={{0,16},{16,0},{1,17},{17,1},{2,18},{18,2},{3,19},{19,3},{4,20},{20... | collective-permute-start | bytes 1572872 | tf_op jit(solution)/shard_map/ppermute | solution.py:269
  0.5 24.3 %collective-permute-start.4 = (bf16[16,128,128]{2,1,0:T(8,128)(2,1)}, bf16[16,128,128]{2,1,0:T(8,128)(2,1)}, u32[]{:S(2)}, u32[]{:S(2)}) collective-permute-start(bf16[16,128,128]{2,1,0:T(8,128)(2,1)} %bitcast.32), channel_id=1, source_target_pairs={{0,8},{8,0},{1,9},{9,1},{2,10},{10,2},{3,11},{11,3},{4,12},{12,4},... | collective-permute-start | bytes 1572872 | tf_op jit(solution)/shard_map/ppermute | solution.py:268
  2.9 1.6 %copy-start = (bf16[1,1,1,64,128,128]{5,4,3,2,1,0:T(8,128)(2,1)S(1)}, bf16[1,1,1,64,128,128]{5,4,3,2,1,0:T(8,128)(2,1)}, u32[]{:S(2)}) copy-start(bf16[1,1,1,64,128,128]{5,4,3,2,1,0:T(8,128)(2,1)} %param.4) | copy-start | bytes 6291460
  7.0 2.0 %copy-start.1 = (bf16[1,1,1,64,128,128]{5,4,3,2,1,0:T(8,128)(2,1)S(1)}, bf16[1,1,1,64,128,128]{5,4,3,2,1,0:T(8,128)(2,1)}, u32[]{:S(2)}) copy-start(bf16[1,1,1,64,128,128]{5,4,3,2,1,0:T(8,128)(2,1)} %param.4) | copy-start | bytes 6291460
  7.0 2.0 %copy-start.11 = (s32[1,1,1,2,32,16]{4,5,3,2,1,0:T(8,128)S(1)}, s32[1,1,1,2,32,16]{4,5,3,2,1,0:T(8,128)}, u32[]{:S(2)}) copy-start(s32[1,1,1,2,32,16]{4,5,3,2,1,0:T(8,128)} %param.6) | copy-start | bytes 12292
  7.0 2.0 %copy-start.13 = (s32[1,1,1,2,32,16]{4,5,3,2,1,0:T(8,128)S(1)}, s32[1,1,1,2,32,16]{4,5,3,2,1,0:T(8,128)}, u32[]{:S(2)}) copy-start(s32[1,1,1,2,32,16]{4,5,3,2,1,0:T(8,128)} %param.7) | copy-start | bytes 12292
  9.0 1.0 %copy-start.5 = (bf16[1,1,1,16,128,128]{5,4,3,2,1,0:T(8,128)(2,1)S(1)}, bf16[1,1,1,16,128,128]{5,4,3,2,1,0:T(8,128)(2,1)}, u32[]{:S(2)}) copy-start(bf16[1,1,1,16,128,128]{5,4,3,2,1,0:T(8,128)(2,1)} %param.5) | copy-start | bytes 1572868
  14.4 10.3 %collective-permute-start.1 = (s16[1040,128]{1,0:T(8,128)(2,1)}, s16[1040,128]{1,0:T(8,128)(2,1)}, u32[]{:S(2)}, u32[]{:S(2)}) collective-permute-start(s16[1040,128]{1,0:T(8,128)(2,1)} %get-tuple-element.26.refs_5_), channel_id=1, source_target_pairs={{0,2},{1,3},{2,0},{3,1},{4,6},{5,7},{6,4},{7,5},{8,10},{9,11},{10,... | collective-permute-start | bytes 798728 | tf_op jit(solution)/shard_map/ppermute | solution.py:244
  16.0 8.7 %collective-permute-start.3 = (s32[32,32]{1,0:T(8,128)S(1)}, s32[32,32]{1,0:T(8,128)S(1)}, u32[]{:S(2)}, u32[]{:S(2)}) collective-permute-start(s32[32,32]{1,0:T(8,128)S(1)} %pad_add_fusion), channel_id=1, source_target_pairs={{0,8},{8,0},{1,9},{9,1},{2,10},{10,2},{3,11},{11,3},{4,12},{12,4},... | collective-permute-start | bytes 12296 | tf_op jit(solution)/shard_map/ppermute | solution.py:271
  25.4 2.1 %collective-permute-start.5 = (bf16[16,128,128]{2,1,0:T(8,128)(2,1)}, bf16[16,128,128]{2,1,0:T(8,128)(2,1)S(1)}, u32[]{:S(2)}, u32[]{:S(2)}) collective-permute-start(bf16[16,128,128]{2,1,0:T(8,128)(2,1)} %shard_map.50.refs_3_), channel_id=1, source_target_pairs={{0,16},{16,0},{1,17},{17,1},{2,18},{18,2},{3,19},{19,3},{4,20},{20... | collective-permute-start | bytes 1572872 | tf_op jit(solution)/shard_map/ppermute | solution.py:282
  25.4 9.5 %collective-permute-start.2 = (s16[1040,128]{1,0:T(8,128)(2,1)S(1)}, s16[1040,128]{1,0:T(8,128)(2,1)S(1)}, u32[]{:S(2)}, u32[]{:S(2)}) collective-permute-start(s16[1040,128]{1,0:T(8,128)(2,1)S(1)} %shard_map.48.refs_5_), channel_id=1, source_target_pairs={{0,2},{1,3},{2,0},{3,1},{4,6},{5,7},{6,4},{7,5},{8,10},{9,11},{10,... | collective-permute-start | bytes 798728 | tf_op jit(solution)/shard_map/ppermute | solution.py:244
  30.9 4.0 %copy-start.3 = (f32[8,128,128]{2,1,0:T(8,128)S(1)}, f32[8,128,128]{2,1,0:T(8,128)}, u32[]{:S(2)}) copy-start(f32[8,128,128]{2,1,0:T(8,128)} %copy-done.2) | copy-start | bytes 1572868
  30.9 4.0 %copy-start.7 = (f32[8,128,128]{2,1,0:T(8,128)S(1)}, f32[8,128,128]{2,1,0:T(8,128)}, u32[]{:S(2)}) copy-start(f32[8,128,128]{2,1,0:T(8,128)} %copy-done.6) | copy-start | bytes 1572868
  30.9 12.4 %collective-permute-start.7 = (s16[1040,128]{1,0:T(8,128)(2,1)S(1)}, s16[1040,128]{1,0:T(8,128)(2,1)S(1)}, u32[]{:S(2)}, u32[]{:S(2)}) collective-permute-start(s16[1040,128]{1,0:T(8,128)(2,1)S(1)} %get-tuple-element.30.refs_4_), channel_id=1, source_target_pairs={{0,1},{1,0},{2,3},{3,2},{4,5},{5,4},{6,7},{7,6},{8,9},{9,8},{10,11... | collective-permute-start | bytes 798728 | tf_op jit(solution)/shard_map/ppermute | solution.py:244
  32.5 7.1 %copy-start.16 = (s32[32,32]{1,0:T(8,128)S(1)}, s32[32,32]{1,0:T(8,128)}, u32[]{:S(2)}) copy-start(s32[32,32]{1,0:T(8,128)} %copy-done.14) | copy-start | bytes 12292
  36.1 14.8 %collective-permute-start.6 = (s16[1040,128]{1,0:T(8,128)(2,1)S(1)}, s16[1040,128]{1,0:T(8,128)(2,1)S(1)}, u32[]{:S(2)}, u32[]{:S(2)}) collective-permute-start(s16[1040,128]{1,0:T(8,128)(2,1)S(1)} %get-tuple-element.32.refs_4_), channel_id=1, source_target_pairs={{0,4},{1,5},{2,6},{3,7},{4,0},{5,1},{6,2},{7,3},{8,12},{9,13},{10,... | collective-permute-start | bytes 798728 | tf_op jit(solution)/shard_map/ppermute | solution.py:244
  38.8 12.9 %collective-permute-start.9 = (s16[1040,128]{1,0:T(8,128)(2,1)S(1)}, s16[1040,128]{1,0:T(8,128)(2,1)S(1)}, u32[]{:S(2)}, u32[]{:S(2)}) collective-permute-start(s16[1040,128]{1,0:T(8,128)(2,1)S(1)} %shard_map.52.refs_5_), channel_id=1, source_target_pairs={{0,1},{1,0},{2,3},{3,2},{4,5},{5,4},{6,7},{7,6},{8,9},{9,8},{10,11... | collective-permute-start | bytes 798728 | tf_op jit(solution)/shard_map/ppermute | solution.py:244
  44.0 9.7 %collective-permute-start.11 = (s16[528,128]{1,0:T(8,128)(2,1)S(1)}, s16[528,128]{1,0:T(8,128)(2,1)S(1)}, u32[]{:S(2)}, u32[]{:S(2)}) collective-permute-start(s16[528,128]{1,0:T(8,128)(2,1)S(1)} %get-tuple-element.34.refs_3_), channel_id=1, source_target_pairs={{0,2},{1,3},{2,0},{3,1},{4,6},{5,7},{6,4},{7,5},{8,10},{9,11},{10,... | collective-permute-start | bytes 405512 | tf_op jit(solution)/shard_map/ppermute | solution.py:244
  52.4 6.1 %collective-permute-start.10 = (s16[528,128]{1,0:T(8,128)(2,1)S(1)}, s16[528,128]{1,0:T(8,128)(2,1)S(1)}, u32[]{:S(2)}, u32[]{:S(2)}) collective-permute-start(s16[528,128]{1,0:T(8,128)(2,1)S(1)} %get-tuple-element.39.refs_3_), channel_id=1, source_target_pairs={{0,2},{1,3},{2,0},{3,1},{4,6},{5,7},{6,4},{7,5},{8,10},{9,11},{10,... | collective-permute-start | bytes 405512 | tf_op jit(solution)/shard_map/ppermute | solution.py:244
  52.4 8.6 %collective-permute-start.8 = (s16[528,128]{1,0:T(8,128)(2,1)S(1)}, s16[528,128]{1,0:T(8,128)(2,1)S(1)}, u32[]{:S(2)}, u32[]{:S(2)}) collective-permute-start(s16[528,128]{1,0:T(8,128)(2,1)S(1)} %get-tuple-element.36.refs_3_), channel_id=1, source_target_pairs={{0,1},{1,0},{2,3},{3,2},{4,5},{5,4},{6,7},{7,6},{8,9},{9,8},{10,11... | collective-permute-start | bytes 405512 | tf_op jit(solution)/shard_map/ppermute | solution.py:244
  54.4 6.6 %collective-permute-start.15 = (s16[272,128]{1,0:T(8,128)(2,1)S(1)}, s16[272,128]{1,0:T(8,128)(2,1)S(1)}, u32[]{:S(2)}, u32[]{:S(2)}) collective-permute-start(s16[272,128]{1,0:T(8,128)(2,1)S(1)} %get-tuple-element.44), channel_id=1, source_target_pairs={{0,8},{1,9},{2,10},{3,11},{4,12},{5,13},{6,14},{7,15},{8,0},{9,1},... | collective-permute-start | bytes 208904 | tf_op jit(solution)/shard_map/ppermute | solution.py:249
  55.9 8.1 %collective-permute-start.14 = (s16[272,128]{1,0:T(8,128)(2,1)S(1)}, s16[272,128]{1,0:T(8,128)(2,1)S(1)}, u32[]{:S(2)}, u32[]{:S(2)}) collective-permute-start(s16[272,128]{1,0:T(8,128)(2,1)S(1)} %get-tuple-element.41.refs_3_), channel_id=1, source_target_pairs={{0,12},{1,13},{2,14},{3,15},{4,8},{5,9},{6,10},{7,11},{8,4},{9,5},... | collective-permute-start | bytes 208904 | tf_op jit(solution)/shard_map/ppermute | solution.py:249
  59.1 6.9 %collective-permute-start.12 = (s16[272,128]{1,0:T(8,128)(2,1)S(1)}, s16[272,128]{1,0:T(8,128)(2,1)S(1)}, u32[]{:S(2)}, u32[]{:S(2)}) collective-permute-start(s16[272,128]{1,0:T(8,128)(2,1)S(1)} %get-tuple-element.42), channel_id=1, source_target_pairs={{0,12},{1,13},{2,14},{3,15},{4,8},{5,9},{6,10},{7,11},{8,4},{9,5},... | collective-permute-start | bytes 208904 | tf_op jit(solution)/shard_map/ppermute | solution.py:249
  60.5 5.6 %collective-permute-start.13 = (s16[272,128]{1,0:T(8,128)(2,1)S(1)}, s16[272,128]{1,0:T(8,128)(2,1)S(1)}, u32[]{:S(2)}, u32[]{:S(2)}) collective-permute-start(s16[272,128]{1,0:T(8,128)(2,1)S(1)} %get-tuple-element.43), channel_id=1, source_target_pairs={{0,8},{1,9},{2,10},{3,11},{4,12},{5,13},{6,14},{7,15},{8,0},{9,1},... | collective-permute-start | bytes 208904 | tf_op jit(solution)/shard_map/ppermute | solution.py:249
  (9 other events, 7.3 us)

commit v4 on v3

--- a/solution.py
+++ b/solution.py
@@ -66,37 +66,35 @@
     return jnp.dot(left, right, preferred_element_type=jnp.float32)
 
 
+def own_bit(bit):
+    return (lax.axis_index("layer") >> bit) & 1
+
+
 def insert(rest, at, bit):
     low = rest & ((1 << at) - 1)
     return ((rest >> at) << (at + 1)) | (bit << at) | low
 
 
-def finder(me_ref, index_refs, fan):
-    if len(index_refs) == 2:
-        ia_ref, ip_ref = index_refs
-        col = me_ref[1]
-        return lambda t: lambda f: (ia_ref[col, f, t], ip_ref[col, f, t])
-    (both_ref,) = index_refs
-    return lambda t: lambda f: (both_ref[f, t], both_ref[fan + f, t])
-
-
-def send_kernel(n_index, n_p, fan, count, chunk, bit):
+def finder(lists_ref, fan):
+    return lambda t: lambda f: (lists_ref[f, t], lists_ref[fan + f, t])
+
+
+def send_kernel(n_p, fan, count, chunk, bit):
     first, size = chunk
 
-    def kernel(me_ref, *refs):
-        find = finder(me_ref, refs[:n_index], fan)
-        a_ref = refs[n_index]
-        p_refs = refs[n_index + 1 : n_index + 1 + n_p]
-        out_ref = refs[n_index + 1 + n_p]
+    def kernel(lists_ref, a_ref, *refs):
+        find = finder(lists_ref, fan)
+        p_refs, out_ref = refs[:n_p], refs[n_p]
         width = out_ref.shape[-1]
         if n_p == 2:
             p_ref = refs[-1]
             held = p_refs[0].shape[0]
-            p_ref[pl.ds(me_ref[0] * held, held)] = p_refs[0][...]
-            p_ref[pl.ds((1 - me_ref[0]) * held, held)] = p_refs[1][...]
+            row = lax.axis_index("row")
+            p_ref[pl.ds(row * held, held)] = p_refs[0][...]
+            p_ref[pl.ds((1 - row) * held, held)] = p_refs[1][...]
         else:
             (p_ref,) = p_refs
-        side = 1 - ((me_ref[2] >> bit) & 1)
+        side = 1 - own_bit(bit)
         total = out_ref.shape[0] // width
 
         def body(step, head):
@@ -112,12 +110,11 @@
     return kernel
 
 
-def keep_kernel(n_index, fan, count, chunks, bit):
-    def kernel(me_ref, *refs):
-        find = finder(me_ref, refs[:n_index], fan)
-        a_ref, p_ref = refs[n_index : n_index + 2]
-        side = (me_ref[2] >> bit) & 1
-        for (first, size), out_ref in zip(chunks, refs[n_index + 2 :]):
+def keep_kernel(fan, count, chunks, bit):
+    def kernel(lists_ref, a_ref, p_ref, *out_refs):
+        find = finder(lists_ref, fan)
+        side = own_bit(bit)
+        for (first, size), out_ref in zip(chunks, out_refs):
 
             def body(step, _):
                 for k in range(GROUP):
@@ -136,11 +133,11 @@
     full = sum(sizes)
     halves = 1 << (len(rest) - 1)
 
-    def kernel(me_ref, *refs):
+    def kernel(*refs):
         n = len(sizes)
         kept_refs, in_refs, (sent_ref, stay_ref) = refs[:n], refs[n : 2 * n], refs[2 * n : 2 * n + 2]
         width = sent_ref.shape[-1]
-        mine = (me_ref[2] >> bit) & 1
+        mine = own_bit(bit)
         heads = [get_head(ref, ref.shape[0] // width) for ref in in_refs]
 
         def sums(place):
@@ -191,6 +188,8 @@
 
 
 def call(kernel, out_shape, smem, vmem, after=(), scratch=(), flops=0):
+    outs = out_shape if isinstance(out_shape, (list, tuple)) else [out_shape]
+    moved = sum(x.size * x.dtype.itemsize for x in (*smem, *vmem, *outs))
     n_real = len(smem) + len(vmem)
 
     def wrapped(*refs):
@@ -204,8 +203,8 @@
         + [pl.BlockSpec(memory_space=pl.ANY)] * len(after),
         out_specs=jax.tree.map(lambda _: pl.BlockSpec(memory_space=VMEM), out_shape),
         scratch_shapes=list(scratch),
-        compiler_params=pltpu.CompilerParams(vmem_limit_bytes=40 * 2**20),
-        cost_estimate=pl.CostEstimate(flops=1, bytes_accessed=1, transcendentals=0),
+        compiler_params=pltpu.CompilerParams(vmem_limit_bytes=moved + 4 * 2**20),
+        cost_estimate=pl.CostEstimate(flops=5 * flops, bytes_accessed=moved, transcendentals=0),
     )(*smem, *vmem, *after)
 
 
@@ -219,6 +218,7 @@
         in_specs=[pl.BlockSpec(memory_space=pl.ANY)] * (1 + len(after)),
         out_specs=pl.BlockSpec(memory_space=pl.ANY),
         input_output_aliases={0: 0},
+        compiler_params=pltpu.CompilerParams(vmem_limit_bytes=2**20),
     )(x, *after)
 
 
@@ -231,7 +231,6 @@
     bits = layers.bit_length() - 1
     count = slots // layers
     swap = [(0, 1), (1, 0)]
-    me = jnp.stack([lax.axis_index("row"), lax.axis_index("col"), lax.axis_index("layer")]).astype(jnp.int32)
 
     half = count // 2
     chunks = [(0, half), (half, count - half)]
@@ -250,28 +249,29 @@
 
     def start(smem, vmem, chunk, bit, after):
         shapes = [message(layers // 2 * chunk[1], width), jax.ShapeDtypeStruct((2 * held, width, width), p.dtype)]
-        return call(send_kernel(len(smem) - 1, 2, fan, count, chunk, bit), shapes, smem, vmem, after, (), flops)
+        return call(send_kernel(2, fan, count, chunk, bit), shapes, smem, vmem, after, (), flops)
 
     def send(smem, vmem, chunk, bit, after):
         shape = message(layers // 2 * chunk[1], width)
-        return call(send_kernel(len(smem) - 1, 1, fan, count, chunk, bit), shape, smem, vmem, after, (), flops)
+        return call(send_kernel(1, fan, count, chunk, bit), shape, smem, vmem, after, (), flops)
 
     def keep(smem, vmem, bit, after):
         shapes = [floats(layers // 2 * size) for _, size in chunks]
-        return call(keep_kernel(len(smem) - 1, fan, count, chunks, bit), shapes, smem, vmem, after, (), 2 * flops)
+        return call(keep_kernel(fan, count, chunks, bit), shapes, smem, vmem, after, (), 2 * flops)
 
     def add(kept, came, sizes, rest, bit, keeps, after):
         n = sum(sizes) << (len(rest) - 1)
         shapes = [message(n, width), floats(n) if keeps else message(n, width)]
-        return call(add_kernel(sizes, rest, bit, keeps), shapes, (me,), (*kept, *came), after)
+        return call(add_kernel(sizes, rest, bit, keeps), shapes, (), (*kept, *came), after)
 
     p_x = lax.ppermute(p, "col", swap)
     p_r = lax.ppermute(p, "row", swap)
-    far = 1 - lax.axis_index("col")
-    lists_x = lax.ppermute(jnp.concatenate([ia[far], ip[far]], axis=0), "col", swap)
-    own_bits = [*range(1, bits), 0]
-    gate = call(lambda *refs: None, jax.ShapeDtypeStruct((8, width), jnp.float32), (ia, ip), (a, p))
-    smem, bit = (me, ia, ip), own_bits[0]
+    col = lax.axis_index("col")
+    lists = jnp.concatenate([ia[col], ip[col]], axis=0)
+    lists_x = lax.ppermute(jnp.concatenate([ia[1 - col], ip[1 - col]], axis=0), "col", swap)
+    own_bits = [*range(bits)]
+    gate = call(lambda *refs: None, jax.ShapeDtypeStruct((8, width), jnp.float32), (lists,), (a, p))
+    smem, bit = (lists,), own_bits[0]
     made, joined = start(smem, (a, p, p_r), chunks[0], bit, (gate,))
     own_sent = [exchange(made, bit)]
     made = send(smem, (a, joined), chunks[1], bit, (made,))
@@ -281,7 +281,7 @@
     p_x = hold(p_x, (own_kept[0], own_sent[0], lists_x))
     p_xr = lax.ppermute(p_x, "row", swap)
 
-    smem, bit = (me, lists_x), 0
+    smem, bit = (lists_x,), 0
     made, joined = start(smem, (a, p_x, p_xr), chunks[0], bit, ())
     other_sent = [exchange(made, bit)]
     made = send(smem, (a, joined), chunks[1], bit, (made,))

time: 67.3 us -> 58 us (0.86)
  Pallas kernels: 25.2 us -> 19.4 us
  local copies, waits for them, and re-layouts: 9.9 us -> 4.15 us
  starting transfers between devices: 17.5 us -> 22.5 us
  waiting for transfers between devices: 13.9 us -> 11.5 us
    unnamed x34 -> x6, local copies, waits for them, and re-layouts: 9.9 us -> 3.4 us
    ppermute x8, starting transfers between devices: 8.06 us -> 14 us  [exchange(): return lax.ppermute(x, 'layer', [(i, i ^ 1 << bit) for i in range(layers)])]
    pallas_call x15, Pallas kernels: 25.2 us -> 19.4 us  [call(): pl.pallas_call(wrapped, out_shape=out_shape, in_specs=[pl.BlockSpec(memor...]
    ppermute x1, waiting for transfers between devices: 2.05 us -> 0.17 us  [on_device(): p_xr = lax.ppermute(p_x, 'row', swap)]
    ppermute x4, waiting for transfers between devices: 4.94 us -> 3.65 us  [cross(): return lax.ppermute(x, ('col', 'layer'), perm)]
    ppermute x8, waiting for transfers between devices: 6.92 us -> 7.72 us  [exchange(): return lax.ppermute(x, 'layer', [(i, i ^ 1 << bit) for i in range(layers)])]
    squeeze x1, local copies, waits for them, and re-layouts: 0.01 us -> 0.75 us  [on_device(): ip[1 - col]]
  transfers between devices with their start and end apart: 16 -> 16, of which waited for: 5 -> 9; matrix products, arithmetic and copies ran while one was open for 0% -> 1% of each run, Pallas kernels for 37% -> 32%
where the time goes in v4:
time: 58 us; the launch traced here: 57.8 us
  starting transfers between devices  22.5 us (39%)
  Pallas kernels  19.4 us (33%)
  waiting for transfers between devices  11.5 us (20%)
  local copies, waits for them, and re-layouts  4.15 us (7%)
    pallas_call x15, Pallas kernels, call(): pl.pallas_call(wrapped, out_shape=out_shape, in_specs=[pl.BlockSpec(memor...  19.4 us
    ppermute x8, starting transfers between devices, exchange(): return lax.ppermute(x, 'layer', [(i, i ^ 1 << bit) for i in range(layers)])  14 us
    ppermute x8, waiting for transfers between devices, exchange(): return lax.ppermute(x, 'layer', [(i, i ^ 1 << bit) for i in range(layers)])  7.72 us
    ppermute x4, starting transfers between devices, cross(): return lax.ppermute(x, ('col', 'layer'), perm)  5.52 us
    ppermute x4, waiting for transfers between devices, cross(): return lax.ppermute(x, ('col', 'layer'), perm)  3.65 us
    unnamed x6, local copies, waits for them, and re-layouts  3.4 us
    ppermute x1, starting transfers between devices, on_device(): p_x = lax.ppermute(p, 'col', swap)  2.49 us
  transfers between devices with their start and end apart: 16, of which 9 were waited for; matrix products, arithmetic and copies ran while one was open for 1% of the time, Pallas kernels for 32%

profile of v4, /device:TPU:0, one launch (start us, length us, event | category | flops | bytes accessed | tf_op | source)
XLA Modules:
  0.0 57.8 jit_solution(13861126431945020634)
XLA Ops:
  0.5 2.5 %collective-permute-start.4 = (bf16[16,128,128]{2,1,0:T(8,128)(2,1)}, bf16[16,128,128]{2,1,0:T(8,128)(2,1)S(1)}, u32[]{:S(2)}, u32[]{:S(2)}) collective-permute-start(bf16[16,128,128]{2,1,0:T(8,128)(2,1)} %bitcast.35), channel_id=1, source_target_pairs={{0,8},{8,0},{1,9},{9,1},{2,10},{10,2},{3,11},{11,3},{4,12},{12,4},... | collective-permute-start | bytes 1572872 | tf_op jit(solution)/shard_map/ppermute | solution.py:267
  3.8 1.6 %copy-done = bf16[1,1,1,64,128,128]{5,4,3,2,1,0:T(8,128)(2,1)S(1)} copy-done((bf16[1,1,1,64,128,128]{5,4,3,2,1,0:T(8,128)(2,1)S(1)}, bf16[1,1,1,64,128,128]{5,4,3,2,1,0:T(8,128)(2,1)}, u32[]{:S(2)}) %copy-start) | copy-done | bytes 2097176
  5.4 1.0 %copy-done.2 = bf16[1,1,1,16,128,128]{5,4,3,2,1,0:T(8,128)(2,1)S(1)} copy-done((bf16[1,1,1,16,128,128]{5,4,3,2,1,0:T(8,128)(2,1)S(1)}, bf16[1,1,1,16,128,128]{5,4,3,2,1,0:T(8,128)(2,1)}, u32[]{:S(2)}) %copy-start.2) | copy-done | bytes 524312
  6.4 0.8 %shard_map.46.refs_4_ = f32[8,128]{1,0:T(8,128)S(1)} custom-call(s32[32,32]{1,0:T(8,128)S(1)} %pad_add_fusion.refs_0_, bf16[64,128,128]{2,1,0:T(8,128)(2,1)S(1)} %bitcast.27, bf16[16,128,128]{2,1,0:T(8,128)(2,1)S(1)} %bitcast.36), custom_call_target="tpu_custom_call" | custom-call | bytes 2629632 | tf_op jit(solution)/shard_map/pallas_call | solution.py:198
  8.0 2.4 %shard_map.47 = (s16[1040,128]{1,0:T(8,128)(2,1)S(1)}, bf16[32,128,128]{2,1,0:T(8,128)(2,1)S(1)}) custom-call(s32[32,32]{1,0:T(8,128)S(1)} %pad_add_fusion.refs_0_, bf16[64,128,128]{2,1,0:T(8,128)(2,1)S(1)} %bitcast.28, bf16[16,128,128]{2,1,0:T(8,128)(2,1)S(1)} %bitcast.37, bf16[16,128,128]{2,1,0:T(8,128)(2,1)S(1)} %collective-permute-done.refs_3_, ...), custom_call_target="tpu_custom_call" | custom-call | flops 2684354560 | bytes 4464640 | tf_op jit(solution)/shard_map/pallas_call | solution.py:198
  10.4 2.1 %collective-permute-start.1 = (s16[1040,128]{1,0:T(8,128)(2,1)S(1)}, s16[1040,128]{1,0:T(8,128)(2,1)S(1)}, u32[]{:S(2)}, u32[]{:S(2)}) collective-permute-start(s16[1040,128]{1,0:T(8,128)(2,1)S(1)} %get-tuple-element.26.refs_3_), channel_id=1, source_target_pairs={{0,1},{1,0},{2,3},{3,2},{4,5},{5,4},{6,7},{7,6},{8,9},{9,8},{10,11... | collective-permute-start | bytes 798728 | tf_op jit(solution)/shard_map/ppermute | solution.py:243
  12.5 2.3 %shard_map.48.refs_3_ = s16[1040,128]{1,0:T(8,128)(2,1)S(1)} custom-call(s32[32,32]{1,0:T(8,128)S(1)} %pad_add_fusion.refs_0_, bf16[64,128,128]{2,1,0:T(8,128)(2,1)S(1)} %bitcast.29, bf16[32,128,128]{2,1,0:T(8,128)(2,1)S(1)} %get-tuple-element.25.refs_2_, s16[1040,128]{1,0:T(8,128)(2,1)S(1)} %get-tuple-element.26.refs_3_), custom_call_target="tpu_custom_call" | custom-call | flops 2684354560 | bytes 3416064 | tf_op jit(solution)/shard_map/pallas_call | solution.py:198
  14.8 3.7 %shard_map.49 = (f32[8,128,128]{2,1,0:T(8,128)S(1)}, f32[8,128,128]{2,1,0:T(8,128)S(1)}) custom-call(s32[32,32]{1,0:T(8,128)S(1)} %pad_add_fusion.refs_0_, bf16[64,128,128]{2,1,0:T(8,128)(2,1)S(1)} %bitcast.30, bf16[32,128,128]{2,1,0:T(8,128)(2,1)S(1)} %get-tuple-element.25.refs_2_, s16[1040,128]{1,0:T(8,128)(2,1)S(1)} %shard_map.48.refs_3_), custom_call_target="tpu_custom_call" | custom-call | flops 5368709120 | bytes 4198400 | tf_op jit(solution)/shard_map/pallas_call | solution.py:198
  19.0 1.7 %collective-permute-start.2 = (s16[1040,128]{1,0:T(8,128)(2,1)S(1)}, s16[1040,128]{1,0:T(8,128)(2,1)S(1)}, u32[]{:S(2)}, u32[]{:S(2)}) collective-permute-start(s16[1040,128]{1,0:T(8,128)(2,1)S(1)} %shard_map.48.refs_3_), channel_id=1, source_target_pairs={{0,1},{1,0},{2,3},{3,2},{4,5},{5,4},{6,7},{7,6},{8,9},{9,8},{10,11... | collective-permute-start | bytes 798728 | tf_op jit(solution)/shard_map/ppermute | solution.py:243
  20.9 2.4 %shard_map.51 = (s16[1040,128]{1,0:T(8,128)(2,1)S(1)}, bf16[32,128,128]{2,1,0:T(8,128)(2,1)S(1)}) custom-call(s32[32,32]{1,0:T(8,128)S(1)} %collective-permute-done.3.refs_3_.refs_0_, bf16[64,128,128]{2,1,0:T(8,128)(2,1)S(1)} %bitcast.31, bf16[16,128,128]{2,1,0:T(8,128)(2,1)S(1)} %shard_map.50.refs_2_, bf16[16,128,128]{2,1,0:T(8,128)(2,1)S(1)} %collective-permute-done.5.refs_3_), custom_call_target="tpu_custom_call" | custom-call | flops 2684354560 | bytes 4464640 | tf_op jit(solution)/shard_map/pallas_call | solution.py:198
  23.3 1.8 %collective-permute-start.7 = (s16[1040,128]{1,0:T(8,128)(2,1)S(1)}, s16[1040,128]{1,0:T(8,128)(2,1)S(1)}, u32[]{:S(2)}, u32[]{:S(2)}) collective-permute-start(s16[1040,128]{1,0:T(8,128)(2,1)S(1)} %get-tuple-element.30.refs_3_), channel_id=1, source_target_pairs={{0,1},{1,0},{2,3},{3,2},{4,5},{5,4},{6,7},{7,6},{8,9},{9,8},{10,11... | collective-permute-start | bytes 798728 | tf_op jit(solution)/shard_map/ppermute | solution.py:243
  25.1 2.3 %shard_map.52.refs_4_ = s16[1040,128]{1,0:T(8,128)(2,1)S(1)} custom-call(s32[32,32]{1,0:T(8,128)S(1)} %collective-permute-done.3.refs_3_.refs_0_, bf16[64,128,128]{2,1,0:T(8,128)(2,1)S(1)} %bitcast.32, bf16[32,128,128]{2,1,0:T(8,128)(2,1)S(1)} %get-tuple-element.29.refs_2_, s16[1040,128]{1,0:T(8,128)(2,1)S(1)} %get-tuple-element.30.refs_3_), custom_call_target="tpu_custom_call" | custom-call | flops 2684354560 | bytes 3416064 | tf_op jit(solution)/shard_map/pallas_call | solution.py:198
  28.5 1.9 %collective-permute-start.6 = (s16[1040,128]{1,0:T(8,128)(2,1)S(1)}, s16[1040,128]{1,0:T(8,128)(2,1)S(1)}, u32[]{:S(2)}, u32[]{:S(2)}) collective-permute-start(s16[1040,128]{1,0:T(8,128)(2,1)S(1)} %get-tuple-element.32.refs_3_), channel_id=1, source_target_pairs={{0,2},{1,3},{2,0},{3,1},{4,6},{5,7},{6,4},{7,5},{8,10},{9,11},{10,... | collective-permute-start | bytes 798728 | tf_op jit(solution)/shard_map/ppermute | solution.py:243
  30.4 3.7 %shard_map.54 = (f32[8,128,128]{2,1,0:T(8,128)S(1)}, f32[8,128,128]{2,1,0:T(8,128)S(1)}) custom-call(s32[32,32]{1,0:T(8,128)S(1)} %collective-permute-done.3.refs_3_.refs_0_, bf16[64,128,128]{2,1,0:T(8,128)(2,1)S(1)} %bitcast.33, bf16[32,128,128]{2,1,0:T(8,128)(2,1)S(1)} %get-tuple-element.29.refs_2_, s16[1040,128]{1,0:T(8,128)(2,1)S(1)} %get-tuple-element.32.refs_3_), custom_call_target="tpu_custom_call" | custom-call | flops 5368709120 | bytes 4198400 | tf_op jit(solution)/shard_map/pallas_call | solution.py:198
  34.3 1.7 %collective-permute-start.11 = (s16[528,128]{1,0:T(8,128)(2,1)S(1)}, s16[528,128]{1,0:T(8,128)(2,1)S(1)}, u32[]{:S(2)}, u32[]{:S(2)}) collective-permute-start(s16[528,128]{1,0:T(8,128)(2,1)S(1)} %get-tuple-element.34.refs_2_), channel_id=1, source_target_pairs={{0,2},{1,3},{2,0},{3,1},{4,6},{5,7},{6,4},{7,5},{8,10},{9,11},{10,... | collective-permute-start | bytes 405512 | tf_op jit(solution)/shard_map/ppermute | solution.py:243
  36.5 2.7 %collective-permute-done.9.refs_1_ = s16[1040,128]{1,0:T(8,128)(2,1)S(1)} collective-permute-done((s16[1040,128]{1,0:T(8,128)(2,1)S(1)}, s16[1040,128]{1,0:T(8,128)(2,1)S(1)}, u32[]{:S(2)}, u32[]{:S(2)}) %collective-permute-start.9) | collective-permute-done | bytes 266272 | tf_op jit(solution)/shard_map/ppermute | solution.py:243
  39.4 1.9 %collective-permute-start.10 = (s16[528,128]{1,0:T(8,128)(2,1)S(1)}, s16[528,128]{1,0:T(8,128)(2,1)S(1)}, u32[]{:S(2)}, u32[]{:S(2)}) collective-permute-start(s16[528,128]{1,0:T(8,128)(2,1)S(1)} %get-tuple-element.39.refs_2_), channel_id=1, source_target_pairs={{0,2},{1,3},{2,0},{3,1},{4,6},{5,7},{6,4},{7,5},{8,10},{9,11},{10,... | collective-permute-start | bytes 405512 | tf_op jit(solution)/shard_map/ppermute | solution.py:243
  41.2 2.6 %collective-permute-start.8 = (s16[528,128]{1,0:T(8,128)(2,1)S(1)}, s16[528,128]{1,0:T(8,128)(2,1)S(1)}, u32[]{:S(2)}, u32[]{:S(2)}) collective-permute-start(s16[528,128]{1,0:T(8,128)(2,1)S(1)} %get-tuple-element.36.refs_2_), channel_id=1, source_target_pairs={{0,4},{1,5},{2,6},{3,7},{4,0},{5,1},{6,2},{7,3},{8,12},{9,13},{10,... | collective-permute-start | bytes 405512 | tf_op jit(solution)/shard_map/ppermute | solution.py:243
  44.0 1.6 %collective-permute-start.15 = (s16[272,128]{1,0:T(8,128)(2,1)S(1)}, s16[272,128]{1,0:T(8,128)(2,1)S(1)}, u32[]{:S(2)}, u32[]{:S(2)}) collective-permute-start(s16[272,128]{1,0:T(8,128)(2,1)S(1)} %get-tuple-element.44), channel_id=1, source_target_pairs={{0,8},{1,9},{2,10},{3,11},{4,12},{5,13},{6,14},{7,15},{8,0},{9,1},... | collective-permute-start | bytes 208904 | tf_op jit(solution)/shard_map/ppermute | solution.py:248
  45.8 0.8 %collective-permute-done.10.refs_1_ = s16[528,128]{1,0:T(8,128)(2,1)S(1)} collective-permute-done((s16[528,128]{1,0:T(8,128)(2,1)S(1)}, s16[528,128]{1,0:T(8,128)(2,1)S(1)}, u32[]{:S(2)}, u32[]{:S(2)}) %collective-permute-start.10) | collective-permute-done | bytes 135200 | tf_op jit(solution)/shard_map/ppermute | solution.py:243
  46.7 3.1 %collective-permute-start.12 = (s16[272,128]{1,0:T(8,128)(2,1)S(1)}, s16[272,128]{1,0:T(8,128)(2,1)S(1)}, u32[]{:S(2)}, u32[]{:S(2)}) collective-permute-start(s16[272,128]{1,0:T(8,128)(2,1)S(1)} %get-tuple-element.42), channel_id=1, source_target_pairs={{0,12},{1,13},{2,14},{3,15},{4,8},{5,9},{6,10},{7,11},{8,4},{9,5},... | collective-permute-start | bytes 208904 | tf_op jit(solution)/shard_map/ppermute | solution.py:248
  50.4 2.9 %collective-permute-done.8.refs_1_ = s16[528,128]{1,0:T(8,128)(2,1)S(1)} collective-permute-done((s16[528,128]{1,0:T(8,128)(2,1)S(1)}, s16[528,128]{1,0:T(8,128)(2,1)S(1)}, u32[]{:S(2)}, u32[]{:S(2)}) %collective-permute-start.8) | collective-permute-done | bytes 135200 | tf_op jit(solution)/shard_map/ppermute | solution.py:243
  53.3 2.5 %collective-permute-done.14.refs_2_ = s16[272,128]{1,0:T(8,128)(2,1)S(1)} collective-permute-done((s16[272,128]{1,0:T(8,128)(2,1)S(1)}, s16[272,128]{1,0:T(8,128)(2,1)S(1)}, u32[]{:S(2)}, u32[]{:S(2)}) %collective-permute-start.14) | collective-permute-done | bytes 69664 | tf_op jit(solution)/shard_map/ppermute | solution.py:248
  55.9 1.1 %collective-permute-done.12.refs_2_ = s16[272,128]{1,0:T(8,128)(2,1)S(1)} collective-permute-done((s16[272,128]{1,0:T(8,128)(2,1)S(1)}, s16[272,128]{1,0:T(8,128)(2,1)S(1)}, u32[]{:S(2)}, u32[]{:S(2)}) %collective-permute-start.12) | collective-permute-done | bytes 69664 | tf_op jit(solution)/shard_map/ppermute | solution.py:248
  (33 shorter events, 6.5 us)
Async XLA Ops:
  0.0 7.2 %collective-permute-start = (bf16[16,128,128]{2,1,0:T(8,128)(2,1)}, bf16[16,128,128]{2,1,0:T(8,128)(2,1)S(1)}, u32[]{:S(2)}, u32[]{:S(2)}) collective-permute-start(bf16[16,128,128]{2,1,0:T(8,128)(2,1)} %bitcast.34), channel_id=1, source_target_pairs={{0,16},{16,0},{1,17},{17,1},{2,18},{18,2},{3,19},{19,3},{4,20},{20... | collective-permute-start | bytes 1572872 | tf_op jit(solution)/shard_map/ppermute | solution.py:268
  0.5 18.0 %collective-permute-start.4 = (bf16[16,128,128]{2,1,0:T(8,128)(2,1)}, bf16[16,128,128]{2,1,0:T(8,128)(2,1)S(1)}, u32[]{:S(2)}, u32[]{:S(2)}) collective-permute-start(bf16[16,128,128]{2,1,0:T(8,128)(2,1)} %bitcast.35), channel_id=1, source_target_pairs={{0,8},{8,0},{1,9},{9,1},{2,10},{10,2},{3,11},{11,3},{4,12},{12,4},... | collective-permute-start | bytes 1572872 | tf_op jit(solution)/shard_map/ppermute | solution.py:267
  3.7 14.8 %collective-permute-start.3 = (s32[32,32]{1,0:T(8,128)S(1)}, s32[32,32]{1,0:T(8,128)S(1)}, u32[]{:S(2)}, u32[]{:S(2)}) collective-permute-start(s32[32,32]{1,0:T(8,128)S(1)} %pad_add_fusion.1), channel_id=1, source_target_pairs={{0,8},{8,0},{1,9},{9,1},{2,10},{10,2},{3,11},{11,3},{4,12},{12,4},... | collective-permute-start | bytes 12296 | tf_op jit(solution)/shard_map/ppermute | solution.py:271
  3.8 1.6 %copy-start = (bf16[1,1,1,64,128,128]{5,4,3,2,1,0:T(8,128)(2,1)S(1)}, bf16[1,1,1,64,128,128]{5,4,3,2,1,0:T(8,128)(2,1)}, u32[]{:S(2)}) copy-start(bf16[1,1,1,64,128,128]{5,4,3,2,1,0:T(8,128)(2,1)} %param.4) | copy-start | bytes 6291460
  5.4 1.0 %copy-start.2 = (bf16[1,1,1,16,128,128]{5,4,3,2,1,0:T(8,128)(2,1)S(1)}, bf16[1,1,1,16,128,128]{5,4,3,2,1,0:T(8,128)(2,1)}, u32[]{:S(2)}) copy-start(bf16[1,1,1,16,128,128]{5,4,3,2,1,0:T(8,128)(2,1)} %param.5) | copy-start | bytes 1572868
  6.4 1.6 %copy-start.1 = (bf16[1,1,1,64,128,128]{5,4,3,2,1,0:T(8,128)(2,1)S(1)}, bf16[1,1,1,64,128,128]{5,4,3,2,1,0:T(8,128)(2,1)}, u32[]{:S(2)}) copy-start(bf16[1,1,1,64,128,128]{5,4,3,2,1,0:T(8,128)(2,1)} %param.4) | copy-start | bytes 6291460
  10.4 8.6 %collective-permute-start.1 = (s16[1040,128]{1,0:T(8,128)(2,1)S(1)}, s16[1040,128]{1,0:T(8,128)(2,1)S(1)}, u32[]{:S(2)}, u32[]{:S(2)}) collective-permute-start(s16[1040,128]{1,0:T(8,128)(2,1)S(1)} %get-tuple-element.26.refs_3_), channel_id=1, source_target_pairs={{0,1},{1,0},{2,3},{3,2},{4,5},{5,4},{6,7},{7,6},{8,9},{9,8},{10,11... | collective-permute-start | bytes 798728 | tf_op jit(solution)/shard_map/ppermute | solution.py:243
  19.0 1.9 %collective-permute-start.5 = (bf16[16,128,128]{2,1,0:T(8,128)(2,1)S(1)}, bf16[16,128,128]{2,1,0:T(8,128)(2,1)S(1)}, u32[]{:S(2)}, u32[]{:S(2)}) collective-permute-start(bf16[16,128,128]{2,1,0:T(8,128)(2,1)S(1)} %shard_map.50.refs_2_), channel_id=1, source_target_pairs={{0,16},{16,0},{1,17},{17,1},{2,18},{18,2},{3,19},{19,3},{4,20},{20... | collective-permute-start | bytes 1572872 | tf_op jit(solution)/shard_map/ppermute | solution.py:282
  19.0 9.2 %collective-permute-start.2 = (s16[1040,128]{1,0:T(8,128)(2,1)S(1)}, s16[1040,128]{1,0:T(8,128)(2,1)S(1)}, u32[]{:S(2)}, u32[]{:S(2)}) collective-permute-start(s16[1040,128]{1,0:T(8,128)(2,1)S(1)} %shard_map.48.refs_3_), channel_id=1, source_target_pairs={{0,1},{1,0},{2,3},{3,2},{4,5},{5,4},{6,7},{7,6},{8,9},{9,8},{10,11... | collective-permute-start | bytes 798728 | tf_op jit(solution)/shard_map/ppermute | solution.py:243
  23.3 10.7 %collective-permute-start.7 = (s16[1040,128]{1,0:T(8,128)(2,1)S(1)}, s16[1040,128]{1,0:T(8,128)(2,1)S(1)}, u32[]{:S(2)}, u32[]{:S(2)}) collective-permute-start(s16[1040,128]{1,0:T(8,128)(2,1)S(1)} %get-tuple-element.30.refs_3_), channel_id=1, source_target_pairs={{0,1},{1,0},{2,3},{3,2},{4,5},{5,4},{6,7},{7,6},{8,9},{9,8},{10,11... | collective-permute-start | bytes 798728 | tf_op jit(solution)/shard_map/ppermute | solution.py:243
  27.5 11.7 %collective-permute-start.9 = (s16[1040,128]{1,0:T(8,128)(2,1)S(1)}, s16[1040,128]{1,0:T(8,128)(2,1)S(1)}, u32[]{:S(2)}, u32[]{:S(2)}) collective-permute-start(s16[1040,128]{1,0:T(8,128)(2,1)S(1)} %shard_map.52.refs_4_), channel_id=1, source_target_pairs={{0,1},{1,0},{2,3},{3,2},{4,5},{5,4},{6,7},{7,6},{8,9},{9,8},{10,11... | collective-permute-start | bytes 798728 | tf_op jit(solution)/shard_map/ppermute | solution.py:243
  28.5 7.8 %collective-permute-start.6 = (s16[1040,128]{1,0:T(8,128)(2,1)S(1)}, s16[1040,128]{1,0:T(8,128)(2,1)S(1)}, u32[]{:S(2)}, u32[]{:S(2)}) collective-permute-start(s16[1040,128]{1,0:T(8,128)(2,1)S(1)} %get-tuple-element.32.refs_3_), channel_id=1, source_target_pairs={{0,2},{1,3},{2,0},{3,1},{4,6},{5,7},{6,4},{7,5},{8,10},{9,11},{10,... | collective-permute-start | bytes 798728 | tf_op jit(solution)/shard_map/ppermute | solution.py:243
  34.3 9.6 %collective-permute-start.11 = (s16[528,128]{1,0:T(8,128)(2,1)S(1)}, s16[528,128]{1,0:T(8,128)(2,1)S(1)}, u32[]{:S(2)}, u32[]{:S(2)}) collective-permute-start(s16[528,128]{1,0:T(8,128)(2,1)S(1)} %get-tuple-element.34.refs_2_), channel_id=1, source_target_pairs={{0,2},{1,3},{2,0},{3,1},{4,6},{5,7},{6,4},{7,5},{8,10},{9,11},{10,... | collective-permute-start | bytes 405512 | tf_op jit(solution)/shard_map/ppermute | solution.py:243
  39.4 7.2 %collective-permute-start.10 = (s16[528,128]{1,0:T(8,128)(2,1)S(1)}, s16[528,128]{1,0:T(8,128)(2,1)S(1)}, u32[]{:S(2)}, u32[]{:S(2)}) collective-permute-start(s16[528,128]{1,0:T(8,128)(2,1)S(1)} %get-tuple-element.39.refs_2_), channel_id=1, source_target_pairs={{0,2},{1,3},{2,0},{3,1},{4,6},{5,7},{6,4},{7,5},{8,10},{9,11},{10,... | collective-permute-start | bytes 405512 | tf_op jit(solution)/shard_map/ppermute | solution.py:243
  41.2 12.1 %collective-permute-start.8 = (s16[528,128]{1,0:T(8,128)(2,1)S(1)}, s16[528,128]{1,0:T(8,128)(2,1)S(1)}, u32[]{:S(2)}, u32[]{:S(2)}) collective-permute-start(s16[528,128]{1,0:T(8,128)(2,1)S(1)} %get-tuple-element.36.refs_2_), channel_id=1, source_target_pairs={{0,4},{1,5},{2,6},{3,7},{4,0},{5,1},{6,2},{7,3},{8,12},{9,13},{10,... | collective-permute-start | bytes 405512 | tf_op jit(solution)/shard_map/ppermute | solution.py:243
  44.0 9.4 %collective-permute-start.15 = (s16[272,128]{1,0:T(8,128)(2,1)S(1)}, s16[272,128]{1,0:T(8,128)(2,1)S(1)}, u32[]{:S(2)}, u32[]{:S(2)}) collective-permute-start(s16[272,128]{1,0:T(8,128)(2,1)S(1)} %get-tuple-element.44), channel_id=1, source_target_pairs={{0,8},{1,9},{2,10},{3,11},{4,12},{5,13},{6,14},{7,15},{8,0},{9,1},... | collective-permute-start | bytes 208904 | tf_op jit(solution)/shard_map/ppermute | solution.py:248
  45.5 10.3 %collective-permute-start.14 = (s16[272,128]{1,0:T(8,128)(2,1)S(1)}, s16[272,128]{1,0:T(8,128)(2,1)S(1)}, u32[]{:S(2)}, u32[]{:S(2)}) collective-permute-start(s16[272,128]{1,0:T(8,128)(2,1)S(1)} %get-tuple-element.41.refs_2_), channel_id=1, source_target_pairs={{0,12},{1,13},{2,14},{3,15},{4,8},{5,9},{6,10},{7,11},{8,4},{9,5},... | collective-permute-start | bytes 208904 | tf_op jit(solution)/shard_map/ppermute | solution.py:248
  46.7 10.3 %collective-permute-start.12 = (s16[272,128]{1,0:T(8,128)(2,1)S(1)}, s16[272,128]{1,0:T(8,128)(2,1)S(1)}, u32[]{:S(2)}, u32[]{:S(2)}) collective-permute-start(s16[272,128]{1,0:T(8,128)(2,1)S(1)} %get-tuple-element.42), channel_id=1, source_target_pairs={{0,12},{1,13},{2,14},{3,15},{4,8},{5,9},{6,10},{7,11},{8,4},{9,5},... | collective-permute-start | bytes 208904 | tf_op jit(solution)/shard_map/ppermute | solution.py:248
  49.9 7.2 %collective-permute-start.13 = (s16[272,128]{1,0:T(8,128)(2,1)S(1)}, s16[272,128]{1,0:T(8,128)(2,1)S(1)}, u32[]{:S(2)}, u32[]{:S(2)}) collective-permute-start(s16[272,128]{1,0:T(8,128)(2,1)S(1)} %get-tuple-element.43), channel_id=1, source_target_pairs={{0,8},{1,9},{2,10},{3,11},{4,12},{5,13},{6,14},{7,15},{8,0},{9,1},... | collective-permute-start | bytes 208904 | tf_op jit(solution)/shard_map/ppermute | solution.py:248

commit v5 on v4

--- a/solution.py
+++ b/solution.py
@@ -110,11 +110,11 @@
     return kernel
 
 
-def keep_kernel(fan, count, chunks, bit):
+def keep_kernel(fan, count, chunks, bits):
     def kernel(lists_ref, a_ref, p_ref, *out_refs):
         find = finder(lists_ref, fan)
-        side = own_bit(bit)
-        for (first, size), out_ref in zip(chunks, out_refs):
+        for (first, size), bit, out_ref in zip(chunks, bits, out_refs):
+            side = own_bit(bit)
 
             def body(step, _):
                 for k in range(GROUP):
@@ -247,74 +247,89 @@
         perm = [(c * layers + i, (1 - c) * layers + (i ^ flip)) for c in range(2) for i in range(layers)]
         return lax.ppermute(x, ("col", "layer"), perm)
 
-    def start(smem, vmem, chunk, bit, after):
-        shapes = [message(layers // 2 * chunk[1], width), jax.ShapeDtypeStruct((2 * held, width, width), p.dtype)]
-        return call(send_kernel(2, fan, count, chunk, bit), shapes, smem, vmem, after, (), flops)
-
-    def send(smem, vmem, chunk, bit, after):
-        shape = message(layers // 2 * chunk[1], width)
-        return call(send_kernel(1, fan, count, chunk, bit), shape, smem, vmem, after, (), flops)
-
-    def keep(smem, vmem, bit, after):
+    def start(lists, vmem, n, after):
+        shapes = [message(layers // 2 * chunks[n][1], width), jax.ShapeDtypeStruct((2 * held, width, width), p.dtype)]
+        return call(send_kernel(2, fan, count, chunks[n], first_bits[n]), shapes, (lists,), vmem, after, (), flops)
+
+    def send(lists, vmem, n, after):
+        shape = message(layers // 2 * chunks[n][1], width)
+        return call(send_kernel(1, fan, count, chunks[n], first_bits[n]), shape, (lists,), vmem, after, (), flops)
+
+    def keep(lists, vmem, after):
         shapes = [floats(layers // 2 * size) for _, size in chunks]
-        return call(keep_kernel(fan, count, chunks, bit), shapes, smem, vmem, after, (), 2 * flops)
-
-    def add(kept, came, sizes, rest, bit, keeps, after):
+        kernel = keep_kernel(fan, count, chunks, first_bits)
+        return call(kernel, shapes, (lists,), vmem, after, (), 2 * flops)
+
+    def add(parts, sizes, rest, bit, keeps, after):
         n = sum(sizes) << (len(rest) - 1)
         shapes = [message(n, width), floats(n) if keeps else message(n, width)]
+        kept, came = zip(*parts)
         return call(add_kernel(sizes, rest, bit, keeps), shapes, (), (*kept, *came), after)
+
+    first_bits = (0, 1)
+    sizes = [size for _, size in chunks]
+    every = list(range(bits))
+
+    def less(rest, bit):
+        return [b for b in rest if b != bit]
 
     p_x = lax.ppermute(p, "col", swap)
     p_r = lax.ppermute(p, "row", swap)
     col = lax.axis_index("col")
     lists = jnp.concatenate([ia[col], ip[col]], axis=0)
     lists_x = lax.ppermute(jnp.concatenate([ia[1 - col], ip[1 - col]], axis=0), "col", swap)
-    own_bits = [*range(bits)]
-    gate = call(lambda *refs: None, jax.ShapeDtypeStruct((8, width), jnp.float32), (lists,), (a, p))
-    smem, bit = (lists,), own_bits[0]
-    made, joined = start(smem, (a, p, p_r), chunks[0], bit, (gate,))
-    own_sent = [exchange(made, bit)]
-    made = send(smem, (a, joined), chunks[1], bit, (made,))
-    own_sent.append(exchange(made, bit))
-    own_kept = keep(smem, (a, joined), bit, (made,))
-
-    p_x = hold(p_x, (own_kept[0], own_sent[0], lists_x))
+
+    token = jax.ShapeDtypeStruct((8, width), jnp.float32)
+    gate = call(lambda *refs: None, token, (), (), (), (), 10**9)
+    gate = call(lambda *refs: None, token, (), (a, p), (gate,))
+
+    made, joined = start(lists, (a, p, p_r), 0, (gate,))
+    own_came = [exchange(made, first_bits[0])]
+    made = send(lists, (a, joined), 1, (made,))
+    own_came.append(exchange(made, first_bits[1]))
+    own_kept = keep(lists, (a, joined), (made,))
+    p_x = hold(p_x, (own_kept[0], own_came[0], lists_x))
     p_xr = lax.ppermute(p_x, "row", swap)
 
-    smem, bit = (lists_x,), 0
-    made, joined = start(smem, (a, p_x, p_xr), chunks[0], bit, ())
-    other_sent = [exchange(made, bit)]
-    made = send(smem, (a, joined), chunks[1], bit, (made,))
-    other_sent.append(exchange(made, bit))
-    rest = sorted(own_bits[1:])
-    sent, own_kept = add(own_kept, own_sent, [s for _, s in chunks], rest, own_bits[1], True, (made,))
-    own_sent = exchange(sent, own_bits[1])
-    other_kept = keep(smem, (a, joined), bit, (sent,))
-
-    streams = [(other_kept[n], other_sent[n]) for n in range(len(chunks))]
-    rest = list(range(1, bits))
-    after = ()
-    for b in range(1, bits - 1):
-        for n, (kept, came) in enumerate(streams):
-            sent, kept = add((kept,), (came,), [chunks[n][1]], rest, b, True, after)
+    def own_second(n, after):
+        b, other = first_bits[n], first_bits[1 - n]
+        sent, kept = add([(own_kept[n], own_came[n])], [sizes[n]], less(every, b), other, True, after)
+        return sent, (kept, exchange(sent, other))
+
+    sent, part_0 = own_second(0, ())
+
+    made, joined = start(lists_x, (a, p_x, p_xr), 0, (sent,))
+    other_came = [exchange(made, first_bits[0])]
+    made = send(lists_x, (a, joined), 1, (made,))
+    other_came.append(exchange(made, first_bits[1]))
+    sent, part_1 = own_second(1, (made,))
+    other_kept = keep(lists_x, (a, joined), (sent,))
+
+    streams, after = [], (other_kept[0],)
+    for n in range(2):
+        b, other = first_bits[n], first_bits[1 - n]
+        sent, kept = add([(other_kept[n], other_came[n])], [sizes[n]], less(every, b), other, True, after)
+        after = (sent,)
+        streams.append((kept, exchange(sent, other)))
+    rest = every[2:]
+    parts, part_sizes = [part_0, part_1], sizes
+    for b in every[2:]:
+        sent, kept = add(parts, part_sizes, rest, b, True, after)
+        after = (sent,)
+        parts, part_sizes = [(kept, exchange(sent, b))], [count]
+        rest = less(rest, b)
+    (own,) = parts
+    rest = every[2:]
+    for b in every[2:-1]:
+        for n in range(2):
+            sent, kept = add([streams[n]], [sizes[n]], rest, b, True, after)
             after = (sent,)
             streams[n] = (kept, exchange(sent, b))
-            if n == 0 and len(own_bits) > 2:
-                own_rest = sorted(own_bits[2:])
-                sent, own_kept = add((own_kept,), (own_sent,), [count], own_rest, own_bits[2], True, after)
-                own_sent = exchange(sent, own_bits[2])
-                own_bits = own_bits[:2] + own_bits[3:]
-                after = (sent,)
-        rest.remove(b)
-    for b in own_bits[2:]:
-        own_rest = sorted(own_bits[own_bits.index(b) :])
-        sent, own_kept = add((own_kept,), (own_sent,), [count], own_rest, b, True, after)
-        own_sent = exchange(sent, b)
-        after = (sent,)
+        rest = less(rest, b)
 
     moved = []
-    for n, (kept, came) in enumerate(streams):
-        sent, stay = add((kept,), (came,), [chunks[n][1]], rest, rest[0], False, after)
+    for n in range(2):
+        sent, stay = add([streams[n]], [sizes[n]], rest, rest[0], False, after)
         after = (sent,)
         moved.append((cross(sent, rest[0]), cross(stay, None)))
     result = ()
@@ -322,7 +337,7 @@
         final = n == len(chunks) - 1
         shape = jax.ShapeDtypeStruct((count if final else size, width, width), jnp.bfloat16)
         kernel = last_kernel(first, size, count, len(moved[n]), len(result))
-        result = (call(kernel, shape, (), (own_kept, own_sent, *moved[n], *result)),)
+        result = (call(kernel, shape, (), (*own, *moved[n], *result)),)
     return result[0][None, None]
 
 

time: 58 us -> 52.4 us (0.903)
  waiting for transfers between devices: 11.5 us -> 8.45 us
  local copies, waits for them, and re-layouts: 4.15 us -> 2.32 us
    ppermute x8 -> x9, waiting for transfers between devices: 7.72 us -> 5.09 us  [exchange(): return lax.ppermute(x, 'layer', [(i, i ^ 1 << bit) for i in range(layers)])]
    unnamed x6 -> x4, local copies, waits for them, and re-layouts: 3.4 us -> 1.57 us
    ppermute x4, waiting for transfers between devices: 3.65 us -> 2.66 us  [cross(): return lax.ppermute(x, ('col', 'layer'), perm)]
    ppermute x1, waiting for transfers between devices: 0.01 us -> 0.69 us  [on_device(): lax.ppermute(jnp.concatenate([ia[1 - col], ip[1 - col]], axis=0), 'col',...]
    ppermute x8 -> x9, starting transfers between devices: 14 us -> 13.3 us  [exchange(): return lax.ppermute(x, 'layer', [(i, i ^ 1 << bit) for i in range(layers)])]
    pallas_call x15 -> x17, Pallas kernels: 19.4 us -> 18.9 us  [call(): pl.pallas_call(wrapped, out_shape=out_shape, in_specs=[pl.BlockSpec(memor...]
  transfers between devices with their start and end apart: 16 -> 17, of which waited for: 9 -> 6; matrix products, arithmetic and copies ran while one was open for 1% -> 1% of each run, Pallas kernels for 32% -> 35%
where the time goes in v5:
time: 52.4 us; the launch traced here: 52.1 us
  starting transfers between devices  22.4 us (43%)
  Pallas kernels  18.9 us (36%)
  waiting for transfers between devices  8.45 us (16%)
  local copies, waits for them, and re-layouts  2.32 us (4%)
    pallas_call x17, Pallas kernels, call(): pl.pallas_call(wrapped, out_shape=out_shape, in_specs=[pl.BlockSpec(memor...  18.9 us
    ppermute x9, starting transfers between devices, exchange(): return lax.ppermute(x, 'layer', [(i, i ^ 1 << bit) for i in range(layers)])  13.3 us
    ppermute x4, starting transfers between devices, cross(): return lax.ppermute(x, ('col', 'layer'), perm)  5.98 us
    ppermute x9, waiting for transfers between devices, exchange(): return lax.ppermute(x, 'layer', [(i, i ^ 1 << bit) for i in range(layers)])  5.09 us
    ppermute x4, waiting for transfers between devices, cross(): return lax.ppermute(x, ('col', 'layer'), perm)  2.66 us
    ppermute x1, starting transfers between devices, on_device(): p_x = lax.ppermute(p, 'col', swap)  2.49 us
    unnamed x4, local copies, waits for them, and re-layouts  1.57 us
  transfers between devices with their start and end apart: 17, of which 6 were waited for; matrix products, arithmetic and copies ran while one was open for 1% of the time, Pallas kernels for 35%

profile of v5, /device:TPU:0, one launch (start us, length us, event | category | flops | bytes accessed | tf_op | source)
XLA Modules:
  0.0 52.1 jit_solution(8038503595767613874)
XLA Ops:
  0.5 2.5 %collective-permute-start.4 = (bf16[16,128,128]{2,1,0:T(8,128)(2,1)}, bf16[16,128,128]{2,1,0:T(8,128)(2,1)S(1)}, u32[]{:S(2)}, u32[]{:S(2)}) collective-permute-start(bf16[16,128,128]{2,1,0:T(8,128)(2,1)} %bitcast.35), channel_id=1, source_target_pairs={{0,8},{8,0},{1,9},{9,1},{2,10},{10,2},{3,11},{11,3},{4,12},{12,4},... | collective-permute-start | bytes 1572872 | tf_op jit(solution)/shard_map/ppermute | solution.py:276
  2.9 0.7 %dynamic-slice_bitcast_fusion = (s32[16,32]{1,0:T(8,128)S(1)}, s32[16,32]{1,0:T(8,128)S(1)}, s32[16,32]{1,0:T(8,128)S(1)}, s32[16,32]{1,0:T(8,128)S(1)}) fusion(s32[1,1,1,2,32,16]{4,5,3,2,1,0:T(8,128)} %param.7, s32[]{:T(128)S(6)} %select_n.9, s32[]{:T(128)S(6)} %select_n.8, s32[1,1,1,2,32,16]{4,5,3,2,1,0:T(8,128)} %param.6), kind=kLoop, calls=%fused_computation.2 | loop fusion | bytes 16392 | tf_op jit(solution)/shard_map/squeeze | solution.py:280
  3.8 1.5 %copy-done = bf16[1,1,1,64,128,128]{5,4,3,2,1,0:T(8,128)(2,1)S(1)} copy-done((bf16[1,1,1,64,128,128]{5,4,3,2,1,0:T(8,128)(2,1)S(1)}, bf16[1,1,1,64,128,128]{5,4,3,2,1,0:T(8,128)(2,1)}, u32[]{:S(2)}) %copy-start) | copy-done | bytes 2097176
  5.4 2.4 %shard_map.48 = (s16[1040,128]{1,0:T(8,128)(2,1)S(1)}, bf16[32,128,128]{2,1,0:T(8,128)(2,1)S(1)}) custom-call(s32[32,32]{1,0:T(8,128)S(1)} %pad_add_fusion.refs_0_, bf16[64,128,128]{2,1,0:T(8,128)(2,1)S(1)} %bitcast.28, bf16[16,128,128]{2,1,0:T(8,128)(2,1)S(1)} %bitcast.37, bf16[16,128,128]{2,1,0:T(8,128)(2,1)S(1)} %collective-permute-done.refs_3_, ...), custom_call_target="tpu_custom_call" | custom-call | flops 2684354560 | bytes 4464640 | tf_op jit(solution)/shard_map/pallas_call | solution.py:198
  7.8 1.6 %collective-permute-start.1 = (s16[1040,128]{1,0:T(8,128)(2,1)S(1)}, s16[1040,128]{1,0:T(8,128)(2,1)S(1)}, u32[]{:S(2)}, u32[]{:S(2)}) collective-permute-start(s16[1040,128]{1,0:T(8,128)(2,1)S(1)} %get-tuple-element.28.refs_3_), channel_id=1, source_target_pairs={{0,1},{1,0},{2,3},{3,2},{4,5},{5,4},{6,7},{7,6},{8,9},{9,8},{10,11... | collective-permute-start | bytes 798728 | tf_op jit(solution)/shard_map/ppermute | solution.py:243
  9.4 2.3 %shard_map.49.refs_3_ = s16[1040,128]{1,0:T(8,128)(2,1)S(1)} custom-call(s32[32,32]{1,0:T(8,128)S(1)} %pad_add_fusion.refs_0_, bf16[64,128,128]{2,1,0:T(8,128)(2,1)S(1)} %bitcast.29, bf16[32,128,128]{2,1,0:T(8,128)(2,1)S(1)} %get-tuple-element.27.refs_2_, s16[1040,128]{1,0:T(8,128)(2,1)S(1)} %get-tuple-element.28.refs_3_), custom_call_target="tpu_custom_call" | custom-call | flops 2684354560 | bytes 3416064 | tf_op jit(solution)/shard_map/pallas_call | solution.py:198
  11.7 3.7 %shard_map.50 = (f32[8,128,128]{2,1,0:T(8,128)S(1)}, f32[8,128,128]{2,1,0:T(8,128)S(1)}) custom-call(s32[32,32]{1,0:T(8,128)S(1)} %pad_add_fusion.refs_0_, bf16[64,128,128]{2,1,0:T(8,128)(2,1)S(1)} %bitcast.30, bf16[32,128,128]{2,1,0:T(8,128)(2,1)S(1)} %get-tuple-element.27.refs_2_, s16[1040,128]{1,0:T(8,128)(2,1)S(1)} %shard_map.49.refs_3_), custom_call_target="tpu_custom_call" | custom-call | flops 5368709120 | bytes 4198400 | tf_op jit(solution)/shard_map/pallas_call | solution.py:198
  15.4 0.7 %collective-permute-done.3.refs_3_.refs_0_ = s32[32,32]{1,0:T(8,128)S(1)} collective-permute-done((s32[32,32]{1,0:T(8,128)S(1)}, s32[32,32]{1,0:T(8,128)S(1)}, u32[]{:S(2)}, u32[]{:S(2)}) %collective-permute-start.3) | collective-permute-done | bytes 4128 | tf_op jit(solution)/shard_map/ppermute | solution.py:280
  16.4 1.7 %collective-permute-start.2 = (s16[1040,128]{1,0:T(8,128)(2,1)S(1)}, s16[1040,128]{1,0:T(8,128)(2,1)S(1)}, u32[]{:S(2)}, u32[]{:S(2)}) collective-permute-start(s16[1040,128]{1,0:T(8,128)(2,1)S(1)} %shard_map.49.refs_3_), channel_id=1, source_target_pairs={{0,2},{1,3},{2,0},{3,1},{4,6},{5,7},{6,4},{7,5},{8,10},{9,11},{10,... | collective-permute-start | bytes 798728 | tf_op jit(solution)/shard_map/ppermute | solution.py:243
  18.7 2.4 %shard_map.53 = (s16[1040,128]{1,0:T(8,128)(2,1)S(1)}, bf16[32,128,128]{2,1,0:T(8,128)(2,1)S(1)}) custom-call(s32[32,32]{1,0:T(8,128)S(1)} %collective-permute-done.3.refs_3_.refs_0_, bf16[64,128,128]{2,1,0:T(8,128)(2,1)S(1)} %bitcast.31, bf16[16,128,128]{2,1,0:T(8,128)(2,1)S(1)} %shard_map.52.refs_2_, ...), custom_call_target="tpu_custom_call" | custom-call | flops 2684354560 | bytes 4464640 | tf_op jit(solution)/shard_map/pallas_call | solution.py:198
  21.1 1.7 %collective-permute-start.9 = (s16[1040,128]{1,0:T(8,128)(2,1)S(1)}, s16[1040,128]{1,0:T(8,128)(2,1)S(1)}, u32[]{:S(2)}, u32[]{:S(2)}) collective-permute-start(s16[1040,128]{1,0:T(8,128)(2,1)S(1)} %get-tuple-element.34.refs_3_), channel_id=1, source_target_pairs={{0,1},{1,0},{2,3},{3,2},{4,5},{5,4},{6,7},{7,6},{8,9},{9,8},{10,11... | collective-permute-start | bytes 798728 | tf_op jit(solution)/shard_map/ppermute | solution.py:243
  22.8 2.4 %shard_map.54.refs_2_ = s16[1040,128]{1,0:T(8,128)(2,1)S(1)} custom-call(s32[32,32]{1,0:T(8,128)S(1)} %collective-permute-done.3.refs_3_.refs_0_, bf16[64,128,128]{2,1,0:T(8,128)(2,1)S(1)} %bitcast.32, bf16[32,128,128]{2,1,0:T(8,128)(2,1)S(1)} %get-tuple-element.33.refs_2_, s16[1040,128]{1,0:T(8,128)(2,1)S(1)} %get-tuple-element.34.refs_3_), custom_call_target="tpu_custom_call" | custom-call | flops 2684354560 | bytes 3416064 | tf_op jit(solution)/shard_map/pallas_call | solution.py:198
  25.2 1.6 %collective-permute-start.8 = (s16[1040,128]{1,0:T(8,128)(2,1)S(1)}, s16[1040,128]{1,0:T(8,128)(2,1)S(1)}, u32[]{:S(2)}, u32[]{:S(2)}) collective-permute-start(s16[1040,128]{1,0:T(8,128)(2,1)S(1)} %shard_map.54.refs_2_), channel_id=1, source_target_pairs={{0,2},{1,3},{2,0},{3,1},{4,6},{5,7},{6,4},{7,5},{8,10},{9,11},{10,... | collective-permute-start | bytes 798728 | tf_op jit(solution)/shard_map/ppermute | solution.py:243
  27.5 3.8 %shard_map.56 = (f32[8,128,128]{2,1,0:T(8,128)S(1)}, f32[8,128,128]{2,1,0:T(8,128)S(1)}) custom-call(s32[32,32]{1,0:T(8,128)S(1)} %collective-permute-done.3.refs_3_.refs_0_, bf16[64,128,128]{2,1,0:T(8,128)(2,1)S(1)} %bitcast.33, bf16[32,128,128]{2,1,0:T(8,128)(2,1)S(1)} %get-tuple-element.33.refs_2_, s16[528,128]{1,0:T(8,128)(2,1)S(1)} %get-tuple-element.36.refs_3_), custom_call_target="tpu_custom_call" | custom-call | flops 5368709120 | bytes 4198400 | tf_op jit(solution)/shard_map/pallas_call | solution.py:198
  31.5 1.5 %collective-permute-start.12 = (s16[528,128]{1,0:T(8,128)(2,1)S(1)}, s16[528,128]{1,0:T(8,128)(2,1)S(1)}, u32[]{:S(2)}, u32[]{:S(2)}) collective-permute-start(s16[528,128]{1,0:T(8,128)(2,1)S(1)} %get-tuple-element.39.refs_2_), channel_id=1, source_target_pairs={{0,2},{1,3},{2,0},{3,1},{4,6},{5,7},{6,4},{7,5},{8,10},{9,11},{10,... | collective-permute-start | bytes 405512 | tf_op jit(solution)/shard_map/ppermute | solution.py:243
  33.1 1.2 %collective-permute-done.8.refs_1_ = s16[1040,128]{1,0:T(8,128)(2,1)S(1)} collective-permute-done((s16[1040,128]{1,0:T(8,128)(2,1)S(1)}, s16[1040,128]{1,0:T(8,128)(2,1)S(1)}, u32[]{:S(2)}, u32[]{:S(2)}) %collective-permute-start.8) | collective-permute-done | bytes 266272 | tf_op jit(solution)/shard_map/ppermute | solution.py:243
  34.5 1.6 %collective-permute-start.11 = (s16[528,128]{1,0:T(8,128)(2,1)S(1)}, s16[528,128]{1,0:T(8,128)(2,1)S(1)}, u32[]{:S(2)}, u32[]{:S(2)}) collective-permute-start(s16[528,128]{1,0:T(8,128)(2,1)S(1)} %get-tuple-element.40.refs_4_), channel_id=1, source_target_pairs={{0,1},{1,0},{2,3},{3,2},{4,5},{5,4},{6,7},{7,6},{8,9},{9,8},{10,11... | collective-permute-start | bytes 405512 | tf_op jit(solution)/shard_map/ppermute | solution.py:243
  36.2 2.7 %collective-permute-start.10 = (s16[528,128]{1,0:T(8,128)(2,1)S(1)}, s16[528,128]{1,0:T(8,128)(2,1)S(1)}, u32[]{:S(2)}, u32[]{:S(2)}) collective-permute-start(s16[528,128]{1,0:T(8,128)(2,1)S(1)} %get-tuple-element.42.refs_2_), channel_id=1, source_target_pairs={{0,4},{1,5},{2,6},{3,7},{4,0},{5,1},{6,2},{7,3},{8,12},{9,13},{10,... | collective-permute-start | bytes 405512 | tf_op jit(solution)/shard_map/ppermute | solution.py:243
  39.0 1.5 %collective-permute-start.15 = (s16[272,128]{1,0:T(8,128)(2,1)S(1)}, s16[272,128]{1,0:T(8,128)(2,1)S(1)}, u32[]{:S(2)}, u32[]{:S(2)}) collective-permute-start(s16[272,128]{1,0:T(8,128)(2,1)S(1)} %get-tuple-element.45.refs_2_), channel_id=1, source_target_pairs={{0,12},{1,13},{2,14},{3,15},{4,8},{5,9},{6,10},{7,11},{8,4},{9,5},... | collective-permute-start | bytes 208904 | tf_op jit(solution)/shard_map/ppermute | solution.py:248
  41.1 3.5 %collective-permute-start.13 = (s16[272,128]{1,0:T(8,128)(2,1)S(1)}, s16[272,128]{1,0:T(8,128)(2,1)S(1)}, u32[]{:S(2)}, u32[]{:S(2)}) collective-permute-start(s16[272,128]{1,0:T(8,128)(2,1)S(1)} %get-tuple-element.46), channel_id=1, source_target_pairs={{0,12},{1,13},{2,14},{3,15},{4,8},{5,9},{6,10},{7,11},{8,4},{9,5},... | collective-permute-start | bytes 208904 | tf_op jit(solution)/shard_map/ppermute | solution.py:248
  45.1 3.6 %collective-permute-done.10.refs_1_ = s16[528,128]{1,0:T(8,128)(2,1)S(1)} collective-permute-done((s16[528,128]{1,0:T(8,128)(2,1)S(1)}, s16[528,128]{1,0:T(8,128)(2,1)S(1)}, u32[]{:S(2)}, u32[]{:S(2)}) %collective-permute-start.10) | collective-permute-done | bytes 135200 | tf_op jit(solution)/shard_map/ppermute | solution.py:243
  48.6 2.0 %collective-permute-done.15.refs_2_ = s16[272,128]{1,0:T(8,128)(2,1)S(1)} collective-permute-done((s16[272,128]{1,0:T(8,128)(2,1)S(1)}, s16[272,128]{1,0:T(8,128)(2,1)S(1)}, u32[]{:S(2)}, u32[]{:S(2)}) %collective-permute-start.15) | collective-permute-done | bytes 69664 | tf_op jit(solution)/shard_map/ppermute | solution.py:248
  50.7 0.7 %collective-permute-done.13.refs_2_ = s16[272,128]{1,0:T(8,128)(2,1)S(1)} collective-permute-done((s16[272,128]{1,0:T(8,128)(2,1)S(1)}, s16[272,128]{1,0:T(8,128)(2,1)S(1)}, u32[]{:S(2)}, u32[]{:S(2)}) %collective-permute-start.13) | collective-permute-done | bytes 69664 | tf_op jit(solution)/shard_map/ppermute | solution.py:248
  51.4 0.7 %shard_map.63 = bf16[4,128,128]{2,1,0:T(8,128)(2,1)} custom-call(f32[4,128,128]{2,1,0:T(8,128)S(1)} %get-tuple-element.41.refs_0_, s16[528,128]{1,0:T(8,128)(2,1)S(1)} %collective-permute-done.10.refs_1_, s16[272,128]{1,0:T(8,128)(2,1)S(1)} %collective-permute-done.13.refs_2_, s16[272,128]{1,0:T(8,128)(2,1)S(1)} %collective-permute-done.14.refs_3_, ...), custom_call_target="tpu_custom_call" | custom-call | bytes 733184 | tf_op jit(solution)/shard_map/pallas_call | solution.py:198
  (35 shorter events, 4.1 us)
Async XLA Ops:
  0.0 5.4 %collective-permute-start = (bf16[16,128,128]{2,1,0:T(8,128)(2,1)}, bf16[16,128,128]{2,1,0:T(8,128)(2,1)S(1)}, u32[]{:S(2)}, u32[]{:S(2)}) collective-permute-start(bf16[16,128,128]{2,1,0:T(8,128)(2,1)} %bitcast.34), channel_id=1, source_target_pairs={{0,16},{16,0},{1,17},{17,1},{2,18},{18,2},{3,19},{19,3},{4,20},{20... | collective-permute-start | bytes 1572872 | tf_op jit(solution)/shard_map/ppermute | solution.py:277
  0.5 15.6 %collective-permute-start.4 = (bf16[16,128,128]{2,1,0:T(8,128)(2,1)}, bf16[16,128,128]{2,1,0:T(8,128)(2,1)S(1)}, u32[]{:S(2)}, u32[]{:S(2)}) collective-permute-start(bf16[16,128,128]{2,1,0:T(8,128)(2,1)} %bitcast.35), channel_id=1, source_target_pairs={{0,8},{8,0},{1,9},{9,1},{2,10},{10,2},{3,11},{11,3},{4,12},{12,4},... | collective-permute-start | bytes 1572872 | tf_op jit(solution)/shard_map/ppermute | solution.py:276
  3.7 1.6 %copy-start = (bf16[1,1,1,64,128,128]{5,4,3,2,1,0:T(8,128)(2,1)S(1)}, bf16[1,1,1,64,128,128]{5,4,3,2,1,0:T(8,128)(2,1)}, u32[]{:S(2)}) copy-start(bf16[1,1,1,64,128,128]{5,4,3,2,1,0:T(8,128)(2,1)} %param.4) | copy-start | bytes 6291460
  3.7 1.7 %copy-start.1 = (bf16[1,1,1,16,128,128]{5,4,3,2,1,0:T(8,128)(2,1)S(1)}, bf16[1,1,1,16,128,128]{5,4,3,2,1,0:T(8,128)(2,1)}, u32[]{:S(2)}) copy-start(bf16[1,1,1,16,128,128]{5,4,3,2,1,0:T(8,128)(2,1)} %param.5) | copy-start | bytes 1572868
  3.7 12.4 %collective-permute-start.3 = (s32[32,32]{1,0:T(8,128)S(1)}, s32[32,32]{1,0:T(8,128)S(1)}, u32[]{:S(2)}, u32[]{:S(2)}) collective-permute-start(s32[32,32]{1,0:T(8,128)S(1)} %pad_add_fusion.1), channel_id=1, source_target_pairs={{0,8},{8,0},{1,9},{9,1},{2,10},{10,2},{3,11},{11,3},{4,12},{12,4},... | collective-permute-start | bytes 12296 | tf_op jit(solution)/shard_map/ppermute | solution.py:280
  7.8 8.6 %collective-permute-start.1 = (s16[1040,128]{1,0:T(8,128)(2,1)S(1)}, s16[1040,128]{1,0:T(8,128)(2,1)S(1)}, u32[]{:S(2)}, u32[]{:S(2)}) collective-permute-start(s16[1040,128]{1,0:T(8,128)(2,1)S(1)} %get-tuple-element.28.refs_3_), channel_id=1, source_target_pairs={{0,1},{1,0},{2,3},{3,2},{4,5},{5,4},{6,7},{7,6},{8,9},{9,8},{10,11... | collective-permute-start | bytes 798728 | tf_op jit(solution)/shard_map/ppermute | solution.py:243
  16.4 2.3 %collective-permute-start.5 = (bf16[16,128,128]{2,1,0:T(8,128)(2,1)S(1)}, bf16[16,128,128]{2,1,0:T(8,128)(2,1)S(1)}, u32[]{:S(2)}, u32[]{:S(2)}) collective-permute-start(bf16[16,128,128]{2,1,0:T(8,128)(2,1)S(1)} %shard_map.52.refs_2_), channel_id=1, source_target_pairs={{0,16},{16,0},{1,17},{17,1},{2,18},{18,2},{3,19},{19,3},{4,20},{20... | collective-permute-start | bytes 1572872 | tf_op jit(solution)/shard_map/ppermute | solution.py:292
  16.4 10.4 %collective-permute-start.2 = (s16[1040,128]{1,0:T(8,128)(2,1)S(1)}, s16[1040,128]{1,0:T(8,128)(2,1)S(1)}, u32[]{:S(2)}, u32[]{:S(2)}) collective-permute-start(s16[1040,128]{1,0:T(8,128)(2,1)S(1)} %shard_map.49.refs_3_), channel_id=1, source_target_pairs={{0,2},{1,3},{2,0},{3,1},{4,6},{5,7},{6,4},{7,5},{8,10},{9,11},{10,... | collective-permute-start | bytes 798728 | tf_op jit(solution)/shard_map/ppermute | solution.py:243
  18.2 17.8 %collective-permute-start.6 = (s16[528,128]{1,0:T(8,128)(2,1)S(1)}, s16[528,128]{1,0:T(8,128)(2,1)S(1)}, u32[]{:S(2)}, u32[]{:S(2)}) collective-permute-start(s16[528,128]{1,0:T(8,128)(2,1)S(1)} %get-tuple-element.32.refs_4_), channel_id=1, source_target_pairs={{0,2},{1,3},{2,0},{3,1},{4,6},{5,7},{6,4},{7,5},{8,10},{9,11},{10,... | collective-permute-start | bytes 405512 | tf_op jit(solution)/shard_map/ppermute | solution.py:243
  21.1 10.3 %collective-permute-start.9 = (s16[1040,128]{1,0:T(8,128)(2,1)S(1)}, s16[1040,128]{1,0:T(8,128)(2,1)S(1)}, u32[]{:S(2)}, u32[]{:S(2)}) collective-permute-start(s16[1040,128]{1,0:T(8,128)(2,1)S(1)} %get-tuple-element.34.refs_3_), channel_id=1, source_target_pairs={{0,1},{1,0},{2,3},{3,2},{4,5},{5,4},{6,7},{7,6},{8,9},{9,8},{10,11... | collective-permute-start | bytes 798728 | tf_op jit(solution)/shard_map/ppermute | solution.py:243
  25.2 9.1 %collective-permute-start.8 = (s16[1040,128]{1,0:T(8,128)(2,1)S(1)}, s16[1040,128]{1,0:T(8,128)(2,1)S(1)}, u32[]{:S(2)}, u32[]{:S(2)}) collective-permute-start(s16[1040,128]{1,0:T(8,128)(2,1)S(1)} %shard_map.54.refs_2_), channel_id=1, source_target_pairs={{0,2},{1,3},{2,0},{3,1},{4,6},{5,7},{6,4},{7,5},{8,10},{9,11},{10,... | collective-permute-start | bytes 798728 | tf_op jit(solution)/shard_map/ppermute | solution.py:243
  27.0 9.1 %collective-permute-start.7 = (s16[528,128]{1,0:T(8,128)(2,1)S(1)}, s16[528,128]{1,0:T(8,128)(2,1)S(1)}, u32[]{:S(2)}, u32[]{:S(2)}) collective-permute-start(s16[528,128]{1,0:T(8,128)(2,1)S(1)} %get-tuple-element.36.refs_3_), channel_id=1, source_target_pairs={{0,1},{1,0},{2,3},{3,2},{4,5},{5,4},{6,7},{7,6},{8,9},{9,8},{10,11... | collective-permute-start | bytes 405512 | tf_op jit(solution)/shard_map/ppermute | solution.py:243
  31.5 7.3 %collective-permute-start.12 = (s16[528,128]{1,0:T(8,128)(2,1)S(1)}, s16[528,128]{1,0:T(8,128)(2,1)S(1)}, u32[]{:S(2)}, u32[]{:S(2)}) collective-permute-start(s16[528,128]{1,0:T(8,128)(2,1)S(1)} %get-tuple-element.39.refs_2_), channel_id=1, source_target_pairs={{0,2},{1,3},{2,0},{3,1},{4,6},{5,7},{6,4},{7,5},{8,10},{9,11},{10,... | collective-permute-start | bytes 405512 | tf_op jit(solution)/shard_map/ppermute | solution.py:243
  34.5 6.5 %collective-permute-start.11 = (s16[528,128]{1,0:T(8,128)(2,1)S(1)}, s16[528,128]{1,0:T(8,128)(2,1)S(1)}, u32[]{:S(2)}, u32[]{:S(2)}) collective-permute-start(s16[528,128]{1,0:T(8,128)(2,1)S(1)} %get-tuple-element.40.refs_4_), channel_id=1, source_target_pairs={{0,1},{1,0},{2,3},{3,2},{4,5},{5,4},{6,7},{7,6},{8,9},{9,8},{10,11... | collective-permute-start | bytes 405512 | tf_op jit(solution)/shard_map/ppermute | solution.py:243
  36.2 12.4 %collective-permute-start.10 = (s16[528,128]{1,0:T(8,128)(2,1)S(1)}, s16[528,128]{1,0:T(8,128)(2,1)S(1)}, u32[]{:S(2)}, u32[]{:S(2)}) collective-permute-start(s16[528,128]{1,0:T(8,128)(2,1)S(1)} %get-tuple-element.42.refs_2_), channel_id=1, source_target_pairs={{0,4},{1,5},{2,6},{3,7},{4,0},{5,1},{6,2},{7,3},{8,12},{9,13},{10,... | collective-permute-start | bytes 405512 | tf_op jit(solution)/shard_map/ppermute | solution.py:243
  39.0 11.7 %collective-permute-start.15 = (s16[272,128]{1,0:T(8,128)(2,1)S(1)}, s16[272,128]{1,0:T(8,128)(2,1)S(1)}, u32[]{:S(2)}, u32[]{:S(2)}) collective-permute-start(s16[272,128]{1,0:T(8,128)(2,1)S(1)} %get-tuple-element.45.refs_2_), channel_id=1, source_target_pairs={{0,12},{1,13},{2,14},{3,15},{4,8},{5,9},{6,10},{7,11},{8,4},{9,5},... | collective-permute-start | bytes 208904 | tf_op jit(solution)/shard_map/ppermute | solution.py:248
  40.4 10.2 %collective-permute-start.16 = (s16[272,128]{1,0:T(8,128)(2,1)S(1)}, s16[272,128]{1,0:T(8,128)(2,1)S(1)}, u32[]{:S(2)}, u32[]{:S(2)}) collective-permute-start(s16[272,128]{1,0:T(8,128)(2,1)S(1)} %get-tuple-element.48), channel_id=1, source_target_pairs={{0,8},{1,9},{2,10},{3,11},{4,12},{5,13},{6,14},{7,15},{8,0},{9,1},... | collective-permute-start | bytes 208904 | tf_op jit(solution)/shard_map/ppermute | solution.py:248
  41.1 10.3 %collective-permute-start.13 = (s16[272,128]{1,0:T(8,128)(2,1)S(1)}, s16[272,128]{1,0:T(8,128)(2,1)S(1)}, u32[]{:S(2)}, u32[]{:S(2)}) collective-permute-start(s16[272,128]{1,0:T(8,128)(2,1)S(1)} %get-tuple-element.46), channel_id=1, source_target_pairs={{0,12},{1,13},{2,14},{3,15},{4,8},{5,9},{6,10},{7,11},{8,4},{9,5},... | collective-permute-start | bytes 208904 | tf_op jit(solution)/shard_map/ppermute | solution.py:248
  44.5 6.8 %collective-permute-start.14 = (s16[272,128]{1,0:T(8,128)(2,1)S(1)}, s16[272,128]{1,0:T(8,128)(2,1)S(1)}, u32[]{:S(2)}, u32[]{:S(2)}) collective-permute-start(s16[272,128]{1,0:T(8,128)(2,1)S(1)} %get-tuple-element.47), channel_id=1, source_target_pairs={{0,8},{1,9},{2,10},{3,11},{4,12},{5,13},{6,14},{7,15},{8,0},{9,1},... | collective-permute-start | bytes 208904 | tf_op jit(solution)/shard_map/ppermute | solution.py:248

commit v6 on v5

--- a/solution.py
+++ b/solution.py
@@ -7,7 +7,7 @@
 
 PEAK = 32766.0
 ROWS = 16
-GROUP = 4
+GROUP = 8
 SMEM = pltpu.MemorySpace.SMEM
 VMEM = pltpu.MemorySpace.VMEM
 
@@ -79,33 +79,27 @@
     return lambda t: lambda f: (lists_ref[f, t], lists_ref[fan + f, t])
 
 
-def send_kernel(n_p, fan, count, chunk, bit):
-    first, size = chunk
-
-    def kernel(lists_ref, a_ref, *refs):
+def send_kernel(fan, count, chunks, bits):
+    def kernel(lists_ref, a_ref, p0_ref, p1_ref, *refs):
         find = finder(lists_ref, fan)
-        p_refs, out_ref = refs[:n_p], refs[n_p]
-        width = out_ref.shape[-1]
-        if n_p == 2:
-            p_ref = refs[-1]
-            held = p_refs[0].shape[0]
-            row = lax.axis_index("row")
-            p_ref[pl.ds(row * held, held)] = p_refs[0][...]
-            p_ref[pl.ds((1 - row) * held, held)] = p_refs[1][...]
-        else:
-            (p_ref,) = p_refs
-        side = 1 - own_bit(bit)
-        total = out_ref.shape[0] // width
-
-        def body(step, head):
-            for k in range(GROUP):
-                slot = step * GROUP + k
-                layer = insert(slot // size, bit, side)
-                tile = product(a_ref, p_ref, find(layer * count + first + slot % size), fan)
-                head = put_tile(out_ref, slot, tile, head)
-            return head
-
-        put_head(out_ref, lax.fori_loop(0, total // GROUP, body, new_head(total, width)))
+        out_refs, p_ref = refs[:-1], refs[-1]
+        held, width = p0_ref.shape[:2]
+        row = lax.axis_index("row")
+        p_ref[pl.ds(row * held, held)] = p0_ref[...]
+        p_ref[pl.ds((1 - row) * held, held)] = p1_ref[...]
+        for (first, size), bit, out_ref in zip(chunks, bits, out_refs):
+            side = 1 - own_bit(bit)
+            total = out_ref.shape[0] // width
+
+            def body(step, head):
+                for k in range(GROUP):
+                    slot = step * GROUP + k
+                    layer = insert(slot // size, bit, side)
+                    tile = product(a_ref, p_ref, find(layer * count + first + slot % size), fan)
+                    head = put_tile(out_ref, slot, tile, head)
+                return head
+
+            put_head(out_ref, lax.fori_loop(0, total // GROUP, body, new_head(total, width)))
 
     return kernel
 
@@ -169,17 +163,23 @@
     return kernel
 
 
-def last_kernel(first, size, n_own, n_messages, n_before):
-    def kernel(own_ref, own_in_ref, *refs):
+def sum_kernel(kept_ref, in_ref, out_ref):
+    count = out_ref.shape[0]
+    head = get_head(in_ref, count)
+    for i in range(count):
+        out_ref[i] = kept_ref[i] + get_tile(in_ref, i, head)
+
+
+def last_kernel(first, size, n_messages, n_before):
+    def kernel(own_ref, *refs):
         in_refs, before_refs, out_ref = refs[:n_messages], refs[n_messages:-1], refs[-1]
         at = 0
         for ref in before_refs:
             out_ref[pl.ds(at, ref.shape[0])] = ref[...]
             at += ref.shape[0]
-        own_head = get_head(own_in_ref, n_own)
         heads = [get_head(ref, size) for ref in in_refs]
         for i in range(size):
-            total = own_ref[first + i] + get_tile(own_in_ref, first + i, own_head)
+            total = own_ref[first + i]
             for ref, head in zip(in_refs, heads):
                 total += get_tile(ref, i, head)
             out_ref[at + i] = total.astype(out_ref.dtype)
@@ -247,13 +247,11 @@
         perm = [(c * layers + i, (1 - c) * layers + (i ^ flip)) for c in range(2) for i in range(layers)]
         return lax.ppermute(x, ("col", "layer"), perm)
 
-    def start(lists, vmem, n, after):
-        shapes = [message(layers // 2 * chunks[n][1], width), jax.ShapeDtypeStruct((2 * held, width, width), p.dtype)]
-        return call(send_kernel(2, fan, count, chunks[n], first_bits[n]), shapes, (lists,), vmem, after, (), flops)
-
-    def send(lists, vmem, n, after):
-        shape = message(layers // 2 * chunks[n][1], width)
-        return call(send_kernel(1, fan, count, chunks[n], first_bits[n]), shape, (lists,), vmem, after, (), flops)
+    def send(lists, vmem, after):
+        shapes = [message(layers // 2 * size, width) for _, size in chunks]
+        shapes.append(jax.ShapeDtypeStruct((2 * held, width, width), p.dtype))
+        *made, joined = call(send_kernel(fan, count, chunks, first_bits), shapes, (lists,), vmem, after, (), 2 * flops)
+        return made, joined, [exchange(x, b) for x, b in zip(made, first_bits)]
 
     def keep(lists, vmem, after):
         shapes = [floats(layers // 2 * size) for _, size in chunks]
@@ -277,33 +275,33 @@
     p_r = lax.ppermute(p, "row", swap)
     col = lax.axis_index("col")
     lists = jnp.concatenate([ia[col], ip[col]], axis=0)
-    lists_x = lax.ppermute(jnp.concatenate([ia[1 - col], ip[1 - col]], axis=0), "col", swap)
+    lists_far = jnp.concatenate([ia[1 - col], ip[1 - col]], axis=0)
 
     token = jax.ShapeDtypeStruct((8, width), jnp.float32)
     gate = call(lambda *refs: None, token, (), (), (), (), 10**9)
     gate = call(lambda *refs: None, token, (), (a, p), (gate,))
 
-    made, joined = start(lists, (a, p, p_r), 0, (gate,))
-    own_came = [exchange(made, first_bits[0])]
-    made = send(lists, (a, joined), 1, (made,))
-    own_came.append(exchange(made, first_bits[1]))
-    own_kept = keep(lists, (a, joined), (made,))
-    p_x = hold(p_x, (own_kept[0], own_came[0], lists_x))
-    p_xr = lax.ppermute(p_x, "row", swap)
-
-    def own_second(n, after):
+    made, joined, own_came = send(lists, (a, p, p_r), (gate,))
+    lists_x = lax.ppermute(hold(lists_far, made[:1]), "col", swap)
+    own_kept = keep(lists, (a, joined), made[:1])
+    parts, after = [], ()
+    for n in range(2):
         b, other = first_bits[n], first_bits[1 - n]
         sent, kept = add([(own_kept[n], own_came[n])], [sizes[n]], less(every, b), other, True, after)
-        return sent, (kept, exchange(sent, other))
-
-    sent, part_0 = own_second(0, ())
-
-    made, joined = start(lists_x, (a, p_x, p_xr), 0, (sent,))
-    other_came = [exchange(made, first_bits[0])]
-    made = send(lists_x, (a, joined), 1, (made,))
-    other_came.append(exchange(made, first_bits[1]))
-    sent, part_1 = own_second(1, (made,))
-    other_kept = keep(lists_x, (a, joined), (sent,))
+        after = (sent,)
+        parts.append((kept, exchange(sent, other)))
+    p_x = hold(p_x, (*after, lists_x))
+    p_xr = lax.ppermute(p_x, "row", swap)
+
+    made, joined, other_came = send(lists_x, (a, p_x, p_xr), ())
+    rest, part_sizes, after = every[2:], sizes, made[:1]
+    for b in every[2:]:
+        sent, kept = add(parts, part_sizes, rest, b, True, after)
+        after = (sent,)
+        parts, part_sizes = [(kept, exchange(sent, b))], [count]
+        rest = less(rest, b)
+    (own,) = parts
+    other_kept = keep(lists_x, (a, joined), after)
 
     streams, after = [], (other_kept[0],)
     for n in range(2):
@@ -312,14 +310,6 @@
         after = (sent,)
         streams.append((kept, exchange(sent, other)))
     rest = every[2:]
-    parts, part_sizes = [part_0, part_1], sizes
-    for b in every[2:]:
-        sent, kept = add(parts, part_sizes, rest, b, True, after)
-        after = (sent,)
-        parts, part_sizes = [(kept, exchange(sent, b))], [count]
-        rest = less(rest, b)
-    (own,) = parts
-    rest = every[2:]
     for b in every[2:-1]:
         for n in range(2):
             sent, kept = add([streams[n]], [sizes[n]], rest, b, True, after)
@@ -327,7 +317,8 @@
             streams[n] = (kept, exchange(sent, b))
         rest = less(rest, b)
 
-    moved = []
+    own = call(sum_kernel, floats(count), (), own, after)
+    moved, after = [], (own,)
     for n in range(2):
         sent, stay = add([streams[n]], [sizes[n]], rest, rest[0], False, after)
         after = (sent,)
@@ -336,8 +327,8 @@
     for n, (first, size) in enumerate(chunks):
         final = n == len(chunks) - 1
         shape = jax.ShapeDtypeStruct((count if final else size, width, width), jnp.bfloat16)
-        kernel = last_kernel(first, size, count, len(moved[n]), len(result))
-        result = (call(kernel, shape, (), (*own, *moved[n], *result)),)
+        kernel = last_kernel(first, size, len(moved[n]), len(result))
+        result = (call(kernel, shape, (), (own, *moved[n], *result)),)
     return result[0][None, None]
 
 

time: 52.4 us -> 53.9 us (1.029)
  waiting for transfers between devices: 8.45 us -> 17.5 us
  Pallas kernels: 18.9 us -> 15.4 us
  starting transfers between devices: 22.4 us -> 19.8 us
  local copies, waits for them, and re-layouts: 2.32 us -> 0.71 us
    ppermute x9, waiting for transfers between devices: 5.09 us -> 11.9 us  [exchange(): return lax.ppermute(x, 'layer', [(i, i ^ 1 << bit) for i in range(layers)])]
    pallas_call x17 -> x16, Pallas kernels: 18.9 us -> 15.4 us  [call(): pl.pallas_call(wrapped, out_shape=out_shape, in_specs=[pl.BlockSpec(memor...]
    ppermute x4, starting transfers between devices: 5.98 us -> 4.34 us  [cross(): return lax.ppermute(x, ('col', 'layer'), perm)]
    ppermute x1, waiting for transfers between devices: 0.01 us -> 1.49 us  [on_device(): p_r = lax.ppermute(p, 'row', swap)]
    ppermute x4, waiting for transfers between devices: 2.66 us -> 4.11 us  [cross(): return lax.ppermute(x, ('col', 'layer'), perm)]
    ppermute x9, starting transfers between devices: 13.3 us -> 11.9 us  [exchange(): return lax.ppermute(x, 'layer', [(i, i ^ 1 << bit) for i in range(layers)])]
    unnamed x4 -> x8, local copies, waits for them, and re-layouts: 1.57 us -> 0.7 us
    squeeze x1, local copies, waits for them, and re-layouts: 0.75 us -> 0.01 us  [on_device(): lists_far = jnp.concatenate([ia[1 - col], ip[1 - col]], axis=0)]
  transfers between devices with their start and end apart: 17 -> 17, of which waited for: 6 -> 8; matrix products, arithmetic and copies ran while one was open for 1% -> 0% of each run, Pallas kernels for 35% -> 27%
where the time goes in v6:
time: 53.9 us; the launch traced here: 53.6 us
  starting transfers between devices  19.8 us (37%)
  waiting for transfers between devices  17.5 us (32%)
  Pallas kernels  15.4 us (29%)
  local copies, waits for them, and re-layouts  0.71 us (1%)
    pallas_call x16, Pallas kernels, call(): pl.pallas_call(wrapped, out_shape=out_shape, in_specs=[pl.BlockSpec(memor...  15.4 us
    ppermute x9, waiting for transfers between devices, exchange(): return lax.ppermute(x, 'layer', [(i, i ^ 1 << bit) for i in range(layers)])  11.9 us
    ppermute x9, starting transfers between devices, exchange(): return lax.ppermute(x, 'layer', [(i, i ^ 1 << bit) for i in range(layers)])  11.9 us
    ppermute x4, starting transfers between devices, cross(): return lax.ppermute(x, ('col', 'layer'), perm)  4.34 us
    ppermute x4, waiting for transfers between devices, cross(): return lax.ppermute(x, ('col', 'layer'), perm)  4.11 us
    ppermute x1, starting transfers between devices, on_device(): p_x = lax.ppermute(p, 'col', swap)  2.94 us
    ppermute x1, waiting for transfers between devices, on_device(): p_r = lax.ppermute(p, 'row', swap)  1.49 us
  transfers between devices with their start and end apart: 17, of which 8 were waited for; matrix products, arithmetic and copies ran while one was open for 0% of the time, Pallas kernels for 27%

profile of v6, /device:TPU:0, one launch (start us, length us, event | category | flops | bytes accessed | tf_op | source)
XLA Modules:
  0.0 53.6 jit_solution(7828199582557573465)
XLA Ops:
  0.0 2.9 %collective-permute-start.6 = (bf16[16,128,128]{2,1,0:T(8,128)(2,1)}, bf16[16,128,128]{2,1,0:T(8,128)(2,1)S(1)}, u32[]{:S(2)}, u32[]{:S(2)}) collective-permute-start(bf16[16,128,128]{2,1,0:T(8,128)(2,1)} %bitcast.32), channel_id=1, source_target_pairs={{0,8},{8,0},{1,9},{9,1},{2,10},{10,2},{3,11},{11,3},{4,12},{12,4},... | collective-permute-start | bytes 1572872 | tf_op jit(solution)/shard_map/ppermute | solution.py:274
  3.0 0.7 %copy-done.2 = s32[1,1,1,2,32,16]{4,5,3,2,1,0:T(8,128)S(1)} copy-done((s32[1,1,1,2,32,16]{4,5,3,2,1,0:T(8,128)S(1)}, s32[1,1,1,2,32,16]{4,5,3,2,1,0:T(8,128)}, u32[]{:S(2)}) %copy-start.2) | copy-done | bytes 4120
  3.7 1.5 %collective-permute-done.refs_3_ = bf16[16,128,128]{2,1,0:T(8,128)(2,1)} collective-permute-done((bf16[16,128,128]{2,1,0:T(8,128)(2,1)}, bf16[16,128,128]{2,1,0:T(8,128)(2,1)}, u32[]{:S(2)}, u32[]{:S(2)}) %collective-permute-start) | collective-permute-done | bytes 524320 | tf_op jit(solution)/shard_map/ppermute | solution.py:275
  5.2 3.8 %shard_map.48 = (s16[1040,128]{1,0:T(8,128)(2,1)S(1)}, s16[1040,128]{1,0:T(8,128)(2,1)S(1)}, bf16[32,128,128]{2,1,0:T(8,128)(2,1)S(1)}) custom-call(s32[32,32]{1,0:T(8,128)S(1)} %pad_add_fusion.refs_0_, bf16[64,128,128]{2,1,0:T(8,128)(2,1)S(1)} %bitcast.28, bf16[16,128,128]{2,1,0:T(8,128)(2,1)S(1)} %bitcast.35, ...), custom_call_target="tpu_custom_call" | custom-call | flops 5368709120 | bytes 4730880 | tf_op jit(solution)/shard_map/pallas_call | solution.py:198
  9.0 1.6 %collective-permute-start.1 = (s16[1040,128]{1,0:T(8,128)(2,1)S(1)}, s16[1040,128]{1,0:T(8,128)(2,1)S(1)}, u32[]{:S(2)}, u32[]{:S(2)}) collective-permute-start(s16[1040,128]{1,0:T(8,128)(2,1)S(1)} %get-tuple-element.30.refs_3_.refs_1_), channel_id=1, source_target_pairs={{0,1},{1,0},{2,3},{3,2},{4,5},{5,4},{6,7},{7,6},{8,9},{9,8},{10,11... | collective-permute-start | bytes 798728 | tf_op jit(solution)/shard_map/ppermute | solution.py:243
  11.1 1.6 %collective-permute-start.2 = (s16[1040,128]{1,0:T(8,128)(2,1)S(1)}, s16[1040,128]{1,0:T(8,128)(2,1)S(1)}, u32[]{:S(2)}, u32[]{:S(2)}) collective-permute-start(s16[1040,128]{1,0:T(8,128)(2,1)S(1)} %get-tuple-element.34), channel_id=1, source_target_pairs={{0,2},{1,3},{2,0},{3,1},{4,6},{5,7},{6,4},{7,5},{8,10},{9,11},{10,... | collective-permute-start | bytes 798728 | tf_op jit(solution)/shard_map/ppermute | solution.py:243
  12.7 3.2 %shard_map.49 = (f32[8,128,128]{2,1,0:T(8,128)S(1)}, f32[8,128,128]{2,1,0:T(8,128)S(1)}) custom-call(s32[32,32]{1,0:T(8,128)S(1)} %pad_add_fusion.refs_0_, bf16[64,128,128]{2,1,0:T(8,128)(2,1)S(1)} %bitcast.29, bf16[32,128,128]{2,1,0:T(8,128)(2,1)S(1)} %get-tuple-element.29.refs_2_, s16[1040,128]{1,0:T(8,128)(2,1)S(1)} %get-tuple-element.30.refs_3_.refs_1_), custom_call_target="tpu_custom_call" | custom-call | flops 5368709120 | bytes 4198400 | tf_op jit(solution)/shard_map/pallas_call | solution.py:198
  15.9 1.6 %collective-permute-done.1.refs_1_ = s16[1040,128]{1,0:T(8,128)(2,1)S(1)} collective-permute-done((s16[1040,128]{1,0:T(8,128)(2,1)S(1)}, s16[1040,128]{1,0:T(8,128)(2,1)S(1)}, u32[]{:S(2)}, u32[]{:S(2)}) %collective-permute-start.1) | collective-permute-done | bytes 266272 | tf_op jit(solution)/shard_map/ppermute | solution.py:243
  17.6 1.3 %collective-permute-done.2.refs_1_ = s16[1040,128]{1,0:T(8,128)(2,1)S(1)} collective-permute-done((s16[1040,128]{1,0:T(8,128)(2,1)S(1)}, s16[1040,128]{1,0:T(8,128)(2,1)S(1)}, u32[]{:S(2)}, u32[]{:S(2)}) %collective-permute-start.2) | collective-permute-done | bytes 266272 | tf_op jit(solution)/shard_map/ppermute | solution.py:243
  19.7 1.7 %collective-permute-start.3 = (s16[528,128]{1,0:T(8,128)(2,1)S(1)}, s16[528,128]{1,0:T(8,128)(2,1)S(1)}, u32[]{:S(2)}, u32[]{:S(2)}) collective-permute-start(s16[528,128]{1,0:T(8,128)(2,1)S(1)} %get-tuple-element.35.refs_2_), channel_id=1, source_target_pairs={{0,2},{1,3},{2,0},{3,1},{4,6},{5,7},{6,4},{7,5},{8,10},{9,11},{10,... | collective-permute-start | bytes 405512 | tf_op jit(solution)/shard_map/ppermute | solution.py:243
  21.4 3.4 %shard_map.54 = (s16[1040,128]{1,0:T(8,128)(2,1)S(1)}, s16[1040,128]{1,0:T(8,128)(2,1)S(1)}, bf16[32,128,128]{2,1,0:T(8,128)(2,1)S(1)}) custom-call(s32[32,32]{1,0:T(8,128)S(1)} %collective-permute-done.5.refs_2_.refs_0_, bf16[64,128,128]{2,1,0:T(8,128)(2,1)S(1)} %bitcast.30, bf16[16,128,128]{2,1,0:T(8,128)(2,1)S(1)} %shard_map.53.refs_2_, ...), custom_call_target="tpu_custom_call" | custom-call | flops 5368709120 | bytes 4730880 | tf_op jit(solution)/shard_map/pallas_call | solution.py:198
  24.8 1.6 %collective-permute-start.10 = (s16[1040,128]{1,0:T(8,128)(2,1)S(1)}, s16[1040,128]{1,0:T(8,128)(2,1)S(1)}, u32[]{:S(2)}, u32[]{:S(2)}) collective-permute-start(s16[1040,128]{1,0:T(8,128)(2,1)S(1)} %get-tuple-element.38.refs_4_), channel_id=1, source_target_pairs={{0,1},{1,0},{2,3},{3,2},{4,5},{5,4},{6,7},{7,6},{8,9},{9,8},{10,11... | collective-permute-start | bytes 798728 | tf_op jit(solution)/shard_map/ppermute | solution.py:243
  26.6 2.7 %collective-permute-start.8 = (s16[528,128]{1,0:T(8,128)(2,1)S(1)}, s16[528,128]{1,0:T(8,128)(2,1)S(1)}, u32[]{:S(2)}, u32[]{:S(2)}) collective-permute-start(s16[528,128]{1,0:T(8,128)(2,1)S(1)} %get-tuple-element.40.refs_3_), channel_id=1, source_target_pairs={{0,4},{1,5},{2,6},{3,7},{4,0},{5,1},{6,2},{7,3},{8,12},{9,13},{10,... | collective-permute-start | bytes 405512 | tf_op jit(solution)/shard_map/ppermute | solution.py:243
  29.2 0.6 %collective-permute-start.9 = (s16[1040,128]{1,0:T(8,128)(2,1)S(1)}, s16[1040,128]{1,0:T(8,128)(2,1)S(1)}, u32[]{:S(2)}, u32[]{:S(2)}) collective-permute-start(s16[1040,128]{1,0:T(8,128)(2,1)S(1)} %get-tuple-element.43), channel_id=1, source_target_pairs={{0,2},{1,3},{2,0},{3,1},{4,6},{5,7},{6,4},{7,5},{8,10},{9,11},{10,... | collective-permute-start | bytes 798728 | tf_op jit(solution)/shard_map/ppermute | solution.py:243
  29.9 3.2 %shard_map.56 = (f32[8,128,128]{2,1,0:T(8,128)S(1)}, f32[8,128,128]{2,1,0:T(8,128)S(1)}) custom-call(s32[32,32]{1,0:T(8,128)S(1)} %collective-permute-done.5.refs_2_.refs_0_, bf16[64,128,128]{2,1,0:T(8,128)(2,1)S(1)} %bitcast.31, bf16[32,128,128]{2,1,0:T(8,128)(2,1)S(1)} %get-tuple-element.41.refs_2_, s16[528,128]{1,0:T(8,128)(2,1)S(1)} %get-tuple-element.40.refs_3_), custom_call_target="tpu_custom_call" | custom-call | flops 5368709120 | bytes 4198400 | tf_op jit(solution)/shard_map/pallas_call | solution.py:198
  33.2 1.6 %collective-permute-start.12 = (s16[528,128]{1,0:T(8,128)(2,1)S(1)}, s16[528,128]{1,0:T(8,128)(2,1)S(1)}, u32[]{:S(2)}, u32[]{:S(2)}) collective-permute-start(s16[528,128]{1,0:T(8,128)(2,1)S(1)} %get-tuple-element.45.refs_2_), channel_id=1, source_target_pairs={{0,2},{1,3},{2,0},{3,1},{4,6},{5,7},{6,4},{7,5},{8,10},{9,11},{10,... | collective-permute-start | bytes 405512 | tf_op jit(solution)/shard_map/ppermute | solution.py:243
  34.9 5.7 %collective-permute-done.9.refs_1_ = s16[1040,128]{1,0:T(8,128)(2,1)S(1)} collective-permute-done((s16[1040,128]{1,0:T(8,128)(2,1)S(1)}, s16[1040,128]{1,0:T(8,128)(2,1)S(1)}, u32[]{:S(2)}, u32[]{:S(2)}) %collective-permute-start.9) | collective-permute-done | bytes 266272 | tf_op jit(solution)/shard_map/ppermute | solution.py:243
  40.9 1.6 %collective-permute-done.12.refs_1_ = s16[528,128]{1,0:T(8,128)(2,1)S(1)} collective-permute-done((s16[528,128]{1,0:T(8,128)(2,1)S(1)}, s16[528,128]{1,0:T(8,128)(2,1)S(1)}, u32[]{:S(2)}, u32[]{:S(2)}) %collective-permute-start.12) | collective-permute-done | bytes 135200 | tf_op jit(solution)/shard_map/ppermute | solution.py:243
  42.6 1.6 %collective-permute-start.16 = (s16[272,128]{1,0:T(8,128)(2,1)S(1)}, s16[272,128]{1,0:T(8,128)(2,1)S(1)}, u32[]{:S(2)}, u32[]{:S(2)}) collective-permute-start(s16[272,128]{1,0:T(8,128)(2,1)S(1)} %get-tuple-element.52), channel_id=1, source_target_pairs={{0,8},{1,9},{2,10},{3,11},{4,12},{5,13},{6,14},{7,15},{8,0},{9,1},... | collective-permute-start | bytes 208904 | tf_op jit(solution)/shard_map/ppermute | solution.py:248
  44.2 1.6 %collective-permute-done.11.refs_1_ = s16[528,128]{1,0:T(8,128)(2,1)S(1)} collective-permute-done((s16[528,128]{1,0:T(8,128)(2,1)S(1)}, s16[528,128]{1,0:T(8,128)(2,1)S(1)}, u32[]{:S(2)}, u32[]{:S(2)}) %collective-permute-start.11) | collective-permute-done | bytes 135200 | tf_op jit(solution)/shard_map/ppermute | solution.py:243
  46.0 2.2 %collective-permute-start.13 = (s16[272,128]{1,0:T(8,128)(2,1)S(1)}, s16[272,128]{1,0:T(8,128)(2,1)S(1)}, u32[]{:S(2)}, u32[]{:S(2)}) collective-permute-start(s16[272,128]{1,0:T(8,128)(2,1)S(1)} %get-tuple-element.50), channel_id=1, source_target_pairs={{0,12},{1,13},{2,14},{3,15},{4,8},{5,9},{6,10},{7,11},{8,4},{9,5},... | collective-permute-start | bytes 208904 | tf_op jit(solution)/shard_map/ppermute | solution.py:248
  48.7 2.6 %collective-permute-done.15.refs_1_ = s16[272,128]{1,0:T(8,128)(2,1)S(1)} collective-permute-done((s16[272,128]{1,0:T(8,128)(2,1)S(1)}, s16[272,128]{1,0:T(8,128)(2,1)S(1)}, u32[]{:S(2)}, u32[]{:S(2)}) %collective-permute-start.15) | collective-permute-done | bytes 69664 | tf_op jit(solution)/shard_map/ppermute | solution.py:248
  51.4 1.5 %collective-permute-done.13.refs_1_ = s16[272,128]{1,0:T(8,128)(2,1)S(1)} collective-permute-done((s16[272,128]{1,0:T(8,128)(2,1)S(1)}, s16[272,128]{1,0:T(8,128)(2,1)S(1)}, u32[]{:S(2)}, u32[]{:S(2)}) %collective-permute-start.13) | collective-permute-done | bytes 69664 | tf_op jit(solution)/shard_map/ppermute | solution.py:248
  52.9 0.7 %shard_map.63 = bf16[4,128,128]{2,1,0:T(8,128)(2,1)} custom-call(f32[4,128,128]{2,1,0:T(8,128)S(1)} %shard_map.59.refs_2_.refs_0_, s16[272,128]{1,0:T(8,128)(2,1)S(1)} %collective-permute-done.13.refs_1_, s16[272,128]{1,0:T(8,128)(2,1)S(1)} %collective-permute-done.14.refs_2_, bf16[2,128,128]{2,1,0:T(8,128)(2,1)S(1)} %shard_map.62.refs_3_), custom_call_target="tpu_custom_call" | custom-call | bytes 598016 | tf_op jit(solution)/shard_map/pallas_call | solution.py:198
  (39 shorter events, 2.8 us)
Async XLA Ops:
  0.0 3.0 %copy-start = (bf16[1,1,1,64,128,128]{5,4,3,2,1,0:T(8,128)(2,1)S(1)}, bf16[1,1,1,64,128,128]{5,4,3,2,1,0:T(8,128)(2,1)}, u32[]{:S(2)}) copy-start(bf16[1,1,1,64,128,128]{5,4,3,2,1,0:T(8,128)(2,1)} %param.4) | copy-start | bytes 6291460
  0.0 3.0 %copy-start.1 = (bf16[1,1,1,16,128,128]{5,4,3,2,1,0:T(8,128)(2,1)S(1)}, bf16[1,1,1,16,128,128]{5,4,3,2,1,0:T(8,128)(2,1)}, u32[]{:S(2)}) copy-start(bf16[1,1,1,16,128,128]{5,4,3,2,1,0:T(8,128)(2,1)} %param.5) | copy-start | bytes 1572868
  0.0 19.1 %collective-permute-start.6 = (bf16[16,128,128]{2,1,0:T(8,128)(2,1)}, bf16[16,128,128]{2,1,0:T(8,128)(2,1)S(1)}, u32[]{:S(2)}, u32[]{:S(2)}) collective-permute-start(bf16[16,128,128]{2,1,0:T(8,128)(2,1)} %bitcast.32), channel_id=1, source_target_pairs={{0,8},{8,0},{1,9},{9,1},{2,10},{10,2},{3,11},{11,3},{4,12},{12,4},... | collective-permute-start | bytes 1572872 | tf_op jit(solution)/shard_map/ppermute | solution.py:274
  2.9 2.3 %collective-permute-start = (bf16[16,128,128]{2,1,0:T(8,128)(2,1)}, bf16[16,128,128]{2,1,0:T(8,128)(2,1)}, u32[]{:S(2)}, u32[]{:S(2)}) collective-permute-start(bf16[16,128,128]{2,1,0:T(8,128)(2,1)} %bitcast.33), channel_id=1, source_target_pairs={{0,16},{16,0},{1,17},{17,1},{2,18},{18,2},{3,19},{19,3},{4,20},{20... | collective-permute-start | bytes 1572872 | tf_op jit(solution)/shard_map/ppermute | solution.py:275
  2.9 0.7 %copy-start.2 = (s32[1,1,1,2,32,16]{4,5,3,2,1,0:T(8,128)S(1)}, s32[1,1,1,2,32,16]{4,5,3,2,1,0:T(8,128)}, u32[]{:S(2)}) copy-start(s32[1,1,1,2,32,16]{4,5,3,2,1,0:T(8,128)} %param.7) | copy-start | bytes 12292
  3.0 0.7 %copy-start.3 = (s32[1,1,1,2,32,16]{4,5,3,2,1,0:T(8,128)S(1)}, s32[1,1,1,2,32,16]{4,5,3,2,1,0:T(8,128)}, u32[]{:S(2)}) copy-start(s32[1,1,1,2,32,16]{4,5,3,2,1,0:T(8,128)} %param.6) | copy-start | bytes 12292
  9.0 8.5 %collective-permute-start.1 = (s16[1040,128]{1,0:T(8,128)(2,1)S(1)}, s16[1040,128]{1,0:T(8,128)(2,1)S(1)}, u32[]{:S(2)}, u32[]{:S(2)}) collective-permute-start(s16[1040,128]{1,0:T(8,128)(2,1)S(1)} %get-tuple-element.30.refs_3_.refs_1_), channel_id=1, source_target_pairs={{0,1},{1,0},{2,3},{3,2},{4,5},{5,4},{6,7},{7,6},{8,9},{9,8},{10,11... | collective-permute-start | bytes 798728 | tf_op jit(solution)/shard_map/ppermute | solution.py:243
  10.6 8.6 %collective-permute-start.5 = (s32[32,32]{1,0:T(8,128)S(1)}, s32[32,32]{1,0:T(8,128)S(1)}, u32[]{:S(2)}, u32[]{:S(2)}) collective-permute-start(s32[32,32]{1,0:T(8,128)S(1)} %shard_map.52), channel_id=1, source_target_pairs={{0,8},{8,0},{1,9},{9,1},{2,10},{10,2},{3,11},{11,3},{4,12},{12,4},... | collective-permute-start | bytes 12296 | tf_op jit(solution)/shard_map/ppermute | solution.py:285
  11.1 7.9 %collective-permute-start.2 = (s16[1040,128]{1,0:T(8,128)(2,1)S(1)}, s16[1040,128]{1,0:T(8,128)(2,1)S(1)}, u32[]{:S(2)}, u32[]{:S(2)}) collective-permute-start(s16[1040,128]{1,0:T(8,128)(2,1)S(1)} %get-tuple-element.34), channel_id=1, source_target_pairs={{0,2},{1,3},{2,0},{3,1},{4,6},{5,7},{6,4},{7,5},{8,10},{9,11},{10,... | collective-permute-start | bytes 798728 | tf_op jit(solution)/shard_map/ppermute | solution.py:243
  19.2 2.2 %collective-permute-start.7 = (bf16[16,128,128]{2,1,0:T(8,128)(2,1)S(1)}, bf16[16,128,128]{2,1,0:T(8,128)(2,1)S(1)}, u32[]{:S(2)}, u32[]{:S(2)}) collective-permute-start(bf16[16,128,128]{2,1,0:T(8,128)(2,1)S(1)} %shard_map.53.refs_2_), channel_id=1, source_target_pairs={{0,16},{16,0},{1,17},{17,1},{2,18},{18,2},{3,19},{19,3},{4,20},{20... | collective-permute-start | bytes 1572872 | tf_op jit(solution)/shard_map/ppermute | solution.py:294
  19.2 7.2 %collective-permute-start.4 = (s16[528,128]{1,0:T(8,128)(2,1)S(1)}, s16[528,128]{1,0:T(8,128)(2,1)S(1)}, u32[]{:S(2)}, u32[]{:S(2)}) collective-permute-start(s16[528,128]{1,0:T(8,128)(2,1)S(1)} %get-tuple-element.37.refs_1_), channel_id=1, source_target_pairs={{0,1},{1,0},{2,3},{3,2},{4,5},{5,4},{6,7},{7,6},{8,9},{9,8},{10,11... | collective-permute-start | bytes 405512 | tf_op jit(solution)/shard_map/ppermute | solution.py:243
  19.7 6.7 %collective-permute-start.3 = (s16[528,128]{1,0:T(8,128)(2,1)S(1)}, s16[528,128]{1,0:T(8,128)(2,1)S(1)}, u32[]{:S(2)}, u32[]{:S(2)}) collective-permute-start(s16[528,128]{1,0:T(8,128)(2,1)S(1)} %get-tuple-element.35.refs_2_), channel_id=1, source_target_pairs={{0,2},{1,3},{2,0},{3,1},{4,6},{5,7},{6,4},{7,5},{8,10},{9,11},{10,... | collective-permute-start | bytes 405512 | tf_op jit(solution)/shard_map/ppermute | solution.py:243
  24.8 8.3 %collective-permute-start.10 = (s16[1040,128]{1,0:T(8,128)(2,1)S(1)}, s16[1040,128]{1,0:T(8,128)(2,1)S(1)}, u32[]{:S(2)}, u32[]{:S(2)}) collective-permute-start(s16[1040,128]{1,0:T(8,128)(2,1)S(1)} %get-tuple-element.38.refs_4_), channel_id=1, source_target_pairs={{0,1},{1,0},{2,3},{3,2},{4,5},{5,4},{6,7},{7,6},{8,9},{9,8},{10,11... | collective-permute-start | bytes 798728 | tf_op jit(solution)/shard_map/ppermute | solution.py:243
  26.6 14.3 %collective-permute-start.8 = (s16[528,128]{1,0:T(8,128)(2,1)S(1)}, s16[528,128]{1,0:T(8,128)(2,1)S(1)}, u32[]{:S(2)}, u32[]{:S(2)}) collective-permute-start(s16[528,128]{1,0:T(8,128)(2,1)S(1)} %get-tuple-element.40.refs_3_), channel_id=1, source_target_pairs={{0,4},{1,5},{2,6},{3,7},{4,0},{5,1},{6,2},{7,3},{8,12},{9,13},{10,... | collective-permute-start | bytes 405512 | tf_op jit(solution)/shard_map/ppermute | solution.py:243
  29.2 11.4 %collective-permute-start.9 = (s16[1040,128]{1,0:T(8,128)(2,1)S(1)}, s16[1040,128]{1,0:T(8,128)(2,1)S(1)}, u32[]{:S(2)}, u32[]{:S(2)}) collective-permute-start(s16[1040,128]{1,0:T(8,128)(2,1)S(1)} %get-tuple-element.43), channel_id=1, source_target_pairs={{0,2},{1,3},{2,0},{3,1},{4,6},{5,7},{6,4},{7,5},{8,10},{9,11},{10,... | collective-permute-start | bytes 798728 | tf_op jit(solution)/shard_map/ppermute | solution.py:243
  33.2 9.3 %collective-permute-start.12 = (s16[528,128]{1,0:T(8,128)(2,1)S(1)}, s16[528,128]{1,0:T(8,128)(2,1)S(1)}, u32[]{:S(2)}, u32[]{:S(2)}) collective-permute-start(s16[528,128]{1,0:T(8,128)(2,1)S(1)} %get-tuple-element.45.refs_2_), channel_id=1, source_target_pairs={{0,2},{1,3},{2,0},{3,1},{4,6},{5,7},{6,4},{7,5},{8,10},{9,11},{10,... | collective-permute-start | bytes 405512 | tf_op jit(solution)/shard_map/ppermute | solution.py:243
  40.8 5.1 %collective-permute-start.11 = (s16[528,128]{1,0:T(8,128)(2,1)S(1)}, s16[528,128]{1,0:T(8,128)(2,1)S(1)}, u32[]{:S(2)}, u32[]{:S(2)}) collective-permute-start(s16[528,128]{1,0:T(8,128)(2,1)S(1)} %get-tuple-element.46.refs_2_), channel_id=1, source_target_pairs={{0,1},{1,0},{2,3},{3,2},{4,5},{5,4},{6,7},{7,6},{8,9},{9,8},{10,11... | collective-permute-start | bytes 405512 | tf_op jit(solution)/shard_map/ppermute | solution.py:243
  42.6 6.1 %collective-permute-start.16 = (s16[272,128]{1,0:T(8,128)(2,1)S(1)}, s16[272,128]{1,0:T(8,128)(2,1)S(1)}, u32[]{:S(2)}, u32[]{:S(2)}) collective-permute-start(s16[272,128]{1,0:T(8,128)(2,1)S(1)} %get-tuple-element.52), channel_id=1, source_target_pairs={{0,8},{1,9},{2,10},{3,11},{4,12},{5,13},{6,14},{7,15},{8,0},{9,1},... | collective-permute-start | bytes 208904 | tf_op jit(solution)/shard_map/ppermute | solution.py:248
  44.2 7.2 %collective-permute-start.15 = (s16[272,128]{1,0:T(8,128)(2,1)S(1)}, s16[272,128]{1,0:T(8,128)(2,1)S(1)}, u32[]{:S(2)}, u32[]{:S(2)}) collective-permute-start(s16[272,128]{1,0:T(8,128)(2,1)S(1)} %get-tuple-element.49.refs_2_), channel_id=1, source_target_pairs={{0,12},{1,13},{2,14},{3,15},{4,8},{5,9},{6,10},{7,11},{8,4},{9,5},... | collective-permute-start | bytes 208904 | tf_op jit(solution)/shard_map/ppermute | solution.py:248
  46.0 6.9 %collective-permute-start.13 = (s16[272,128]{1,0:T(8,128)(2,1)S(1)}, s16[272,128]{1,0:T(8,128)(2,1)S(1)}, u32[]{:S(2)}, u32[]{:S(2)}) collective-permute-start(s16[272,128]{1,0:T(8,128)(2,1)S(1)} %get-tuple-element.50), channel_id=1, source_target_pairs={{0,12},{1,13},{2,14},{3,15},{4,8},{5,9},{6,10},{7,11},{8,4},{9,5},... | collective-permute-start | bytes 208904 | tf_op jit(solution)/shard_map/ppermute | solution.py:248
  48.2 4.7 %collective-permute-start.14 = (s16[272,128]{1,0:T(8,128)(2,1)S(1)}, s16[272,128]{1,0:T(8,128)(2,1)S(1)}, u32[]{:S(2)}, u32[]{:S(2)}) collective-permute-start(s16[272,128]{1,0:T(8,128)(2,1)S(1)} %get-tuple-element.51), channel_id=1, source_target_pairs={{0,8},{1,9},{2,10},{3,11},{4,12},{5,13},{6,14},{7,15},{8,0},{9,1},... | collective-permute-start | bytes 208904 | tf_op jit(solution)/shard_map/ppermute | solution.py:248

commit v7 on v6

--- a/solution.py
+++ b/solution.py
@@ -79,14 +79,23 @@
     return lambda t: lambda f: (lists_ref[f, t], lists_ref[fan + f, t])
 
 
-def send_kernel(fan, count, chunks, bits):
-    def kernel(lists_ref, a_ref, p0_ref, p1_ref, *refs):
+def send_kernel(fan, count, chunks, bits, joins):
+    def kernel(lists_ref, a_ref, *refs):
         find = finder(lists_ref, fan)
-        out_refs, p_ref = refs[:-1], refs[-1]
-        held, width = p0_ref.shape[:2]
-        row = lax.axis_index("row")
-        p_ref[pl.ds(row * held, held)] = p0_ref[...]
-        p_ref[pl.ds((1 - row) * held, held)] = p1_ref[...]
+        n_out = len(chunks) + joins
+        p_refs, out_refs = refs[:-n_out], refs[-n_out:]
+        if joins:
+            out_refs, p_ref = out_refs[:-1], out_refs[-1]
+            held = p_ref.shape[0] // 2
+            row = lax.axis_index("row")
+            p_ref[pl.ds(row * held, held)] = p_refs[0][...]
+            at = (1 - row) * held
+            for ref in p_refs[1:]:
+                p_ref[pl.ds(at, ref.shape[0])] = ref[...]
+                at += ref.shape[0]
+        else:
+            (p_ref,) = p_refs
+        width = p_ref.shape[-1]
         for (first, size), bit, out_ref in zip(chunks, bits, out_refs):
             side = 1 - own_bit(bit)
             total = out_ref.shape[0] // width
@@ -102,6 +111,13 @@
             put_head(out_ref, lax.fori_loop(0, total // GROUP, body, new_head(total, width)))
 
     return kernel
+
+
+def split_kernel(in_ref, *out_refs):
+    at = 0
+    for ref in out_refs:
+        ref[...] = in_ref[pl.ds(at, ref.shape[0])]
+        at += ref.shape[0]
 
 
 def keep_kernel(fan, count, chunks, bits):
@@ -204,7 +220,7 @@
         out_specs=jax.tree.map(lambda _: pl.BlockSpec(memory_space=VMEM), out_shape),
         scratch_shapes=list(scratch),
         compiler_params=pltpu.CompilerParams(vmem_limit_bytes=moved + 4 * 2**20),
-        cost_estimate=pl.CostEstimate(flops=5 * flops, bytes_accessed=moved, transcendentals=0),
+        cost_estimate=pl.CostEstimate(flops=5 * flops, bytes_accessed=moved if flops else 1, transcendentals=0),
     )(*smem, *vmem, *after)
 
 
@@ -247,16 +263,19 @@
         perm = [(c * layers + i, (1 - c) * layers + (i ^ flip)) for c in range(2) for i in range(layers)]
         return lax.ppermute(x, ("col", "layer"), perm)
 
-    def send(lists, vmem, after):
-        shapes = [message(layers // 2 * size, width) for _, size in chunks]
-        shapes.append(jax.ShapeDtypeStruct((2 * held, width, width), p.dtype))
-        *made, joined = call(send_kernel(fan, count, chunks, first_bits), shapes, (lists,), vmem, after, (), 2 * flops)
-        return made, joined, [exchange(x, b) for x, b in zip(made, first_bits)]
-
-    def keep(lists, vmem, after):
+    def send(lists, vmem, which, bits, joins, after, cost):
+        picked = [chunks[n] for n in which]
+        shapes = [message(layers // 2 * size, width) for _, size in picked]
+        if joins:
+            shapes.append(jax.ShapeDtypeStruct((2 * held, width, width), p.dtype))
+        kernel = send_kernel(fan, count, picked, bits, joins)
+        made = call(kernel, shapes, (lists,), vmem, after, (), cost * len(which) * flops)
+        return made, [exchange(x, b) for x, b in zip(made, bits)]
+
+    def keep(lists, vmem, bits, after, cost):
         shapes = [floats(layers // 2 * size) for _, size in chunks]
-        kernel = keep_kernel(fan, count, chunks, first_bits)
-        return call(kernel, shapes, (lists,), vmem, after, (), 2 * flops)
+        kernel = keep_kernel(fan, count, chunks, bits)
+        return call(kernel, shapes, (lists,), vmem, after, (), cost * 2 * flops)
 
     def add(parts, sizes, rest, bit, keeps, after):
         n = sum(sizes) << (len(rest) - 1)
@@ -264,12 +283,16 @@
         kept, came = zip(*parts)
         return call(add_kernel(sizes, rest, bit, keeps), shapes, (), (*kept, *came), after)
 
-    first_bits = (0, 1)
+    own_bits, other_bits = (0, 1), (1, 0)
     sizes = [size for _, size in chunks]
     every = list(range(bits))
 
     def less(rest, bit):
         return [b for b in rest if b != bit]
+
+    def second(kept, came, size, bit, after):
+        sent, kept = add([(kept, came)], [size], less(every, bit), 1 - bit, True, after)
+        return sent, (kept, exchange(sent, 1 - bit))
 
     p_x = lax.ppermute(p, "col", swap)
     p_r = lax.ppermute(p, "row", swap)
@@ -281,34 +304,35 @@
     gate = call(lambda *refs: None, token, (), (), (), (), 10**9)
     gate = call(lambda *refs: None, token, (), (a, p), (gate,))
 
-    made, joined, own_came = send(lists, (a, p, p_r), (gate,))
-    lists_x = lax.ppermute(hold(lists_far, made[:1]), "col", swap)
-    own_kept = keep(lists, (a, joined), made[:1])
+    (*made, joined), own_came = send(lists, (a, p, p_r), (0, 1), own_bits, True, (gate,), 1)
+    own_kept = keep(lists, (a, joined), own_bits, made[:1], 1)
+    lists_x = lax.ppermute(hold(lists_far, own_kept[:1]), "col", swap)
+    pieces = [jax.ShapeDtypeStruct((held // 2, width, width), p.dtype)] * 2
+    pieces = call(split_kernel, pieces, (), (p_x,), (own_kept[0], lists_x))
+    p_xr = [lax.ppermute(x, "row", swap) for x in pieces]
     parts, after = [], ()
     for n in range(2):
-        b, other = first_bits[n], first_bits[1 - n]
-        sent, kept = add([(own_kept[n], own_came[n])], [sizes[n]], less(every, b), other, True, after)
+        sent, part = second(own_kept[n], own_came[n], sizes[n], own_bits[n], after)
+        parts.append(part)
         after = (sent,)
-        parts.append((kept, exchange(sent, other)))
-    p_x = hold(p_x, (*after, lists_x))
-    p_xr = lax.ppermute(p_x, "row", swap)
-
-    made, joined, other_came = send(lists_x, (a, p_x, p_xr), ())
-    rest, part_sizes, after = every[2:], sizes, made[:1]
+
+    (made, joined), came_0 = send(lists_x, (a, p_x, *p_xr), (0,), other_bits[:1], True, after, 0)
+    (made,), came_1 = send(lists_x, (a, joined), (1,), other_bits[1:], False, (made,), 0)
+    other_came = came_0 + came_1
+    rest, part_sizes, after = every[2:], sizes, (made,)
     for b in every[2:]:
         sent, kept = add(parts, part_sizes, rest, b, True, after)
         after = (sent,)
         parts, part_sizes = [(kept, exchange(sent, b))], [count]
         rest = less(rest, b)
     (own,) = parts
-    other_kept = keep(lists_x, (a, joined), after)
+    other_kept = keep(lists_x, (a, joined), other_bits, after, 1)
 
     streams, after = [], (other_kept[0],)
     for n in range(2):
-        b, other = first_bits[n], first_bits[1 - n]
-        sent, kept = add([(other_kept[n], other_came[n])], [sizes[n]], less(every, b), other, True, after)
+        sent, part = second(other_kept[n], other_came[n], sizes[n], other_bits[n], after)
+        streams.append(part)
         after = (sent,)
-        streams.append((kept, exchange(sent, other)))
     rest = every[2:]
     for b in every[2:-1]:
         for n in range(2):

time: 53.9 us -> 49.6 us (0.920)
  waiting for transfers between devices: 17.5 us -> 9.1 us
  starting transfers between devices: 19.8 us -> 22.9 us
  Pallas kernels: 15.4 us -> 16.5 us
    ppermute x9, waiting for transfers between devices: 11.9 us -> 3.11 us  [exchange(): return lax.ppermute(x, 'layer', [(i, i ^ 1 << bit) for i in range(layers)])]
    ppermute x2 -> x3, waiting for transfers between devices: 0.01 us -> 2.06 us  [the longest x1 2.06 us: on_device(): lists_x = lax.ppermute(hold(lists_far, own_kept[:1]), 'col', swap)]
    ppermute x4, starting transfers between devices: 4.34 us -> 5.98 us  [cross(): return lax.ppermute(x, ('col', 'layer'), perm)]
    ppermute x1, waiting for transfers between devices: 1.49 us -> 0.01 us  [on_device(): p_r = lax.ppermute(p, 'row', swap)]
    ppermute x2 -> x3, starting transfers between devices: 0.6 us -> 2.01 us  [the longest x1 1.44 us: on_device(): lists_x = lax.ppermute(hold(lists_far, own_kept[:1]), 'col', swap)]
    pallas_call x16 -> x18, Pallas kernels: 15.4 us -> 16.5 us  [call(): pl.pallas_call(wrapped, out_shape=out_shape, in_specs=[pl.BlockSpec(memor...]
  transfers between devices with their start and end apart: 17 -> 18, of which waited for: 8 -> 6; matrix products, arithmetic and copies ran while one was open for 0% -> 0% of each run, Pallas kernels for 27% -> 32%
where the time goes in v7:
time: 49.6 us; the launch traced here: 49.3 us
  starting transfers between devices  22.9 us (46%)
  Pallas kernels  16.5 us (33%)
  waiting for transfers between devices  9.1 us (18%)
  local copies, waits for them, and re-layouts  0.73 us (1%)
    pallas_call x18, Pallas kernels, call(): pl.pallas_call(wrapped, out_shape=out_shape, in_specs=[pl.BlockSpec(memor...  16.5 us
    ppermute x9, starting transfers between devices, exchange(): return lax.ppermute(x, 'layer', [(i, i ^ 1 << bit) for i in range(layers)])  11.9 us
    ppermute x4, starting transfers between devices, cross(): return lax.ppermute(x, ('col', 'layer'), perm)  5.98 us
    ppermute x4, waiting for transfers between devices, cross(): return lax.ppermute(x, ('col', 'layer'), perm)  3.62 us
    ppermute x9, waiting for transfers between devices, exchange(): return lax.ppermute(x, 'layer', [(i, i ^ 1 << bit) for i in range(layers)])  3.11 us
    ppermute x1, starting transfers between devices, on_device(): p_x = lax.ppermute(p, 'col', swap)  2.56 us
    ppermute x1, waiting for transfers between devices, on_device(): lists_x = lax.ppermute(hold(lists_far, own_kept[:1]), 'col', swap)  2.06 us
    ppermute x1, starting transfers between devices, on_device(): lists_x = lax.ppermute(hold(lists_far, own_kept[:1]), 'col', swap)  1.44 us
  transfers between devices with their start and end apart: 18, of which 6 were waited for; matrix products, arithmetic and copies ran while one was open for 0% of the time, Pallas kernels for 32%

profile of v7, /device:TPU:0, one launch (start us, length us, event | category | flops | bytes accessed | tf_op | source)
XLA Modules:
  0.0 49.3 jit_solution(11168642606897547220)
XLA Ops:
  0.5 2.6 %collective-permute-start.6 = (bf16[16,128,128]{2,1,0:T(8,128)(2,1)}, bf16[16,128,128]{2,1,0:T(8,128)(2,1)S(1)}, u32[]{:S(2)}, u32[]{:S(2)}) collective-permute-start(bf16[16,128,128]{2,1,0:T(8,128)(2,1)} %bitcast.34), channel_id=1, source_target_pairs={{0,8},{8,0},{1,9},{9,1},{2,10},{10,2},{3,11},{11,3},{4,12},{12,4},... | collective-permute-start | bytes 1572872 | tf_op jit(solution)/shard_map/ppermute | solution.py:297
  3.0 0.7 %copy-done.2 = s32[1,1,1,2,32,16]{4,5,3,2,1,0:T(8,128)S(1)} copy-done((s32[1,1,1,2,32,16]{4,5,3,2,1,0:T(8,128)S(1)}, s32[1,1,1,2,32,16]{4,5,3,2,1,0:T(8,128)}, u32[]{:S(2)}) %copy-start.2) | copy-done | bytes 4120
  3.8 3.8 %shard_map.48 = (s16[1040,128]{1,0:T(8,128)(2,1)S(1)}, s16[1040,128]{1,0:T(8,128)(2,1)S(1)}, bf16[32,128,128]{2,1,0:T(8,128)(2,1)S(1)}) custom-call(s32[32,32]{1,0:T(8,128)S(1)} %pad_add_fusion.refs_0_, bf16[64,128,128]{2,1,0:T(8,128)(2,1)S(1)} %bitcast.28, bf16[16,128,128]{2,1,0:T(8,128)(2,1)S(1)} %bitcast.36, ...), custom_call_target="tpu_custom_call" | custom-call | flops 5368709120 | bytes 4730880 | tf_op jit(solution)/shard_map/pallas_call | solution.py:214
  7.6 1.6 %collective-permute-start.1 = (s16[1040,128]{1,0:T(8,128)(2,1)S(1)}, s16[1040,128]{1,0:T(8,128)(2,1)S(1)}, u32[]{:S(2)}, u32[]{:S(2)}) collective-permute-start(s16[1040,128]{1,0:T(8,128)(2,1)S(1)} %get-tuple-element.31.refs_3_), channel_id=1, source_target_pairs={{0,1},{1,0},{2,3},{3,2},{4,5},{5,4},{6,7},{7,6},{8,9},{9,8},{10,11... | collective-permute-start | bytes 798728 | tf_op jit(solution)/shard_map/ppermute | solution.py:259
  9.2 1.6 %collective-permute-start.2 = (s16[1040,128]{1,0:T(8,128)(2,1)S(1)}, s16[1040,128]{1,0:T(8,128)(2,1)S(1)}, u32[]{:S(2)}, u32[]{:S(2)}) collective-permute-start(s16[1040,128]{1,0:T(8,128)(2,1)S(1)} %get-tuple-element.35), channel_id=1, source_target_pairs={{0,2},{1,3},{2,0},{3,1},{4,6},{5,7},{6,4},{7,5},{8,10},{9,11},{10,... | collective-permute-start | bytes 798728 | tf_op jit(solution)/shard_map/ppermute | solution.py:259
  10.8 3.2 %shard_map.49 = (f32[8,128,128]{2,1,0:T(8,128)S(1)}, f32[8,128,128]{2,1,0:T(8,128)S(1)}) custom-call(s32[32,32]{1,0:T(8,128)S(1)} %pad_add_fusion.refs_0_, bf16[64,128,128]{2,1,0:T(8,128)(2,1)S(1)} %bitcast.29, bf16[32,128,128]{2,1,0:T(8,128)(2,1)S(1)} %get-tuple-element.30.refs_2_, s16[1040,128]{1,0:T(8,128)(2,1)S(1)} %get-tuple-element.31.refs_3_), custom_call_target="tpu_custom_call" | custom-call | flops 5368709120 | bytes 4198400 | tf_op jit(solution)/shard_map/pallas_call | solution.py:214
  14.0 1.4 %collective-permute-start.5 = (s32[32,32]{1,0:T(8,128)S(1)}, s32[32,32]{1,0:T(8,128)S(1)}, u32[]{:S(2)}, u32[]{:S(2)}) collective-permute-start(s32[32,32]{1,0:T(8,128)S(1)} %shard_map.52), channel_id=1, source_target_pairs={{0,8},{8,0},{1,9},{9,1},{2,10},{10,2},{3,11},{11,3},{4,12},{12,4},... | collective-permute-start | bytes 12296 | tf_op jit(solution)/shard_map/ppermute | solution.py:309
  15.8 2.1 %collective-permute-done.5.refs_2_.refs_0_ = s32[32,32]{1,0:T(8,128)S(1)} collective-permute-done((s32[32,32]{1,0:T(8,128)S(1)}, s32[32,32]{1,0:T(8,128)S(1)}, u32[]{:S(2)}, u32[]{:S(2)}) %collective-permute-start.5) | collective-permute-done | bytes 4128 | tf_op jit(solution)/shard_map/ppermute | solution.py:309
  19.3 1.1 %collective-permute-start.3 = (s16[528,128]{1,0:T(8,128)(2,1)S(1)}, s16[528,128]{1,0:T(8,128)(2,1)S(1)}, u32[]{:S(2)}, u32[]{:S(2)}) collective-permute-start(s16[528,128]{1,0:T(8,128)(2,1)S(1)} %get-tuple-element.36.refs_2_), channel_id=1, source_target_pairs={{0,2},{1,3},{2,0},{3,1},{4,6},{5,7},{6,4},{7,5},{8,10},{9,11},{10,... | collective-permute-start | bytes 405512 | tf_op jit(solution)/shard_map/ppermute | solution.py:259
  20.5 2.3 %shard_map.54 = (s16[1040,128]{1,0:T(8,128)(2,1)S(1)}, bf16[32,128,128]{2,1,0:T(8,128)(2,1)S(1)}) custom-call(s32[32,32]{1,0:T(8,128)S(1)} %collective-permute-done.5.refs_2_.refs_0_, bf16[64,128,128]{2,1,0:T(8,128)(2,1)S(1)} %bitcast.30, bf16[16,128,128]{2,1,0:T(8,128)(2,1)S(1)} %collective-permute-done.6.refs_0_.refs_2_, ...), custom_call_target="tpu_custom_call" | custom-call | bytes 1 | tf_op jit(solution)/shard_map/pallas_call | solution.py:214
  22.7 1.0 %collective-permute-start.11 = (s16[1040,128]{1,0:T(8,128)(2,1)S(1)}, s16[1040,128]{1,0:T(8,128)(2,1)S(1)}, u32[]{:S(2)}, u32[]{:S(2)}) collective-permute-start(s16[1040,128]{1,0:T(8,128)(2,1)S(1)} %get-tuple-element.42.refs_3_), channel_id=1, source_target_pairs={{0,2},{1,3},{2,0},{3,1},{4,6},{5,7},{6,4},{7,5},{8,10},{9,11},{10,... | collective-permute-start | bytes 798728 | tf_op jit(solution)/shard_map/ppermute | solution.py:259
  23.7 2.1 %shard_map.55.refs_4_ = s16[1040,128]{1,0:T(8,128)(2,1)S(1)} custom-call(s32[32,32]{1,0:T(8,128)S(1)} %collective-permute-done.5.refs_2_.refs_0_, bf16[64,128,128]{2,1,0:T(8,128)(2,1)S(1)} %bitcast.31, bf16[32,128,128]{2,1,0:T(8,128)(2,1)S(1)} %get-tuple-element.41.refs_2_, s16[1040,128]{1,0:T(8,128)(2,1)S(1)} %get-tuple-element.42.refs_3_), custom_call_target="tpu_custom_call" | custom-call | bytes 1 | tf_op jit(solution)/shard_map/pallas_call | solution.py:214
  25.9 1.6 %collective-permute-start.10 = (s16[1040,128]{1,0:T(8,128)(2,1)S(1)}, s16[1040,128]{1,0:T(8,128)(2,1)S(1)}, u32[]{:S(2)}, u32[]{:S(2)}) collective-permute-start(s16[1040,128]{1,0:T(8,128)(2,1)S(1)} %shard_map.55.refs_4_), channel_id=1, source_target_pairs={{0,1},{1,0},{2,3},{3,2},{4,5},{5,4},{6,7},{7,6},{8,9},{9,8},{10,11... | collective-permute-start | bytes 798728 | tf_op jit(solution)/shard_map/ppermute | solution.py:259
  27.6 2.7 %collective-permute-start.9 = (s16[528,128]{1,0:T(8,128)(2,1)S(1)}, s16[528,128]{1,0:T(8,128)(2,1)S(1)}, u32[]{:S(2)}, u32[]{:S(2)}) collective-permute-start(s16[528,128]{1,0:T(8,128)(2,1)S(1)} %get-tuple-element.44.refs_3_), channel_id=1, source_target_pairs={{0,4},{1,5},{2,6},{3,7},{4,0},{5,1},{6,2},{7,3},{8,12},{9,13},{10,... | collective-permute-start | bytes 405512 | tf_op jit(solution)/shard_map/ppermute | solution.py:259
  30.3 3.2 %shard_map.57 = (f32[8,128,128]{2,1,0:T(8,128)S(1)}, f32[8,128,128]{2,1,0:T(8,128)S(1)}) custom-call(s32[32,32]{1,0:T(8,128)S(1)} %collective-permute-done.5.refs_2_.refs_0_, bf16[64,128,128]{2,1,0:T(8,128)(2,1)S(1)} %bitcast.32, bf16[32,128,128]{2,1,0:T(8,128)(2,1)S(1)} %get-tuple-element.41.refs_2_, s16[528,128]{1,0:T(8,128)(2,1)S(1)} %get-tuple-element.44.refs_3_), custom_call_target="tpu_custom_call" | custom-call | flops 5368709120 | bytes 4198400 | tf_op jit(solution)/shard_map/pallas_call | solution.py:214
  33.7 0.6 %collective-permute-start.13 = (s16[528,128]{1,0:T(8,128)(2,1)S(1)}, s16[528,128]{1,0:T(8,128)(2,1)S(1)}, u32[]{:S(2)}, u32[]{:S(2)}) collective-permute-start(s16[528,128]{1,0:T(8,128)(2,1)S(1)} %get-tuple-element.47.refs_2_), channel_id=1, source_target_pairs={{0,1},{1,0},{2,3},{3,2},{4,5},{5,4},{6,7},{7,6},{8,9},{9,8},{10,11... | collective-permute-start | bytes 405512 | tf_op jit(solution)/shard_map/ppermute | solution.py:259
  34.5 1.1 %collective-permute-start.12 = (s16[528,128]{1,0:T(8,128)(2,1)S(1)}, s16[528,128]{1,0:T(8,128)(2,1)S(1)}, u32[]{:S(2)}, u32[]{:S(2)}) collective-permute-start(s16[528,128]{1,0:T(8,128)(2,1)S(1)} %get-tuple-element.48.refs_2_), channel_id=1, source_target_pairs={{0,2},{1,3},{2,0},{3,1},{4,6},{5,7},{6,4},{7,5},{8,10},{9,11},{10,... | collective-permute-start | bytes 405512 | tf_op jit(solution)/shard_map/ppermute | solution.py:259
  36.1 2.6 %collective-permute-done.13.refs_1_ = s16[528,128]{1,0:T(8,128)(2,1)S(1)} collective-permute-done((s16[528,128]{1,0:T(8,128)(2,1)S(1)}, s16[528,128]{1,0:T(8,128)(2,1)S(1)}, u32[]{:S(2)}, u32[]{:S(2)}) %collective-permute-start.13) | collective-permute-done | bytes 135200 | tf_op jit(solution)/shard_map/ppermute | solution.py:259
  38.9 2.2 %collective-permute-start.16 = (s16[272,128]{1,0:T(8,128)(2,1)S(1)}, s16[272,128]{1,0:T(8,128)(2,1)S(1)}, u32[]{:S(2)}, u32[]{:S(2)}) collective-permute-start(s16[272,128]{1,0:T(8,128)(2,1)S(1)} %get-tuple-element.51.refs_2_), channel_id=1, source_target_pairs={{0,12},{1,13},{2,14},{3,15},{4,8},{5,9},{6,10},{7,11},{8,4},{9,5},... | collective-permute-start | bytes 208904 | tf_op jit(solution)/shard_map/ppermute | solution.py:264
  41.7 2.6 %collective-permute-start.14 = (s16[272,128]{1,0:T(8,128)(2,1)S(1)}, s16[272,128]{1,0:T(8,128)(2,1)S(1)}, u32[]{:S(2)}, u32[]{:S(2)}) collective-permute-start(s16[272,128]{1,0:T(8,128)(2,1)S(1)} %get-tuple-element.52), channel_id=1, source_target_pairs={{0,12},{1,13},{2,14},{3,15},{4,8},{5,9},{6,10},{7,11},{8,4},{9,5},... | collective-permute-start | bytes 208904 | tf_op jit(solution)/shard_map/ppermute | solution.py:264
  44.3 0.6 %collective-permute-start.15 = (s16[272,128]{1,0:T(8,128)(2,1)S(1)}, s16[272,128]{1,0:T(8,128)(2,1)S(1)}, u32[]{:S(2)}, u32[]{:S(2)}) collective-permute-start(s16[272,128]{1,0:T(8,128)(2,1)S(1)} %get-tuple-element.53), channel_id=1, source_target_pairs={{0,8},{1,9},{2,10},{3,11},{4,12},{5,13},{6,14},{7,15},{8,0},{9,1},... | collective-permute-start | bytes 208904 | tf_op jit(solution)/shard_map/ppermute | solution.py:264
  45.0 1.1 %collective-permute-done.16.refs_1_ = s16[272,128]{1,0:T(8,128)(2,1)S(1)} collective-permute-done((s16[272,128]{1,0:T(8,128)(2,1)S(1)}, s16[272,128]{1,0:T(8,128)(2,1)S(1)}, u32[]{:S(2)}, u32[]{:S(2)}) %collective-permute-start.16) | collective-permute-done | bytes 69664 | tf_op jit(solution)/shard_map/ppermute | solution.py:264
  46.1 2.5 %collective-permute-done.14.refs_1_ = s16[272,128]{1,0:T(8,128)(2,1)S(1)} collective-permute-done((s16[272,128]{1,0:T(8,128)(2,1)S(1)}, s16[272,128]{1,0:T(8,128)(2,1)S(1)}, u32[]{:S(2)}, u32[]{:S(2)}) %collective-permute-start.14) | collective-permute-done | bytes 69664 | tf_op jit(solution)/shard_map/ppermute | solution.py:264
  48.6 0.7 %shard_map.64 = bf16[4,128,128]{2,1,0:T(8,128)(2,1)} custom-call(f32[4,128,128]{2,1,0:T(8,128)S(1)} %shard_map.60.refs_2_.refs_0_, s16[272,128]{1,0:T(8,128)(2,1)S(1)} %collective-permute-done.14.refs_1_, s16[272,128]{1,0:T(8,128)(2,1)S(1)} %collective-permute-done.15.refs_2_, bf16[2,128,128]{2,1,0:T(8,128)(2,1)S(1)} %shard_map.63.refs_3_), custom_call_target="tpu_custom_call" | custom-call | bytes 1 | tf_op jit(solution)/shard_map/pallas_call | solution.py:214
  (42 shorter events, 4.2 us)
Async XLA Ops:
  0.0 3.0 %copy-start = (bf16[1,1,1,64,128,128]{5,4,3,2,1,0:T(8,128)(2,1)S(1)}, bf16[1,1,1,64,128,128]{5,4,3,2,1,0:T(8,128)(2,1)}, u32[]{:S(2)}) copy-start(bf16[1,1,1,64,128,128]{5,4,3,2,1,0:T(8,128)(2,1)} %param.4) | copy-start | bytes 6291460
  0.0 3.0 %copy-start.1 = (bf16[1,1,1,16,128,128]{5,4,3,2,1,0:T(8,128)(2,1)S(1)}, bf16[1,1,1,16,128,128]{5,4,3,2,1,0:T(8,128)(2,1)}, u32[]{:S(2)}) copy-start(bf16[1,1,1,16,128,128]{5,4,3,2,1,0:T(8,128)(2,1)} %param.5) | copy-start | bytes 1572868
  0.0 3.8 %collective-permute-start = (bf16[16,128,128]{2,1,0:T(8,128)(2,1)}, bf16[16,128,128]{2,1,0:T(8,128)(2,1)}, u32[]{:S(2)}, u32[]{:S(2)}) collective-permute-start(bf16[16,128,128]{2,1,0:T(8,128)(2,1)} %bitcast.33), channel_id=1, source_target_pairs={{0,16},{16,0},{1,17},{17,1},{2,18},{18,2},{3,19},{19,3},{4,20},{20... | collective-permute-start | bytes 1572872 | tf_op jit(solution)/shard_map/ppermute | solution.py:298
  0.5 15.3 %collective-permute-start.6 = (bf16[16,128,128]{2,1,0:T(8,128)(2,1)}, bf16[16,128,128]{2,1,0:T(8,128)(2,1)S(1)}, u32[]{:S(2)}, u32[]{:S(2)}) collective-permute-start(bf16[16,128,128]{2,1,0:T(8,128)(2,1)} %bitcast.34), channel_id=1, source_target_pairs={{0,8},{8,0},{1,9},{9,1},{2,10},{10,2},{3,11},{11,3},{4,12},{12,4},... | collective-permute-start | bytes 1572872 | tf_op jit(solution)/shard_map/ppermute | solution.py:297
  3.0 0.7 %copy-start.2 = (s32[1,1,1,2,32,16]{4,5,3,2,1,0:T(8,128)S(1)}, s32[1,1,1,2,32,16]{4,5,3,2,1,0:T(8,128)}, u32[]{:S(2)}) copy-start(s32[1,1,1,2,32,16]{4,5,3,2,1,0:T(8,128)} %param.7) | copy-start | bytes 12292
  3.0 0.7 %copy-start.3 = (s32[1,1,1,2,32,16]{4,5,3,2,1,0:T(8,128)S(1)}, s32[1,1,1,2,32,16]{4,5,3,2,1,0:T(8,128)}, u32[]{:S(2)}) copy-start(s32[1,1,1,2,32,16]{4,5,3,2,1,0:T(8,128)} %param.6) | copy-start | bytes 12292
  7.6 10.9 %collective-permute-start.1 = (s16[1040,128]{1,0:T(8,128)(2,1)S(1)}, s16[1040,128]{1,0:T(8,128)(2,1)S(1)}, u32[]{:S(2)}, u32[]{:S(2)}) collective-permute-start(s16[1040,128]{1,0:T(8,128)(2,1)S(1)} %get-tuple-element.31.refs_3_), channel_id=1, source_target_pairs={{0,1},{1,0},{2,3},{3,2},{4,5},{5,4},{6,7},{7,6},{8,9},{9,8},{10,11... | collective-permute-start | bytes 798728 | tf_op jit(solution)/shard_map/ppermute | solution.py:259
  9.2 9.4 %collective-permute-start.2 = (s16[1040,128]{1,0:T(8,128)(2,1)S(1)}, s16[1040,128]{1,0:T(8,128)(2,1)S(1)}, u32[]{:S(2)}, u32[]{:S(2)}) collective-permute-start(s16[1040,128]{1,0:T(8,128)(2,1)S(1)} %get-tuple-element.35), channel_id=1, source_target_pairs={{0,2},{1,3},{2,0},{3,1},{4,6},{5,7},{6,4},{7,5},{8,10},{9,11},{10,... | collective-permute-start | bytes 798728 | tf_op jit(solution)/shard_map/ppermute | solution.py:259
  14.0 3.8 %collective-permute-start.5 = (s32[32,32]{1,0:T(8,128)S(1)}, s32[32,32]{1,0:T(8,128)S(1)}, u32[]{:S(2)}, u32[]{:S(2)}) collective-permute-start(s32[32,32]{1,0:T(8,128)S(1)} %shard_map.52), channel_id=1, source_target_pairs={{0,8},{8,0},{1,9},{9,1},{2,10},{10,2},{3,11},{11,3},{4,12},{12,4},... | collective-permute-start | bytes 12296 | tf_op jit(solution)/shard_map/ppermute | solution.py:309
  17.8 2.6 %collective-permute-start.7 = (bf16[8,128,128]{2,1,0:T(8,128)(2,1)S(1)}, bf16[8,128,128]{2,1,0:T(8,128)(2,1)S(1)}, u32[]{:S(2)}, u32[]{:S(2)}) collective-permute-start(bf16[8,128,128]{2,1,0:T(8,128)(2,1)S(1)} %get-tuple-element.39), channel_id=1, source_target_pairs={{0,16},{16,0},{1,17},{17,1},{2,18},{18,2},{3,19},{19,3},{4,20},{20... | collective-permute-start | bytes 786440 | tf_op jit(solution)/shard_map/ppermute | solution.py:312
  17.9 2.6 %collective-permute-start.8 = (bf16[8,128,128]{2,1,0:T(8,128)(2,1)S(1)}, bf16[8,128,128]{2,1,0:T(8,128)(2,1)S(1)}, u32[]{:S(2)}, u32[]{:S(2)}) collective-permute-start(bf16[8,128,128]{2,1,0:T(8,128)(2,1)S(1)} %get-tuple-element.40), channel_id=1, source_target_pairs={{0,16},{16,0},{1,17},{17,1},{2,18},{18,2},{3,19},{19,3},{4,20},{20... | collective-permute-start | bytes 786440 | tf_op jit(solution)/shard_map/ppermute | solution.py:312
  18.8 8.7 %collective-permute-start.4 = (s16[528,128]{1,0:T(8,128)(2,1)S(1)}, s16[528,128]{1,0:T(8,128)(2,1)S(1)}, u32[]{:S(2)}, u32[]{:S(2)}) collective-permute-start(s16[528,128]{1,0:T(8,128)(2,1)S(1)} %get-tuple-element.38.refs_5_), channel_id=1, source_target_pairs={{0,1},{1,0},{2,3},{3,2},{4,5},{5,4},{6,7},{7,6},{8,9},{9,8},{10,11... | collective-permute-start | bytes 405512 | tf_op jit(solution)/shard_map/ppermute | solution.py:259
  19.3 8.1 %collective-permute-start.3 = (s16[528,128]{1,0:T(8,128)(2,1)S(1)}, s16[528,128]{1,0:T(8,128)(2,1)S(1)}, u32[]{:S(2)}, u32[]{:S(2)}) collective-permute-start(s16[528,128]{1,0:T(8,128)(2,1)S(1)} %get-tuple-element.36.refs_2_), channel_id=1, source_target_pairs={{0,2},{1,3},{2,0},{3,1},{4,6},{5,7},{6,4},{7,5},{8,10},{9,11},{10,... | collective-permute-start | bytes 405512 | tf_op jit(solution)/shard_map/ppermute | solution.py:259
  22.7 10.7 %collective-permute-start.11 = (s16[1040,128]{1,0:T(8,128)(2,1)S(1)}, s16[1040,128]{1,0:T(8,128)(2,1)S(1)}, u32[]{:S(2)}, u32[]{:S(2)}) collective-permute-start(s16[1040,128]{1,0:T(8,128)(2,1)S(1)} %get-tuple-element.42.refs_3_), channel_id=1, source_target_pairs={{0,2},{1,3},{2,0},{3,1},{4,6},{5,7},{6,4},{7,5},{8,10},{9,11},{10,... | collective-permute-start | bytes 798728 | tf_op jit(solution)/shard_map/ppermute | solution.py:259
  25.9 8.4 %collective-permute-start.10 = (s16[1040,128]{1,0:T(8,128)(2,1)S(1)}, s16[1040,128]{1,0:T(8,128)(2,1)S(1)}, u32[]{:S(2)}, u32[]{:S(2)}) collective-permute-start(s16[1040,128]{1,0:T(8,128)(2,1)S(1)} %shard_map.55.refs_4_), channel_id=1, source_target_pairs={{0,1},{1,0},{2,3},{3,2},{4,5},{5,4},{6,7},{7,6},{8,9},{9,8},{10,11... | collective-permute-start | bytes 798728 | tf_op jit(solution)/shard_map/ppermute | solution.py:259
  27.6 8.5 %collective-permute-start.9 = (s16[528,128]{1,0:T(8,128)(2,1)S(1)}, s16[528,128]{1,0:T(8,128)(2,1)S(1)}, u32[]{:S(2)}, u32[]{:S(2)}) collective-permute-start(s16[528,128]{1,0:T(8,128)(2,1)S(1)} %get-tuple-element.44.refs_3_), channel_id=1, source_target_pairs={{0,4},{1,5},{2,6},{3,7},{4,0},{5,1},{6,2},{7,3},{8,12},{9,13},{10,... | collective-permute-start | bytes 405512 | tf_op jit(solution)/shard_map/ppermute | solution.py:259
  33.7 5.1 %collective-permute-start.13 = (s16[528,128]{1,0:T(8,128)(2,1)S(1)}, s16[528,128]{1,0:T(8,128)(2,1)S(1)}, u32[]{:S(2)}, u32[]{:S(2)}) collective-permute-start(s16[528,128]{1,0:T(8,128)(2,1)S(1)} %get-tuple-element.47.refs_2_), channel_id=1, source_target_pairs={{0,1},{1,0},{2,3},{3,2},{4,5},{5,4},{6,7},{7,6},{8,9},{9,8},{10,11... | collective-permute-start | bytes 405512 | tf_op jit(solution)/shard_map/ppermute | solution.py:259
  34.5 7.1 %collective-permute-start.12 = (s16[528,128]{1,0:T(8,128)(2,1)S(1)}, s16[528,128]{1,0:T(8,128)(2,1)S(1)}, u32[]{:S(2)}, u32[]{:S(2)}) collective-permute-start(s16[528,128]{1,0:T(8,128)(2,1)S(1)} %get-tuple-element.48.refs_2_), channel_id=1, source_target_pairs={{0,2},{1,3},{2,0},{3,1},{4,6},{5,7},{6,4},{7,5},{8,10},{9,11},{10,... | collective-permute-start | bytes 405512 | tf_op jit(solution)/shard_map/ppermute | solution.py:259
  38.9 7.2 %collective-permute-start.16 = (s16[272,128]{1,0:T(8,128)(2,1)S(1)}, s16[272,128]{1,0:T(8,128)(2,1)S(1)}, u32[]{:S(2)}, u32[]{:S(2)}) collective-permute-start(s16[272,128]{1,0:T(8,128)(2,1)S(1)} %get-tuple-element.51.refs_2_), channel_id=1, source_target_pairs={{0,12},{1,13},{2,14},{3,15},{4,8},{5,9},{6,10},{7,11},{8,4},{9,5},... | collective-permute-start | bytes 208904 | tf_op jit(solution)/shard_map/ppermute | solution.py:264
  41.0 5.1 %collective-permute-start.17 = (s16[272,128]{1,0:T(8,128)(2,1)S(1)}, s16[272,128]{1,0:T(8,128)(2,1)S(1)}, u32[]{:S(2)}, u32[]{:S(2)}) collective-permute-start(s16[272,128]{1,0:T(8,128)(2,1)S(1)} %get-tuple-element.54), channel_id=1, source_target_pairs={{0,8},{1,9},{2,10},{3,11},{4,12},{5,13},{6,14},{7,15},{8,0},{9,1},... | collective-permute-start | bytes 208904 | tf_op jit(solution)/shard_map/ppermute | solution.py:264
  41.7 7.0 %collective-permute-start.14 = (s16[272,128]{1,0:T(8,128)(2,1)S(1)}, s16[272,128]{1,0:T(8,128)(2,1)S(1)}, u32[]{:S(2)}, u32[]{:S(2)}) collective-permute-start(s16[272,128]{1,0:T(8,128)(2,1)S(1)} %get-tuple-element.52), channel_id=1, source_target_pairs={{0,12},{1,13},{2,14},{3,15},{4,8},{5,9},{6,10},{7,11},{8,4},{9,5},... | collective-permute-start | bytes 208904 | tf_op jit(solution)/shard_map/ppermute | solution.py:264
  44.3 4.3 %collective-permute-start.15 = (s16[272,128]{1,0:T(8,128)(2,1)S(1)}, s16[272,128]{1,0:T(8,128)(2,1)S(1)}, u32[]{:S(2)}, u32[]{:S(2)}) collective-permute-start(s16[272,128]{1,0:T(8,128)(2,1)S(1)} %get-tuple-element.53), channel_id=1, source_target_pairs={{0,8},{1,9},{2,10},{3,11},{4,12},{5,13},{6,14},{7,15},{8,0},{9,1},... | collective-permute-start | bytes 208904 | tf_op jit(solution)/shard_map/ppermute | solution.py:264

commit v8 on v7

--- a/solution.py
+++ b/solution.py
@@ -7,6 +7,7 @@
 
 PEAK = 32766.0
 ROWS = 16
+LANES = 128
 GROUP = 8
 SMEM = pltpu.MemorySpace.SMEM
 VMEM = pltpu.MemorySpace.VMEM
@@ -75,13 +76,39 @@
     return ((rest >> at) << (at + 1)) | (bit << at) | low
 
 
-def finder(lists_ref, fan):
-    return lambda t: lambda f: (lists_ref[f, t], lists_ref[fan + f, t])
-
-
-def send_kernel(fan, count, chunks, bits, joins):
+def loop(turns, body, start):
+    return body(0, start) if turns == 1 else lax.fori_loop(0, turns, body, start)
+
+
+def packing(slots, lanes):
+    return max(1, lanes // slots)
+
+
+def pack_kernel(ia_ref, ip_ref, own_ref, far_ref):
+    fan, slots = ia_ref.shape[1:]
+    per = packing(slots, own_ref.shape[1])
+    col = lax.axis_index("col")
+    for out_ref, column in ((own_ref, col), (far_ref, 1 - col)):
+        for which, ref in enumerate((ia_ref, ip_ref)):
+            lists = ref[column]
+            for f in range(fan):
+                row, at = divmod(which * fan + f, per)
+                out_ref[pl.ds(row, 1), pl.ds(at * slots, slots)] = lists[f : f + 1]
+
+
+def finder(lists_ref, fan, slots):
+    per = packing(slots, lists_ref.shape[1])
+
+    def place(which, f, t):
+        row, at = divmod(which * fan + f, per)
+        return lists_ref[row, at * slots + t]
+
+    return lambda t: lambda f: (place(0, f, t), place(1, f, t))
+
+
+def send_kernel(fan, slots, count, chunks, bits, joins):
     def kernel(lists_ref, a_ref, *refs):
-        find = finder(lists_ref, fan)
+        find = finder(lists_ref, fan, slots)
         n_out = len(chunks) + joins
         p_refs, out_refs = refs[:-n_out], refs[-n_out:]
         if joins:
@@ -108,7 +135,7 @@
                     head = put_tile(out_ref, slot, tile, head)
                 return head
 
-            put_head(out_ref, lax.fori_loop(0, total // GROUP, body, new_head(total, width)))
+            put_head(out_ref, loop(total // GROUP, body, new_head(total, width)))
 
     return kernel
 
@@ -120,9 +147,9 @@
         at += ref.shape[0]
 
 
-def keep_kernel(fan, count, chunks, bits):
+def keep_kernel(fan, slots, count, chunks, bits):
     def kernel(lists_ref, a_ref, p_ref, *out_refs):
-        find = finder(lists_ref, fan)
+        find = finder(lists_ref, fan, slots)
         for (first, size), bit, out_ref in zip(chunks, bits, out_refs):
             side = own_bit(bit)
 
@@ -133,7 +160,7 @@
                     out_ref[slot] = product(a_ref, p_ref, find(layer * count + first + slot % size), fan)
                 return 0
 
-            lax.fori_loop(0, out_ref.shape[0] // GROUP, body, 0)
+            loop(out_ref.shape[0] // GROUP, body, 0)
 
     return kernel
 
@@ -268,13 +295,13 @@
         shapes = [message(layers // 2 * size, width) for _, size in picked]
         if joins:
             shapes.append(jax.ShapeDtypeStruct((2 * held, width, width), p.dtype))
-        kernel = send_kernel(fan, count, picked, bits, joins)
+        kernel = send_kernel(fan, slots, count, picked, bits, joins)
         made = call(kernel, shapes, (lists,), vmem, after, (), cost * len(which) * flops)
         return made, [exchange(x, b) for x, b in zip(made, bits)]
 
     def keep(lists, vmem, bits, after, cost):
         shapes = [floats(layers // 2 * size) for _, size in chunks]
-        kernel = keep_kernel(fan, count, chunks, bits)
+        kernel = keep_kernel(fan, slots, count, chunks, bits)
         return call(kernel, shapes, (lists,), vmem, after, (), cost * 2 * flops)
 
     def add(parts, sizes, rest, bit, keeps, after):
@@ -296,9 +323,8 @@
 
     p_x = lax.ppermute(p, "col", swap)
     p_r = lax.ppermute(p, "row", swap)
-    col = lax.axis_index("col")
-    lists = jnp.concatenate([ia[col], ip[col]], axis=0)
-    lists_far = jnp.concatenate([ia[1 - col], ip[1 - col]], axis=0)
+    packed = jax.ShapeDtypeStruct((-(-2 * fan // packing(slots, LANES)), max(slots, LANES)), jnp.int32)
+    lists, lists_far = call(pack_kernel, [packed] * 2, (), (ia, ip))
 
     token = jax.ShapeDtypeStruct((8, width), jnp.float32)
     gate = call(lambda *refs: None, token, (), (), (), (), 10**9)

time: 49.6 us -> 49 us (0.988)
  Pallas kernels: 16.5 us -> 15.2 us
  waiting for transfers between devices: 9.1 us -> 9.75 us
    pallas_call x18 -> x19, Pallas kernels: 16.5 us -> 15.2 us  [call(): pl.pallas_call(wrapped, out_shape=out_shape, in_specs=[pl.BlockSpec(memor...]
    ppermute x1, waiting for transfers between devices: 0.3 us -> 1.09 us  [on_device(): p_x = lax.ppermute(p, 'col', swap)]
    ppermute x4, waiting for transfers between devices: 3.62 us -> 4.4 us  [cross(): return lax.ppermute(x, ('col', 'layer'), perm)]
    ppermute x1, waiting for transfers between devices: 2.06 us -> 1.35 us  [on_device(): lists_x = lax.ppermute(hold(lists_far, own_kept[:1]), 'col', swap)]
  transfers between devices with their start and end apart: 18 -> 18, of which waited for: 6 -> 8; matrix products, arithmetic and copies ran while one was open for 0% -> 0% of each run, Pallas kernels for 32% -> 30%
where the time goes in v8:
time: 49 us; the launch traced here: 48.8 us
  starting transfers between devices  23 us (47%)
  Pallas kernels  15.2 us (31%)
  waiting for transfers between devices  9.75 us (20%)
  local copies, waits for them, and re-layouts  0.72 us (1%)
    pallas_call x19, Pallas kernels, call(): pl.pallas_call(wrapped, out_shape=out_shape, in_specs=[pl.BlockSpec(memor...  15.2 us
    ppermute x9, starting transfers between devices, exchange(): return lax.ppermute(x, 'layer', [(i, i ^ 1 << bit) for i in range(layers)])  12.2 us
    ppermute x4, starting transfers between devices, cross(): return lax.ppermute(x, ('col', 'layer'), perm)  5.98 us
    ppermute x4, waiting for transfers between devices, cross(): return lax.ppermute(x, ('col', 'layer'), perm)  4.4 us
    ppermute x9, waiting for transfers between devices, exchange(): return lax.ppermute(x, 'layer', [(i, i ^ 1 << bit) for i in range(layers)])  2.9 us
    ppermute x1, starting transfers between devices, on_device(): p_x = lax.ppermute(p, 'col', swap)  2.56 us
    ppermute x1, waiting for transfers between devices, on_device(): lists_x = lax.ppermute(hold(lists_far, own_kept[:1]), 'col', swap)  1.35 us
    ppermute x1, starting transfers between devices, on_device(): lists_x = lax.ppermute(hold(lists_far, own_kept[:1]), 'col', swap)  1.23 us
  transfers between devices with their start and end apart: 18, of which 8 were waited for; matrix products, arithmetic and copies ran while one was open for 0% of the time, Pallas kernels for 30%

profile of v8, /device:TPU:0, one launch (start us, length us, event | category | flops | bytes accessed | tf_op | source)
XLA Modules:
  0.0 48.8 jit_solution(5190009488008082447)
XLA Ops:
  0.5 2.6 %collective-permute-start.6 = (bf16[16,128,128]{2,1,0:T(8,128)(2,1)}, bf16[16,128,128]{2,1,0:T(8,128)(2,1)S(1)}, u32[]{:S(2)}, u32[]{:S(2)}) collective-permute-start(bf16[16,128,128]{2,1,0:T(8,128)(2,1)} %bitcast.16), channel_id=1, source_target_pairs={{0,8},{8,0},{1,9},{9,1},{2,10},{10,2},{3,11},{11,3},{4,12},{12,4},... | collective-permute-start | bytes 1572872 | tf_op jit(solution)/shard_map/ppermute | solution.py:324
  3.0 0.7 %copy-done.2 = s32[1,1,1,2,32,16]{4,5,3,2,1,0:T(8,128)S(1)} copy-done((s32[1,1,1,2,32,16]{4,5,3,2,1,0:T(8,128)S(1)}, s32[1,1,1,2,32,16]{4,5,3,2,1,0:T(8,128)}, u32[]{:S(2)}) %copy-start.2) | copy-done | bytes 4120
  3.9 3.3 %shard_map.49 = (s16[1040,128]{1,0:T(8,128)(2,1)S(1)}, s16[1040,128]{1,0:T(8,128)(2,1)S(1)}, bf16[32,128,128]{2,1,0:T(8,128)(2,1)S(1)}) custom-call(s32[8,128]{1,0:T(8,128)S(1)} %get-tuple-element.32.refs_0_, bf16[64,128,128]{2,1,0:T(8,128)(2,1)S(1)} %bitcast.10, bf16[16,128,128]{2,1,0:T(8,128)(2,1)S(1)} %bitcast.18, ...), custom_call_target="tpu_custom_call" | custom-call | flops 5368709120 | bytes 4730880 | tf_op jit(solution)/shard_map/pallas_call | solution.py:241
  7.2 1.6 %collective-permute-start.1 = (s16[1040,128]{1,0:T(8,128)(2,1)S(1)}, s16[1040,128]{1,0:T(8,128)(2,1)S(1)}, u32[]{:S(2)}, u32[]{:S(2)}) collective-permute-start(s16[1040,128]{1,0:T(8,128)(2,1)S(1)} %get-tuple-element.34.refs_3_), channel_id=1, source_target_pairs={{0,1},{1,0},{2,3},{3,2},{4,5},{5,4},{6,7},{7,6},{8,9},{9,8},{10,11... | collective-permute-start | bytes 798728 | tf_op jit(solution)/shard_map/ppermute | solution.py:286
  8.8 1.6 %collective-permute-start.2 = (s16[1040,128]{1,0:T(8,128)(2,1)S(1)}, s16[1040,128]{1,0:T(8,128)(2,1)S(1)}, u32[]{:S(2)}, u32[]{:S(2)}) collective-permute-start(s16[1040,128]{1,0:T(8,128)(2,1)S(1)} %get-tuple-element.38), channel_id=1, source_target_pairs={{0,2},{1,3},{2,0},{3,1},{4,6},{5,7},{6,4},{7,5},{8,10},{9,11},{10,... | collective-permute-start | bytes 798728 | tf_op jit(solution)/shard_map/ppermute | solution.py:286
  10.4 3.0 %shard_map.50 = (f32[8,128,128]{2,1,0:T(8,128)S(1)}, f32[8,128,128]{2,1,0:T(8,128)S(1)}) custom-call(s32[8,128]{1,0:T(8,128)S(1)} %get-tuple-element.32.refs_0_, bf16[64,128,128]{2,1,0:T(8,128)(2,1)S(1)} %bitcast.11, bf16[32,128,128]{2,1,0:T(8,128)(2,1)S(1)} %get-tuple-element.33.refs_2_, s16[1040,128]{1,0:T(8,128)(2,1)S(1)} %get-tuple-element.34.refs_3_), custom_call_target="tpu_custom_call" | custom-call | flops 5368709120 | bytes 4198400 | tf_op jit(solution)/shard_map/pallas_call | solution.py:241
  13.4 1.2 %collective-permute-start.5 = (s32[8,128]{1,0:T(8,128)S(1)}, s32[8,128]{1,0:T(8,128)S(1)}, u32[]{:S(2)}, u32[]{:S(2)}) collective-permute-start(s32[8,128]{1,0:T(8,128)S(1)} %shard_map.53), channel_id=1, source_target_pairs={{0,8},{8,0},{1,9},{9,1},{2,10},{10,2},{3,11},{11,3},{4,12},{12,4},... | collective-permute-start | bytes 12296 | tf_op jit(solution)/shard_map/ppermute | solution.py:335
  14.7 1.1 %collective-permute-done.6.refs_0_.refs_2_ = bf16[16,128,128]{2,1,0:T(8,128)(2,1)S(1)} collective-permute-done((bf16[16,128,128]{2,1,0:T(8,128)(2,1)}, bf16[16,128,128]{2,1,0:T(8,128)(2,1)S(1)}, u32[]{:S(2)}, u32[]{:S(2)}) %collective-permute-start.6) | collective-permute-done | bytes 524320 | tf_op jit(solution)/shard_map/ppermute | solution.py:324
  15.8 1.3 %collective-permute-done.5.refs_2_.refs_0_ = s32[8,128]{1,0:T(8,128)S(1)} collective-permute-done((s32[8,128]{1,0:T(8,128)S(1)}, s32[8,128]{1,0:T(8,128)S(1)}, u32[]{:S(2)}, u32[]{:S(2)}) %collective-permute-start.5) | collective-permute-done | bytes 4128 | tf_op jit(solution)/shard_map/ppermute | solution.py:335
  18.1 0.6 %collective-permute-start.4 = (s16[528,128]{1,0:T(8,128)(2,1)S(1)}, s16[528,128]{1,0:T(8,128)(2,1)S(1)}, u32[]{:S(2)}, u32[]{:S(2)}) collective-permute-start(s16[528,128]{1,0:T(8,128)(2,1)S(1)} %get-tuple-element.41.refs_5_), channel_id=1, source_target_pairs={{0,1},{1,0},{2,3},{3,2},{4,5},{5,4},{6,7},{7,6},{8,9},{9,8},{10,11... | collective-permute-start | bytes 405512 | tf_op jit(solution)/shard_map/ppermute | solution.py:286
  18.6 1.6 %collective-permute-start.3 = (s16[528,128]{1,0:T(8,128)(2,1)S(1)}, s16[528,128]{1,0:T(8,128)(2,1)S(1)}, u32[]{:S(2)}, u32[]{:S(2)}) collective-permute-start(s16[528,128]{1,0:T(8,128)(2,1)S(1)} %get-tuple-element.39.refs_2_), channel_id=1, source_target_pairs={{0,2},{1,3},{2,0},{3,1},{4,6},{5,7},{6,4},{7,5},{8,10},{9,11},{10,... | collective-permute-start | bytes 405512 | tf_op jit(solution)/shard_map/ppermute | solution.py:286
  20.2 2.0 %shard_map.55 = (s16[1040,128]{1,0:T(8,128)(2,1)S(1)}, bf16[32,128,128]{2,1,0:T(8,128)(2,1)S(1)}) custom-call(s32[8,128]{1,0:T(8,128)S(1)} %collective-permute-done.5.refs_2_.refs_0_, bf16[64,128,128]{2,1,0:T(8,128)(2,1)S(1)} %bitcast.12, bf16[16,128,128]{2,1,0:T(8,128)(2,1)S(1)} %collective-permute-done.6.refs_0_.refs_2_, ...), custom_call_target="tpu_custom_call" | custom-call | bytes 1 | tf_op jit(solution)/shard_map/pallas_call | solution.py:241
  22.8 1.9 %shard_map.56.refs_4_ = s16[1040,128]{1,0:T(8,128)(2,1)S(1)} custom-call(s32[8,128]{1,0:T(8,128)S(1)} %collective-permute-done.5.refs_2_.refs_0_, bf16[64,128,128]{2,1,0:T(8,128)(2,1)S(1)} %bitcast.13, bf16[32,128,128]{2,1,0:T(8,128)(2,1)S(1)} %get-tuple-element.45.refs_2_, s16[1040,128]{1,0:T(8,128)(2,1)S(1)} %get-tuple-element.46.refs_3_), custom_call_target="tpu_custom_call" | custom-call | bytes 1 | tf_op jit(solution)/shard_map/pallas_call | solution.py:241
  24.7 1.6 %collective-permute-start.10 = (s16[1040,128]{1,0:T(8,128)(2,1)S(1)}, s16[1040,128]{1,0:T(8,128)(2,1)S(1)}, u32[]{:S(2)}, u32[]{:S(2)}) collective-permute-start(s16[1040,128]{1,0:T(8,128)(2,1)S(1)} %shard_map.56.refs_4_), channel_id=1, source_target_pairs={{0,1},{1,0},{2,3},{3,2},{4,5},{5,4},{6,7},{7,6},{8,9},{9,8},{10,11... | collective-permute-start | bytes 798728 | tf_op jit(solution)/shard_map/ppermute | solution.py:286
  26.5 2.6 %collective-permute-start.9 = (s16[528,128]{1,0:T(8,128)(2,1)S(1)}, s16[528,128]{1,0:T(8,128)(2,1)S(1)}, u32[]{:S(2)}, u32[]{:S(2)}) collective-permute-start(s16[528,128]{1,0:T(8,128)(2,1)S(1)} %get-tuple-element.48.refs_3_), channel_id=1, source_target_pairs={{0,4},{1,5},{2,6},{3,7},{4,0},{5,1},{6,2},{7,3},{8,12},{9,13},{10,... | collective-permute-start | bytes 405512 | tf_op jit(solution)/shard_map/ppermute | solution.py:286
  29.1 3.0 %shard_map.58 = (f32[8,128,128]{2,1,0:T(8,128)S(1)}, f32[8,128,128]{2,1,0:T(8,128)S(1)}) custom-call(s32[8,128]{1,0:T(8,128)S(1)} %collective-permute-done.5.refs_2_.refs_0_, bf16[64,128,128]{2,1,0:T(8,128)(2,1)S(1)} %bitcast.14, bf16[32,128,128]{2,1,0:T(8,128)(2,1)S(1)} %get-tuple-element.45.refs_2_, s16[528,128]{1,0:T(8,128)(2,1)S(1)} %get-tuple-element.48.refs_3_), custom_call_target="tpu_custom_call" | custom-call | flops 5368709120 | bytes 4198400 | tf_op jit(solution)/shard_map/pallas_call | solution.py:241
  32.3 1.9 %collective-permute-start.13 = (s16[528,128]{1,0:T(8,128)(2,1)S(1)}, s16[528,128]{1,0:T(8,128)(2,1)S(1)}, u32[]{:S(2)}, u32[]{:S(2)}) collective-permute-start(s16[528,128]{1,0:T(8,128)(2,1)S(1)} %get-tuple-element.51.refs_2_), channel_id=1, source_target_pairs={{0,1},{1,0},{2,3},{3,2},{4,5},{5,4},{6,7},{7,6},{8,9},{9,8},{10,11... | collective-permute-start | bytes 405512 | tf_op jit(solution)/shard_map/ppermute | solution.py:286
  34.6 0.6 %collective-permute-done.9.refs_1_ = s16[528,128]{1,0:T(8,128)(2,1)S(1)} collective-permute-done((s16[528,128]{1,0:T(8,128)(2,1)S(1)}, s16[528,128]{1,0:T(8,128)(2,1)S(1)}, u32[]{:S(2)}, u32[]{:S(2)}) %collective-permute-start.9) | collective-permute-done | bytes 135200 | tf_op jit(solution)/shard_map/ppermute | solution.py:286
  35.2 2.2 %collective-permute-done.13.refs_1_ = s16[528,128]{1,0:T(8,128)(2,1)S(1)} collective-permute-done((s16[528,128]{1,0:T(8,128)(2,1)S(1)}, s16[528,128]{1,0:T(8,128)(2,1)S(1)}, u32[]{:S(2)}, u32[]{:S(2)}) %collective-permute-start.13) | collective-permute-done | bytes 135200 | tf_op jit(solution)/shard_map/ppermute | solution.py:286
  37.5 3.0 %collective-permute-start.16 = (s16[272,128]{1,0:T(8,128)(2,1)S(1)}, s16[272,128]{1,0:T(8,128)(2,1)S(1)}, u32[]{:S(2)}, u32[]{:S(2)}) collective-permute-start(s16[272,128]{1,0:T(8,128)(2,1)S(1)} %get-tuple-element.55.refs_2_), channel_id=1, source_target_pairs={{0,12},{1,13},{2,14},{3,15},{4,8},{5,9},{6,10},{7,11},{8,4},{9,5},... | collective-permute-start | bytes 208904 | tf_op jit(solution)/shard_map/ppermute | solution.py:291
  41.2 2.3 %collective-permute-start.14 = (s16[272,128]{1,0:T(8,128)(2,1)S(1)}, s16[272,128]{1,0:T(8,128)(2,1)S(1)}, u32[]{:S(2)}, u32[]{:S(2)}) collective-permute-start(s16[272,128]{1,0:T(8,128)(2,1)S(1)} %get-tuple-element.56), channel_id=1, source_target_pairs={{0,12},{1,13},{2,14},{3,15},{4,8},{5,9},{6,10},{7,11},{8,4},{9,5},... | collective-permute-start | bytes 208904 | tf_op jit(solution)/shard_map/ppermute | solution.py:291
  43.6 1.6 %collective-permute-done.16.refs_1_ = s16[272,128]{1,0:T(8,128)(2,1)S(1)} collective-permute-done((s16[272,128]{1,0:T(8,128)(2,1)S(1)}, s16[272,128]{1,0:T(8,128)(2,1)S(1)}, u32[]{:S(2)}, u32[]{:S(2)}) %collective-permute-start.16) | collective-permute-done | bytes 69664 | tf_op jit(solution)/shard_map/ppermute | solution.py:291
  45.5 2.6 %collective-permute-done.14.refs_1_ = s16[272,128]{1,0:T(8,128)(2,1)S(1)} collective-permute-done((s16[272,128]{1,0:T(8,128)(2,1)S(1)}, s16[272,128]{1,0:T(8,128)(2,1)S(1)}, u32[]{:S(2)}, u32[]{:S(2)}) %collective-permute-start.14) | collective-permute-done | bytes 69664 | tf_op jit(solution)/shard_map/ppermute | solution.py:291
  48.1 0.7 %shard_map.65 = bf16[4,128,128]{2,1,0:T(8,128)(2,1)} custom-call(f32[4,128,128]{2,1,0:T(8,128)S(1)} %shard_map.61.refs_2_.refs_0_, s16[272,128]{1,0:T(8,128)(2,1)S(1)} %collective-permute-done.14.refs_1_, s16[272,128]{1,0:T(8,128)(2,1)S(1)} %collective-permute-done.15.refs_2_, bf16[2,128,128]{2,1,0:T(8,128)(2,1)S(1)} %shard_map.64.refs_3_), custom_call_target="tpu_custom_call" | custom-call | bytes 1 | tf_op jit(solution)/shard_map/pallas_call | solution.py:241
  (40 shorter events, 4.1 us)
Async XLA Ops:
  0.0 3.0 %copy-start = (bf16[1,1,1,64,128,128]{5,4,3,2,1,0:T(8,128)(2,1)S(1)}, bf16[1,1,1,64,128,128]{5,4,3,2,1,0:T(8,128)(2,1)}, u32[]{:S(2)}) copy-start(bf16[1,1,1,64,128,128]{5,4,3,2,1,0:T(8,128)(2,1)} %param.4) | copy-start | bytes 6291460
  0.0 3.0 %copy-start.1 = (bf16[1,1,1,16,128,128]{5,4,3,2,1,0:T(8,128)(2,1)S(1)}, bf16[1,1,1,16,128,128]{5,4,3,2,1,0:T(8,128)(2,1)}, u32[]{:S(2)}) copy-start(bf16[1,1,1,16,128,128]{5,4,3,2,1,0:T(8,128)(2,1)} %param.5) | copy-start | bytes 1572868
  0.0 3.8 %collective-permute-start = (bf16[16,128,128]{2,1,0:T(8,128)(2,1)}, bf16[16,128,128]{2,1,0:T(8,128)(2,1)S(1)}, u32[]{:S(2)}, u32[]{:S(2)}) collective-permute-start(bf16[16,128,128]{2,1,0:T(8,128)(2,1)} %bitcast.15), channel_id=1, source_target_pairs={{0,16},{16,0},{1,17},{17,1},{2,18},{18,2},{3,19},{19,3},{4,20},{20... | collective-permute-start | bytes 1572872 | tf_op jit(solution)/shard_map/ppermute | solution.py:325
  0.5 15.3 %collective-permute-start.6 = (bf16[16,128,128]{2,1,0:T(8,128)(2,1)}, bf16[16,128,128]{2,1,0:T(8,128)(2,1)S(1)}, u32[]{:S(2)}, u32[]{:S(2)}) collective-permute-start(bf16[16,128,128]{2,1,0:T(8,128)(2,1)} %bitcast.16), channel_id=1, source_target_pairs={{0,8},{8,0},{1,9},{9,1},{2,10},{10,2},{3,11},{11,3},{4,12},{12,4},... | collective-permute-start | bytes 1572872 | tf_op jit(solution)/shard_map/ppermute | solution.py:324
  3.0 0.7 %copy-start.2 = (s32[1,1,1,2,32,16]{4,5,3,2,1,0:T(8,128)S(1)}, s32[1,1,1,2,32,16]{4,5,3,2,1,0:T(8,128)}, u32[]{:S(2)}) copy-start(s32[1,1,1,2,32,16]{4,5,3,2,1,0:T(8,128)} %param.6) | copy-start | bytes 12292
  3.0 0.7 %copy-start.3 = (s32[1,1,1,2,32,16]{4,5,3,2,1,0:T(8,128)S(1)}, s32[1,1,1,2,32,16]{4,5,3,2,1,0:T(8,128)}, u32[]{:S(2)}) copy-start(s32[1,1,1,2,32,16]{4,5,3,2,1,0:T(8,128)} %param.7) | copy-start | bytes 12292
  7.2 10.5 %collective-permute-start.1 = (s16[1040,128]{1,0:T(8,128)(2,1)S(1)}, s16[1040,128]{1,0:T(8,128)(2,1)S(1)}, u32[]{:S(2)}, u32[]{:S(2)}) collective-permute-start(s16[1040,128]{1,0:T(8,128)(2,1)S(1)} %get-tuple-element.34.refs_3_), channel_id=1, source_target_pairs={{0,1},{1,0},{2,3},{3,2},{4,5},{5,4},{6,7},{7,6},{8,9},{9,8},{10,11... | collective-permute-start | bytes 798728 | tf_op jit(solution)/shard_map/ppermute | solution.py:286
  8.8 9.1 %collective-permute-start.2 = (s16[1040,128]{1,0:T(8,128)(2,1)S(1)}, s16[1040,128]{1,0:T(8,128)(2,1)S(1)}, u32[]{:S(2)}, u32[]{:S(2)}) collective-permute-start(s16[1040,128]{1,0:T(8,128)(2,1)S(1)} %get-tuple-element.38), channel_id=1, source_target_pairs={{0,2},{1,3},{2,0},{3,1},{4,6},{5,7},{6,4},{7,5},{8,10},{9,11},{10,... | collective-permute-start | bytes 798728 | tf_op jit(solution)/shard_map/ppermute | solution.py:286
  13.4 3.7 %collective-permute-start.5 = (s32[8,128]{1,0:T(8,128)S(1)}, s32[8,128]{1,0:T(8,128)S(1)}, u32[]{:S(2)}, u32[]{:S(2)}) collective-permute-start(s32[8,128]{1,0:T(8,128)S(1)} %shard_map.53), channel_id=1, source_target_pairs={{0,8},{8,0},{1,9},{9,1},{2,10},{10,2},{3,11},{11,3},{4,12},{12,4},... | collective-permute-start | bytes 12296 | tf_op jit(solution)/shard_map/ppermute | solution.py:335
  17.2 3.1 %collective-permute-start.7 = (bf16[8,128,128]{2,1,0:T(8,128)(2,1)S(1)}, bf16[8,128,128]{2,1,0:T(8,128)(2,1)S(1)}, u32[]{:S(2)}, u32[]{:S(2)}) collective-permute-start(bf16[8,128,128]{2,1,0:T(8,128)(2,1)S(1)} %get-tuple-element.43), channel_id=1, source_target_pairs={{0,16},{16,0},{1,17},{17,1},{2,18},{18,2},{3,19},{19,3},{4,20},{20... | collective-permute-start | bytes 786440 | tf_op jit(solution)/shard_map/ppermute | solution.py:338
  17.2 3.0 %collective-permute-start.8 = (bf16[8,128,128]{2,1,0:T(8,128)(2,1)S(1)}, bf16[8,128,128]{2,1,0:T(8,128)(2,1)S(1)}, u32[]{:S(2)}, u32[]{:S(2)}) collective-permute-start(bf16[8,128,128]{2,1,0:T(8,128)(2,1)S(1)} %get-tuple-element.44), channel_id=1, source_target_pairs={{0,16},{16,0},{1,17},{17,1},{2,18},{18,2},{3,19},{19,3},{4,20},{20... | collective-permute-start | bytes 786440 | tf_op jit(solution)/shard_map/ppermute | solution.py:338
  18.1 8.2 %collective-permute-start.4 = (s16[528,128]{1,0:T(8,128)(2,1)S(1)}, s16[528,128]{1,0:T(8,128)(2,1)S(1)}, u32[]{:S(2)}, u32[]{:S(2)}) collective-permute-start(s16[528,128]{1,0:T(8,128)(2,1)S(1)} %get-tuple-element.41.refs_5_), channel_id=1, source_target_pairs={{0,1},{1,0},{2,3},{3,2},{4,5},{5,4},{6,7},{7,6},{8,9},{9,8},{10,11... | collective-permute-start | bytes 405512 | tf_op jit(solution)/shard_map/ppermute | solution.py:286
  18.6 7.6 %collective-permute-start.3 = (s16[528,128]{1,0:T(8,128)(2,1)S(1)}, s16[528,128]{1,0:T(8,128)(2,1)S(1)}, u32[]{:S(2)}, u32[]{:S(2)}) collective-permute-start(s16[528,128]{1,0:T(8,128)(2,1)S(1)} %get-tuple-element.39.refs_2_), channel_id=1, source_target_pairs={{0,2},{1,3},{2,0},{3,1},{4,6},{5,7},{6,4},{7,5},{8,10},{9,11},{10,... | collective-permute-start | bytes 405512 | tf_op jit(solution)/shard_map/ppermute | solution.py:286
  22.3 9.9 %collective-permute-start.11 = (s16[1040,128]{1,0:T(8,128)(2,1)S(1)}, s16[1040,128]{1,0:T(8,128)(2,1)S(1)}, u32[]{:S(2)}, u32[]{:S(2)}) collective-permute-start(s16[1040,128]{1,0:T(8,128)(2,1)S(1)} %get-tuple-element.46.refs_3_), channel_id=1, source_target_pairs={{0,2},{1,3},{2,0},{3,1},{4,6},{5,7},{6,4},{7,5},{8,10},{9,11},{10,... | collective-permute-start | bytes 798728 | tf_op jit(solution)/shard_map/ppermute | solution.py:286
  24.7 9.6 %collective-permute-start.10 = (s16[1040,128]{1,0:T(8,128)(2,1)S(1)}, s16[1040,128]{1,0:T(8,128)(2,1)S(1)}, u32[]{:S(2)}, u32[]{:S(2)}) collective-permute-start(s16[1040,128]{1,0:T(8,128)(2,1)S(1)} %shard_map.56.refs_4_), channel_id=1, source_target_pairs={{0,1},{1,0},{2,3},{3,2},{4,5},{5,4},{6,7},{7,6},{8,9},{9,8},{10,11... | collective-permute-start | bytes 798728 | tf_op jit(solution)/shard_map/ppermute | solution.py:286
  26.5 8.7 %collective-permute-start.9 = (s16[528,128]{1,0:T(8,128)(2,1)S(1)}, s16[528,128]{1,0:T(8,128)(2,1)S(1)}, u32[]{:S(2)}, u32[]{:S(2)}) collective-permute-start(s16[528,128]{1,0:T(8,128)(2,1)S(1)} %get-tuple-element.48.refs_3_), channel_id=1, source_target_pairs={{0,4},{1,5},{2,6},{3,7},{4,0},{5,1},{6,2},{7,3},{8,12},{9,13},{10,... | collective-permute-start | bytes 405512 | tf_op jit(solution)/shard_map/ppermute | solution.py:286
  32.3 5.1 %collective-permute-start.13 = (s16[528,128]{1,0:T(8,128)(2,1)S(1)}, s16[528,128]{1,0:T(8,128)(2,1)S(1)}, u32[]{:S(2)}, u32[]{:S(2)}) collective-permute-start(s16[528,128]{1,0:T(8,128)(2,1)S(1)} %get-tuple-element.51.refs_2_), channel_id=1, source_target_pairs={{0,1},{1,0},{2,3},{3,2},{4,5},{5,4},{6,7},{7,6},{8,9},{9,8},{10,11... | collective-permute-start | bytes 405512 | tf_op jit(solution)/shard_map/ppermute | solution.py:286
  34.5 6.6 %collective-permute-start.12 = (s16[528,128]{1,0:T(8,128)(2,1)S(1)}, s16[528,128]{1,0:T(8,128)(2,1)S(1)}, u32[]{:S(2)}, u32[]{:S(2)}) collective-permute-start(s16[528,128]{1,0:T(8,128)(2,1)S(1)} %get-tuple-element.52.refs_2_), channel_id=1, source_target_pairs={{0,2},{1,3},{2,0},{3,1},{4,6},{5,7},{6,4},{7,5},{8,10},{9,11},{10,... | collective-permute-start | bytes 405512 | tf_op jit(solution)/shard_map/ppermute | solution.py:286
  37.5 7.7 %collective-permute-start.16 = (s16[272,128]{1,0:T(8,128)(2,1)S(1)}, s16[272,128]{1,0:T(8,128)(2,1)S(1)}, u32[]{:S(2)}, u32[]{:S(2)}) collective-permute-start(s16[272,128]{1,0:T(8,128)(2,1)S(1)} %get-tuple-element.55.refs_2_), channel_id=1, source_target_pairs={{0,12},{1,13},{2,14},{3,15},{4,8},{5,9},{6,10},{7,11},{8,4},{9,5},... | collective-permute-start | bytes 208904 | tf_op jit(solution)/shard_map/ppermute | solution.py:291
  40.5 5.0 %collective-permute-start.17 = (s16[272,128]{1,0:T(8,128)(2,1)S(1)}, s16[272,128]{1,0:T(8,128)(2,1)S(1)}, u32[]{:S(2)}, u32[]{:S(2)}) collective-permute-start(s16[272,128]{1,0:T(8,128)(2,1)S(1)} %get-tuple-element.58), channel_id=1, source_target_pairs={{0,8},{1,9},{2,10},{3,11},{4,12},{5,13},{6,14},{7,15},{8,0},{9,1},... | collective-permute-start | bytes 208904 | tf_op jit(solution)/shard_map/ppermute | solution.py:291
  41.2 6.9 %collective-permute-start.14 = (s16[272,128]{1,0:T(8,128)(2,1)S(1)}, s16[272,128]{1,0:T(8,128)(2,1)S(1)}, u32[]{:S(2)}, u32[]{:S(2)}) collective-permute-start(s16[272,128]{1,0:T(8,128)(2,1)S(1)} %get-tuple-element.56), channel_id=1, source_target_pairs={{0,12},{1,13},{2,14},{3,15},{4,8},{5,9},{6,10},{7,11},{8,4},{9,5},... | collective-permute-start | bytes 208904 | tf_op jit(solution)/shard_map/ppermute | solution.py:291
  43.4 4.7 %collective-permute-start.15 = (s16[272,128]{1,0:T(8,128)(2,1)S(1)}, s16[272,128]{1,0:T(8,128)(2,1)S(1)}, u32[]{:S(2)}, u32[]{:S(2)}) collective-permute-start(s16[272,128]{1,0:T(8,128)(2,1)S(1)} %get-tuple-element.57), channel_id=1, source_target_pairs={{0,8},{1,9},{2,10},{3,11},{4,12},{5,13},{6,14},{7,15},{8,0},{9,1},... | collective-permute-start | bytes 208904 | tf_op jit(solution)/shard_map/ppermute | solution.py:291

commit v9 on v8

--- a/solution.py
+++ b/solution.py
@@ -67,8 +67,12 @@
     return jnp.dot(left, right, preferred_element_type=jnp.float32)
 
 
+def place_of(bit):
+    return bit ^ lax.axis_index("row") if bit < 2 else bit
+
+
 def own_bit(bit):
-    return (lax.axis_index("layer") >> bit) & 1
+    return (lax.axis_index("layer") >> place_of(bit)) & 1
 
 
 def insert(rest, at, bit):
@@ -124,13 +128,13 @@
             (p_ref,) = p_refs
         width = p_ref.shape[-1]
         for (first, size), bit, out_ref in zip(chunks, bits, out_refs):
-            side = 1 - own_bit(bit)
+            side, place = 1 - own_bit(bit), place_of(bit)
             total = out_ref.shape[0] // width
 
             def body(step, head):
                 for k in range(GROUP):
                     slot = step * GROUP + k
-                    layer = insert(slot // size, bit, side)
+                    layer = insert(slot // size, place, side)
                     tile = product(a_ref, p_ref, find(layer * count + first + slot % size), fan)
                     head = put_tile(out_ref, slot, tile, head)
                 return head
@@ -151,12 +155,12 @@
     def kernel(lists_ref, a_ref, p_ref, *out_refs):
         find = finder(lists_ref, fan, slots)
         for (first, size), bit, out_ref in zip(chunks, bits, out_refs):
-            side = own_bit(bit)
+            side, place = own_bit(bit), place_of(bit)
 
             def body(step, _):
                 for k in range(GROUP):
                     slot = step * GROUP + k
-                    layer = insert(slot // size, bit, side)
+                    layer = insert(slot // size, place, side)
                     out_ref[slot] = product(a_ref, p_ref, find(layer * count + first + slot % size), fan)
                 return 0
 
@@ -191,6 +195,8 @@
 
             put_head(ref, lax.fori_loop(0, halves, body, new_head(halves * full, width), unroll=halves <= 4))
 
+        if not keeps:
+            mine = mine ^ lax.axis_index("row")
         send(sent_ref, 1 - mine)
         if keeps:
 
@@ -283,12 +289,19 @@
         return jax.ShapeDtypeStruct((size, width, width), jnp.float32)
 
     def exchange(x, bit):
-        return lax.ppermute(x, "layer", [(i, i ^ (1 << bit)) for i in range(layers)])
-
-    def cross(x, bit):
-        flip = 0 if bit is None else 1 << bit
-        perm = [(c * layers + i, (1 - c) * layers + (i ^ flip)) for c in range(2) for i in range(layers)]
-        return lax.ppermute(x, ("col", "layer"), perm)
+        if bit >= 2:
+            return lax.ppermute(x, "layer", [(i, i ^ (1 << bit)) for i in range(layers)])
+        perm = [(r * layers + i, r * layers + (i ^ (1 << (bit ^ r)))) for r in range(2) for i in range(layers)]
+        return lax.ppermute(x, ("row", "layer"), perm)
+
+    def cross(x, bit, first):
+        perm = []
+        for r in range(2):
+            flip = 1 << bit if first == (r == 0) else 0
+            for c in range(2):
+                for i in range(layers):
+                    perm.append(((r * 2 + c) * layers + i, (r * 2 + 1 - c) * layers + (i ^ flip)))
+        return lax.ppermute(x, ("row", "col", "layer"), perm)
 
     def send(lists, vmem, which, bits, joins, after, cost):
         picked = [chunks[n] for n in which]
@@ -372,7 +385,7 @@
     for n in range(2):
         sent, stay = add([streams[n]], [sizes[n]], rest, rest[0], False, after)
         after = (sent,)
-        moved.append((cross(sent, rest[0]), cross(stay, None)))
+        moved.append((cross(sent, rest[0], True), cross(stay, rest[0], False)))
     result = ()
     for n, (first, size) in enumerate(chunks):
         final = n == len(chunks) - 1

time: 49 us -> 50.9 us (1.039)
  waiting for transfers between devices: 9.75 us -> 13.2 us
  starting transfers between devices: 23 us -> 21.4 us
    ppermute x9 -> x1, starting transfers between devices: 12.2 us -> 2.65 us  [exchange(): return lax.ppermute(x, 'layer', [(i, i ^ 1 << bit) for i in range(layers)])]
    ppermute x4 -> x12, starting transfers between devices: 5.98 us -> 13.9 us  [the longest x8 7.94 us: exchange(): return lax.ppermute(x, ('row', 'layer'), perm)]
    ppermute x4 -> x12, waiting for transfers between devices: 4.4 us -> 10.8 us  [the longest x8 7.02 us: exchange(): return lax.ppermute(x, ('row', 'layer'), perm)]
    ppermute x9 -> x1, waiting for transfers between devices: 2.9 us -> 0.01 us  [exchange(): return lax.ppermute(x, 'layer', [(i, i ^ 1 << bit) for i in range(layers)])]
  transfers between devices with their start and end apart: 18 -> 18, of which waited for: 8 -> 7; matrix products, arithmetic and copies ran while one was open for 0% -> 0% of each run, Pallas kernels for 30% -> 29%
where the time goes in v9:
time: 50.9 us; the launch traced here: 50.8 us
  starting transfers between devices  21.4 us (42%)
  Pallas kernels  15.3 us (30%)
  waiting for transfers between devices  13.2 us (26%)
  local copies, waits for them, and re-layouts  0.72 us (1%)
    pallas_call x19, Pallas kernels, call(): pl.pallas_call(wrapped, out_shape=out_shape, in_specs=[pl.BlockSpec(memor...  15.3 us
    ppermute x8, starting transfers between devices, exchange(): return lax.ppermute(x, ('row', 'layer'), perm)  7.94 us
    ppermute x8, waiting for transfers between devices, exchange(): return lax.ppermute(x, ('row', 'layer'), perm)  7.02 us
    ppermute x4, starting transfers between devices, cross(): return lax.ppermute(x, ('row', 'col', 'layer'), perm)  5.98 us
    ppermute x4, waiting for transfers between devices, cross(): return lax.ppermute(x, ('row', 'col', 'layer'), perm)  3.77 us
    ppermute x1, starting transfers between devices, exchange(): return lax.ppermute(x, 'layer', [(i, i ^ 1 << bit) for i in range(layers)])  2.65 us
    ppermute x1, starting transfers between devices, on_device(): p_x = lax.ppermute(p, 'col', swap)  2.56 us
    ppermute x1, waiting for transfers between devices, on_device(): lists_x = lax.ppermute(hold(lists_far, own_kept[:1]), 'col', swap)  1.4 us
  transfers between devices with their start and end apart: 18, of which 7 were waited for; matrix products, arithmetic and copies ran while one was open for 0% of the time, Pallas kernels for 29%

profile of v9, /device:TPU:0, one launch (start us, length us, event | category | flops | bytes accessed | tf_op | source)
XLA Modules:
  0.0 50.8 jit_solution(16414702158248234186)
XLA Ops:
  0.5 2.6 %collective-permute-start.6 = (bf16[16,128,128]{2,1,0:T(8,128)(2,1)}, bf16[16,128,128]{2,1,0:T(8,128)(2,1)S(1)}, u32[]{:S(2)}, u32[]{:S(2)}) collective-permute-start(bf16[16,128,128]{2,1,0:T(8,128)(2,1)} %bitcast.16), channel_id=1, source_target_pairs={{0,8},{8,0},{1,9},{9,1},{2,10},{10,2},{3,11},{11,3},{4,12},{12,4},... | collective-permute-start | bytes 1572872 | tf_op jit(solution)/shard_map/ppermute | solution.py:337
  3.0 0.7 %copy-done.2 = s32[1,1,1,2,32,16]{4,5,3,2,1,0:T(8,128)S(1)} copy-done((s32[1,1,1,2,32,16]{4,5,3,2,1,0:T(8,128)S(1)}, s32[1,1,1,2,32,16]{4,5,3,2,1,0:T(8,128)}, u32[]{:S(2)}) %copy-start.2) | copy-done | bytes 4120
  3.9 3.4 %shard_map.49 = (s16[1040,128]{1,0:T(8,128)(2,1)S(1)}, s16[1040,128]{1,0:T(8,128)(2,1)S(1)}, bf16[32,128,128]{2,1,0:T(8,128)(2,1)S(1)}) custom-call(s32[8,128]{1,0:T(8,128)S(1)} %get-tuple-element.32.refs_0_, bf16[64,128,128]{2,1,0:T(8,128)(2,1)S(1)} %bitcast.10, bf16[16,128,128]{2,1,0:T(8,128)(2,1)S(1)} %bitcast.18, ...), custom_call_target="tpu_custom_call" | custom-call | flops 5368709120 | bytes 4730880 | tf_op jit(solution)/shard_map/pallas_call | solution.py:247
  7.2 1.6 %collective-permute-start.1 = (s16[1040,128]{1,0:T(8,128)(2,1)S(1)}, s16[1040,128]{1,0:T(8,128)(2,1)S(1)}, u32[]{:S(2)}, u32[]{:S(2)}) collective-permute-start(s16[1040,128]{1,0:T(8,128)(2,1)S(1)} %get-tuple-element.34.refs_3_), channel_id=1, source_target_pairs={{0,1},{1,0},{2,3},{3,2},{4,5},{5,4},{6,7},{7,6},{16,18},{17,19},{1... | collective-permute-start | bytes 798728 | tf_op jit(solution)/shard_map/ppermute | solution.py:295
  8.8 1.6 %collective-permute-start.2 = (s16[1040,128]{1,0:T(8,128)(2,1)S(1)}, s16[1040,128]{1,0:T(8,128)(2,1)S(1)}, u32[]{:S(2)}, u32[]{:S(2)}) collective-permute-start(s16[1040,128]{1,0:T(8,128)(2,1)S(1)} %get-tuple-element.38), channel_id=1, source_target_pairs={{0,2},{1,3},{2,0},{3,1},{4,6},{5,7},{6,4},{7,5},{16,17},{17,16},{1... | collective-permute-start | bytes 798728 | tf_op jit(solution)/shard_map/ppermute | solution.py:295
  10.4 3.0 %shard_map.50 = (f32[8,128,128]{2,1,0:T(8,128)S(1)}, f32[8,128,128]{2,1,0:T(8,128)S(1)}) custom-call(s32[8,128]{1,0:T(8,128)S(1)} %get-tuple-element.32.refs_0_, bf16[64,128,128]{2,1,0:T(8,128)(2,1)S(1)} %bitcast.11, bf16[32,128,128]{2,1,0:T(8,128)(2,1)S(1)} %get-tuple-element.33.refs_2_, s16[1040,128]{1,0:T(8,128)(2,1)S(1)} %get-tuple-element.34.refs_3_), custom_call_target="tpu_custom_call" | custom-call | flops 5368709120 | bytes 4198400 | tf_op jit(solution)/shard_map/pallas_call | solution.py:247
  13.5 1.2 %collective-permute-start.5 = (s32[8,128]{1,0:T(8,128)S(1)}, s32[8,128]{1,0:T(8,128)S(1)}, u32[]{:S(2)}, u32[]{:S(2)}) collective-permute-start(s32[8,128]{1,0:T(8,128)S(1)} %shard_map.53), channel_id=1, source_target_pairs={{0,8},{8,0},{1,9},{9,1},{2,10},{10,2},{3,11},{11,3},{4,12},{12,4},... | collective-permute-start | bytes 12296 | tf_op jit(solution)/shard_map/ppermute | solution.py:348
  14.7 1.0 %collective-permute-done.6.refs_0_.refs_2_ = bf16[16,128,128]{2,1,0:T(8,128)(2,1)S(1)} collective-permute-done((bf16[16,128,128]{2,1,0:T(8,128)(2,1)}, bf16[16,128,128]{2,1,0:T(8,128)(2,1)S(1)}, u32[]{:S(2)}, u32[]{:S(2)}) %collective-permute-start.6) | collective-permute-done | bytes 524320 | tf_op jit(solution)/shard_map/ppermute | solution.py:337
  15.8 1.4 %collective-permute-done.5.refs_2_.refs_0_ = s32[8,128]{1,0:T(8,128)S(1)} collective-permute-done((s32[8,128]{1,0:T(8,128)S(1)}, s32[8,128]{1,0:T(8,128)S(1)}, u32[]{:S(2)}, u32[]{:S(2)}) %collective-permute-start.5) | collective-permute-done | bytes 4128 | tf_op jit(solution)/shard_map/ppermute | solution.py:348
  18.7 1.5 %collective-permute-start.3 = (s16[528,128]{1,0:T(8,128)(2,1)S(1)}, s16[528,128]{1,0:T(8,128)(2,1)S(1)}, u32[]{:S(2)}, u32[]{:S(2)}) collective-permute-start(s16[528,128]{1,0:T(8,128)(2,1)S(1)} %get-tuple-element.39.refs_2_), channel_id=1, source_target_pairs={{0,2},{1,3},{2,0},{3,1},{4,6},{5,7},{6,4},{7,5},{16,17},{17,16},{1... | collective-permute-start | bytes 405512 | tf_op jit(solution)/shard_map/ppermute | solution.py:295
  20.2 2.0 %shard_map.55 = (s16[1040,128]{1,0:T(8,128)(2,1)S(1)}, bf16[32,128,128]{2,1,0:T(8,128)(2,1)S(1)}) custom-call(s32[8,128]{1,0:T(8,128)S(1)} %collective-permute-done.5.refs_2_.refs_0_, bf16[64,128,128]{2,1,0:T(8,128)(2,1)S(1)} %bitcast.12, bf16[16,128,128]{2,1,0:T(8,128)(2,1)S(1)} %collective-permute-done.6.refs_0_.refs_2_, ...), custom_call_target="tpu_custom_call" | custom-call | bytes 1 | tf_op jit(solution)/shard_map/pallas_call | solution.py:247
  22.8 1.9 %shard_map.56.refs_4_ = s16[1040,128]{1,0:T(8,128)(2,1)S(1)} custom-call(s32[8,128]{1,0:T(8,128)S(1)} %collective-permute-done.5.refs_2_.refs_0_, bf16[64,128,128]{2,1,0:T(8,128)(2,1)S(1)} %bitcast.13, bf16[32,128,128]{2,1,0:T(8,128)(2,1)S(1)} %get-tuple-element.45.refs_2_, s16[1040,128]{1,0:T(8,128)(2,1)S(1)} %get-tuple-element.46.refs_3_), custom_call_target="tpu_custom_call" | custom-call | bytes 1 | tf_op jit(solution)/shard_map/pallas_call | solution.py:247
  24.7 1.6 %collective-permute-start.10 = (s16[1040,128]{1,0:T(8,128)(2,1)S(1)}, s16[1040,128]{1,0:T(8,128)(2,1)S(1)}, u32[]{:S(2)}, u32[]{:S(2)}) collective-permute-start(s16[1040,128]{1,0:T(8,128)(2,1)S(1)} %shard_map.56.refs_4_), channel_id=1, source_target_pairs={{0,1},{1,0},{2,3},{3,2},{4,5},{5,4},{6,7},{7,6},{16,18},{17,19},{1... | collective-permute-start | bytes 798728 | tf_op jit(solution)/shard_map/ppermute | solution.py:295
  26.5 2.7 %collective-permute-start.9 = (s16[528,128]{1,0:T(8,128)(2,1)S(1)}, s16[528,128]{1,0:T(8,128)(2,1)S(1)}, u32[]{:S(2)}, u32[]{:S(2)}) collective-permute-start(s16[528,128]{1,0:T(8,128)(2,1)S(1)} %get-tuple-element.48.refs_3_), channel_id=1, source_target_pairs={{0,4},{1,5},{2,6},{3,7},{4,0},{5,1},{6,2},{7,3},{8,12},{9,13},{10,... | collective-permute-start | bytes 405512 | tf_op jit(solution)/shard_map/ppermute | solution.py:293
  29.1 3.0 %shard_map.58 = (f32[8,128,128]{2,1,0:T(8,128)S(1)}, f32[8,128,128]{2,1,0:T(8,128)S(1)}) custom-call(s32[8,128]{1,0:T(8,128)S(1)} %collective-permute-done.5.refs_2_.refs_0_, bf16[64,128,128]{2,1,0:T(8,128)(2,1)S(1)} %bitcast.14, bf16[32,128,128]{2,1,0:T(8,128)(2,1)S(1)} %get-tuple-element.45.refs_2_, s16[528,128]{1,0:T(8,128)(2,1)S(1)} %get-tuple-element.48.refs_3_), custom_call_target="tpu_custom_call" | custom-call | flops 5368709120 | bytes 4198400 | tf_op jit(solution)/shard_map/pallas_call | solution.py:247
  32.1 1.7 %collective-permute-done.11.refs_1_ = s16[1040,128]{1,0:T(8,128)(2,1)S(1)} collective-permute-done((s16[1040,128]{1,0:T(8,128)(2,1)S(1)}, s16[1040,128]{1,0:T(8,128)(2,1)S(1)}, u32[]{:S(2)}, u32[]{:S(2)}) %collective-permute-start.11) | collective-permute-done | bytes 266272 | tf_op jit(solution)/shard_map/ppermute | solution.py:295
  34.7 5.3 %collective-permute-done.13.refs_1_ = s16[528,128]{1,0:T(8,128)(2,1)S(1)} collective-permute-done((s16[528,128]{1,0:T(8,128)(2,1)S(1)}, s16[528,128]{1,0:T(8,128)(2,1)S(1)}, u32[]{:S(2)}, u32[]{:S(2)}) %collective-permute-start.13) | collective-permute-done | bytes 135200 | tf_op jit(solution)/shard_map/ppermute | solution.py:295
  40.1 0.6 %collective-permute-start.16 = (s16[272,128]{1,0:T(8,128)(2,1)S(1)}, s16[272,128]{1,0:T(8,128)(2,1)S(1)}, u32[]{:S(2)}, u32[]{:S(2)}) collective-permute-start(s16[272,128]{1,0:T(8,128)(2,1)S(1)} %get-tuple-element.55.refs_2_), channel_id=1, source_target_pairs={{0,12},{1,13},{2,14},{3,15},{4,8},{5,9},{6,10},{7,11},{8,4},{9,5},... | collective-permute-start | bytes 208904 | tf_op jit(solution)/shard_map/ppermute | solution.py:304
  40.7 1.0 %collective-permute-start.17 = (s16[272,128]{1,0:T(8,128)(2,1)S(1)}, s16[272,128]{1,0:T(8,128)(2,1)S(1)}, u32[]{:S(2)}, u32[]{:S(2)}) collective-permute-start(s16[272,128]{1,0:T(8,128)(2,1)S(1)} %get-tuple-element.58), channel_id=1, source_target_pairs={{0,8},{1,9},{2,10},{3,11},{4,12},{5,13},{6,14},{7,15},{8,0},{9,1},... | collective-permute-start | bytes 208904 | tf_op jit(solution)/shard_map/ppermute | solution.py:304
  41.9 3.8 %collective-permute-start.14 = (s16[272,128]{1,0:T(8,128)(2,1)S(1)}, s16[272,128]{1,0:T(8,128)(2,1)S(1)}, u32[]{:S(2)}, u32[]{:S(2)}) collective-permute-start(s16[272,128]{1,0:T(8,128)(2,1)S(1)} %get-tuple-element.56), channel_id=1, source_target_pairs={{0,12},{1,13},{2,14},{3,15},{4,8},{5,9},{6,10},{7,11},{8,4},{9,5},... | collective-permute-start | bytes 208904 | tf_op jit(solution)/shard_map/ppermute | solution.py:304
  46.2 1.6 %collective-permute-done.16.refs_1_ = s16[272,128]{1,0:T(8,128)(2,1)S(1)} collective-permute-done((s16[272,128]{1,0:T(8,128)(2,1)S(1)}, s16[272,128]{1,0:T(8,128)(2,1)S(1)}, u32[]{:S(2)}, u32[]{:S(2)}) %collective-permute-start.16) | collective-permute-done | bytes 69664 | tf_op jit(solution)/shard_map/ppermute | solution.py:304
  47.9 1.4 %collective-permute-done.14.refs_1_ = s16[272,128]{1,0:T(8,128)(2,1)S(1)} collective-permute-done((s16[272,128]{1,0:T(8,128)(2,1)S(1)}, s16[272,128]{1,0:T(8,128)(2,1)S(1)}, u32[]{:S(2)}, u32[]{:S(2)}) %collective-permute-start.14) | collective-permute-done | bytes 69664 | tf_op jit(solution)/shard_map/ppermute | solution.py:304
  49.3 0.7 %collective-permute-done.15.refs_2_ = s16[272,128]{1,0:T(8,128)(2,1)S(1)} collective-permute-done((s16[272,128]{1,0:T(8,128)(2,1)S(1)}, s16[272,128]{1,0:T(8,128)(2,1)S(1)}, u32[]{:S(2)}, u32[]{:S(2)}) %collective-permute-start.15) | collective-permute-done | bytes 69664 | tf_op jit(solution)/shard_map/ppermute | solution.py:304
  50.1 0.7 %shard_map.65 = bf16[4,128,128]{2,1,0:T(8,128)(2,1)} custom-call(f32[4,128,128]{2,1,0:T(8,128)S(1)} %shard_map.61.refs_2_.refs_0_, s16[272,128]{1,0:T(8,128)(2,1)S(1)} %collective-permute-done.14.refs_1_, s16[272,128]{1,0:T(8,128)(2,1)S(1)} %collective-permute-done.15.refs_2_, bf16[2,128,128]{2,1,0:T(8,128)(2,1)S(1)} %shard_map.64.refs_3_), custom_call_target="tpu_custom_call" | custom-call | bytes 1 | tf_op jit(solution)/shard_map/pallas_call | solution.py:247
  (40 shorter events, 4.5 us)
Async XLA Ops:
  0.0 3.0 %copy-start = (bf16[1,1,1,64,128,128]{5,4,3,2,1,0:T(8,128)(2,1)S(1)}, bf16[1,1,1,64,128,128]{5,4,3,2,1,0:T(8,128)(2,1)}, u32[]{:S(2)}) copy-start(bf16[1,1,1,64,128,128]{5,4,3,2,1,0:T(8,128)(2,1)} %param.4) | copy-start | bytes 6291460
  0.0 3.0 %copy-start.1 = (bf16[1,1,1,16,128,128]{5,4,3,2,1,0:T(8,128)(2,1)S(1)}, bf16[1,1,1,16,128,128]{5,4,3,2,1,0:T(8,128)(2,1)}, u32[]{:S(2)}) copy-start(bf16[1,1,1,16,128,128]{5,4,3,2,1,0:T(8,128)(2,1)} %param.5) | copy-start | bytes 1572868
  0.0 3.8 %collective-permute-start = (bf16[16,128,128]{2,1,0:T(8,128)(2,1)}, bf16[16,128,128]{2,1,0:T(8,128)(2,1)S(1)}, u32[]{:S(2)}, u32[]{:S(2)}) collective-permute-start(bf16[16,128,128]{2,1,0:T(8,128)(2,1)} %bitcast.15), channel_id=1, source_target_pairs={{0,16},{16,0},{1,17},{17,1},{2,18},{18,2},{3,19},{19,3},{4,20},{20... | collective-permute-start | bytes 1572872 | tf_op jit(solution)/shard_map/ppermute | solution.py:338
  0.5 15.3 %collective-permute-start.6 = (bf16[16,128,128]{2,1,0:T(8,128)(2,1)}, bf16[16,128,128]{2,1,0:T(8,128)(2,1)S(1)}, u32[]{:S(2)}, u32[]{:S(2)}) collective-permute-start(bf16[16,128,128]{2,1,0:T(8,128)(2,1)} %bitcast.16), channel_id=1, source_target_pairs={{0,8},{8,0},{1,9},{9,1},{2,10},{10,2},{3,11},{11,3},{4,12},{12,4},... | collective-permute-start | bytes 1572872 | tf_op jit(solution)/shard_map/ppermute | solution.py:337
  3.0 0.7 %copy-start.2 = (s32[1,1,1,2,32,16]{4,5,3,2,1,0:T(8,128)S(1)}, s32[1,1,1,2,32,16]{4,5,3,2,1,0:T(8,128)}, u32[]{:S(2)}) copy-start(s32[1,1,1,2,32,16]{4,5,3,2,1,0:T(8,128)} %param.6) | copy-start | bytes 12292
  3.0 0.7 %copy-start.3 = (s32[1,1,1,2,32,16]{4,5,3,2,1,0:T(8,128)S(1)}, s32[1,1,1,2,32,16]{4,5,3,2,1,0:T(8,128)}, u32[]{:S(2)}) copy-start(s32[1,1,1,2,32,16]{4,5,3,2,1,0:T(8,128)} %param.7) | copy-start | bytes 12292
  7.2 10.5 %collective-permute-start.1 = (s16[1040,128]{1,0:T(8,128)(2,1)S(1)}, s16[1040,128]{1,0:T(8,128)(2,1)S(1)}, u32[]{:S(2)}, u32[]{:S(2)}) collective-permute-start(s16[1040,128]{1,0:T(8,128)(2,1)S(1)} %get-tuple-element.34.refs_3_), channel_id=1, source_target_pairs={{0,1},{1,0},{2,3},{3,2},{4,5},{5,4},{6,7},{7,6},{16,18},{17,19},{1... | collective-permute-start | bytes 798728 | tf_op jit(solution)/shard_map/ppermute | solution.py:295
  8.8 9.1 %collective-permute-start.2 = (s16[1040,128]{1,0:T(8,128)(2,1)S(1)}, s16[1040,128]{1,0:T(8,128)(2,1)S(1)}, u32[]{:S(2)}, u32[]{:S(2)}) collective-permute-start(s16[1040,128]{1,0:T(8,128)(2,1)S(1)} %get-tuple-element.38), channel_id=1, source_target_pairs={{0,2},{1,3},{2,0},{3,1},{4,6},{5,7},{6,4},{7,5},{16,17},{17,16},{1... | collective-permute-start | bytes 798728 | tf_op jit(solution)/shard_map/ppermute | solution.py:295
  13.5 3.7 %collective-permute-start.5 = (s32[8,128]{1,0:T(8,128)S(1)}, s32[8,128]{1,0:T(8,128)S(1)}, u32[]{:S(2)}, u32[]{:S(2)}) collective-permute-start(s32[8,128]{1,0:T(8,128)S(1)} %shard_map.53), channel_id=1, source_target_pairs={{0,8},{8,0},{1,9},{9,1},{2,10},{10,2},{3,11},{11,3},{4,12},{12,4},... | collective-permute-start | bytes 12296 | tf_op jit(solution)/shard_map/ppermute | solution.py:348
  17.2 3.0 %collective-permute-start.7 = (bf16[8,128,128]{2,1,0:T(8,128)(2,1)S(1)}, bf16[8,128,128]{2,1,0:T(8,128)(2,1)S(1)}, u32[]{:S(2)}, u32[]{:S(2)}) collective-permute-start(bf16[8,128,128]{2,1,0:T(8,128)(2,1)S(1)} %get-tuple-element.43), channel_id=1, source_target_pairs={{0,16},{16,0},{1,17},{17,1},{2,18},{18,2},{3,19},{19,3},{4,20},{20... | collective-permute-start | bytes 786440 | tf_op jit(solution)/shard_map/ppermute | solution.py:351
  17.3 3.0 %collective-permute-start.8 = (bf16[8,128,128]{2,1,0:T(8,128)(2,1)S(1)}, bf16[8,128,128]{2,1,0:T(8,128)(2,1)S(1)}, u32[]{:S(2)}, u32[]{:S(2)}) collective-permute-start(bf16[8,128,128]{2,1,0:T(8,128)(2,1)S(1)} %get-tuple-element.44), channel_id=1, source_target_pairs={{0,16},{16,0},{1,17},{17,1},{2,18},{18,2},{3,19},{19,3},{4,20},{20... | collective-permute-start | bytes 786440 | tf_op jit(solution)/shard_map/ppermute | solution.py:351
  18.1 8.2 %collective-permute-start.4 = (s16[528,128]{1,0:T(8,128)(2,1)S(1)}, s16[528,128]{1,0:T(8,128)(2,1)S(1)}, u32[]{:S(2)}, u32[]{:S(2)}) collective-permute-start(s16[528,128]{1,0:T(8,128)(2,1)S(1)} %get-tuple-element.41.refs_5_), channel_id=1, source_target_pairs={{0,1},{1,0},{2,3},{3,2},{4,5},{5,4},{6,7},{7,6},{16,18},{17,19},{1... | collective-permute-start | bytes 405512 | tf_op jit(solution)/shard_map/ppermute | solution.py:295
  18.7 7.6 %collective-permute-start.3 = (s16[528,128]{1,0:T(8,128)(2,1)S(1)}, s16[528,128]{1,0:T(8,128)(2,1)S(1)}, u32[]{:S(2)}, u32[]{:S(2)}) collective-permute-start(s16[528,128]{1,0:T(8,128)(2,1)S(1)} %get-tuple-element.39.refs_2_), channel_id=1, source_target_pairs={{0,2},{1,3},{2,0},{3,1},{4,6},{5,7},{6,4},{7,5},{16,17},{17,16},{1... | collective-permute-start | bytes 405512 | tf_op jit(solution)/shard_map/ppermute | solution.py:295
  22.3 11.5 %collective-permute-start.11 = (s16[1040,128]{1,0:T(8,128)(2,1)S(1)}, s16[1040,128]{1,0:T(8,128)(2,1)S(1)}, u32[]{:S(2)}, u32[]{:S(2)}) collective-permute-start(s16[1040,128]{1,0:T(8,128)(2,1)S(1)} %get-tuple-element.46.refs_3_), channel_id=1, source_target_pairs={{0,2},{1,3},{2,0},{3,1},{4,6},{5,7},{6,4},{7,5},{16,17},{17,16},{1... | collective-permute-start | bytes 798728 | tf_op jit(solution)/shard_map/ppermute | solution.py:295
  24.7 9.3 %collective-permute-start.10 = (s16[1040,128]{1,0:T(8,128)(2,1)S(1)}, s16[1040,128]{1,0:T(8,128)(2,1)S(1)}, u32[]{:S(2)}, u32[]{:S(2)}) collective-permute-start(s16[1040,128]{1,0:T(8,128)(2,1)S(1)} %shard_map.56.refs_4_), channel_id=1, source_target_pairs={{0,1},{1,0},{2,3},{3,2},{4,5},{5,4},{6,7},{7,6},{16,18},{17,19},{1... | collective-permute-start | bytes 798728 | tf_op jit(solution)/shard_map/ppermute | solution.py:295
  26.5 8.1 %collective-permute-start.9 = (s16[528,128]{1,0:T(8,128)(2,1)S(1)}, s16[528,128]{1,0:T(8,128)(2,1)S(1)}, u32[]{:S(2)}, u32[]{:S(2)}) collective-permute-start(s16[528,128]{1,0:T(8,128)(2,1)S(1)} %get-tuple-element.48.refs_3_), channel_id=1, source_target_pairs={{0,4},{1,5},{2,6},{3,7},{4,0},{5,1},{6,2},{7,3},{8,12},{9,13},{10,... | collective-permute-start | bytes 405512 | tf_op jit(solution)/shard_map/ppermute | solution.py:293
  33.9 6.1 %collective-permute-start.13 = (s16[528,128]{1,0:T(8,128)(2,1)S(1)}, s16[528,128]{1,0:T(8,128)(2,1)S(1)}, u32[]{:S(2)}, u32[]{:S(2)}) collective-permute-start(s16[528,128]{1,0:T(8,128)(2,1)S(1)} %get-tuple-element.51.refs_2_), channel_id=1, source_target_pairs={{0,1},{1,0},{2,3},{3,2},{4,5},{5,4},{6,7},{7,6},{16,18},{17,19},{1... | collective-permute-start | bytes 405512 | tf_op jit(solution)/shard_map/ppermute | solution.py:295
  34.2 7.6 %collective-permute-start.12 = (s16[528,128]{1,0:T(8,128)(2,1)S(1)}, s16[528,128]{1,0:T(8,128)(2,1)S(1)}, u32[]{:S(2)}, u32[]{:S(2)}) collective-permute-start(s16[528,128]{1,0:T(8,128)(2,1)S(1)} %get-tuple-element.52.refs_2_), channel_id=1, source_target_pairs={{0,2},{1,3},{2,0},{3,1},{4,6},{5,7},{6,4},{7,5},{16,17},{17,16},{1... | collective-permute-start | bytes 405512 | tf_op jit(solution)/shard_map/ppermute | solution.py:295
  40.1 7.7 %collective-permute-start.16 = (s16[272,128]{1,0:T(8,128)(2,1)S(1)}, s16[272,128]{1,0:T(8,128)(2,1)S(1)}, u32[]{:S(2)}, u32[]{:S(2)}) collective-permute-start(s16[272,128]{1,0:T(8,128)(2,1)S(1)} %get-tuple-element.55.refs_2_), channel_id=1, source_target_pairs={{0,12},{1,13},{2,14},{3,15},{4,8},{5,9},{6,10},{7,11},{8,4},{9,5},... | collective-permute-start | bytes 208904 | tf_op jit(solution)/shard_map/ppermute | solution.py:304
  40.7 7.1 %collective-permute-start.17 = (s16[272,128]{1,0:T(8,128)(2,1)S(1)}, s16[272,128]{1,0:T(8,128)(2,1)S(1)}, u32[]{:S(2)}, u32[]{:S(2)}) collective-permute-start(s16[272,128]{1,0:T(8,128)(2,1)S(1)} %get-tuple-element.58), channel_id=1, source_target_pairs={{0,8},{1,9},{2,10},{3,11},{4,12},{5,13},{6,14},{7,15},{8,0},{9,1},... | collective-permute-start | bytes 208904 | tf_op jit(solution)/shard_map/ppermute | solution.py:304
  41.9 7.4 %collective-permute-start.14 = (s16[272,128]{1,0:T(8,128)(2,1)S(1)}, s16[272,128]{1,0:T(8,128)(2,1)S(1)}, u32[]{:S(2)}, u32[]{:S(2)}) collective-permute-start(s16[272,128]{1,0:T(8,128)(2,1)S(1)} %get-tuple-element.56), channel_id=1, source_target_pairs={{0,12},{1,13},{2,14},{3,15},{4,8},{5,9},{6,10},{7,11},{8,4},{9,5},... | collective-permute-start | bytes 208904 | tf_op jit(solution)/shard_map/ppermute | solution.py:304
  45.7 4.4 %collective-permute-start.15 = (s16[272,128]{1,0:T(8,128)(2,1)S(1)}, s16[272,128]{1,0:T(8,128)(2,1)S(1)}, u32[]{:S(2)}, u32[]{:S(2)}) collective-permute-start(s16[272,128]{1,0:T(8,128)(2,1)S(1)} %get-tuple-element.57), channel_id=1, source_target_pairs={{0,8},{1,9},{2,10},{3,11},{4,12},{5,13},{6,14},{7,15},{8,0},{9,1},... | collective-permute-start | bytes 208904 | tf_op jit(solution)/shard_map/ppermute | solution.py:304

commit v10 on v8

--- a/solution.py
+++ b/solution.py
@@ -165,7 +165,33 @@
     return kernel
 
 
-def add_kernel(sizes, rest, bit, keeps):
+def cross_kernel(sizes, bit, whose):
+    def kernel(*refs):
+        n = len(sizes)
+        kept_refs, in_refs, out_refs = refs[:n], refs[n : 2 * n], refs[2 * n :]
+        width = out_refs[0].shape[-1]
+        mine = own_bit(bit)
+        heads = [get_head(ref, ref.shape[0] // width) for ref in in_refs]
+
+        def put(out_ref, side, chosen):
+            count = out_ref.shape[0] // width
+            head, slot = new_head(count, width), 0
+            for c in chosen:
+                for i in range(sizes[c]):
+                    at = side * sizes[c] + i
+                    tile = kept_refs[c][at] + get_tile(in_refs[c], at, heads[c])
+                    head = put_tile(out_ref, slot, tile, head)
+                    slot += 1
+            put_head(out_ref, head)
+
+        put(out_refs[0], 1 - mine, [whose])
+        if len(out_refs) > 1:
+            put(out_refs[1], mine, range(n))
+
+    return kernel
+
+
+def add_kernel(sizes, rest, bit):
     at = rest.index(bit)
     full = sum(sizes)
     halves = 1 << (len(rest) - 1)
@@ -192,16 +218,13 @@
             put_head(ref, lax.fori_loop(0, halves, body, new_head(halves * full, width), unroll=halves <= 4))
 
         send(sent_ref, 1 - mine)
-        if keeps:
-
-            def body(half, _):
-                for i, tile in enumerate(sums(insert(half, at, mine))):
-                    stay_ref[half * full + i] = tile
-                return 0
-
-            lax.fori_loop(0, halves, body, 0, unroll=halves <= 4)
-        else:
-            send(stay_ref, mine)
+
+        def body(half, _):
+            for i, tile in enumerate(sums(insert(half, at, mine))):
+                stay_ref[half * full + i] = tile
+            return 0
+
+        lax.fori_loop(0, halves, body, 0, unroll=halves <= 4)
 
     return kernel
 
@@ -213,21 +236,24 @@
         out_ref[i] = kept_ref[i] + get_tile(in_ref, i, head)
 
 
-def last_kernel(first, size, n_messages, n_before):
-    def kernel(own_ref, *refs):
-        in_refs, before_refs, out_ref = refs[:n_messages], refs[n_messages:-1], refs[-1]
-        at = 0
-        for ref in before_refs:
-            out_ref[pl.ds(at, ref.shape[0])] = ref[...]
-            at += ref.shape[0]
-        heads = [get_head(ref, size) for ref in in_refs]
+def early_kernel(first):
+    def kernel(own_ref, far_ref, out_ref):
+        size = out_ref.shape[0]
+        head = get_head(far_ref, size)
         for i in range(size):
-            total = own_ref[first + i]
-            for ref, head in zip(in_refs, heads):
-                total += get_tile(ref, i, head)
-            out_ref[at + i] = total.astype(out_ref.dtype)
+            out_ref[i] = own_ref[first + i] + get_tile(far_ref, i, head)
 
     return kernel
+
+
+def last_kernel(near_ref, *refs):
+    early_refs, out_ref = refs[:-1], refs[-1]
+    count = out_ref.shape[0]
+    head, at = get_head(near_ref, count), 0
+    for ref in early_refs:
+        for i in range(ref.shape[0]):
+            out_ref[at] = (ref[i] + get_tile(near_ref, at, head)).astype(out_ref.dtype)
+            at += 1
 
 
 def call(kernel, out_shape, smem, vmem, after=(), scratch=(), flops=0):
@@ -304,11 +330,11 @@
         kernel = keep_kernel(fan, slots, count, chunks, bits)
         return call(kernel, shapes, (lists,), vmem, after, (), cost * 2 * flops)
 
-    def add(parts, sizes, rest, bit, keeps, after):
+    def add(parts, sizes, rest, bit, after):
         n = sum(sizes) << (len(rest) - 1)
-        shapes = [message(n, width), floats(n) if keeps else message(n, width)]
+        shapes = [message(n, width), floats(n)]
         kept, came = zip(*parts)
-        return call(add_kernel(sizes, rest, bit, keeps), shapes, (), (*kept, *came), after)
+        return call(add_kernel(sizes, rest, bit), shapes, (), (*kept, *came), after)
 
     own_bits, other_bits = (0, 1), (1, 0)
     sizes = [size for _, size in chunks]
@@ -318,7 +344,7 @@
         return [b for b in rest if b != bit]
 
     def second(kept, came, size, bit, after):
-        sent, kept = add([(kept, came)], [size], less(every, bit), 1 - bit, True, after)
+        sent, kept = add([(kept, came)], [size], less(every, bit), 1 - bit, after)
         return sent, (kept, exchange(sent, 1 - bit))
 
     p_x = lax.ppermute(p, "col", swap)
@@ -347,7 +373,7 @@
     other_came = came_0 + came_1
     rest, part_sizes, after = every[2:], sizes, (made,)
     for b in every[2:]:
-        sent, kept = add(parts, part_sizes, rest, b, True, after)
+        sent, kept = add(parts, part_sizes, rest, b, after)
         after = (sent,)
         parts, part_sizes = [(kept, exchange(sent, b))], [count]
         rest = less(rest, b)
@@ -362,24 +388,26 @@
     rest = every[2:]
     for b in every[2:-1]:
         for n in range(2):
-            sent, kept = add([streams[n]], [sizes[n]], rest, b, True, after)
+            sent, kept = add([streams[n]], [sizes[n]], rest, b, after)
             after = (sent,)
             streams[n] = (kept, exchange(sent, b))
         rest = less(rest, b)
 
     own = call(sum_kernel, floats(count), (), own, after)
-    moved, after = [], (own,)
+    moved, top, after = [], rest[0], (own,)
     for n in range(2):
-        sent, stay = add([streams[n]], [sizes[n]], rest, rest[0], False, after)
-        after = (sent,)
-        moved.append((cross(sent, rest[0]), cross(stay, None)))
-    result = ()
+        shapes = [message(sizes[n], width)] + [message(count, width)] * n
+        used, used_sizes = ([streams[0]], sizes[:1]) if n == 0 else (streams, sizes)
+        kept, came = zip(*used)
+        sent = call(cross_kernel(used_sizes, top, n), shapes, (), (*kept, *came), after)
+        after = (sent[0],)
+        moved.append(cross(sent[0], top))
+    near = cross(sent[1], None)
+    early = []
     for n, (first, size) in enumerate(chunks):
-        final = n == len(chunks) - 1
-        shape = jax.ShapeDtypeStruct((count if final else size, width, width), jnp.bfloat16)
-        kernel = last_kernel(first, size, len(moved[n]), len(result))
-        result = (call(kernel, shape, (), (own, *moved[n], *result)),)
-    return result[0][None, None]
+        early.append(call(early_kernel(first), floats(size), (), (own, moved[n]), early[-1:], (), 10**9))
+    result = jax.ShapeDtypeStruct((count, width, width), jnp.bfloat16)
+    return call(last_kernel, result, (), (near, *early))[None, None]
 
 
 def solution(mesh):

time: 49 us -> 49.1 us (level)
    ppermute x4 -> x3, waiting for transfers between devices: 4.4 us -> 4.75 us  [cross(): return lax.ppermute(x, ('col', 'layer'), perm)]
    ppermute x4 -> x3, starting transfers between devices: 5.98 us -> 5.79 us  [cross(): return lax.ppermute(x, ('col', 'layer'), perm)]
    pallas_call x19 -> x20, Pallas kernels: 15.2 us -> 15.2 us  [call(): pl.pallas_call(wrapped, out_shape=out_shape, in_specs=[pl.BlockSpec(memor...]
  transfers between devices with their start and end apart: 18 -> 17, of which waited for: 8 -> 8; matrix products, arithmetic and copies ran while one was open for 0% -> 0% of each run, Pallas kernels for 30% -> 30%
where the time goes in v10:
time: 49.1 us; the launch traced here: 49 us
  starting transfers between devices  22.8 us (46%)
  Pallas kernels  15.2 us (31%)
  waiting for transfers between devices  10.1 us (21%)
  local copies, waits for them, and re-layouts  0.72 us (1%)
    pallas_call x20, Pallas kernels, call(): pl.pallas_call(wrapped, out_shape=out_shape, in_specs=[pl.BlockSpec(memor...  15.2 us
    ppermute x9, starting transfers between devices, exchange(): return lax.ppermute(x, 'layer', [(i, i ^ 1 << bit) for i in range(layers)])  12.2 us
    ppermute x3, starting transfers between devices, cross(): return lax.ppermute(x, ('col', 'layer'), perm)  5.79 us
    ppermute x3, waiting for transfers between devices, cross(): return lax.ppermute(x, ('col', 'layer'), perm)  4.75 us
    ppermute x9, waiting for transfers between devices, exchange(): return lax.ppermute(x, 'layer', [(i, i ^ 1 << bit) for i in range(layers)])  2.91 us
    ppermute x1, starting transfers between devices, on_device(): p_x = lax.ppermute(p, 'col', swap)  2.56 us
    ppermute x1, waiting for transfers between devices, on_device(): lists_x = lax.ppermute(hold(lists_far, own_kept[:1]), 'col', swap)  1.35 us
    ppermute x1, starting transfers between devices, on_device(): lists_x = lax.ppermute(hold(lists_far, own_kept[:1]), 'col', swap)  1.23 us
  transfers between devices with their start and end apart: 17, of which 8 were waited for; matrix products, arithmetic and copies ran while one was open for 0% of the time, Pallas kernels for 30%

profile of v10, /device:TPU:0, one launch (start us, length us, event | category | flops | bytes accessed | tf_op | source)
XLA Modules:
  0.0 49.0 jit_solution(3519159858555181724)
XLA Ops:
  0.5 2.6 %collective-permute-start.2 = (bf16[16,128,128]{2,1,0:T(8,128)(2,1)}, bf16[16,128,128]{2,1,0:T(8,128)(2,1)S(1)}, u32[]{:S(2)}, u32[]{:S(2)}) collective-permute-start(bf16[16,128,128]{2,1,0:T(8,128)(2,1)} %bitcast.16), channel_id=1, source_target_pairs={{0,8},{8,0},{1,9},{9,1},{2,10},{10,2},{3,11},{11,3},{4,12},{12,4},... | collective-permute-start | bytes 1572872 | tf_op jit(solution)/shard_map/ppermute | solution.py:350
  3.0 0.7 %copy-done.2 = s32[1,1,1,2,32,16]{4,5,3,2,1,0:T(8,128)S(1)} copy-done((s32[1,1,1,2,32,16]{4,5,3,2,1,0:T(8,128)S(1)}, s32[1,1,1,2,32,16]{4,5,3,2,1,0:T(8,128)}, u32[]{:S(2)}) %copy-start.2) | copy-done | bytes 4120
  3.9 3.3 %shard_map.49 = (s16[1040,128]{1,0:T(8,128)(2,1)S(1)}, s16[1040,128]{1,0:T(8,128)(2,1)S(1)}, bf16[32,128,128]{2,1,0:T(8,128)(2,1)S(1)}) custom-call(s32[8,128]{1,0:T(8,128)S(1)} %get-tuple-element.31.refs_0_, bf16[64,128,128]{2,1,0:T(8,128)(2,1)S(1)} %bitcast.10, bf16[16,128,128]{2,1,0:T(8,128)(2,1)S(1)} %bitcast.18, ...), custom_call_target="tpu_custom_call" | custom-call | flops 5368709120 | bytes 4730880 | tf_op jit(solution)/shard_map/pallas_call | solution.py:267
  7.2 1.6 %collective-permute-start.6 = (s16[1040,128]{1,0:T(8,128)(2,1)S(1)}, s16[1040,128]{1,0:T(8,128)(2,1)S(1)}, u32[]{:S(2)}, u32[]{:S(2)}) collective-permute-start(s16[1040,128]{1,0:T(8,128)(2,1)S(1)} %get-tuple-element.33.refs_3_), channel_id=1, source_target_pairs={{0,1},{1,0},{2,3},{3,2},{4,5},{5,4},{6,7},{7,6},{8,9},{9,8},{10,11... | collective-permute-start | bytes 798728 | tf_op jit(solution)/shard_map/ppermute | solution.py:312
  8.8 1.6 %collective-permute-start.5 = (s16[1040,128]{1,0:T(8,128)(2,1)S(1)}, s16[1040,128]{1,0:T(8,128)(2,1)S(1)}, u32[]{:S(2)}, u32[]{:S(2)}) collective-permute-start(s16[1040,128]{1,0:T(8,128)(2,1)S(1)} %get-tuple-element.38), channel_id=1, source_target_pairs={{0,2},{1,3},{2,0},{3,1},{4,6},{5,7},{6,4},{7,5},{8,10},{9,11},{10,... | collective-permute-start | bytes 798728 | tf_op jit(solution)/shard_map/ppermute | solution.py:312
  10.4 3.0 %shard_map.50 = (f32[8,128,128]{2,1,0:T(8,128)S(1)}, f32[8,128,128]{2,1,0:T(8,128)S(1)}) custom-call(s32[8,128]{1,0:T(8,128)S(1)} %get-tuple-element.31.refs_0_, bf16[64,128,128]{2,1,0:T(8,128)(2,1)S(1)} %bitcast.11, bf16[32,128,128]{2,1,0:T(8,128)(2,1)S(1)} %get-tuple-element.32.refs_2_, s16[1040,128]{1,0:T(8,128)(2,1)S(1)} %get-tuple-element.33.refs_3_), custom_call_target="tpu_custom_call" | custom-call | flops 5368709120 | bytes 4198400 | tf_op jit(solution)/shard_map/pallas_call | solution.py:267
  13.4 1.2 %collective-permute-start.1 = (s32[8,128]{1,0:T(8,128)S(1)}, s32[8,128]{1,0:T(8,128)S(1)}, u32[]{:S(2)}, u32[]{:S(2)}) collective-permute-start(s32[8,128]{1,0:T(8,128)S(1)} %shard_map.51), channel_id=1, source_target_pairs={{0,8},{8,0},{1,9},{9,1},{2,10},{10,2},{3,11},{11,3},{4,12},{12,4},... | collective-permute-start | bytes 12296 | tf_op jit(solution)/shard_map/ppermute | solution.py:361
  14.7 1.1 %collective-permute-done.2.refs_0_.refs_2_ = bf16[16,128,128]{2,1,0:T(8,128)(2,1)S(1)} collective-permute-done((bf16[16,128,128]{2,1,0:T(8,128)(2,1)}, bf16[16,128,128]{2,1,0:T(8,128)(2,1)S(1)}, u32[]{:S(2)}, u32[]{:S(2)}) %collective-permute-start.2) | collective-permute-done | bytes 524320 | tf_op jit(solution)/shard_map/ppermute | solution.py:350
  15.8 1.3 %collective-permute-done.1.refs_2_.refs_0_ = s32[8,128]{1,0:T(8,128)S(1)} collective-permute-done((s32[8,128]{1,0:T(8,128)S(1)}, s32[8,128]{1,0:T(8,128)S(1)}, u32[]{:S(2)}, u32[]{:S(2)}) %collective-permute-start.1) | collective-permute-done | bytes 4128 | tf_op jit(solution)/shard_map/ppermute | solution.py:361
  18.1 0.6 %collective-permute-start.8 = (s16[528,128]{1,0:T(8,128)(2,1)S(1)}, s16[528,128]{1,0:T(8,128)(2,1)S(1)}, u32[]{:S(2)}, u32[]{:S(2)}) collective-permute-start(s16[528,128]{1,0:T(8,128)(2,1)S(1)} %get-tuple-element.40.refs_5_), channel_id=1, source_target_pairs={{0,1},{1,0},{2,3},{3,2},{4,5},{5,4},{6,7},{7,6},{8,9},{9,8},{10,11... | collective-permute-start | bytes 405512 | tf_op jit(solution)/shard_map/ppermute | solution.py:312
  18.6 1.6 %collective-permute-start.7 = (s16[528,128]{1,0:T(8,128)(2,1)S(1)}, s16[528,128]{1,0:T(8,128)(2,1)S(1)}, u32[]{:S(2)}, u32[]{:S(2)}) collective-permute-start(s16[528,128]{1,0:T(8,128)(2,1)S(1)} %get-tuple-element.39.refs_2_), channel_id=1, source_target_pairs={{0,2},{1,3},{2,0},{3,1},{4,6},{5,7},{6,4},{7,5},{8,10},{9,11},{10,... | collective-permute-start | bytes 405512 | tf_op jit(solution)/shard_map/ppermute | solution.py:312
  20.2 2.0 %shard_map.55 = (s16[1040,128]{1,0:T(8,128)(2,1)S(1)}, bf16[32,128,128]{2,1,0:T(8,128)(2,1)S(1)}) custom-call(s32[8,128]{1,0:T(8,128)S(1)} %collective-permute-done.1.refs_2_.refs_0_, bf16[64,128,128]{2,1,0:T(8,128)(2,1)S(1)} %bitcast.12, bf16[16,128,128]{2,1,0:T(8,128)(2,1)S(1)} %collective-permute-done.2.refs_0_.refs_2_, ...), custom_call_target="tpu_custom_call" | custom-call | bytes 1 | tf_op jit(solution)/shard_map/pallas_call | solution.py:267
  22.8 1.9 %shard_map.56.refs_4_ = s16[1040,128]{1,0:T(8,128)(2,1)S(1)} custom-call(s32[8,128]{1,0:T(8,128)S(1)} %collective-permute-done.1.refs_2_.refs_0_, bf16[64,128,128]{2,1,0:T(8,128)(2,1)S(1)} %bitcast.13, bf16[32,128,128]{2,1,0:T(8,128)(2,1)S(1)} %get-tuple-element.41.refs_2_, s16[1040,128]{1,0:T(8,128)(2,1)S(1)} %get-tuple-element.44.refs_3_), custom_call_target="tpu_custom_call" | custom-call | bytes 1 | tf_op jit(solution)/shard_map/pallas_call | solution.py:267
  24.7 1.6 %collective-permute-start.10 = (s16[1040,128]{1,0:T(8,128)(2,1)S(1)}, s16[1040,128]{1,0:T(8,128)(2,1)S(1)}, u32[]{:S(2)}, u32[]{:S(2)}) collective-permute-start(s16[1040,128]{1,0:T(8,128)(2,1)S(1)} %shard_map.56.refs_4_), channel_id=1, source_target_pairs={{0,1},{1,0},{2,3},{3,2},{4,5},{5,4},{6,7},{7,6},{8,9},{9,8},{10,11... | collective-permute-start | bytes 798728 | tf_op jit(solution)/shard_map/ppermute | solution.py:312
  26.5 2.6 %collective-permute-start.13 = (s16[528,128]{1,0:T(8,128)(2,1)S(1)}, s16[528,128]{1,0:T(8,128)(2,1)S(1)}, u32[]{:S(2)}, u32[]{:S(2)}) collective-permute-start(s16[528,128]{1,0:T(8,128)(2,1)S(1)} %get-tuple-element.45.refs_3_), channel_id=1, source_target_pairs={{0,4},{1,5},{2,6},{3,7},{4,0},{5,1},{6,2},{7,3},{8,12},{9,13},{10,... | collective-permute-start | bytes 405512 | tf_op jit(solution)/shard_map/ppermute | solution.py:312
  29.1 3.0 %shard_map.58 = (f32[8,128,128]{2,1,0:T(8,128)S(1)}, f32[8,128,128]{2,1,0:T(8,128)S(1)}) custom-call(s32[8,128]{1,0:T(8,128)S(1)} %collective-permute-done.1.refs_2_.refs_0_, bf16[64,128,128]{2,1,0:T(8,128)(2,1)S(1)} %bitcast.14, bf16[32,128,128]{2,1,0:T(8,128)(2,1)S(1)} %get-tuple-element.41.refs_2_, s16[528,128]{1,0:T(8,128)(2,1)S(1)} %get-tuple-element.45.refs_3_), custom_call_target="tpu_custom_call" | custom-call | flops 5368709120 | bytes 4198400 | tf_op jit(solution)/shard_map/pallas_call | solution.py:267
  32.3 1.9 %collective-permute-start.11 = (s16[528,128]{1,0:T(8,128)(2,1)S(1)}, s16[528,128]{1,0:T(8,128)(2,1)S(1)}, u32[]{:S(2)}, u32[]{:S(2)}) collective-permute-start(s16[528,128]{1,0:T(8,128)(2,1)S(1)} %get-tuple-element.49.refs_2_), channel_id=1, source_target_pairs={{0,1},{1,0},{2,3},{3,2},{4,5},{5,4},{6,7},{7,6},{8,9},{9,8},{10,11... | collective-permute-start | bytes 405512 | tf_op jit(solution)/shard_map/ppermute | solution.py:312
  35.2 2.2 %collective-permute-done.11.refs_1_.refs_2_ = s16[528,128]{1,0:T(8,128)(2,1)S(1)} collective-permute-done((s16[528,128]{1,0:T(8,128)(2,1)S(1)}, s16[528,128]{1,0:T(8,128)(2,1)S(1)}, u32[]{:S(2)}, u32[]{:S(2)}) %collective-permute-start.11) | collective-permute-done | bytes 135200 | tf_op jit(solution)/shard_map/ppermute | solution.py:312
  37.5 3.0 %collective-permute-start.15 = (s16[272,128]{1,0:T(8,128)(2,1)S(1)}, s16[272,128]{1,0:T(8,128)(2,1)S(1)}, u32[]{:S(2)}, u32[]{:S(2)}) collective-permute-start(s16[272,128]{1,0:T(8,128)(2,1)S(1)} %shard_map.62.refs_4_), channel_id=1, source_target_pairs={{0,12},{1,13},{2,14},{3,15},{4,8},{5,9},{6,10},{7,11},{8,4},{9,5},... | collective-permute-start | bytes 208904 | tf_op jit(solution)/shard_map/ppermute | solution.py:317
  40.7 1.9 %collective-permute-start.16 = (s16[272,128]{1,0:T(8,128)(2,1)S(1)}, s16[272,128]{1,0:T(8,128)(2,1)S(1)}, u32[]{:S(2)}, u32[]{:S(2)}) collective-permute-start(s16[272,128]{1,0:T(8,128)(2,1)S(1)} %get-tuple-element.54), channel_id=1, source_target_pairs={{0,12},{1,13},{2,14},{3,15},{4,8},{5,9},{6,10},{7,11},{8,4},{9,5},... | collective-permute-start | bytes 208904 | tf_op jit(solution)/shard_map/ppermute | solution.py:317
  42.5 0.9 %collective-permute-start.14 = (s16[528,128]{1,0:T(8,128)(2,1)S(1)}, s16[528,128]{1,0:T(8,128)(2,1)S(1)}, u32[]{:S(2)}, u32[]{:S(2)}) collective-permute-start(s16[528,128]{1,0:T(8,128)(2,1)S(1)} %get-tuple-element.53), channel_id=1, source_target_pairs={{0,8},{1,9},{2,10},{3,11},{4,12},{5,13},{6,14},{7,15},{8,0},{9,1},... | collective-permute-start | bytes 405512 | tf_op jit(solution)/shard_map/ppermute | solution.py:317
  43.5 1.7 %collective-permute-done.15.refs_1_ = s16[272,128]{1,0:T(8,128)(2,1)S(1)} collective-permute-done((s16[272,128]{1,0:T(8,128)(2,1)S(1)}, s16[272,128]{1,0:T(8,128)(2,1)S(1)}, u32[]{:S(2)}, u32[]{:S(2)}) %collective-permute-start.15) | collective-permute-done | bytes 69664 | tf_op jit(solution)/shard_map/ppermute | solution.py:317
  45.2 2.5 %collective-permute-done.16.refs_1_ = s16[272,128]{1,0:T(8,128)(2,1)S(1)} collective-permute-done((s16[272,128]{1,0:T(8,128)(2,1)S(1)}, s16[272,128]{1,0:T(8,128)(2,1)S(1)}, u32[]{:S(2)}, u32[]{:S(2)}) %collective-permute-start.16) | collective-permute-done | bytes 69664 | tf_op jit(solution)/shard_map/ppermute | solution.py:317
  48.3 0.7 %shard_map.66 = bf16[4,128,128]{2,1,0:T(8,128)(2,1)} custom-call(s16[528,128]{1,0:T(8,128)(2,1)S(1)} %collective-permute-done.14.refs_0_, f32[2,128,128]{2,1,0:T(8,128)S(1)} %shard_map.64.refs_2_.refs_1_, f32[2,128,128]{2,1,0:T(8,128)S(1)} %shard_map.65.refs_2_), custom_call_target="tpu_custom_call" | custom-call | bytes 1 | tf_op jit(solution)/shard_map/pallas_call | solution.py:267
  (39 shorter events, 4.3 us)
Async XLA Ops:
  0.0 3.0 %copy-start = (bf16[1,1,1,64,128,128]{5,4,3,2,1,0:T(8,128)(2,1)S(1)}, bf16[1,1,1,64,128,128]{5,4,3,2,1,0:T(8,128)(2,1)}, u32[]{:S(2)}) copy-start(bf16[1,1,1,64,128,128]{5,4,3,2,1,0:T(8,128)(2,1)} %param.4) | copy-start | bytes 6291460
  0.0 3.0 %copy-start.1 = (bf16[1,1,1,16,128,128]{5,4,3,2,1,0:T(8,128)(2,1)S(1)}, bf16[1,1,1,16,128,128]{5,4,3,2,1,0:T(8,128)(2,1)}, u32[]{:S(2)}) copy-start(bf16[1,1,1,16,128,128]{5,4,3,2,1,0:T(8,128)(2,1)} %param.5) | copy-start | bytes 1572868
  0.0 3.8 %collective-permute-start = (bf16[16,128,128]{2,1,0:T(8,128)(2,1)}, bf16[16,128,128]{2,1,0:T(8,128)(2,1)S(1)}, u32[]{:S(2)}, u32[]{:S(2)}) collective-permute-start(bf16[16,128,128]{2,1,0:T(8,128)(2,1)} %bitcast.15), channel_id=1, source_target_pairs={{0,16},{16,0},{1,17},{17,1},{2,18},{18,2},{3,19},{19,3},{4,20},{20... | collective-permute-start | bytes 1572872 | tf_op jit(solution)/shard_map/ppermute | solution.py:351
  0.5 15.3 %collective-permute-start.2 = (bf16[16,128,128]{2,1,0:T(8,128)(2,1)}, bf16[16,128,128]{2,1,0:T(8,128)(2,1)S(1)}, u32[]{:S(2)}, u32[]{:S(2)}) collective-permute-start(bf16[16,128,128]{2,1,0:T(8,128)(2,1)} %bitcast.16), channel_id=1, source_target_pairs={{0,8},{8,0},{1,9},{9,1},{2,10},{10,2},{3,11},{11,3},{4,12},{12,4},... | collective-permute-start | bytes 1572872 | tf_op jit(solution)/shard_map/ppermute | solution.py:350
  3.0 0.7 %copy-start.2 = (s32[1,1,1,2,32,16]{4,5,3,2,1,0:T(8,128)S(1)}, s32[1,1,1,2,32,16]{4,5,3,2,1,0:T(8,128)}, u32[]{:S(2)}) copy-start(s32[1,1,1,2,32,16]{4,5,3,2,1,0:T(8,128)} %param.6) | copy-start | bytes 12292
  3.0 0.7 %copy-start.3 = (s32[1,1,1,2,32,16]{4,5,3,2,1,0:T(8,128)S(1)}, s32[1,1,1,2,32,16]{4,5,3,2,1,0:T(8,128)}, u32[]{:S(2)}) copy-start(s32[1,1,1,2,32,16]{4,5,3,2,1,0:T(8,128)} %param.7) | copy-start | bytes 12292
  7.2 10.5 %collective-permute-start.6 = (s16[1040,128]{1,0:T(8,128)(2,1)S(1)}, s16[1040,128]{1,0:T(8,128)(2,1)S(1)}, u32[]{:S(2)}, u32[]{:S(2)}) collective-permute-start(s16[1040,128]{1,0:T(8,128)(2,1)S(1)} %get-tuple-element.33.refs_3_), channel_id=1, source_target_pairs={{0,1},{1,0},{2,3},{3,2},{4,5},{5,4},{6,7},{7,6},{8,9},{9,8},{10,11... | collective-permute-start | bytes 798728 | tf_op jit(solution)/shard_map/ppermute | solution.py:312
  8.8 9.1 %collective-permute-start.5 = (s16[1040,128]{1,0:T(8,128)(2,1)S(1)}, s16[1040,128]{1,0:T(8,128)(2,1)S(1)}, u32[]{:S(2)}, u32[]{:S(2)}) collective-permute-start(s16[1040,128]{1,0:T(8,128)(2,1)S(1)} %get-tuple-element.38), channel_id=1, source_target_pairs={{0,2},{1,3},{2,0},{3,1},{4,6},{5,7},{6,4},{7,5},{8,10},{9,11},{10,... | collective-permute-start | bytes 798728 | tf_op jit(solution)/shard_map/ppermute | solution.py:312
  13.4 3.7 %collective-permute-start.1 = (s32[8,128]{1,0:T(8,128)S(1)}, s32[8,128]{1,0:T(8,128)S(1)}, u32[]{:S(2)}, u32[]{:S(2)}) collective-permute-start(s32[8,128]{1,0:T(8,128)S(1)} %shard_map.51), channel_id=1, source_target_pairs={{0,8},{8,0},{1,9},{9,1},{2,10},{10,2},{3,11},{11,3},{4,12},{12,4},... | collective-permute-start | bytes 12296 | tf_op jit(solution)/shard_map/ppermute | solution.py:361
  17.2 3.1 %collective-permute-start.3 = (bf16[8,128,128]{2,1,0:T(8,128)(2,1)S(1)}, bf16[8,128,128]{2,1,0:T(8,128)(2,1)S(1)}, u32[]{:S(2)}, u32[]{:S(2)}) collective-permute-start(bf16[8,128,128]{2,1,0:T(8,128)(2,1)S(1)} %get-tuple-element.35), channel_id=1, source_target_pairs={{0,16},{16,0},{1,17},{17,1},{2,18},{18,2},{3,19},{19,3},{4,20},{20... | collective-permute-start | bytes 786440 | tf_op jit(solution)/shard_map/ppermute | solution.py:364
  17.2 3.0 %collective-permute-start.4 = (bf16[8,128,128]{2,1,0:T(8,128)(2,1)S(1)}, bf16[8,128,128]{2,1,0:T(8,128)(2,1)S(1)}, u32[]{:S(2)}, u32[]{:S(2)}) collective-permute-start(bf16[8,128,128]{2,1,0:T(8,128)(2,1)S(1)} %get-tuple-element.36), channel_id=1, source_target_pairs={{0,16},{16,0},{1,17},{17,1},{2,18},{18,2},{3,19},{19,3},{4,20},{20... | collective-permute-start | bytes 786440 | tf_op jit(solution)/shard_map/ppermute | solution.py:364
  18.1 8.2 %collective-permute-start.8 = (s16[528,128]{1,0:T(8,128)(2,1)S(1)}, s16[528,128]{1,0:T(8,128)(2,1)S(1)}, u32[]{:S(2)}, u32[]{:S(2)}) collective-permute-start(s16[528,128]{1,0:T(8,128)(2,1)S(1)} %get-tuple-element.40.refs_5_), channel_id=1, source_target_pairs={{0,1},{1,0},{2,3},{3,2},{4,5},{5,4},{6,7},{7,6},{8,9},{9,8},{10,11... | collective-permute-start | bytes 405512 | tf_op jit(solution)/shard_map/ppermute | solution.py:312
  18.6 7.6 %collective-permute-start.7 = (s16[528,128]{1,0:T(8,128)(2,1)S(1)}, s16[528,128]{1,0:T(8,128)(2,1)S(1)}, u32[]{:S(2)}, u32[]{:S(2)}) collective-permute-start(s16[528,128]{1,0:T(8,128)(2,1)S(1)} %get-tuple-element.39.refs_2_), channel_id=1, source_target_pairs={{0,2},{1,3},{2,0},{3,1},{4,6},{5,7},{6,4},{7,5},{8,10},{9,11},{10,... | collective-permute-start | bytes 405512 | tf_op jit(solution)/shard_map/ppermute | solution.py:312
  22.3 9.9 %collective-permute-start.9 = (s16[1040,128]{1,0:T(8,128)(2,1)S(1)}, s16[1040,128]{1,0:T(8,128)(2,1)S(1)}, u32[]{:S(2)}, u32[]{:S(2)}) collective-permute-start(s16[1040,128]{1,0:T(8,128)(2,1)S(1)} %get-tuple-element.44.refs_3_), channel_id=1, source_target_pairs={{0,2},{1,3},{2,0},{3,1},{4,6},{5,7},{6,4},{7,5},{8,10},{9,11},{10,... | collective-permute-start | bytes 798728 | tf_op jit(solution)/shard_map/ppermute | solution.py:312
  24.7 9.6 %collective-permute-start.10 = (s16[1040,128]{1,0:T(8,128)(2,1)S(1)}, s16[1040,128]{1,0:T(8,128)(2,1)S(1)}, u32[]{:S(2)}, u32[]{:S(2)}) collective-permute-start(s16[1040,128]{1,0:T(8,128)(2,1)S(1)} %shard_map.56.refs_4_), channel_id=1, source_target_pairs={{0,1},{1,0},{2,3},{3,2},{4,5},{5,4},{6,7},{7,6},{8,9},{9,8},{10,11... | collective-permute-start | bytes 798728 | tf_op jit(solution)/shard_map/ppermute | solution.py:312
  26.5 8.7 %collective-permute-start.13 = (s16[528,128]{1,0:T(8,128)(2,1)S(1)}, s16[528,128]{1,0:T(8,128)(2,1)S(1)}, u32[]{:S(2)}, u32[]{:S(2)}) collective-permute-start(s16[528,128]{1,0:T(8,128)(2,1)S(1)} %get-tuple-element.45.refs_3_), channel_id=1, source_target_pairs={{0,4},{1,5},{2,6},{3,7},{4,0},{5,1},{6,2},{7,3},{8,12},{9,13},{10,... | collective-permute-start | bytes 405512 | tf_op jit(solution)/shard_map/ppermute | solution.py:312
  32.3 5.1 %collective-permute-start.11 = (s16[528,128]{1,0:T(8,128)(2,1)S(1)}, s16[528,128]{1,0:T(8,128)(2,1)S(1)}, u32[]{:S(2)}, u32[]{:S(2)}) collective-permute-start(s16[528,128]{1,0:T(8,128)(2,1)S(1)} %get-tuple-element.49.refs_2_), channel_id=1, source_target_pairs={{0,1},{1,0},{2,3},{3,2},{4,5},{5,4},{6,7},{7,6},{8,9},{9,8},{10,11... | collective-permute-start | bytes 405512 | tf_op jit(solution)/shard_map/ppermute | solution.py:312
  34.5 6.0 %collective-permute-start.12 = (s16[528,128]{1,0:T(8,128)(2,1)S(1)}, s16[528,128]{1,0:T(8,128)(2,1)S(1)}, u32[]{:S(2)}, u32[]{:S(2)}) collective-permute-start(s16[528,128]{1,0:T(8,128)(2,1)S(1)} %get-tuple-element.51.refs_2_), channel_id=1, source_target_pairs={{0,2},{1,3},{2,0},{3,1},{4,6},{5,7},{6,4},{7,5},{8,10},{9,11},{10,... | collective-permute-start | bytes 405512 | tf_op jit(solution)/shard_map/ppermute | solution.py:312
  37.5 7.6 %collective-permute-start.15 = (s16[272,128]{1,0:T(8,128)(2,1)S(1)}, s16[272,128]{1,0:T(8,128)(2,1)S(1)}, u32[]{:S(2)}, u32[]{:S(2)}) collective-permute-start(s16[272,128]{1,0:T(8,128)(2,1)S(1)} %shard_map.62.refs_4_), channel_id=1, source_target_pairs={{0,12},{1,13},{2,14},{3,15},{4,8},{5,9},{6,10},{7,11},{8,4},{9,5},... | collective-permute-start | bytes 208904 | tf_op jit(solution)/shard_map/ppermute | solution.py:317
  40.7 7.0 %collective-permute-start.16 = (s16[272,128]{1,0:T(8,128)(2,1)S(1)}, s16[272,128]{1,0:T(8,128)(2,1)S(1)}, u32[]{:S(2)}, u32[]{:S(2)}) collective-permute-start(s16[272,128]{1,0:T(8,128)(2,1)S(1)} %get-tuple-element.54), channel_id=1, source_target_pairs={{0,12},{1,13},{2,14},{3,15},{4,8},{5,9},{6,10},{7,11},{8,4},{9,5},... | collective-permute-start | bytes 208904 | tf_op jit(solution)/shard_map/ppermute | solution.py:317
  42.5 5.8 %collective-permute-start.14 = (s16[528,128]{1,0:T(8,128)(2,1)S(1)}, s16[528,128]{1,0:T(8,128)(2,1)S(1)}, u32[]{:S(2)}, u32[]{:S(2)}) collective-permute-start(s16[528,128]{1,0:T(8,128)(2,1)S(1)} %get-tuple-element.53), channel_id=1, source_target_pairs={{0,8},{1,9},{2,10},{3,11},{4,12},{5,13},{6,14},{7,15},{8,0},{9,1},... | collective-permute-start | bytes 405512 | tf_op jit(solution)/shard_map/ppermute | solution.py:317

commit v11 on v10

--- a/solution.py
+++ b/solution.py
@@ -368,10 +368,8 @@
         parts.append(part)
         after = (sent,)
 
-    (made, joined), came_0 = send(lists_x, (a, p_x, *p_xr), (0,), other_bits[:1], True, after, 0)
-    (made,), came_1 = send(lists_x, (a, joined), (1,), other_bits[1:], False, (made,), 0)
-    other_came = came_0 + came_1
-    rest, part_sizes, after = every[2:], sizes, (made,)
+    (*made, joined), other_came = send(lists_x, (a, p_x, *p_xr), (0, 1), other_bits, True, after, 0)
+    rest, part_sizes, after = every[2:], sizes, made[:1]
     for b in every[2:]:
         sent, kept = add(parts, part_sizes, rest, b, after)
         after = (sent,)

time: 49.1 us -> 50.4 us (1.026)
  waiting for transfers between devices: 10.1 us -> 13.7 us
  starting transfers between devices: 22.8 us -> 20.9 us
    ppermute x9, waiting for transfers between devices: 2.91 us -> 7.07 us  [exchange(): return lax.ppermute(x, 'layer', [(i, i ^ 1 << bit) for i in range(layers)])]
    ppermute x9, starting transfers between devices: 12.2 us -> 10.7 us  [exchange(): return lax.ppermute(x, 'layer', [(i, i ^ 1 << bit) for i in range(layers)])]
    ppermute x3, waiting for transfers between devices: 4.75 us -> 4.2 us  [cross(): return lax.ppermute(x, ('col', 'layer'), perm)]
    pallas_call x20 -> x19, Pallas kernels: 15.2 us -> 14.7 us  [call(): pl.pallas_call(wrapped, out_shape=out_shape, in_specs=[pl.BlockSpec(memor...]
  transfers between devices with their start and end apart: 17 -> 17, of which waited for: 8 -> 7; matrix products, arithmetic and copies ran while one was open for 0% -> 0% of each run, Pallas kernels for 30% -> 28%
where the time goes in v11:
time: 50.4 us; the launch traced here: 50.2 us
  starting transfers between devices  20.9 us (41%)
  Pallas kernels  14.7 us (29%)
  waiting for transfers between devices  13.7 us (27%)
  local copies, waits for them, and re-layouts  0.72 us (1%)
    pallas_call x19, Pallas kernels, call(): pl.pallas_call(wrapped, out_shape=out_shape, in_specs=[pl.BlockSpec(memor...  14.7 us
    ppermute x9, starting transfers between devices, exchange(): return lax.ppermute(x, 'layer', [(i, i ^ 1 << bit) for i in range(layers)])  10.7 us
    ppermute x9, waiting for transfers between devices, exchange(): return lax.ppermute(x, 'layer', [(i, i ^ 1 << bit) for i in range(layers)])  7.07 us
    ppermute x3, starting transfers between devices, cross(): return lax.ppermute(x, ('col', 'layer'), perm)  5.45 us
    ppermute x3, waiting for transfers between devices, cross(): return lax.ppermute(x, ('col', 'layer'), perm)  4.2 us
    ppermute x1, starting transfers between devices, on_device(): p_x = lax.ppermute(p, 'col', swap)  2.56 us
    ppermute x1, waiting for transfers between devices, on_device(): lists_x = lax.ppermute(hold(lists_far, own_kept[:1]), 'col', swap)  1.35 us
    ppermute x1, starting transfers between devices, on_device(): lists_x = lax.ppermute(hold(lists_far, own_kept[:1]), 'col', swap)  1.23 us
  transfers between devices with their start and end apart: 17, of which 7 were waited for; matrix products, arithmetic and copies ran while one was open for 0% of the time, Pallas kernels for 28%

profile of v11, /device:TPU:0, one launch (start us, length us, event | category | flops | bytes accessed | tf_op | source)
XLA Modules:
  0.0 50.2 jit_solution(6749103308937398846)
XLA Ops:
  0.5 2.6 %collective-permute-start.2 = (bf16[16,128,128]{2,1,0:T(8,128)(2,1)}, bf16[16,128,128]{2,1,0:T(8,128)(2,1)S(1)}, u32[]{:S(2)}, u32[]{:S(2)}) collective-permute-start(bf16[16,128,128]{2,1,0:T(8,128)(2,1)} %bitcast.15), channel_id=1, source_target_pairs={{0,8},{8,0},{1,9},{9,1},{2,10},{10,2},{3,11},{11,3},{4,12},{12,4},... | collective-permute-start | bytes 1572872 | tf_op jit(solution)/shard_map/ppermute | solution.py:350
  3.0 0.7 %copy-done.2 = s32[1,1,1,2,32,16]{4,5,3,2,1,0:T(8,128)S(1)} copy-done((s32[1,1,1,2,32,16]{4,5,3,2,1,0:T(8,128)S(1)}, s32[1,1,1,2,32,16]{4,5,3,2,1,0:T(8,128)}, u32[]{:S(2)}) %copy-start.2) | copy-done | bytes 4120
  3.9 3.3 %shard_map.49 = (s16[1040,128]{1,0:T(8,128)(2,1)S(1)}, s16[1040,128]{1,0:T(8,128)(2,1)S(1)}, bf16[32,128,128]{2,1,0:T(8,128)(2,1)S(1)}) custom-call(s32[8,128]{1,0:T(8,128)S(1)} %get-tuple-element.32.refs_0_, bf16[64,128,128]{2,1,0:T(8,128)(2,1)S(1)} %bitcast.10, bf16[16,128,128]{2,1,0:T(8,128)(2,1)S(1)} %bitcast.17, ...), custom_call_target="tpu_custom_call" | custom-call | flops 5368709120 | bytes 4730880 | tf_op jit(solution)/shard_map/pallas_call | solution.py:267
  7.2 1.6 %collective-permute-start.6 = (s16[1040,128]{1,0:T(8,128)(2,1)S(1)}, s16[1040,128]{1,0:T(8,128)(2,1)S(1)}, u32[]{:S(2)}, u32[]{:S(2)}) collective-permute-start(s16[1040,128]{1,0:T(8,128)(2,1)S(1)} %get-tuple-element.34.refs_3_), channel_id=1, source_target_pairs={{0,1},{1,0},{2,3},{3,2},{4,5},{5,4},{6,7},{7,6},{8,9},{9,8},{10,11... | collective-permute-start | bytes 798728 | tf_op jit(solution)/shard_map/ppermute | solution.py:312
  8.8 1.6 %collective-permute-start.5 = (s16[1040,128]{1,0:T(8,128)(2,1)S(1)}, s16[1040,128]{1,0:T(8,128)(2,1)S(1)}, u32[]{:S(2)}, u32[]{:S(2)}) collective-permute-start(s16[1040,128]{1,0:T(8,128)(2,1)S(1)} %get-tuple-element.39), channel_id=1, source_target_pairs={{0,2},{1,3},{2,0},{3,1},{4,6},{5,7},{6,4},{7,5},{8,10},{9,11},{10,... | collective-permute-start | bytes 798728 | tf_op jit(solution)/shard_map/ppermute | solution.py:312
  10.4 3.0 %shard_map.50 = (f32[8,128,128]{2,1,0:T(8,128)S(1)}, f32[8,128,128]{2,1,0:T(8,128)S(1)}) custom-call(s32[8,128]{1,0:T(8,128)S(1)} %get-tuple-element.32.refs_0_, bf16[64,128,128]{2,1,0:T(8,128)(2,1)S(1)} %bitcast.11, bf16[32,128,128]{2,1,0:T(8,128)(2,1)S(1)} %get-tuple-element.33.refs_2_, s16[1040,128]{1,0:T(8,128)(2,1)S(1)} %get-tuple-element.34.refs_3_), custom_call_target="tpu_custom_call" | custom-call | flops 5368709120 | bytes 4198400 | tf_op jit(solution)/shard_map/pallas_call | solution.py:267
  13.4 1.2 %collective-permute-start.1 = (s32[8,128]{1,0:T(8,128)S(1)}, s32[8,128]{1,0:T(8,128)S(1)}, u32[]{:S(2)}, u32[]{:S(2)}) collective-permute-start(s32[8,128]{1,0:T(8,128)S(1)} %shard_map.51), channel_id=1, source_target_pairs={{0,8},{8,0},{1,9},{9,1},{2,10},{10,2},{3,11},{11,3},{4,12},{12,4},... | collective-permute-start | bytes 12296 | tf_op jit(solution)/shard_map/ppermute | solution.py:361
  14.7 1.1 %collective-permute-done.2.refs_0_.refs_2_ = bf16[16,128,128]{2,1,0:T(8,128)(2,1)S(1)} collective-permute-done((bf16[16,128,128]{2,1,0:T(8,128)(2,1)}, bf16[16,128,128]{2,1,0:T(8,128)(2,1)S(1)}, u32[]{:S(2)}, u32[]{:S(2)}) %collective-permute-start.2) | collective-permute-done | bytes 524320 | tf_op jit(solution)/shard_map/ppermute | solution.py:350
  15.8 1.3 %collective-permute-done.1.refs_2_.refs_0_ = s32[8,128]{1,0:T(8,128)S(1)} collective-permute-done((s32[8,128]{1,0:T(8,128)S(1)}, s32[8,128]{1,0:T(8,128)S(1)}, u32[]{:S(2)}, u32[]{:S(2)}) %collective-permute-start.1) | collective-permute-done | bytes 4128 | tf_op jit(solution)/shard_map/ppermute | solution.py:361
  18.6 1.6 %collective-permute-start.7 = (s16[528,128]{1,0:T(8,128)(2,1)S(1)}, s16[528,128]{1,0:T(8,128)(2,1)S(1)}, u32[]{:S(2)}, u32[]{:S(2)}) collective-permute-start(s16[528,128]{1,0:T(8,128)(2,1)S(1)} %get-tuple-element.40.refs_2_), channel_id=1, source_target_pairs={{0,2},{1,3},{2,0},{3,1},{4,6},{5,7},{6,4},{7,5},{8,10},{9,11},{10,... | collective-permute-start | bytes 405512 | tf_op jit(solution)/shard_map/ppermute | solution.py:312
  20.2 3.3 %shard_map.55 = (s16[1040,128]{1,0:T(8,128)(2,1)S(1)}, s16[1040,128]{1,0:T(8,128)(2,1)S(1)}, bf16[32,128,128]{2,1,0:T(8,128)(2,1)S(1)}) custom-call(s32[8,128]{1,0:T(8,128)S(1)} %collective-permute-done.1.refs_2_.refs_0_, bf16[64,128,128]{2,1,0:T(8,128)(2,1)S(1)} %bitcast.12, bf16[16,128,128]{2,1,0:T(8,128)(2,1)S(1)} %collective-permute-done.2.refs_0_.refs_2_, ...), custom_call_target="tpu_custom_call" | custom-call | bytes 1 | tf_op jit(solution)/shard_map/pallas_call | solution.py:267
  24.1 1.5 %collective-permute-start.10 = (s16[1040,128]{1,0:T(8,128)(2,1)S(1)}, s16[1040,128]{1,0:T(8,128)(2,1)S(1)}, u32[]{:S(2)}, u32[]{:S(2)}) collective-permute-start(s16[1040,128]{1,0:T(8,128)(2,1)S(1)} %get-tuple-element.50), channel_id=1, source_target_pairs={{0,1},{1,0},{2,3},{3,2},{4,5},{5,4},{6,7},{7,6},{8,9},{9,8},{10,11... | collective-permute-start | bytes 798728 | tf_op jit(solution)/shard_map/ppermute | solution.py:312
  25.7 2.7 %collective-permute-start.13 = (s16[528,128]{1,0:T(8,128)(2,1)S(1)}, s16[528,128]{1,0:T(8,128)(2,1)S(1)}, u32[]{:S(2)}, u32[]{:S(2)}) collective-permute-start(s16[528,128]{1,0:T(8,128)(2,1)S(1)} %get-tuple-element.46.refs_3_), channel_id=1, source_target_pairs={{0,4},{1,5},{2,6},{3,7},{4,0},{5,1},{6,2},{7,3},{8,12},{9,13},{10,... | collective-permute-start | bytes 405512 | tf_op jit(solution)/shard_map/ppermute | solution.py:312
  28.4 3.0 %shard_map.57 = (f32[8,128,128]{2,1,0:T(8,128)S(1)}, f32[8,128,128]{2,1,0:T(8,128)S(1)}) custom-call(s32[8,128]{1,0:T(8,128)S(1)} %collective-permute-done.1.refs_2_.refs_0_, bf16[64,128,128]{2,1,0:T(8,128)(2,1)S(1)} %bitcast.13, bf16[32,128,128]{2,1,0:T(8,128)(2,1)S(1)} %get-tuple-element.42.refs_2_, s16[528,128]{1,0:T(8,128)(2,1)S(1)} %get-tuple-element.46.refs_3_), custom_call_target="tpu_custom_call" | custom-call | flops 5368709120 | bytes 4198400 | tf_op jit(solution)/shard_map/pallas_call | solution.py:267
  31.4 2.9 %collective-permute-done.9.refs_1_ = s16[1040,128]{1,0:T(8,128)(2,1)S(1)} collective-permute-done((s16[1040,128]{1,0:T(8,128)(2,1)S(1)}, s16[1040,128]{1,0:T(8,128)(2,1)S(1)}, u32[]{:S(2)}, u32[]{:S(2)}) %collective-permute-start.9) | collective-permute-done | bytes 266272 | tf_op jit(solution)/shard_map/ppermute | solution.py:312
  34.5 0.6 %collective-permute-start.11 = (s16[528,128]{1,0:T(8,128)(2,1)S(1)}, s16[528,128]{1,0:T(8,128)(2,1)S(1)}, u32[]{:S(2)}, u32[]{:S(2)}) collective-permute-start(s16[528,128]{1,0:T(8,128)(2,1)S(1)} %get-tuple-element.51.refs_2_), channel_id=1, source_target_pairs={{0,1},{1,0},{2,3},{3,2},{4,5},{5,4},{6,7},{7,6},{8,9},{9,8},{10,11... | collective-permute-start | bytes 405512 | tf_op jit(solution)/shard_map/ppermute | solution.py:312
  35.4 4.2 %collective-permute-done.11.refs_1_.refs_2_ = s16[528,128]{1,0:T(8,128)(2,1)S(1)} collective-permute-done((s16[528,128]{1,0:T(8,128)(2,1)S(1)}, s16[528,128]{1,0:T(8,128)(2,1)S(1)}, u32[]{:S(2)}, u32[]{:S(2)}) %collective-permute-start.11) | collective-permute-done | bytes 135200 | tf_op jit(solution)/shard_map/ppermute | solution.py:312
  39.6 2.1 %collective-permute-start.15 = (s16[272,128]{1,0:T(8,128)(2,1)S(1)}, s16[272,128]{1,0:T(8,128)(2,1)S(1)}, u32[]{:S(2)}, u32[]{:S(2)}) collective-permute-start(s16[272,128]{1,0:T(8,128)(2,1)S(1)} %shard_map.61.refs_4_), channel_id=1, source_target_pairs={{0,12},{1,13},{2,14},{3,15},{4,8},{5,9},{6,10},{7,11},{8,4},{9,5},... | collective-permute-start | bytes 208904 | tf_op jit(solution)/shard_map/ppermute | solution.py:317
  41.9 1.8 %collective-permute-start.16 = (s16[272,128]{1,0:T(8,128)(2,1)S(1)}, s16[272,128]{1,0:T(8,128)(2,1)S(1)}, u32[]{:S(2)}, u32[]{:S(2)}) collective-permute-start(s16[272,128]{1,0:T(8,128)(2,1)S(1)} %get-tuple-element.56), channel_id=1, source_target_pairs={{0,12},{1,13},{2,14},{3,15},{4,8},{5,9},{6,10},{7,11},{8,4},{9,5},... | collective-permute-start | bytes 208904 | tf_op jit(solution)/shard_map/ppermute | solution.py:317
  43.7 1.5 %collective-permute-start.14 = (s16[528,128]{1,0:T(8,128)(2,1)S(1)}, s16[528,128]{1,0:T(8,128)(2,1)S(1)}, u32[]{:S(2)}, u32[]{:S(2)}) collective-permute-start(s16[528,128]{1,0:T(8,128)(2,1)S(1)} %get-tuple-element.55), channel_id=1, source_target_pairs={{0,8},{1,9},{2,10},{3,11},{4,12},{5,13},{6,14},{7,15},{8,0},{9,1},... | collective-permute-start | bytes 405512 | tf_op jit(solution)/shard_map/ppermute | solution.py:317
  45.2 1.4 %collective-permute-done.15.refs_1_ = s16[272,128]{1,0:T(8,128)(2,1)S(1)} collective-permute-done((s16[272,128]{1,0:T(8,128)(2,1)S(1)}, s16[272,128]{1,0:T(8,128)(2,1)S(1)}, u32[]{:S(2)}, u32[]{:S(2)}) %collective-permute-start.15) | collective-permute-done | bytes 69664 | tf_op jit(solution)/shard_map/ppermute | solution.py:317
  46.7 1.5 %collective-permute-done.16.refs_1_ = s16[272,128]{1,0:T(8,128)(2,1)S(1)} collective-permute-done((s16[272,128]{1,0:T(8,128)(2,1)S(1)}, s16[272,128]{1,0:T(8,128)(2,1)S(1)}, u32[]{:S(2)}, u32[]{:S(2)}) %collective-permute-start.16) | collective-permute-done | bytes 69664 | tf_op jit(solution)/shard_map/ppermute | solution.py:317
  48.2 1.3 %collective-permute-done.14.refs_0_ = s16[528,128]{1,0:T(8,128)(2,1)S(1)} collective-permute-done((s16[528,128]{1,0:T(8,128)(2,1)S(1)}, s16[528,128]{1,0:T(8,128)(2,1)S(1)}, u32[]{:S(2)}, u32[]{:S(2)}) %collective-permute-start.14) | collective-permute-done | bytes 135200 | tf_op jit(solution)/shard_map/ppermute | solution.py:317
  49.5 0.7 %shard_map.65 = bf16[4,128,128]{2,1,0:T(8,128)(2,1)} custom-call(s16[528,128]{1,0:T(8,128)(2,1)S(1)} %collective-permute-done.14.refs_0_, f32[2,128,128]{2,1,0:T(8,128)S(1)} %shard_map.63.refs_2_.refs_1_, f32[2,128,128]{2,1,0:T(8,128)S(1)} %shard_map.64.refs_2_), custom_call_target="tpu_custom_call" | custom-call | bytes 1 | tf_op jit(solution)/shard_map/pallas_call | solution.py:267
  (38 shorter events, 3.5 us)
Async XLA Ops:
  0.0 3.0 %copy-start = (bf16[1,1,1,64,128,128]{5,4,3,2,1,0:T(8,128)(2,1)S(1)}, bf16[1,1,1,64,128,128]{5,4,3,2,1,0:T(8,128)(2,1)}, u32[]{:S(2)}) copy-start(bf16[1,1,1,64,128,128]{5,4,3,2,1,0:T(8,128)(2,1)} %param.4) | copy-start | bytes 6291460
  0.0 3.0 %copy-start.1 = (bf16[1,1,1,16,128,128]{5,4,3,2,1,0:T(8,128)(2,1)S(1)}, bf16[1,1,1,16,128,128]{5,4,3,2,1,0:T(8,128)(2,1)}, u32[]{:S(2)}) copy-start(bf16[1,1,1,16,128,128]{5,4,3,2,1,0:T(8,128)(2,1)} %param.5) | copy-start | bytes 1572868
  0.0 3.8 %collective-permute-start = (bf16[16,128,128]{2,1,0:T(8,128)(2,1)}, bf16[16,128,128]{2,1,0:T(8,128)(2,1)S(1)}, u32[]{:S(2)}, u32[]{:S(2)}) collective-permute-start(bf16[16,128,128]{2,1,0:T(8,128)(2,1)} %bitcast.14), channel_id=1, source_target_pairs={{0,16},{16,0},{1,17},{17,1},{2,18},{18,2},{3,19},{19,3},{4,20},{20... | collective-permute-start | bytes 1572872 | tf_op jit(solution)/shard_map/ppermute | solution.py:351
  0.5 15.3 %collective-permute-start.2 = (bf16[16,128,128]{2,1,0:T(8,128)(2,1)}, bf16[16,128,128]{2,1,0:T(8,128)(2,1)S(1)}, u32[]{:S(2)}, u32[]{:S(2)}) collective-permute-start(bf16[16,128,128]{2,1,0:T(8,128)(2,1)} %bitcast.15), channel_id=1, source_target_pairs={{0,8},{8,0},{1,9},{9,1},{2,10},{10,2},{3,11},{11,3},{4,12},{12,4},... | collective-permute-start | bytes 1572872 | tf_op jit(solution)/shard_map/ppermute | solution.py:350
  3.0 0.7 %copy-start.2 = (s32[1,1,1,2,32,16]{4,5,3,2,1,0:T(8,128)S(1)}, s32[1,1,1,2,32,16]{4,5,3,2,1,0:T(8,128)}, u32[]{:S(2)}) copy-start(s32[1,1,1,2,32,16]{4,5,3,2,1,0:T(8,128)} %param.6) | copy-start | bytes 12292
  3.0 0.7 %copy-start.3 = (s32[1,1,1,2,32,16]{4,5,3,2,1,0:T(8,128)S(1)}, s32[1,1,1,2,32,16]{4,5,3,2,1,0:T(8,128)}, u32[]{:S(2)}) copy-start(s32[1,1,1,2,32,16]{4,5,3,2,1,0:T(8,128)} %param.7) | copy-start | bytes 12292
  7.2 10.5 %collective-permute-start.6 = (s16[1040,128]{1,0:T(8,128)(2,1)S(1)}, s16[1040,128]{1,0:T(8,128)(2,1)S(1)}, u32[]{:S(2)}, u32[]{:S(2)}) collective-permute-start(s16[1040,128]{1,0:T(8,128)(2,1)S(1)} %get-tuple-element.34.refs_3_), channel_id=1, source_target_pairs={{0,1},{1,0},{2,3},{3,2},{4,5},{5,4},{6,7},{7,6},{8,9},{9,8},{10,11... | collective-permute-start | bytes 798728 | tf_op jit(solution)/shard_map/ppermute | solution.py:312
  8.8 9.1 %collective-permute-start.5 = (s16[1040,128]{1,0:T(8,128)(2,1)S(1)}, s16[1040,128]{1,0:T(8,128)(2,1)S(1)}, u32[]{:S(2)}, u32[]{:S(2)}) collective-permute-start(s16[1040,128]{1,0:T(8,128)(2,1)S(1)} %get-tuple-element.39), channel_id=1, source_target_pairs={{0,2},{1,3},{2,0},{3,1},{4,6},{5,7},{6,4},{7,5},{8,10},{9,11},{10,... | collective-permute-start | bytes 798728 | tf_op jit(solution)/shard_map/ppermute | solution.py:312
  13.4 3.7 %collective-permute-start.1 = (s32[8,128]{1,0:T(8,128)S(1)}, s32[8,128]{1,0:T(8,128)S(1)}, u32[]{:S(2)}, u32[]{:S(2)}) collective-permute-start(s32[8,128]{1,0:T(8,128)S(1)} %shard_map.51), channel_id=1, source_target_pairs={{0,8},{8,0},{1,9},{9,1},{2,10},{10,2},{3,11},{11,3},{4,12},{12,4},... | collective-permute-start | bytes 12296 | tf_op jit(solution)/shard_map/ppermute | solution.py:361
  17.2 3.1 %collective-permute-start.3 = (bf16[8,128,128]{2,1,0:T(8,128)(2,1)S(1)}, bf16[8,128,128]{2,1,0:T(8,128)(2,1)S(1)}, u32[]{:S(2)}, u32[]{:S(2)}) collective-permute-start(bf16[8,128,128]{2,1,0:T(8,128)(2,1)S(1)} %get-tuple-element.36), channel_id=1, source_target_pairs={{0,16},{16,0},{1,17},{17,1},{2,18},{18,2},{3,19},{19,3},{4,20},{20... | collective-permute-start | bytes 786440 | tf_op jit(solution)/shard_map/ppermute | solution.py:364
  17.2 3.0 %collective-permute-start.4 = (bf16[8,128,128]{2,1,0:T(8,128)(2,1)S(1)}, bf16[8,128,128]{2,1,0:T(8,128)(2,1)S(1)}, u32[]{:S(2)}, u32[]{:S(2)}) collective-permute-start(bf16[8,128,128]{2,1,0:T(8,128)(2,1)S(1)} %get-tuple-element.37), channel_id=1, source_target_pairs={{0,16},{16,0},{1,17},{17,1},{2,18},{18,2},{3,19},{19,3},{4,20},{20... | collective-permute-start | bytes 786440 | tf_op jit(solution)/shard_map/ppermute | solution.py:364
  18.1 7.5 %collective-permute-start.8 = (s16[528,128]{1,0:T(8,128)(2,1)S(1)}, s16[528,128]{1,0:T(8,128)(2,1)S(1)}, u32[]{:S(2)}, u32[]{:S(2)}) collective-permute-start(s16[528,128]{1,0:T(8,128)(2,1)S(1)} %get-tuple-element.41.refs_5_), channel_id=1, source_target_pairs={{0,1},{1,0},{2,3},{3,2},{4,5},{5,4},{6,7},{7,6},{8,9},{9,8},{10,11... | collective-permute-start | bytes 405512 | tf_op jit(solution)/shard_map/ppermute | solution.py:312
  18.6 6.9 %collective-permute-start.7 = (s16[528,128]{1,0:T(8,128)(2,1)S(1)}, s16[528,128]{1,0:T(8,128)(2,1)S(1)}, u32[]{:S(2)}, u32[]{:S(2)}) collective-permute-start(s16[528,128]{1,0:T(8,128)(2,1)S(1)} %get-tuple-element.40.refs_2_), channel_id=1, source_target_pairs={{0,2},{1,3},{2,0},{3,1},{4,6},{5,7},{6,4},{7,5},{8,10},{9,11},{10,... | collective-permute-start | bytes 405512 | tf_op jit(solution)/shard_map/ppermute | solution.py:312
  23.5 10.8 %collective-permute-start.9 = (s16[1040,128]{1,0:T(8,128)(2,1)S(1)}, s16[1040,128]{1,0:T(8,128)(2,1)S(1)}, u32[]{:S(2)}, u32[]{:S(2)}) collective-permute-start(s16[1040,128]{1,0:T(8,128)(2,1)S(1)} %get-tuple-element.45.refs_4_), channel_id=1, source_target_pairs={{0,2},{1,3},{2,0},{3,1},{4,6},{5,7},{6,4},{7,5},{8,10},{9,11},{10,... | collective-permute-start | bytes 798728 | tf_op jit(solution)/shard_map/ppermute | solution.py:312
  24.1 11.0 %collective-permute-start.10 = (s16[1040,128]{1,0:T(8,128)(2,1)S(1)}, s16[1040,128]{1,0:T(8,128)(2,1)S(1)}, u32[]{:S(2)}, u32[]{:S(2)}) collective-permute-start(s16[1040,128]{1,0:T(8,128)(2,1)S(1)} %get-tuple-element.50), channel_id=1, source_target_pairs={{0,1},{1,0},{2,3},{3,2},{4,5},{5,4},{6,7},{7,6},{8,9},{9,8},{10,11... | collective-permute-start | bytes 798728 | tf_op jit(solution)/shard_map/ppermute | solution.py:312
  25.7 9.6 %collective-permute-start.13 = (s16[528,128]{1,0:T(8,128)(2,1)S(1)}, s16[528,128]{1,0:T(8,128)(2,1)S(1)}, u32[]{:S(2)}, u32[]{:S(2)}) collective-permute-start(s16[528,128]{1,0:T(8,128)(2,1)S(1)} %get-tuple-element.46.refs_3_), channel_id=1, source_target_pairs={{0,4},{1,5},{2,6},{3,7},{4,0},{5,1},{6,2},{7,3},{8,12},{9,13},{10,... | collective-permute-start | bytes 405512 | tf_op jit(solution)/shard_map/ppermute | solution.py:312
  34.5 5.1 %collective-permute-start.11 = (s16[528,128]{1,0:T(8,128)(2,1)S(1)}, s16[528,128]{1,0:T(8,128)(2,1)S(1)}, u32[]{:S(2)}, u32[]{:S(2)}) collective-permute-start(s16[528,128]{1,0:T(8,128)(2,1)S(1)} %get-tuple-element.51.refs_2_), channel_id=1, source_target_pairs={{0,1},{1,0},{2,3},{3,2},{4,5},{5,4},{6,7},{7,6},{8,9},{9,8},{10,11... | collective-permute-start | bytes 405512 | tf_op jit(solution)/shard_map/ppermute | solution.py:312
  35.2 6.6 %collective-permute-start.12 = (s16[528,128]{1,0:T(8,128)(2,1)S(1)}, s16[528,128]{1,0:T(8,128)(2,1)S(1)}, u32[]{:S(2)}, u32[]{:S(2)}) collective-permute-start(s16[528,128]{1,0:T(8,128)(2,1)S(1)} %get-tuple-element.53.refs_2_), channel_id=1, source_target_pairs={{0,2},{1,3},{2,0},{3,1},{4,6},{5,7},{6,4},{7,5},{8,10},{9,11},{10,... | collective-permute-start | bytes 405512 | tf_op jit(solution)/shard_map/ppermute | solution.py:312
  39.6 7.0 %collective-permute-start.15 = (s16[272,128]{1,0:T(8,128)(2,1)S(1)}, s16[272,128]{1,0:T(8,128)(2,1)S(1)}, u32[]{:S(2)}, u32[]{:S(2)}) collective-permute-start(s16[272,128]{1,0:T(8,128)(2,1)S(1)} %shard_map.61.refs_4_), channel_id=1, source_target_pairs={{0,12},{1,13},{2,14},{3,15},{4,8},{5,9},{6,10},{7,11},{8,4},{9,5},... | collective-permute-start | bytes 208904 | tf_op jit(solution)/shard_map/ppermute | solution.py:317
  41.9 6.3 %collective-permute-start.16 = (s16[272,128]{1,0:T(8,128)(2,1)S(1)}, s16[272,128]{1,0:T(8,128)(2,1)S(1)}, u32[]{:S(2)}, u32[]{:S(2)}) collective-permute-start(s16[272,128]{1,0:T(8,128)(2,1)S(1)} %get-tuple-element.56), channel_id=1, source_target_pairs={{0,12},{1,13},{2,14},{3,15},{4,8},{5,9},{6,10},{7,11},{8,4},{9,5},... | collective-permute-start | bytes 208904 | tf_op jit(solution)/shard_map/ppermute | solution.py:317
  43.7 5.8 %collective-permute-start.14 = (s16[528,128]{1,0:T(8,128)(2,1)S(1)}, s16[528,128]{1,0:T(8,128)(2,1)S(1)}, u32[]{:S(2)}, u32[]{:S(2)}) collective-permute-start(s16[528,128]{1,0:T(8,128)(2,1)S(1)} %get-tuple-element.55), channel_id=1, source_target_pairs={{0,8},{1,9},{2,10},{3,11},{4,12},{5,13},{6,14},{7,15},{8,0},{9,1},... | collective-permute-start | bytes 405512 | tf_op jit(solution)/shard_map/ppermute | solution.py:317

commit v12 on v10

--- a/solution.py
+++ b/solution.py
@@ -140,13 +140,6 @@
     return kernel
 
 
-def split_kernel(in_ref, *out_refs):
-    at = 0
-    for ref in out_refs:
-        ref[...] = in_ref[pl.ds(at, ref.shape[0])]
-        at += ref.shape[0]
-
-
 def keep_kernel(fan, slots, count, chunks, bits):
     def kernel(lists_ref, a_ref, p_ref, *out_refs):
         find = finder(lists_ref, fan, slots)
@@ -359,16 +352,15 @@
     (*made, joined), own_came = send(lists, (a, p, p_r), (0, 1), own_bits, True, (gate,), 1)
     own_kept = keep(lists, (a, joined), own_bits, made[:1], 1)
     lists_x = lax.ppermute(hold(lists_far, own_kept[:1]), "col", swap)
-    pieces = [jax.ShapeDtypeStruct((held // 2, width, width), p.dtype)] * 2
-    pieces = call(split_kernel, pieces, (), (p_x,), (own_kept[0], lists_x))
-    p_xr = [lax.ppermute(x, "row", swap) for x in pieces]
     parts, after = [], ()
     for n in range(2):
         sent, part = second(own_kept[n], own_came[n], sizes[n], own_bits[n], after)
         parts.append(part)
         after = (sent,)
-
-    (made, joined), came_0 = send(lists_x, (a, p_x, *p_xr), (0,), other_bits[:1], True, after, 0)
+    p_x = hold(p_x, (*after, lists_x))
+    p_xr = lax.ppermute(p_x, "row", swap)
+
+    (made, joined), came_0 = send(lists_x, (a, p_x, p_xr), (0,), other_bits[:1], True, (), 0)
     (made,), came_1 = send(lists_x, (a, joined), (1,), other_bits[1:], False, (made,), 0)
     other_came = came_0 + came_1
     rest, part_sizes, after = every[2:], sizes, (made,)

time: 49.1 us -> 49.7 us (1.012)
  waiting for transfers between devices: 10.1 us -> 13.1 us
  starting transfers between devices: 22.8 us -> 20.3 us
    ppermute x9, waiting for transfers between devices: 2.91 us -> 8.38 us  [exchange(): return lax.ppermute(x, 'layer', [(i, i ^ 1 << bit) for i in range(layers)])]
    ppermute x1, waiting for transfers between devices: 1.35 us -> 0.01 us  [on_device(): lists_x = lax.ppermute(hold(lists_far, own_kept[:1]), 'col', swap)]
    ppermute x1, waiting for transfers between devices: 1.09 us -> 0.01 us  [on_device(): p_x = lax.ppermute(p, 'col', swap)]
    ppermute x3, starting transfers between devices: 5.79 us -> 4.79 us  [cross(): return lax.ppermute(x, ('col', 'layer'), perm)]
    ppermute x9, starting transfers between devices: 12.2 us -> 11.2 us  [exchange(): return lax.ppermute(x, 'layer', [(i, i ^ 1 << bit) for i in range(layers)])]
    pallas_call x20 -> x19, Pallas kernels: 15.2 us -> 15.2 us  [call(): pl.pallas_call(wrapped, out_shape=out_shape, in_specs=[pl.BlockSpec(memor...]
  transfers between devices with their start and end apart: 17 -> 16, of which waited for: 8 -> 7; matrix products, arithmetic and copies ran while one was open for 0% -> 0% of each run, Pallas kernels for 30% -> 29%
where the time goes in v12:
time: 49.7 us; the launch traced here: 49.5 us
  starting transfers between devices  20.3 us (41%)
  Pallas kernels  15.2 us (31%)
  waiting for transfers between devices  13.1 us (26%)
  local copies, waits for them, and re-layouts  0.72 us (1%)
    pallas_call x19, Pallas kernels, call(): pl.pallas_call(wrapped, out_shape=out_shape, in_specs=[pl.BlockSpec(memor...  15.2 us
    ppermute x9, starting transfers between devices, exchange(): return lax.ppermute(x, 'layer', [(i, i ^ 1 << bit) for i in range(layers)])  11.2 us
    ppermute x9, waiting for transfers between devices, exchange(): return lax.ppermute(x, 'layer', [(i, i ^ 1 << bit) for i in range(layers)])  8.38 us
    ppermute x3, starting transfers between devices, cross(): return lax.ppermute(x, ('col', 'layer'), perm)  4.79 us
    ppermute x3, waiting for transfers between devices, cross(): return lax.ppermute(x, ('col', 'layer'), perm)  4.66 us
    ppermute x1, starting transfers between devices, on_device(): p_x = lax.ppermute(p, 'col', swap)  2.56 us
    ppermute x1, starting transfers between devices, on_device(): lists_x = lax.ppermute(hold(lists_far, own_kept[:1]), 'col', swap)  1.23 us
  transfers between devices with their start and end apart: 16, of which 7 were waited for; matrix products, arithmetic and copies ran while one was open for 0% of the time, Pallas kernels for 29%

profile of v12, /device:TPU:0, one launch (start us, length us, event | category | flops | bytes accessed | tf_op | source)
XLA Modules:
  0.0 49.5 jit_solution(15765627199803365020)
XLA Ops:
  0.5 2.6 %collective-permute-start.2 = (bf16[16,128,128]{2,1,0:T(8,128)(2,1)}, bf16[16,128,128]{2,1,0:T(8,128)(2,1)S(1)}, u32[]{:S(2)}, u32[]{:S(2)}) collective-permute-start(bf16[16,128,128]{2,1,0:T(8,128)(2,1)} %bitcast.16), channel_id=1, source_target_pairs={{0,8},{8,0},{1,9},{9,1},{2,10},{10,2},{3,11},{11,3},{4,12},{12,4},... | collective-permute-start | bytes 1572872 | tf_op jit(solution)/shard_map/ppermute | solution.py:343
  3.0 0.7 %copy-done.2 = s32[1,1,1,2,32,16]{4,5,3,2,1,0:T(8,128)S(1)} copy-done((s32[1,1,1,2,32,16]{4,5,3,2,1,0:T(8,128)S(1)}, s32[1,1,1,2,32,16]{4,5,3,2,1,0:T(8,128)}, u32[]{:S(2)}) %copy-start.2) | copy-done | bytes 4120
  3.9 3.3 %shard_map.49 = (s16[1040,128]{1,0:T(8,128)(2,1)S(1)}, s16[1040,128]{1,0:T(8,128)(2,1)S(1)}, bf16[32,128,128]{2,1,0:T(8,128)(2,1)S(1)}) custom-call(s32[8,128]{1,0:T(8,128)S(1)} %get-tuple-element.29.refs_0_, bf16[64,128,128]{2,1,0:T(8,128)(2,1)S(1)} %bitcast.10, bf16[16,128,128]{2,1,0:T(8,128)(2,1)S(1)} %bitcast.18, ...), custom_call_target="tpu_custom_call" | custom-call | flops 5368709120 | bytes 4730880 | tf_op jit(solution)/shard_map/pallas_call | solution.py:260
  7.2 1.7 %collective-permute-start.3 = (s16[1040,128]{1,0:T(8,128)(2,1)S(1)}, s16[1040,128]{1,0:T(8,128)(2,1)S(1)}, u32[]{:S(2)}, u32[]{:S(2)}) collective-permute-start(s16[1040,128]{1,0:T(8,128)(2,1)S(1)} %get-tuple-element.34), channel_id=1, source_target_pairs={{0,2},{1,3},{2,0},{3,1},{4,6},{5,7},{6,4},{7,5},{8,10},{9,11},{10,... | collective-permute-start | bytes 798728 | tf_op jit(solution)/shard_map/ppermute | solution.py:305
  8.9 1.5 %collective-permute-start.4 = (s16[1040,128]{1,0:T(8,128)(2,1)S(1)}, s16[1040,128]{1,0:T(8,128)(2,1)S(1)}, u32[]{:S(2)}, u32[]{:S(2)}) collective-permute-start(s16[1040,128]{1,0:T(8,128)(2,1)S(1)} %get-tuple-element.31.refs_3_), channel_id=1, source_target_pairs={{0,1},{1,0},{2,3},{3,2},{4,5},{5,4},{6,7},{7,6},{8,9},{9,8},{10,11... | collective-permute-start | bytes 798728 | tf_op jit(solution)/shard_map/ppermute | solution.py:305
  10.4 3.0 %shard_map.50 = (f32[8,128,128]{2,1,0:T(8,128)S(1)}, f32[8,128,128]{2,1,0:T(8,128)S(1)}) custom-call(s32[8,128]{1,0:T(8,128)S(1)} %get-tuple-element.29.refs_0_, bf16[64,128,128]{2,1,0:T(8,128)(2,1)S(1)} %bitcast.11, bf16[32,128,128]{2,1,0:T(8,128)(2,1)S(1)} %get-tuple-element.30.refs_2_, s16[1040,128]{1,0:T(8,128)(2,1)S(1)} %get-tuple-element.31.refs_3_), custom_call_target="tpu_custom_call" | custom-call | flops 5368709120 | bytes 4198400 | tf_op jit(solution)/shard_map/pallas_call | solution.py:260
  13.4 1.2 %collective-permute-start.1 = (s32[8,128]{1,0:T(8,128)S(1)}, s32[8,128]{1,0:T(8,128)S(1)}, u32[]{:S(2)}, u32[]{:S(2)}) collective-permute-start(s32[8,128]{1,0:T(8,128)S(1)} %shard_map.51), channel_id=1, source_target_pairs={{0,8},{8,0},{1,9},{9,1},{2,10},{10,2},{3,11},{11,3},{4,12},{12,4},... | collective-permute-start | bytes 12296 | tf_op jit(solution)/shard_map/ppermute | solution.py:354
  14.7 2.3 %collective-permute-done.4.refs_1_ = s16[1040,128]{1,0:T(8,128)(2,1)S(1)} collective-permute-done((s16[1040,128]{1,0:T(8,128)(2,1)S(1)}, s16[1040,128]{1,0:T(8,128)(2,1)S(1)}, u32[]{:S(2)}, u32[]{:S(2)}) %collective-permute-start.4) | collective-permute-done | bytes 266272 | tf_op jit(solution)/shard_map/ppermute | solution.py:305
  17.5 1.6 %collective-permute-start.7 = (s16[528,128]{1,0:T(8,128)(2,1)S(1)}, s16[528,128]{1,0:T(8,128)(2,1)S(1)}, u32[]{:S(2)}, u32[]{:S(2)}) collective-permute-start(s16[528,128]{1,0:T(8,128)(2,1)S(1)} %get-tuple-element.36.refs_1_), channel_id=1, source_target_pairs={{0,1},{1,0},{2,3},{3,2},{4,5},{5,4},{6,7},{7,6},{8,9},{9,8},{10,11... | collective-permute-start | bytes 405512 | tf_op jit(solution)/shard_map/ppermute | solution.py:305
  19.5 2.0 %shard_map.55 = (s16[1040,128]{1,0:T(8,128)(2,1)S(1)}, bf16[32,128,128]{2,1,0:T(8,128)(2,1)S(1)}) custom-call(s32[8,128]{1,0:T(8,128)S(1)} %collective-permute-done.1.refs_2_.refs_0_, bf16[64,128,128]{2,1,0:T(8,128)(2,1)S(1)} %bitcast.12, bf16[16,128,128]{2,1,0:T(8,128)(2,1)S(1)} %shard_map.54.refs_2_, bf16[16,128,128]{2,1,0:T(8,128)(2,1)S(1)} %collective-permute-done.5.refs_3_), custom_call_target="tpu_custom_call" | custom-call | bytes 1 | tf_op jit(solution)/shard_map/pallas_call | solution.py:260
  21.6 1.6 %collective-permute-start.8 = (s16[1040,128]{1,0:T(8,128)(2,1)S(1)}, s16[1040,128]{1,0:T(8,128)(2,1)S(1)}, u32[]{:S(2)}, u32[]{:S(2)}) collective-permute-start(s16[1040,128]{1,0:T(8,128)(2,1)S(1)} %get-tuple-element.40.refs_3_), channel_id=1, source_target_pairs={{0,2},{1,3},{2,0},{3,1},{4,6},{5,7},{6,4},{7,5},{8,10},{9,11},{10,... | collective-permute-start | bytes 798728 | tf_op jit(solution)/shard_map/ppermute | solution.py:305
  23.2 1.9 %shard_map.56.refs_4_ = s16[1040,128]{1,0:T(8,128)(2,1)S(1)} custom-call(s32[8,128]{1,0:T(8,128)S(1)} %collective-permute-done.1.refs_2_.refs_0_, bf16[64,128,128]{2,1,0:T(8,128)(2,1)S(1)} %bitcast.13, bf16[32,128,128]{2,1,0:T(8,128)(2,1)S(1)} %get-tuple-element.37.refs_2_, s16[1040,128]{1,0:T(8,128)(2,1)S(1)} %get-tuple-element.40.refs_3_), custom_call_target="tpu_custom_call" | custom-call | bytes 1 | tf_op jit(solution)/shard_map/pallas_call | solution.py:260
  25.8 2.7 %collective-permute-start.12 = (s16[528,128]{1,0:T(8,128)(2,1)S(1)}, s16[528,128]{1,0:T(8,128)(2,1)S(1)}, u32[]{:S(2)}, u32[]{:S(2)}) collective-permute-start(s16[528,128]{1,0:T(8,128)(2,1)S(1)} %get-tuple-element.41.refs_3_), channel_id=1, source_target_pairs={{0,4},{1,5},{2,6},{3,7},{4,0},{5,1},{6,2},{7,3},{8,12},{9,13},{10,... | collective-permute-start | bytes 405512 | tf_op jit(solution)/shard_map/ppermute | solution.py:305
  28.5 3.0 %shard_map.58 = (f32[8,128,128]{2,1,0:T(8,128)S(1)}, f32[8,128,128]{2,1,0:T(8,128)S(1)}) custom-call(s32[8,128]{1,0:T(8,128)S(1)} %collective-permute-done.1.refs_2_.refs_0_, bf16[64,128,128]{2,1,0:T(8,128)(2,1)S(1)} %bitcast.14, bf16[32,128,128]{2,1,0:T(8,128)(2,1)S(1)} %get-tuple-element.37.refs_2_, s16[528,128]{1,0:T(8,128)(2,1)S(1)} %get-tuple-element.41.refs_3_), custom_call_target="tpu_custom_call" | custom-call | flops 5368709120 | bytes 4198400 | tf_op jit(solution)/shard_map/pallas_call | solution.py:260
  31.5 1.9 %collective-permute-done.8.refs_1_ = s16[1040,128]{1,0:T(8,128)(2,1)S(1)} collective-permute-done((s16[1040,128]{1,0:T(8,128)(2,1)S(1)}, s16[1040,128]{1,0:T(8,128)(2,1)S(1)}, u32[]{:S(2)}, u32[]{:S(2)}) %collective-permute-start.8) | collective-permute-done | bytes 266272 | tf_op jit(solution)/shard_map/ppermute | solution.py:305
  33.5 1.1 %collective-permute-start.10 = (s16[528,128]{1,0:T(8,128)(2,1)S(1)}, s16[528,128]{1,0:T(8,128)(2,1)S(1)}, u32[]{:S(2)}, u32[]{:S(2)}) collective-permute-start(s16[528,128]{1,0:T(8,128)(2,1)S(1)} %get-tuple-element.45.refs_2_), channel_id=1, source_target_pairs={{0,1},{1,0},{2,3},{3,2},{4,5},{5,4},{6,7},{7,6},{8,9},{9,8},{10,11... | collective-permute-start | bytes 405512 | tf_op jit(solution)/shard_map/ppermute | solution.py:305
  34.9 3.8 %collective-permute-done.10.refs_1_.refs_2_ = s16[528,128]{1,0:T(8,128)(2,1)S(1)} collective-permute-done((s16[528,128]{1,0:T(8,128)(2,1)S(1)}, s16[528,128]{1,0:T(8,128)(2,1)S(1)}, u32[]{:S(2)}, u32[]{:S(2)}) %collective-permute-start.10) | collective-permute-done | bytes 135200 | tf_op jit(solution)/shard_map/ppermute | solution.py:305
  38.8 0.7 %collective-permute-start.14 = (s16[272,128]{1,0:T(8,128)(2,1)S(1)}, s16[272,128]{1,0:T(8,128)(2,1)S(1)}, u32[]{:S(2)}, u32[]{:S(2)}) collective-permute-start(s16[272,128]{1,0:T(8,128)(2,1)S(1)} %shard_map.62.refs_4_), channel_id=1, source_target_pairs={{0,12},{1,13},{2,14},{3,15},{4,8},{5,9},{6,10},{7,11},{8,4},{9,5},... | collective-permute-start | bytes 208904 | tf_op jit(solution)/shard_map/ppermute | solution.py:310
  40.0 2.9 %collective-permute-start.15 = (s16[272,128]{1,0:T(8,128)(2,1)S(1)}, s16[272,128]{1,0:T(8,128)(2,1)S(1)}, u32[]{:S(2)}, u32[]{:S(2)}) collective-permute-start(s16[272,128]{1,0:T(8,128)(2,1)S(1)} %get-tuple-element.50), channel_id=1, source_target_pairs={{0,12},{1,13},{2,14},{3,15},{4,8},{5,9},{6,10},{7,11},{8,4},{9,5},... | collective-permute-start | bytes 208904 | tf_op jit(solution)/shard_map/ppermute | solution.py:310
  42.9 1.2 %collective-permute-start.13 = (s16[528,128]{1,0:T(8,128)(2,1)S(1)}, s16[528,128]{1,0:T(8,128)(2,1)S(1)}, u32[]{:S(2)}, u32[]{:S(2)}) collective-permute-start(s16[528,128]{1,0:T(8,128)(2,1)S(1)} %get-tuple-element.49), channel_id=1, source_target_pairs={{0,8},{1,9},{2,10},{3,11},{4,12},{5,13},{6,14},{7,15},{8,0},{9,1},... | collective-permute-start | bytes 405512 | tf_op jit(solution)/shard_map/ppermute | solution.py:310
  44.1 1.8 %collective-permute-done.14.refs_1_ = s16[272,128]{1,0:T(8,128)(2,1)S(1)} collective-permute-done((s16[272,128]{1,0:T(8,128)(2,1)S(1)}, s16[272,128]{1,0:T(8,128)(2,1)S(1)}, u32[]{:S(2)}, u32[]{:S(2)}) %collective-permute-start.14) | collective-permute-done | bytes 69664 | tf_op jit(solution)/shard_map/ppermute | solution.py:310
  45.9 1.5 %collective-permute-done.15.refs_1_ = s16[272,128]{1,0:T(8,128)(2,1)S(1)} collective-permute-done((s16[272,128]{1,0:T(8,128)(2,1)S(1)}, s16[272,128]{1,0:T(8,128)(2,1)S(1)}, u32[]{:S(2)}, u32[]{:S(2)}) %collective-permute-start.15) | collective-permute-done | bytes 69664 | tf_op jit(solution)/shard_map/ppermute | solution.py:310
  47.4 1.4 %collective-permute-done.13.refs_0_ = s16[528,128]{1,0:T(8,128)(2,1)S(1)} collective-permute-done((s16[528,128]{1,0:T(8,128)(2,1)S(1)}, s16[528,128]{1,0:T(8,128)(2,1)S(1)}, u32[]{:S(2)}, u32[]{:S(2)}) %collective-permute-start.13) | collective-permute-done | bytes 135200 | tf_op jit(solution)/shard_map/ppermute | solution.py:310
  48.8 0.7 %shard_map.66 = bf16[4,128,128]{2,1,0:T(8,128)(2,1)} custom-call(s16[528,128]{1,0:T(8,128)(2,1)S(1)} %collective-permute-done.13.refs_0_, f32[2,128,128]{2,1,0:T(8,128)S(1)} %shard_map.64.refs_2_.refs_1_, f32[2,128,128]{2,1,0:T(8,128)S(1)} %shard_map.65.refs_2_), custom_call_target="tpu_custom_call" | custom-call | bytes 1 | tf_op jit(solution)/shard_map/pallas_call | solution.py:260
  (37 shorter events, 3.2 us)
Async XLA Ops:
  0.0 3.0 %copy-start = (bf16[1,1,1,64,128,128]{5,4,3,2,1,0:T(8,128)(2,1)S(1)}, bf16[1,1,1,64,128,128]{5,4,3,2,1,0:T(8,128)(2,1)}, u32[]{:S(2)}) copy-start(bf16[1,1,1,64,128,128]{5,4,3,2,1,0:T(8,128)(2,1)} %param.4) | copy-start | bytes 6291460
  0.0 3.0 %copy-start.1 = (bf16[1,1,1,16,128,128]{5,4,3,2,1,0:T(8,128)(2,1)S(1)}, bf16[1,1,1,16,128,128]{5,4,3,2,1,0:T(8,128)(2,1)}, u32[]{:S(2)}) copy-start(bf16[1,1,1,16,128,128]{5,4,3,2,1,0:T(8,128)(2,1)} %param.5) | copy-start | bytes 1572868
  0.0 3.8 %collective-permute-start = (bf16[16,128,128]{2,1,0:T(8,128)(2,1)}, bf16[16,128,128]{2,1,0:T(8,128)(2,1)S(1)}, u32[]{:S(2)}, u32[]{:S(2)}) collective-permute-start(bf16[16,128,128]{2,1,0:T(8,128)(2,1)} %bitcast.15), channel_id=1, source_target_pairs={{0,16},{16,0},{1,17},{17,1},{2,18},{18,2},{3,19},{19,3},{4,20},{20... | collective-permute-start | bytes 1572872 | tf_op jit(solution)/shard_map/ppermute | solution.py:344
  0.5 16.9 %collective-permute-start.2 = (bf16[16,128,128]{2,1,0:T(8,128)(2,1)}, bf16[16,128,128]{2,1,0:T(8,128)(2,1)S(1)}, u32[]{:S(2)}, u32[]{:S(2)}) collective-permute-start(bf16[16,128,128]{2,1,0:T(8,128)(2,1)} %bitcast.16), channel_id=1, source_target_pairs={{0,8},{8,0},{1,9},{9,1},{2,10},{10,2},{3,11},{11,3},{4,12},{12,4},... | collective-permute-start | bytes 1572872 | tf_op jit(solution)/shard_map/ppermute | solution.py:343
  3.0 0.7 %copy-start.2 = (s32[1,1,1,2,32,16]{4,5,3,2,1,0:T(8,128)S(1)}, s32[1,1,1,2,32,16]{4,5,3,2,1,0:T(8,128)}, u32[]{:S(2)}) copy-start(s32[1,1,1,2,32,16]{4,5,3,2,1,0:T(8,128)} %param.6) | copy-start | bytes 12292
  3.0 0.7 %copy-start.3 = (s32[1,1,1,2,32,16]{4,5,3,2,1,0:T(8,128)S(1)}, s32[1,1,1,2,32,16]{4,5,3,2,1,0:T(8,128)}, u32[]{:S(2)}) copy-start(s32[1,1,1,2,32,16]{4,5,3,2,1,0:T(8,128)} %param.7) | copy-start | bytes 12292
  7.2 10.0 %collective-permute-start.3 = (s16[1040,128]{1,0:T(8,128)(2,1)S(1)}, s16[1040,128]{1,0:T(8,128)(2,1)S(1)}, u32[]{:S(2)}, u32[]{:S(2)}) collective-permute-start(s16[1040,128]{1,0:T(8,128)(2,1)S(1)} %get-tuple-element.34), channel_id=1, source_target_pairs={{0,2},{1,3},{2,0},{3,1},{4,6},{5,7},{6,4},{7,5},{8,10},{9,11},{10,... | collective-permute-start | bytes 798728 | tf_op jit(solution)/shard_map/ppermute | solution.py:305
  8.9 8.1 %collective-permute-start.4 = (s16[1040,128]{1,0:T(8,128)(2,1)S(1)}, s16[1040,128]{1,0:T(8,128)(2,1)S(1)}, u32[]{:S(2)}, u32[]{:S(2)}) collective-permute-start(s16[1040,128]{1,0:T(8,128)(2,1)S(1)} %get-tuple-element.31.refs_3_), channel_id=1, source_target_pairs={{0,1},{1,0},{2,3},{3,2},{4,5},{5,4},{6,7},{7,6},{8,9},{9,8},{10,11... | collective-permute-start | bytes 798728 | tf_op jit(solution)/shard_map/ppermute | solution.py:305
  13.4 3.9 %collective-permute-start.1 = (s32[8,128]{1,0:T(8,128)S(1)}, s32[8,128]{1,0:T(8,128)S(1)}, u32[]{:S(2)}, u32[]{:S(2)}) collective-permute-start(s32[8,128]{1,0:T(8,128)S(1)} %shard_map.51), channel_id=1, source_target_pairs={{0,8},{8,0},{1,9},{9,1},{2,10},{10,2},{3,11},{11,3},{4,12},{12,4},... | collective-permute-start | bytes 12296 | tf_op jit(solution)/shard_map/ppermute | solution.py:354
  17.4 2.1 %collective-permute-start.5 = (bf16[16,128,128]{2,1,0:T(8,128)(2,1)S(1)}, bf16[16,128,128]{2,1,0:T(8,128)(2,1)S(1)}, u32[]{:S(2)}, u32[]{:S(2)}) collective-permute-start(bf16[16,128,128]{2,1,0:T(8,128)(2,1)S(1)} %shard_map.54.refs_2_), channel_id=1, source_target_pairs={{0,16},{16,0},{1,17},{17,1},{2,18},{18,2},{3,19},{19,3},{4,20},{20... | collective-permute-start | bytes 1572872 | tf_op jit(solution)/shard_map/ppermute | solution.py:361
  17.5 8.2 %collective-permute-start.7 = (s16[528,128]{1,0:T(8,128)(2,1)S(1)}, s16[528,128]{1,0:T(8,128)(2,1)S(1)}, u32[]{:S(2)}, u32[]{:S(2)}) collective-permute-start(s16[528,128]{1,0:T(8,128)(2,1)S(1)} %get-tuple-element.36.refs_1_), channel_id=1, source_target_pairs={{0,1},{1,0},{2,3},{3,2},{4,5},{5,4},{6,7},{7,6},{8,9},{9,8},{10,11... | collective-permute-start | bytes 405512 | tf_op jit(solution)/shard_map/ppermute | solution.py:305
  19.1 6.6 %collective-permute-start.6 = (s16[528,128]{1,0:T(8,128)(2,1)S(1)}, s16[528,128]{1,0:T(8,128)(2,1)S(1)}, u32[]{:S(2)}, u32[]{:S(2)}) collective-permute-start(s16[528,128]{1,0:T(8,128)(2,1)S(1)} %get-tuple-element.35.refs_2_), channel_id=1, source_target_pairs={{0,2},{1,3},{2,0},{3,1},{4,6},{5,7},{6,4},{7,5},{8,10},{9,11},{10,... | collective-permute-start | bytes 405512 | tf_op jit(solution)/shard_map/ppermute | solution.py:305
  21.6 11.8 %collective-permute-start.8 = (s16[1040,128]{1,0:T(8,128)(2,1)S(1)}, s16[1040,128]{1,0:T(8,128)(2,1)S(1)}, u32[]{:S(2)}, u32[]{:S(2)}) collective-permute-start(s16[1040,128]{1,0:T(8,128)(2,1)S(1)} %get-tuple-element.40.refs_3_), channel_id=1, source_target_pairs={{0,2},{1,3},{2,0},{3,1},{4,6},{5,7},{6,4},{7,5},{8,10},{9,11},{10,... | collective-permute-start | bytes 798728 | tf_op jit(solution)/shard_map/ppermute | solution.py:305
  25.1 9.5 %collective-permute-start.9 = (s16[1040,128]{1,0:T(8,128)(2,1)S(1)}, s16[1040,128]{1,0:T(8,128)(2,1)S(1)}, u32[]{:S(2)}, u32[]{:S(2)}) collective-permute-start(s16[1040,128]{1,0:T(8,128)(2,1)S(1)} %shard_map.56.refs_4_), channel_id=1, source_target_pairs={{0,1},{1,0},{2,3},{3,2},{4,5},{5,4},{6,7},{7,6},{8,9},{9,8},{10,11... | collective-permute-start | bytes 798728 | tf_op jit(solution)/shard_map/ppermute | solution.py:305
  25.8 9.0 %collective-permute-start.12 = (s16[528,128]{1,0:T(8,128)(2,1)S(1)}, s16[528,128]{1,0:T(8,128)(2,1)S(1)}, u32[]{:S(2)}, u32[]{:S(2)}) collective-permute-start(s16[528,128]{1,0:T(8,128)(2,1)S(1)} %get-tuple-element.41.refs_3_), channel_id=1, source_target_pairs={{0,4},{1,5},{2,6},{3,7},{4,0},{5,1},{6,2},{7,3},{8,12},{9,13},{10,... | collective-permute-start | bytes 405512 | tf_op jit(solution)/shard_map/ppermute | solution.py:305
  33.5 5.2 %collective-permute-start.10 = (s16[528,128]{1,0:T(8,128)(2,1)S(1)}, s16[528,128]{1,0:T(8,128)(2,1)S(1)}, u32[]{:S(2)}, u32[]{:S(2)}) collective-permute-start(s16[528,128]{1,0:T(8,128)(2,1)S(1)} %get-tuple-element.45.refs_2_), channel_id=1, source_target_pairs={{0,1},{1,0},{2,3},{3,2},{4,5},{5,4},{6,7},{7,6},{8,9},{9,8},{10,11... | collective-permute-start | bytes 405512 | tf_op jit(solution)/shard_map/ppermute | solution.py:305
  34.7 5.1 %collective-permute-start.11 = (s16[528,128]{1,0:T(8,128)(2,1)S(1)}, s16[528,128]{1,0:T(8,128)(2,1)S(1)}, u32[]{:S(2)}, u32[]{:S(2)}) collective-permute-start(s16[528,128]{1,0:T(8,128)(2,1)S(1)} %get-tuple-element.47.refs_2_), channel_id=1, source_target_pairs={{0,2},{1,3},{2,0},{3,1},{4,6},{5,7},{6,4},{7,5},{8,10},{9,11},{10,... | collective-permute-start | bytes 405512 | tf_op jit(solution)/shard_map/ppermute | solution.py:305
  38.8 7.0 %collective-permute-start.14 = (s16[272,128]{1,0:T(8,128)(2,1)S(1)}, s16[272,128]{1,0:T(8,128)(2,1)S(1)}, u32[]{:S(2)}, u32[]{:S(2)}) collective-permute-start(s16[272,128]{1,0:T(8,128)(2,1)S(1)} %shard_map.62.refs_4_), channel_id=1, source_target_pairs={{0,12},{1,13},{2,14},{3,15},{4,8},{5,9},{6,10},{7,11},{8,4},{9,5},... | collective-permute-start | bytes 208904 | tf_op jit(solution)/shard_map/ppermute | solution.py:310
  40.0 7.4 %collective-permute-start.15 = (s16[272,128]{1,0:T(8,128)(2,1)S(1)}, s16[272,128]{1,0:T(8,128)(2,1)S(1)}, u32[]{:S(2)}, u32[]{:S(2)}) collective-permute-start(s16[272,128]{1,0:T(8,128)(2,1)S(1)} %get-tuple-element.50), channel_id=1, source_target_pairs={{0,12},{1,13},{2,14},{3,15},{4,8},{5,9},{6,10},{7,11},{8,4},{9,5},... | collective-permute-start | bytes 208904 | tf_op jit(solution)/shard_map/ppermute | solution.py:310
  42.9 5.9 %collective-permute-start.13 = (s16[528,128]{1,0:T(8,128)(2,1)S(1)}, s16[528,128]{1,0:T(8,128)(2,1)S(1)}, u32[]{:S(2)}, u32[]{:S(2)}) collective-permute-start(s16[528,128]{1,0:T(8,128)(2,1)S(1)} %get-tuple-element.49), channel_id=1, source_target_pairs={{0,8},{1,9},{2,10},{3,11},{4,12},{5,13},{6,14},{7,15},{8,0},{9,1},... | collective-permute-start | bytes 405512 | tf_op jit(solution)/shard_map/ppermute | solution.py:310

commit v13 on v12

--- a/solution.py
+++ b/solution.py
@@ -266,7 +266,7 @@
         out_specs=jax.tree.map(lambda _: pl.BlockSpec(memory_space=VMEM), out_shape),
         scratch_shapes=list(scratch),
         compiler_params=pltpu.CompilerParams(vmem_limit_bytes=moved + 4 * 2**20),
-        cost_estimate=pl.CostEstimate(flops=5 * flops, bytes_accessed=moved if flops else 1, transcendentals=0),
+        cost_estimate=pl.CostEstimate(flops=int(5 * flops), bytes_accessed=moved if flops else 1, transcendentals=0),
     )(*smem, *vmem, *after)
 
 
@@ -363,16 +363,16 @@
     (made, joined), came_0 = send(lists_x, (a, p_x, p_xr), (0,), other_bits[:1], True, (), 0)
     (made,), came_1 = send(lists_x, (a, joined), (1,), other_bits[1:], False, (made,), 0)
     other_came = came_0 + came_1
-    rest, part_sizes, after = every[2:], sizes, (made,)
+    other_kept = keep(lists_x, (a, joined), other_bits, (made,), 1)
+
+    rest, part_sizes, after = every[2:], sizes, other_kept[:1]
     for b in every[2:]:
         sent, kept = add(parts, part_sizes, rest, b, after)
         after = (sent,)
         parts, part_sizes = [(kept, exchange(sent, b))], [count]
         rest = less(rest, b)
     (own,) = parts
-    other_kept = keep(lists_x, (a, joined), other_bits, after, 1)
-
-    streams, after = [], (other_kept[0],)
+    streams = []
     for n in range(2):
         sent, part = second(other_kept[n], other_came[n], sizes[n], other_bits[n], after)
         streams.append(part)

time: 49.7 us -> 48.8 us (0.982)
  waiting for transfers between devices: 13.1 us -> 11 us
  starting transfers between devices: 20.3 us -> 21.7 us
    ppermute x9, waiting for transfers between devices: 8.38 us -> 6.24 us  [exchange(): return lax.ppermute(x, 'layer', [(i, i ^ 1 << bit) for i in range(layers)])]
    ppermute x9, starting transfers between devices: 11.2 us -> 12.2 us  [exchange(): return lax.ppermute(x, 'layer', [(i, i ^ 1 << bit) for i in range(layers)])]
  transfers between devices with their start and end apart: 16 -> 16, of which waited for: 7 -> 6; matrix products, arithmetic and copies ran while one was open for 0% -> 0% of each run, Pallas kernels for 29% -> 29%
where the time goes in v13:
time: 48.8 us; the launch traced here: 48.7 us
  starting transfers between devices  21.7 us (44%)
  Pallas kernels  15 us (31%)
  waiting for transfers between devices  11 us (23%)
  local copies, waits for them, and re-layouts  0.72 us (1%)
    pallas_call x19, Pallas kernels, call(): pl.pallas_call(wrapped, out_shape=out_shape, in_specs=[pl.BlockSpec(memor...  15 us
    ppermute x9, starting transfers between devices, exchange(): return lax.ppermute(x, 'layer', [(i, i ^ 1 << bit) for i in range(layers)])  12.2 us
    ppermute x9, waiting for transfers between devices, exchange(): return lax.ppermute(x, 'layer', [(i, i ^ 1 << bit) for i in range(layers)])  6.24 us
    ppermute x3, starting transfers between devices, cross(): return lax.ppermute(x, ('col', 'layer'), perm)  5.19 us
    ppermute x3, waiting for transfers between devices, cross(): return lax.ppermute(x, ('col', 'layer'), perm)  4.77 us
    ppermute x1, starting transfers between devices, on_device(): p_x = lax.ppermute(p, 'col', swap)  2.56 us
    ppermute x1, starting transfers between devices, on_device(): lists_x = lax.ppermute(hold(lists_far, own_kept[:1]), 'col', swap)  1.24 us
  transfers between devices with their start and end apart: 16, of which 6 were waited for; matrix products, arithmetic and copies ran while one was open for 0% of the time, Pallas kernels for 29%

profile of v13, /device:TPU:0, one launch (start us, length us, event | category | flops | bytes accessed | tf_op | source)
XLA Modules:
  0.0 48.7 jit_solution(4202416130619726408)
XLA Ops:
  0.5 2.6 %collective-permute-start.2 = (bf16[16,128,128]{2,1,0:T(8,128)(2,1)}, bf16[16,128,128]{2,1,0:T(8,128)(2,1)S(1)}, u32[]{:S(2)}, u32[]{:S(2)}) collective-permute-start(bf16[16,128,128]{2,1,0:T(8,128)(2,1)} %bitcast.16), channel_id=1, source_target_pairs={{0,8},{8,0},{1,9},{9,1},{2,10},{10,2},{3,11},{11,3},{4,12},{12,4},... | collective-permute-start | bytes 1572872 | tf_op jit(solution)/shard_map/ppermute | solution.py:343
  3.0 0.7 %copy-done.2 = s32[1,1,1,2,32,16]{4,5,3,2,1,0:T(8,128)S(1)} copy-done((s32[1,1,1,2,32,16]{4,5,3,2,1,0:T(8,128)S(1)}, s32[1,1,1,2,32,16]{4,5,3,2,1,0:T(8,128)}, u32[]{:S(2)}) %copy-start.2) | copy-done | bytes 4120
  3.9 3.2 %shard_map.49 = (s16[1040,128]{1,0:T(8,128)(2,1)S(1)}, s16[1040,128]{1,0:T(8,128)(2,1)S(1)}, bf16[32,128,128]{2,1,0:T(8,128)(2,1)S(1)}) custom-call(s32[8,128]{1,0:T(8,128)S(1)} %get-tuple-element.29.refs_0_, bf16[64,128,128]{2,1,0:T(8,128)(2,1)S(1)} %bitcast.10, bf16[16,128,128]{2,1,0:T(8,128)(2,1)S(1)} %bitcast.18, ...), custom_call_target="tpu_custom_call" | custom-call | flops 5368709120 | bytes 4730880 | tf_op jit(solution)/shard_map/pallas_call | solution.py:260
  7.1 1.7 %collective-permute-start.3 = (s16[1040,128]{1,0:T(8,128)(2,1)S(1)}, s16[1040,128]{1,0:T(8,128)(2,1)S(1)}, u32[]{:S(2)}, u32[]{:S(2)}) collective-permute-start(s16[1040,128]{1,0:T(8,128)(2,1)S(1)} %get-tuple-element.34), channel_id=1, source_target_pairs={{0,2},{1,3},{2,0},{3,1},{4,6},{5,7},{6,4},{7,5},{8,10},{9,11},{10,... | collective-permute-start | bytes 798728 | tf_op jit(solution)/shard_map/ppermute | solution.py:305
  8.8 1.5 %collective-permute-start.4 = (s16[1040,128]{1,0:T(8,128)(2,1)S(1)}, s16[1040,128]{1,0:T(8,128)(2,1)S(1)}, u32[]{:S(2)}, u32[]{:S(2)}) collective-permute-start(s16[1040,128]{1,0:T(8,128)(2,1)S(1)} %get-tuple-element.31.refs_3_), channel_id=1, source_target_pairs={{0,1},{1,0},{2,3},{3,2},{4,5},{5,4},{6,7},{7,6},{8,9},{9,8},{10,11... | collective-permute-start | bytes 798728 | tf_op jit(solution)/shard_map/ppermute | solution.py:305
  10.3 3.0 %shard_map.50 = (f32[8,128,128]{2,1,0:T(8,128)S(1)}, f32[8,128,128]{2,1,0:T(8,128)S(1)}) custom-call(s32[8,128]{1,0:T(8,128)S(1)} %get-tuple-element.29.refs_0_, bf16[64,128,128]{2,1,0:T(8,128)(2,1)S(1)} %bitcast.11, bf16[32,128,128]{2,1,0:T(8,128)(2,1)S(1)} %get-tuple-element.30.refs_2_, s16[1040,128]{1,0:T(8,128)(2,1)S(1)} %get-tuple-element.31.refs_3_), custom_call_target="tpu_custom_call" | custom-call | flops 5368709120 | bytes 4198400 | tf_op jit(solution)/shard_map/pallas_call | solution.py:260
  13.3 1.2 %collective-permute-start.1 = (s32[8,128]{1,0:T(8,128)S(1)}, s32[8,128]{1,0:T(8,128)S(1)}, u32[]{:S(2)}, u32[]{:S(2)}) collective-permute-start(s32[8,128]{1,0:T(8,128)S(1)} %shard_map.51), channel_id=1, source_target_pairs={{0,8},{8,0},{1,9},{9,1},{2,10},{10,2},{3,11},{11,3},{4,12},{12,4},... | collective-permute-start | bytes 12296 | tf_op jit(solution)/shard_map/ppermute | solution.py:354
  14.5 2.4 %collective-permute-done.4.refs_1_ = s16[1040,128]{1,0:T(8,128)(2,1)S(1)} collective-permute-done((s16[1040,128]{1,0:T(8,128)(2,1)S(1)}, s16[1040,128]{1,0:T(8,128)(2,1)S(1)}, u32[]{:S(2)}, u32[]{:S(2)}) %collective-permute-start.4) | collective-permute-done | bytes 266272 | tf_op jit(solution)/shard_map/ppermute | solution.py:305
  17.4 1.6 %collective-permute-start.8 = (s16[528,128]{1,0:T(8,128)(2,1)S(1)}, s16[528,128]{1,0:T(8,128)(2,1)S(1)}, u32[]{:S(2)}, u32[]{:S(2)}) collective-permute-start(s16[528,128]{1,0:T(8,128)(2,1)S(1)} %get-tuple-element.36.refs_1_), channel_id=1, source_target_pairs={{0,1},{1,0},{2,3},{3,2},{4,5},{5,4},{6,7},{7,6},{8,9},{9,8},{10,11... | collective-permute-start | bytes 405512 | tf_op jit(solution)/shard_map/ppermute | solution.py:305
  19.4 2.0 %shard_map.55 = (s16[1040,128]{1,0:T(8,128)(2,1)S(1)}, bf16[32,128,128]{2,1,0:T(8,128)(2,1)S(1)}) custom-call(s32[8,128]{1,0:T(8,128)S(1)} %collective-permute-done.1.refs_2_.refs_0_, bf16[64,128,128]{2,1,0:T(8,128)(2,1)S(1)} %bitcast.12, bf16[16,128,128]{2,1,0:T(8,128)(2,1)S(1)} %shard_map.54.refs_2_, bf16[16,128,128]{2,1,0:T(8,128)(2,1)S(1)} %collective-permute-done.5.refs_3_), custom_call_target="tpu_custom_call" | custom-call | bytes 1 | tf_op jit(solution)/shard_map/pallas_call | solution.py:260
  21.5 1.6 %collective-permute-start.6 = (s16[1040,128]{1,0:T(8,128)(2,1)S(1)}, s16[1040,128]{1,0:T(8,128)(2,1)S(1)}, u32[]{:S(2)}, u32[]{:S(2)}) collective-permute-start(s16[1040,128]{1,0:T(8,128)(2,1)S(1)} %get-tuple-element.38.refs_3_), channel_id=1, source_target_pairs={{0,2},{1,3},{2,0},{3,1},{4,6},{5,7},{6,4},{7,5},{8,10},{9,11},{10,... | collective-permute-start | bytes 798728 | tf_op jit(solution)/shard_map/ppermute | solution.py:305
  23.1 1.9 %shard_map.56.refs_3_ = s16[1040,128]{1,0:T(8,128)(2,1)S(1)} custom-call(s32[8,128]{1,0:T(8,128)S(1)} %collective-permute-done.1.refs_2_.refs_0_, bf16[64,128,128]{2,1,0:T(8,128)(2,1)S(1)} %bitcast.13, bf16[32,128,128]{2,1,0:T(8,128)(2,1)S(1)} %get-tuple-element.37.refs_2_, s16[1040,128]{1,0:T(8,128)(2,1)S(1)} %get-tuple-element.38.refs_3_), custom_call_target="tpu_custom_call" | custom-call | bytes 1 | tf_op jit(solution)/shard_map/pallas_call | solution.py:260
  25.0 0.6 %collective-permute-start.9 = (s16[1040,128]{1,0:T(8,128)(2,1)S(1)}, s16[1040,128]{1,0:T(8,128)(2,1)S(1)}, u32[]{:S(2)}, u32[]{:S(2)}) collective-permute-start(s16[1040,128]{1,0:T(8,128)(2,1)S(1)} %shard_map.56.refs_3_), channel_id=1, source_target_pairs={{0,1},{1,0},{2,3},{3,2},{4,5},{5,4},{6,7},{7,6},{8,9},{9,8},{10,11... | collective-permute-start | bytes 798728 | tf_op jit(solution)/shard_map/ppermute | solution.py:305
  25.6 3.0 %shard_map.57 = (f32[8,128,128]{2,1,0:T(8,128)S(1)}, f32[8,128,128]{2,1,0:T(8,128)S(1)}) custom-call(s32[8,128]{1,0:T(8,128)S(1)} %collective-permute-done.1.refs_2_.refs_0_, bf16[64,128,128]{2,1,0:T(8,128)(2,1)S(1)} %bitcast.14, bf16[32,128,128]{2,1,0:T(8,128)(2,1)S(1)} %get-tuple-element.37.refs_2_, s16[1040,128]{1,0:T(8,128)(2,1)S(1)} %shard_map.56.refs_3_), custom_call_target="tpu_custom_call" | custom-call | flops 5368709120 | bytes 4198400 | tf_op jit(solution)/shard_map/pallas_call | solution.py:260
  28.7 2.7 %collective-permute-start.12 = (s16[528,128]{1,0:T(8,128)(2,1)S(1)}, s16[528,128]{1,0:T(8,128)(2,1)S(1)}, u32[]{:S(2)}, u32[]{:S(2)}) collective-permute-start(s16[528,128]{1,0:T(8,128)(2,1)S(1)} %get-tuple-element.42.refs_2_), channel_id=1, source_target_pairs={{0,4},{1,5},{2,6},{3,7},{4,0},{5,1},{6,2},{7,3},{8,12},{9,13},{10,... | collective-permute-start | bytes 405512 | tf_op jit(solution)/shard_map/ppermute | solution.py:305
  31.6 1.6 %collective-permute-start.10 = (s16[528,128]{1,0:T(8,128)(2,1)S(1)}, s16[528,128]{1,0:T(8,128)(2,1)S(1)}, u32[]{:S(2)}, u32[]{:S(2)}) collective-permute-start(s16[528,128]{1,0:T(8,128)(2,1)S(1)} %get-tuple-element.45.refs_2_), channel_id=1, source_target_pairs={{0,1},{1,0},{2,3},{3,2},{4,5},{5,4},{6,7},{7,6},{8,9},{9,8},{10,11... | collective-permute-start | bytes 405512 | tf_op jit(solution)/shard_map/ppermute | solution.py:305
  33.8 3.7 %collective-permute-done.12.refs_1_ = s16[528,128]{1,0:T(8,128)(2,1)S(1)} collective-permute-done((s16[528,128]{1,0:T(8,128)(2,1)S(1)}, s16[528,128]{1,0:T(8,128)(2,1)S(1)}, u32[]{:S(2)}, u32[]{:S(2)}) %collective-permute-start.12) | collective-permute-done | bytes 135200 | tf_op jit(solution)/shard_map/ppermute | solution.py:305
  37.7 1.6 %collective-permute-start.14 = (s16[272,128]{1,0:T(8,128)(2,1)S(1)}, s16[272,128]{1,0:T(8,128)(2,1)S(1)}, u32[]{:S(2)}, u32[]{:S(2)}) collective-permute-start(s16[272,128]{1,0:T(8,128)(2,1)S(1)} %shard_map.62.refs_4_), channel_id=1, source_target_pairs={{0,12},{1,13},{2,14},{3,15},{4,8},{5,9},{6,10},{7,11},{8,4},{9,5},... | collective-permute-start | bytes 208904 | tf_op jit(solution)/shard_map/ppermute | solution.py:310
  39.6 2.3 %collective-permute-start.15 = (s16[272,128]{1,0:T(8,128)(2,1)S(1)}, s16[272,128]{1,0:T(8,128)(2,1)S(1)}, u32[]{:S(2)}, u32[]{:S(2)}) collective-permute-start(s16[272,128]{1,0:T(8,128)(2,1)S(1)} %get-tuple-element.50), channel_id=1, source_target_pairs={{0,12},{1,13},{2,14},{3,15},{4,8},{5,9},{6,10},{7,11},{8,4},{9,5},... | collective-permute-start | bytes 208904 | tf_op jit(solution)/shard_map/ppermute | solution.py:310
  41.9 1.3 %collective-permute-start.13 = (s16[528,128]{1,0:T(8,128)(2,1)S(1)}, s16[528,128]{1,0:T(8,128)(2,1)S(1)}, u32[]{:S(2)}, u32[]{:S(2)}) collective-permute-start(s16[528,128]{1,0:T(8,128)(2,1)S(1)} %get-tuple-element.49), channel_id=1, source_target_pairs={{0,8},{1,9},{2,10},{3,11},{4,12},{5,13},{6,14},{7,15},{8,0},{9,1},... | collective-permute-start | bytes 405512 | tf_op jit(solution)/shard_map/ppermute | solution.py:310
  43.1 2.6 %collective-permute-done.14.refs_1_ = s16[272,128]{1,0:T(8,128)(2,1)S(1)} collective-permute-done((s16[272,128]{1,0:T(8,128)(2,1)S(1)}, s16[272,128]{1,0:T(8,128)(2,1)S(1)}, u32[]{:S(2)}, u32[]{:S(2)}) %collective-permute-start.14) | collective-permute-done | bytes 69664 | tf_op jit(solution)/shard_map/ppermute | solution.py:310
  45.8 1.5 %collective-permute-done.15.refs_1_ = s16[272,128]{1,0:T(8,128)(2,1)S(1)} collective-permute-done((s16[272,128]{1,0:T(8,128)(2,1)S(1)}, s16[272,128]{1,0:T(8,128)(2,1)S(1)}, u32[]{:S(2)}, u32[]{:S(2)}) %collective-permute-start.15) | collective-permute-done | bytes 69664 | tf_op jit(solution)/shard_map/ppermute | solution.py:310
  47.3 0.7 %collective-permute-done.13.refs_0_ = s16[528,128]{1,0:T(8,128)(2,1)S(1)} collective-permute-done((s16[528,128]{1,0:T(8,128)(2,1)S(1)}, s16[528,128]{1,0:T(8,128)(2,1)S(1)}, u32[]{:S(2)}, u32[]{:S(2)}) %collective-permute-start.13) | collective-permute-done | bytes 135200 | tf_op jit(solution)/shard_map/ppermute | solution.py:310
  48.0 0.7 %shard_map.66 = bf16[4,128,128]{2,1,0:T(8,128)(2,1)} custom-call(s16[528,128]{1,0:T(8,128)(2,1)S(1)} %collective-permute-done.13.refs_0_, f32[2,128,128]{2,1,0:T(8,128)S(1)} %shard_map.64.refs_2_.refs_1_, f32[2,128,128]{2,1,0:T(8,128)S(1)} %shard_map.65.refs_2_), custom_call_target="tpu_custom_call" | custom-call | bytes 1 | tf_op jit(solution)/shard_map/pallas_call | solution.py:260
  (37 shorter events, 2.9 us)
Async XLA Ops:
  0.0 3.0 %copy-start = (bf16[1,1,1,64,128,128]{5,4,3,2,1,0:T(8,128)(2,1)S(1)}, bf16[1,1,1,64,128,128]{5,4,3,2,1,0:T(8,128)(2,1)}, u32[]{:S(2)}) copy-start(bf16[1,1,1,64,128,128]{5,4,3,2,1,0:T(8,128)(2,1)} %param.4) | copy-start | bytes 6291460
  0.0 3.0 %copy-start.1 = (bf16[1,1,1,16,128,128]{5,4,3,2,1,0:T(8,128)(2,1)S(1)}, bf16[1,1,1,16,128,128]{5,4,3,2,1,0:T(8,128)(2,1)}, u32[]{:S(2)}) copy-start(bf16[1,1,1,16,128,128]{5,4,3,2,1,0:T(8,128)(2,1)} %param.5) | copy-start | bytes 1572868
  0.0 3.8 %collective-permute-start = (bf16[16,128,128]{2,1,0:T(8,128)(2,1)}, bf16[16,128,128]{2,1,0:T(8,128)(2,1)S(1)}, u32[]{:S(2)}, u32[]{:S(2)}) collective-permute-start(bf16[16,128,128]{2,1,0:T(8,128)(2,1)} %bitcast.15), channel_id=1, source_target_pairs={{0,16},{16,0},{1,17},{17,1},{2,18},{18,2},{3,19},{19,3},{4,20},{20... | collective-permute-start | bytes 1572872 | tf_op jit(solution)/shard_map/ppermute | solution.py:344
  0.5 16.8 %collective-permute-start.2 = (bf16[16,128,128]{2,1,0:T(8,128)(2,1)}, bf16[16,128,128]{2,1,0:T(8,128)(2,1)S(1)}, u32[]{:S(2)}, u32[]{:S(2)}) collective-permute-start(bf16[16,128,128]{2,1,0:T(8,128)(2,1)} %bitcast.16), channel_id=1, source_target_pairs={{0,8},{8,0},{1,9},{9,1},{2,10},{10,2},{3,11},{11,3},{4,12},{12,4},... | collective-permute-start | bytes 1572872 | tf_op jit(solution)/shard_map/ppermute | solution.py:343
  3.0 0.7 %copy-start.2 = (s32[1,1,1,2,32,16]{4,5,3,2,1,0:T(8,128)S(1)}, s32[1,1,1,2,32,16]{4,5,3,2,1,0:T(8,128)}, u32[]{:S(2)}) copy-start(s32[1,1,1,2,32,16]{4,5,3,2,1,0:T(8,128)} %param.6) | copy-start | bytes 12292
  3.0 0.7 %copy-start.3 = (s32[1,1,1,2,32,16]{4,5,3,2,1,0:T(8,128)S(1)}, s32[1,1,1,2,32,16]{4,5,3,2,1,0:T(8,128)}, u32[]{:S(2)}) copy-start(s32[1,1,1,2,32,16]{4,5,3,2,1,0:T(8,128)} %param.7) | copy-start | bytes 12292
  7.1 10.0 %collective-permute-start.3 = (s16[1040,128]{1,0:T(8,128)(2,1)S(1)}, s16[1040,128]{1,0:T(8,128)(2,1)S(1)}, u32[]{:S(2)}, u32[]{:S(2)}) collective-permute-start(s16[1040,128]{1,0:T(8,128)(2,1)S(1)} %get-tuple-element.34), channel_id=1, source_target_pairs={{0,2},{1,3},{2,0},{3,1},{4,6},{5,7},{6,4},{7,5},{8,10},{9,11},{10,... | collective-permute-start | bytes 798728 | tf_op jit(solution)/shard_map/ppermute | solution.py:305
  8.8 8.1 %collective-permute-start.4 = (s16[1040,128]{1,0:T(8,128)(2,1)S(1)}, s16[1040,128]{1,0:T(8,128)(2,1)S(1)}, u32[]{:S(2)}, u32[]{:S(2)}) collective-permute-start(s16[1040,128]{1,0:T(8,128)(2,1)S(1)} %get-tuple-element.31.refs_3_), channel_id=1, source_target_pairs={{0,1},{1,0},{2,3},{3,2},{4,5},{5,4},{6,7},{7,6},{8,9},{9,8},{10,11... | collective-permute-start | bytes 798728 | tf_op jit(solution)/shard_map/ppermute | solution.py:305
  13.3 4.0 %collective-permute-start.1 = (s32[8,128]{1,0:T(8,128)S(1)}, s32[8,128]{1,0:T(8,128)S(1)}, u32[]{:S(2)}, u32[]{:S(2)}) collective-permute-start(s32[8,128]{1,0:T(8,128)S(1)} %shard_map.51), channel_id=1, source_target_pairs={{0,8},{8,0},{1,9},{9,1},{2,10},{10,2},{3,11},{11,3},{4,12},{12,4},... | collective-permute-start | bytes 12296 | tf_op jit(solution)/shard_map/ppermute | solution.py:354
  17.3 2.1 %collective-permute-start.5 = (bf16[16,128,128]{2,1,0:T(8,128)(2,1)S(1)}, bf16[16,128,128]{2,1,0:T(8,128)(2,1)S(1)}, u32[]{:S(2)}, u32[]{:S(2)}) collective-permute-start(bf16[16,128,128]{2,1,0:T(8,128)(2,1)S(1)} %shard_map.54.refs_2_), channel_id=1, source_target_pairs={{0,16},{16,0},{1,17},{17,1},{2,18},{18,2},{3,19},{19,3},{4,20},{20... | collective-permute-start | bytes 1572872 | tf_op jit(solution)/shard_map/ppermute | solution.py:361
  17.4 11.2 %collective-permute-start.8 = (s16[528,128]{1,0:T(8,128)(2,1)S(1)}, s16[528,128]{1,0:T(8,128)(2,1)S(1)}, u32[]{:S(2)}, u32[]{:S(2)}) collective-permute-start(s16[528,128]{1,0:T(8,128)(2,1)S(1)} %get-tuple-element.36.refs_1_), channel_id=1, source_target_pairs={{0,1},{1,0},{2,3},{3,2},{4,5},{5,4},{6,7},{7,6},{8,9},{9,8},{10,11... | collective-permute-start | bytes 405512 | tf_op jit(solution)/shard_map/ppermute | solution.py:305
  19.0 9.6 %collective-permute-start.7 = (s16[528,128]{1,0:T(8,128)(2,1)S(1)}, s16[528,128]{1,0:T(8,128)(2,1)S(1)}, u32[]{:S(2)}, u32[]{:S(2)}) collective-permute-start(s16[528,128]{1,0:T(8,128)(2,1)S(1)} %get-tuple-element.35.refs_2_), channel_id=1, source_target_pairs={{0,2},{1,3},{2,0},{3,1},{4,6},{5,7},{6,4},{7,5},{8,10},{9,11},{10,... | collective-permute-start | bytes 405512 | tf_op jit(solution)/shard_map/ppermute | solution.py:305
  21.5 9.9 %collective-permute-start.6 = (s16[1040,128]{1,0:T(8,128)(2,1)S(1)}, s16[1040,128]{1,0:T(8,128)(2,1)S(1)}, u32[]{:S(2)}, u32[]{:S(2)}) collective-permute-start(s16[1040,128]{1,0:T(8,128)(2,1)S(1)} %get-tuple-element.38.refs_3_), channel_id=1, source_target_pairs={{0,2},{1,3},{2,0},{3,1},{4,6},{5,7},{6,4},{7,5},{8,10},{9,11},{10,... | collective-permute-start | bytes 798728 | tf_op jit(solution)/shard_map/ppermute | solution.py:305
  25.0 8.1 %collective-permute-start.9 = (s16[1040,128]{1,0:T(8,128)(2,1)S(1)}, s16[1040,128]{1,0:T(8,128)(2,1)S(1)}, u32[]{:S(2)}, u32[]{:S(2)}) collective-permute-start(s16[1040,128]{1,0:T(8,128)(2,1)S(1)} %shard_map.56.refs_3_), channel_id=1, source_target_pairs={{0,1},{1,0},{2,3},{3,2},{4,5},{5,4},{6,7},{7,6},{8,9},{9,8},{10,11... | collective-permute-start | bytes 798728 | tf_op jit(solution)/shard_map/ppermute | solution.py:305
  28.7 8.8 %collective-permute-start.12 = (s16[528,128]{1,0:T(8,128)(2,1)S(1)}, s16[528,128]{1,0:T(8,128)(2,1)S(1)}, u32[]{:S(2)}, u32[]{:S(2)}) collective-permute-start(s16[528,128]{1,0:T(8,128)(2,1)S(1)} %get-tuple-element.42.refs_2_), channel_id=1, source_target_pairs={{0,4},{1,5},{2,6},{3,7},{4,0},{5,1},{6,2},{7,3},{8,12},{9,13},{10,... | collective-permute-start | bytes 405512 | tf_op jit(solution)/shard_map/ppermute | solution.py:305
  31.6 6.0 %collective-permute-start.10 = (s16[528,128]{1,0:T(8,128)(2,1)S(1)}, s16[528,128]{1,0:T(8,128)(2,1)S(1)}, u32[]{:S(2)}, u32[]{:S(2)}) collective-permute-start(s16[528,128]{1,0:T(8,128)(2,1)S(1)} %get-tuple-element.45.refs_2_), channel_id=1, source_target_pairs={{0,1},{1,0},{2,3},{3,2},{4,5},{5,4},{6,7},{7,6},{8,9},{9,8},{10,11... | collective-permute-start | bytes 405512 | tf_op jit(solution)/shard_map/ppermute | solution.py:305
  33.3 6.1 %collective-permute-start.11 = (s16[528,128]{1,0:T(8,128)(2,1)S(1)}, s16[528,128]{1,0:T(8,128)(2,1)S(1)}, u32[]{:S(2)}, u32[]{:S(2)}) collective-permute-start(s16[528,128]{1,0:T(8,128)(2,1)S(1)} %get-tuple-element.47.refs_2_), channel_id=1, source_target_pairs={{0,2},{1,3},{2,0},{3,1},{4,6},{5,7},{6,4},{7,5},{8,10},{9,11},{10,... | collective-permute-start | bytes 405512 | tf_op jit(solution)/shard_map/ppermute | solution.py:305
  37.7 8.1 %collective-permute-start.14 = (s16[272,128]{1,0:T(8,128)(2,1)S(1)}, s16[272,128]{1,0:T(8,128)(2,1)S(1)}, u32[]{:S(2)}, u32[]{:S(2)}) collective-permute-start(s16[272,128]{1,0:T(8,128)(2,1)S(1)} %shard_map.62.refs_4_), channel_id=1, source_target_pairs={{0,12},{1,13},{2,14},{3,15},{4,8},{5,9},{6,10},{7,11},{8,4},{9,5},... | collective-permute-start | bytes 208904 | tf_op jit(solution)/shard_map/ppermute | solution.py:310
  39.6 7.7 %collective-permute-start.15 = (s16[272,128]{1,0:T(8,128)(2,1)S(1)}, s16[272,128]{1,0:T(8,128)(2,1)S(1)}, u32[]{:S(2)}, u32[]{:S(2)}) collective-permute-start(s16[272,128]{1,0:T(8,128)(2,1)S(1)} %get-tuple-element.50), channel_id=1, source_target_pairs={{0,12},{1,13},{2,14},{3,15},{4,8},{5,9},{6,10},{7,11},{8,4},{9,5},... | collective-permute-start | bytes 208904 | tf_op jit(solution)/shard_map/ppermute | solution.py:310
  41.9 6.1 %collective-permute-start.13 = (s16[528,128]{1,0:T(8,128)(2,1)S(1)}, s16[528,128]{1,0:T(8,128)(2,1)S(1)}, u32[]{:S(2)}, u32[]{:S(2)}) collective-permute-start(s16[528,128]{1,0:T(8,128)(2,1)S(1)} %get-tuple-element.49), channel_id=1, source_target_pairs={{0,8},{1,9},{2,10},{3,11},{4,12},{5,13},{6,14},{7,15},{8,0},{9,1},... | collective-permute-start | bytes 405512 | tf_op jit(solution)/shard_map/ppermute | solution.py:310

commit v14 on v13

--- a/solution.py
+++ b/solution.py
@@ -385,8 +385,7 @@
             streams[n] = (kept, exchange(sent, b))
         rest = less(rest, b)
 
-    own = call(sum_kernel, floats(count), (), own, after)
-    moved, top, after = [], rest[0], (own,)
+    moved, top = [], rest[0]
     for n in range(2):
         shapes = [message(sizes[n], width)] + [message(count, width)] * n
         used, used_sizes = ([streams[0]], sizes[:1]) if n == 0 else (streams, sizes)
@@ -394,6 +393,9 @@
         sent = call(cross_kernel(used_sizes, top, n), shapes, (), (*kept, *came), after)
         after = (sent[0],)
         moved.append(cross(sent[0], top))
+        if n == 0:
+            own = call(sum_kernel, floats(count), (), own, after)
+            after = (own,)
     near = cross(sent[1], None)
     early = []
     for n, (first, size) in enumerate(chunks):

time: 48.8 us -> 49.8 us (1.020)
  waiting for transfers between devices: 11 us -> 13 us
  starting transfers between devices: 21.7 us -> 20.6 us
    ppermute x9, waiting for transfers between devices: 6.24 us -> 7.64 us  [exchange(): return lax.ppermute(x, 'layer', [(i, i ^ 1 << bit) for i in range(layers)])]
    ppermute x3, waiting for transfers between devices: 4.77 us -> 5.39 us  [cross(): return lax.ppermute(x, ('col', 'layer'), perm)]
    ppermute x9, starting transfers between devices: 12.2 us -> 11.6 us  [exchange(): return lax.ppermute(x, 'layer', [(i, i ^ 1 << bit) for i in range(layers)])]
where the time goes in v14:
time: 49.8 us; the launch traced here: 49.6 us
  starting transfers between devices  20.6 us (41%)
  Pallas kernels  15 us (30%)
  waiting for transfers between devices  13 us (26%)
  local copies, waits for them, and re-layouts  0.72 us (1%)
    pallas_call x19, Pallas kernels, call(): pl.pallas_call(wrapped, out_shape=out_shape, in_specs=[pl.BlockSpec(memor...  15 us
    ppermute x9, starting transfers between devices, exchange(): return lax.ppermute(x, 'layer', [(i, i ^ 1 << bit) for i in range(layers)])  11.6 us
    ppermute x9, waiting for transfers between devices, exchange(): return lax.ppermute(x, 'layer', [(i, i ^ 1 << bit) for i in range(layers)])  7.64 us
    ppermute x3, waiting for transfers between devices, cross(): return lax.ppermute(x, ('col', 'layer'), perm)  5.39 us
    ppermute x3, starting transfers between devices, cross(): return lax.ppermute(x, ('col', 'layer'), perm)  4.7 us
    ppermute x1, starting transfers between devices, on_device(): p_x = lax.ppermute(p, 'col', swap)  2.56 us
    ppermute x1, starting transfers between devices, on_device(): lists_x = lax.ppermute(hold(lists_far, own_kept[:1]), 'col', swap)  1.24 us
  transfers between devices with their start and end apart: 16, of which 6 were waited for; matrix products, arithmetic and copies ran while one was open for 0% of the time, Pallas kernels for 29%

profile of v14, /device:TPU:0, one launch (start us, length us, event | category | flops | bytes accessed | tf_op | source)
XLA Modules:
  0.0 49.6 jit_solution(11451768602874091995)
XLA Ops:
  0.5 2.6 %collective-permute-start.2 = (bf16[16,128,128]{2,1,0:T(8,128)(2,1)}, bf16[16,128,128]{2,1,0:T(8,128)(2,1)S(1)}, u32[]{:S(2)}, u32[]{:S(2)}) collective-permute-start(bf16[16,128,128]{2,1,0:T(8,128)(2,1)} %bitcast.16), channel_id=1, source_target_pairs={{0,8},{8,0},{1,9},{9,1},{2,10},{10,2},{3,11},{11,3},{4,12},{12,4},... | collective-permute-start | bytes 1572872 | tf_op jit(solution)/shard_map/ppermute | solution.py:343
  3.0 0.7 %copy-done.2 = s32[1,1,1,2,32,16]{4,5,3,2,1,0:T(8,128)S(1)} copy-done((s32[1,1,1,2,32,16]{4,5,3,2,1,0:T(8,128)S(1)}, s32[1,1,1,2,32,16]{4,5,3,2,1,0:T(8,128)}, u32[]{:S(2)}) %copy-start.2) | copy-done | bytes 4120
  3.9 3.2 %shard_map.49 = (s16[1040,128]{1,0:T(8,128)(2,1)S(1)}, s16[1040,128]{1,0:T(8,128)(2,1)S(1)}, bf16[32,128,128]{2,1,0:T(8,128)(2,1)S(1)}) custom-call(s32[8,128]{1,0:T(8,128)S(1)} %get-tuple-element.29.refs_0_, bf16[64,128,128]{2,1,0:T(8,128)(2,1)S(1)} %bitcast.10, bf16[16,128,128]{2,1,0:T(8,128)(2,1)S(1)} %bitcast.18, ...), custom_call_target="tpu_custom_call" | custom-call | flops 5368709120 | bytes 4730880 | tf_op jit(solution)/shard_map/pallas_call | solution.py:260
  7.1 1.7 %collective-permute-start.3 = (s16[1040,128]{1,0:T(8,128)(2,1)S(1)}, s16[1040,128]{1,0:T(8,128)(2,1)S(1)}, u32[]{:S(2)}, u32[]{:S(2)}) collective-permute-start(s16[1040,128]{1,0:T(8,128)(2,1)S(1)} %get-tuple-element.34), channel_id=1, source_target_pairs={{0,2},{1,3},{2,0},{3,1},{4,6},{5,7},{6,4},{7,5},{8,10},{9,11},{10,... | collective-permute-start | bytes 798728 | tf_op jit(solution)/shard_map/ppermute | solution.py:305
  8.8 1.5 %collective-permute-start.4 = (s16[1040,128]{1,0:T(8,128)(2,1)S(1)}, s16[1040,128]{1,0:T(8,128)(2,1)S(1)}, u32[]{:S(2)}, u32[]{:S(2)}) collective-permute-start(s16[1040,128]{1,0:T(8,128)(2,1)S(1)} %get-tuple-element.31.refs_3_), channel_id=1, source_target_pairs={{0,1},{1,0},{2,3},{3,2},{4,5},{5,4},{6,7},{7,6},{8,9},{9,8},{10,11... | collective-permute-start | bytes 798728 | tf_op jit(solution)/shard_map/ppermute | solution.py:305
  10.3 3.0 %shard_map.50 = (f32[8,128,128]{2,1,0:T(8,128)S(1)}, f32[8,128,128]{2,1,0:T(8,128)S(1)}) custom-call(s32[8,128]{1,0:T(8,128)S(1)} %get-tuple-element.29.refs_0_, bf16[64,128,128]{2,1,0:T(8,128)(2,1)S(1)} %bitcast.11, bf16[32,128,128]{2,1,0:T(8,128)(2,1)S(1)} %get-tuple-element.30.refs_2_, s16[1040,128]{1,0:T(8,128)(2,1)S(1)} %get-tuple-element.31.refs_3_), custom_call_target="tpu_custom_call" | custom-call | flops 5368709120 | bytes 4198400 | tf_op jit(solution)/shard_map/pallas_call | solution.py:260
  13.3 1.2 %collective-permute-start.1 = (s32[8,128]{1,0:T(8,128)S(1)}, s32[8,128]{1,0:T(8,128)S(1)}, u32[]{:S(2)}, u32[]{:S(2)}) collective-permute-start(s32[8,128]{1,0:T(8,128)S(1)} %shard_map.51), channel_id=1, source_target_pairs={{0,8},{8,0},{1,9},{9,1},{2,10},{10,2},{3,11},{11,3},{4,12},{12,4},... | collective-permute-start | bytes 12296 | tf_op jit(solution)/shard_map/ppermute | solution.py:354
  14.5 2.4 %collective-permute-done.4.refs_1_ = s16[1040,128]{1,0:T(8,128)(2,1)S(1)} collective-permute-done((s16[1040,128]{1,0:T(8,128)(2,1)S(1)}, s16[1040,128]{1,0:T(8,128)(2,1)S(1)}, u32[]{:S(2)}, u32[]{:S(2)}) %collective-permute-start.4) | collective-permute-done | bytes 266272 | tf_op jit(solution)/shard_map/ppermute | solution.py:305
  17.4 1.6 %collective-permute-start.8 = (s16[528,128]{1,0:T(8,128)(2,1)S(1)}, s16[528,128]{1,0:T(8,128)(2,1)S(1)}, u32[]{:S(2)}, u32[]{:S(2)}) collective-permute-start(s16[528,128]{1,0:T(8,128)(2,1)S(1)} %get-tuple-element.36.refs_1_), channel_id=1, source_target_pairs={{0,1},{1,0},{2,3},{3,2},{4,5},{5,4},{6,7},{7,6},{8,9},{9,8},{10,11... | collective-permute-start | bytes 405512 | tf_op jit(solution)/shard_map/ppermute | solution.py:305
  19.4 2.0 %shard_map.55 = (s16[1040,128]{1,0:T(8,128)(2,1)S(1)}, bf16[32,128,128]{2,1,0:T(8,128)(2,1)S(1)}) custom-call(s32[8,128]{1,0:T(8,128)S(1)} %collective-permute-done.1.refs_2_.refs_0_, bf16[64,128,128]{2,1,0:T(8,128)(2,1)S(1)} %bitcast.12, bf16[16,128,128]{2,1,0:T(8,128)(2,1)S(1)} %shard_map.54.refs_2_, bf16[16,128,128]{2,1,0:T(8,128)(2,1)S(1)} %collective-permute-done.5.refs_3_), custom_call_target="tpu_custom_call" | custom-call | bytes 1 | tf_op jit(solution)/shard_map/pallas_call | solution.py:260
  21.5 1.6 %collective-permute-start.6 = (s16[1040,128]{1,0:T(8,128)(2,1)S(1)}, s16[1040,128]{1,0:T(8,128)(2,1)S(1)}, u32[]{:S(2)}, u32[]{:S(2)}) collective-permute-start(s16[1040,128]{1,0:T(8,128)(2,1)S(1)} %get-tuple-element.38.refs_3_), channel_id=1, source_target_pairs={{0,2},{1,3},{2,0},{3,1},{4,6},{5,7},{6,4},{7,5},{8,10},{9,11},{10,... | collective-permute-start | bytes 798728 | tf_op jit(solution)/shard_map/ppermute | solution.py:305
  23.1 1.9 %shard_map.56.refs_3_ = s16[1040,128]{1,0:T(8,128)(2,1)S(1)} custom-call(s32[8,128]{1,0:T(8,128)S(1)} %collective-permute-done.1.refs_2_.refs_0_, bf16[64,128,128]{2,1,0:T(8,128)(2,1)S(1)} %bitcast.13, bf16[32,128,128]{2,1,0:T(8,128)(2,1)S(1)} %get-tuple-element.37.refs_2_, s16[1040,128]{1,0:T(8,128)(2,1)S(1)} %get-tuple-element.38.refs_3_), custom_call_target="tpu_custom_call" | custom-call | bytes 1 | tf_op jit(solution)/shard_map/pallas_call | solution.py:260
  25.0 0.6 %collective-permute-start.9 = (s16[1040,128]{1,0:T(8,128)(2,1)S(1)}, s16[1040,128]{1,0:T(8,128)(2,1)S(1)}, u32[]{:S(2)}, u32[]{:S(2)}) collective-permute-start(s16[1040,128]{1,0:T(8,128)(2,1)S(1)} %shard_map.56.refs_3_), channel_id=1, source_target_pairs={{0,1},{1,0},{2,3},{3,2},{4,5},{5,4},{6,7},{7,6},{8,9},{9,8},{10,11... | collective-permute-start | bytes 798728 | tf_op jit(solution)/shard_map/ppermute | solution.py:305
  25.6 3.0 %shard_map.57 = (f32[8,128,128]{2,1,0:T(8,128)S(1)}, f32[8,128,128]{2,1,0:T(8,128)S(1)}) custom-call(s32[8,128]{1,0:T(8,128)S(1)} %collective-permute-done.1.refs_2_.refs_0_, bf16[64,128,128]{2,1,0:T(8,128)(2,1)S(1)} %bitcast.14, bf16[32,128,128]{2,1,0:T(8,128)(2,1)S(1)} %get-tuple-element.37.refs_2_, s16[1040,128]{1,0:T(8,128)(2,1)S(1)} %shard_map.56.refs_3_), custom_call_target="tpu_custom_call" | custom-call | flops 5368709120 | bytes 4198400 | tf_op jit(solution)/shard_map/pallas_call | solution.py:260
  28.7 1.6 %collective-permute-done.6.refs_1_ = s16[1040,128]{1,0:T(8,128)(2,1)S(1)} collective-permute-done((s16[1040,128]{1,0:T(8,128)(2,1)S(1)}, s16[1040,128]{1,0:T(8,128)(2,1)S(1)}, u32[]{:S(2)}, u32[]{:S(2)}) %collective-permute-start.6) | collective-permute-done | bytes 266272 | tf_op jit(solution)/shard_map/ppermute | solution.py:305
  30.5 1.1 %collective-permute-start.10 = (s16[528,128]{1,0:T(8,128)(2,1)S(1)}, s16[528,128]{1,0:T(8,128)(2,1)S(1)}, u32[]{:S(2)}, u32[]{:S(2)}) collective-permute-start(s16[528,128]{1,0:T(8,128)(2,1)S(1)} %get-tuple-element.45.refs_2_), channel_id=1, source_target_pairs={{0,1},{1,0},{2,3},{3,2},{4,5},{5,4},{6,7},{7,6},{8,9},{9,8},{10,11... | collective-permute-start | bytes 405512 | tf_op jit(solution)/shard_map/ppermute | solution.py:305
  31.6 2.6 %collective-permute-start.12 = (s16[528,128]{1,0:T(8,128)(2,1)S(1)}, s16[528,128]{1,0:T(8,128)(2,1)S(1)}, u32[]{:S(2)}, u32[]{:S(2)}) collective-permute-start(s16[528,128]{1,0:T(8,128)(2,1)S(1)} %get-tuple-element.42.refs_2_), channel_id=1, source_target_pairs={{0,4},{1,5},{2,6},{3,7},{4,0},{5,1},{6,2},{7,3},{8,12},{9,13},{10,... | collective-permute-start | bytes 405512 | tf_op jit(solution)/shard_map/ppermute | solution.py:305
  34.8 1.0 %collective-permute-done.10.refs_1_.refs_2_ = s16[528,128]{1,0:T(8,128)(2,1)S(1)} collective-permute-done((s16[528,128]{1,0:T(8,128)(2,1)S(1)}, s16[528,128]{1,0:T(8,128)(2,1)S(1)}, u32[]{:S(2)}, u32[]{:S(2)}) %collective-permute-start.10) | collective-permute-done | bytes 135200 | tf_op jit(solution)/shard_map/ppermute | solution.py:305
  36.0 3.3 %collective-permute-start.14 = (s16[272,128]{1,0:T(8,128)(2,1)S(1)}, s16[272,128]{1,0:T(8,128)(2,1)S(1)}, u32[]{:S(2)}, u32[]{:S(2)}) collective-permute-start(s16[272,128]{1,0:T(8,128)(2,1)S(1)} %shard_map.61.refs_2_), channel_id=1, source_target_pairs={{0,12},{1,13},{2,14},{3,15},{4,8},{5,9},{6,10},{7,11},{8,4},{9,5},... | collective-permute-start | bytes 208904 | tf_op jit(solution)/shard_map/ppermute | solution.py:310
  39.2 1.6 %collective-permute-done.12.refs_1_ = s16[528,128]{1,0:T(8,128)(2,1)S(1)} collective-permute-done((s16[528,128]{1,0:T(8,128)(2,1)S(1)}, s16[528,128]{1,0:T(8,128)(2,1)S(1)}, u32[]{:S(2)}, u32[]{:S(2)}) %collective-permute-start.12) | collective-permute-done | bytes 135200 | tf_op jit(solution)/shard_map/ppermute | solution.py:305
  40.8 1.0 %collective-permute-done.11.refs_3_ = s16[528,128]{1,0:T(8,128)(2,1)S(1)} collective-permute-done((s16[528,128]{1,0:T(8,128)(2,1)S(1)}, s16[528,128]{1,0:T(8,128)(2,1)S(1)}, u32[]{:S(2)}, u32[]{:S(2)}) %collective-permute-start.11) | collective-permute-done | bytes 135200 | tf_op jit(solution)/shard_map/ppermute | solution.py:305
  42.6 0.9 %collective-permute-start.13 = (s16[528,128]{1,0:T(8,128)(2,1)S(1)}, s16[528,128]{1,0:T(8,128)(2,1)S(1)}, u32[]{:S(2)}, u32[]{:S(2)}) collective-permute-start(s16[528,128]{1,0:T(8,128)(2,1)S(1)} %get-tuple-element.49), channel_id=1, source_target_pairs={{0,8},{1,9},{2,10},{3,11},{4,12},{5,13},{6,14},{7,15},{8,0},{9,1},... | collective-permute-start | bytes 405512 | tf_op jit(solution)/shard_map/ppermute | solution.py:310
  43.5 5.3 %collective-permute-done.15.refs_1_ = s16[272,128]{1,0:T(8,128)(2,1)S(1)} collective-permute-done((s16[272,128]{1,0:T(8,128)(2,1)S(1)}, s16[272,128]{1,0:T(8,128)(2,1)S(1)}, u32[]{:S(2)}, u32[]{:S(2)}) %collective-permute-start.15) | collective-permute-done | bytes 69664 | tf_op jit(solution)/shard_map/ppermute | solution.py:310
  48.9 0.7 %shard_map.66 = bf16[4,128,128]{2,1,0:T(8,128)(2,1)} custom-call(s16[528,128]{1,0:T(8,128)(2,1)S(1)} %collective-permute-done.13.refs_0_, f32[2,128,128]{2,1,0:T(8,128)S(1)} %shard_map.64.refs_2_.refs_1_, f32[2,128,128]{2,1,0:T(8,128)S(1)} %shard_map.65.refs_2_), custom_call_target="tpu_custom_call" | custom-call | bytes 1 | tf_op jit(solution)/shard_map/pallas_call | solution.py:260
  (37 shorter events, 3.4 us)
Async XLA Ops:
  0.0 3.0 %copy-start = (bf16[1,1,1,64,128,128]{5,4,3,2,1,0:T(8,128)(2,1)S(1)}, bf16[1,1,1,64,128,128]{5,4,3,2,1,0:T(8,128)(2,1)}, u32[]{:S(2)}) copy-start(bf16[1,1,1,64,128,128]{5,4,3,2,1,0:T(8,128)(2,1)} %param.4) | copy-start | bytes 6291460
  0.0 3.0 %copy-start.1 = (bf16[1,1,1,16,128,128]{5,4,3,2,1,0:T(8,128)(2,1)S(1)}, bf16[1,1,1,16,128,128]{5,4,3,2,1,0:T(8,128)(2,1)}, u32[]{:S(2)}) copy-start(bf16[1,1,1,16,128,128]{5,4,3,2,1,0:T(8,128)(2,1)} %param.5) | copy-start | bytes 1572868
  0.0 3.8 %collective-permute-start = (bf16[16,128,128]{2,1,0:T(8,128)(2,1)}, bf16[16,128,128]{2,1,0:T(8,128)(2,1)S(1)}, u32[]{:S(2)}, u32[]{:S(2)}) collective-permute-start(bf16[16,128,128]{2,1,0:T(8,128)(2,1)} %bitcast.15), channel_id=1, source_target_pairs={{0,16},{16,0},{1,17},{17,1},{2,18},{18,2},{3,19},{19,3},{4,20},{20... | collective-permute-start | bytes 1572872 | tf_op jit(solution)/shard_map/ppermute | solution.py:344
  0.5 16.8 %collective-permute-start.2 = (bf16[16,128,128]{2,1,0:T(8,128)(2,1)}, bf16[16,128,128]{2,1,0:T(8,128)(2,1)S(1)}, u32[]{:S(2)}, u32[]{:S(2)}) collective-permute-start(bf16[16,128,128]{2,1,0:T(8,128)(2,1)} %bitcast.16), channel_id=1, source_target_pairs={{0,8},{8,0},{1,9},{9,1},{2,10},{10,2},{3,11},{11,3},{4,12},{12,4},... | collective-permute-start | bytes 1572872 | tf_op jit(solution)/shard_map/ppermute | solution.py:343
  3.0 0.7 %copy-start.2 = (s32[1,1,1,2,32,16]{4,5,3,2,1,0:T(8,128)S(1)}, s32[1,1,1,2,32,16]{4,5,3,2,1,0:T(8,128)}, u32[]{:S(2)}) copy-start(s32[1,1,1,2,32,16]{4,5,3,2,1,0:T(8,128)} %param.6) | copy-start | bytes 12292
  3.0 0.7 %copy-start.3 = (s32[1,1,1,2,32,16]{4,5,3,2,1,0:T(8,128)S(1)}, s32[1,1,1,2,32,16]{4,5,3,2,1,0:T(8,128)}, u32[]{:S(2)}) copy-start(s32[1,1,1,2,32,16]{4,5,3,2,1,0:T(8,128)} %param.7) | copy-start | bytes 12292
  7.1 10.0 %collective-permute-start.3 = (s16[1040,128]{1,0:T(8,128)(2,1)S(1)}, s16[1040,128]{1,0:T(8,128)(2,1)S(1)}, u32[]{:S(2)}, u32[]{:S(2)}) collective-permute-start(s16[1040,128]{1,0:T(8,128)(2,1)S(1)} %get-tuple-element.34), channel_id=1, source_target_pairs={{0,2},{1,3},{2,0},{3,1},{4,6},{5,7},{6,4},{7,5},{8,10},{9,11},{10,... | collective-permute-start | bytes 798728 | tf_op jit(solution)/shard_map/ppermute | solution.py:305
  8.8 8.1 %collective-permute-start.4 = (s16[1040,128]{1,0:T(8,128)(2,1)S(1)}, s16[1040,128]{1,0:T(8,128)(2,1)S(1)}, u32[]{:S(2)}, u32[]{:S(2)}) collective-permute-start(s16[1040,128]{1,0:T(8,128)(2,1)S(1)} %get-tuple-element.31.refs_3_), channel_id=1, source_target_pairs={{0,1},{1,0},{2,3},{3,2},{4,5},{5,4},{6,7},{7,6},{8,9},{9,8},{10,11... | collective-permute-start | bytes 798728 | tf_op jit(solution)/shard_map/ppermute | solution.py:305
  13.3 4.0 %collective-permute-start.1 = (s32[8,128]{1,0:T(8,128)S(1)}, s32[8,128]{1,0:T(8,128)S(1)}, u32[]{:S(2)}, u32[]{:S(2)}) collective-permute-start(s32[8,128]{1,0:T(8,128)S(1)} %shard_map.51), channel_id=1, source_target_pairs={{0,8},{8,0},{1,9},{9,1},{2,10},{10,2},{3,11},{11,3},{4,12},{12,4},... | collective-permute-start | bytes 12296 | tf_op jit(solution)/shard_map/ppermute | solution.py:354
  17.3 2.1 %collective-permute-start.5 = (bf16[16,128,128]{2,1,0:T(8,128)(2,1)S(1)}, bf16[16,128,128]{2,1,0:T(8,128)(2,1)S(1)}, u32[]{:S(2)}, u32[]{:S(2)}) collective-permute-start(bf16[16,128,128]{2,1,0:T(8,128)(2,1)S(1)} %shard_map.54.refs_2_), channel_id=1, source_target_pairs={{0,16},{16,0},{1,17},{17,1},{2,18},{18,2},{3,19},{19,3},{4,20},{20... | collective-permute-start | bytes 1572872 | tf_op jit(solution)/shard_map/ppermute | solution.py:361
  17.4 11.2 %collective-permute-start.8 = (s16[528,128]{1,0:T(8,128)(2,1)S(1)}, s16[528,128]{1,0:T(8,128)(2,1)S(1)}, u32[]{:S(2)}, u32[]{:S(2)}) collective-permute-start(s16[528,128]{1,0:T(8,128)(2,1)S(1)} %get-tuple-element.36.refs_1_), channel_id=1, source_target_pairs={{0,1},{1,0},{2,3},{3,2},{4,5},{5,4},{6,7},{7,6},{8,9},{9,8},{10,11... | collective-permute-start | bytes 405512 | tf_op jit(solution)/shard_map/ppermute | solution.py:305
  19.0 9.6 %collective-permute-start.7 = (s16[528,128]{1,0:T(8,128)(2,1)S(1)}, s16[528,128]{1,0:T(8,128)(2,1)S(1)}, u32[]{:S(2)}, u32[]{:S(2)}) collective-permute-start(s16[528,128]{1,0:T(8,128)(2,1)S(1)} %get-tuple-element.35.refs_2_), channel_id=1, source_target_pairs={{0,2},{1,3},{2,0},{3,1},{4,6},{5,7},{6,4},{7,5},{8,10},{9,11},{10,... | collective-permute-start | bytes 405512 | tf_op jit(solution)/shard_map/ppermute | solution.py:305
  21.5 8.9 %collective-permute-start.6 = (s16[1040,128]{1,0:T(8,128)(2,1)S(1)}, s16[1040,128]{1,0:T(8,128)(2,1)S(1)}, u32[]{:S(2)}, u32[]{:S(2)}) collective-permute-start(s16[1040,128]{1,0:T(8,128)(2,1)S(1)} %get-tuple-element.38.refs_3_), channel_id=1, source_target_pairs={{0,2},{1,3},{2,0},{3,1},{4,6},{5,7},{6,4},{7,5},{8,10},{9,11},{10,... | collective-permute-start | bytes 798728 | tf_op jit(solution)/shard_map/ppermute | solution.py:305
  25.0 9.1 %collective-permute-start.9 = (s16[1040,128]{1,0:T(8,128)(2,1)S(1)}, s16[1040,128]{1,0:T(8,128)(2,1)S(1)}, u32[]{:S(2)}, u32[]{:S(2)}) collective-permute-start(s16[1040,128]{1,0:T(8,128)(2,1)S(1)} %shard_map.56.refs_3_), channel_id=1, source_target_pairs={{0,1},{1,0},{2,3},{3,2},{4,5},{5,4},{6,7},{7,6},{8,9},{9,8},{10,11... | collective-permute-start | bytes 798728 | tf_op jit(solution)/shard_map/ppermute | solution.py:305
  30.5 5.4 %collective-permute-start.10 = (s16[528,128]{1,0:T(8,128)(2,1)S(1)}, s16[528,128]{1,0:T(8,128)(2,1)S(1)}, u32[]{:S(2)}, u32[]{:S(2)}) collective-permute-start(s16[528,128]{1,0:T(8,128)(2,1)S(1)} %get-tuple-element.45.refs_2_), channel_id=1, source_target_pairs={{0,1},{1,0},{2,3},{3,2},{4,5},{5,4},{6,7},{7,6},{8,9},{9,8},{10,11... | collective-permute-start | bytes 405512 | tf_op jit(solution)/shard_map/ppermute | solution.py:305
  31.6 9.2 %collective-permute-start.12 = (s16[528,128]{1,0:T(8,128)(2,1)S(1)}, s16[528,128]{1,0:T(8,128)(2,1)S(1)}, u32[]{:S(2)}, u32[]{:S(2)}) collective-permute-start(s16[528,128]{1,0:T(8,128)(2,1)S(1)} %get-tuple-element.42.refs_2_), channel_id=1, source_target_pairs={{0,4},{1,5},{2,6},{3,7},{4,0},{5,1},{6,2},{7,3},{8,12},{9,13},{10,... | collective-permute-start | bytes 405512 | tf_op jit(solution)/shard_map/ppermute | solution.py:305
  34.3 7.5 %collective-permute-start.11 = (s16[528,128]{1,0:T(8,128)(2,1)S(1)}, s16[528,128]{1,0:T(8,128)(2,1)S(1)}, u32[]{:S(2)}, u32[]{:S(2)}) collective-permute-start(s16[528,128]{1,0:T(8,128)(2,1)S(1)} %get-tuple-element.47.refs_2_), channel_id=1, source_target_pairs={{0,2},{1,3},{2,0},{3,1},{4,6},{5,7},{6,4},{7,5},{8,10},{9,11},{10,... | collective-permute-start | bytes 405512 | tf_op jit(solution)/shard_map/ppermute | solution.py:305
  36.0 7.5 %collective-permute-start.14 = (s16[272,128]{1,0:T(8,128)(2,1)S(1)}, s16[272,128]{1,0:T(8,128)(2,1)S(1)}, u32[]{:S(2)}, u32[]{:S(2)}) collective-permute-start(s16[272,128]{1,0:T(8,128)(2,1)S(1)} %shard_map.61.refs_2_), channel_id=1, source_target_pairs={{0,12},{1,13},{2,14},{3,15},{4,8},{5,9},{6,10},{7,11},{8,4},{9,5},... | collective-permute-start | bytes 208904 | tf_op jit(solution)/shard_map/ppermute | solution.py:310
  42.0 6.9 %collective-permute-start.15 = (s16[272,128]{1,0:T(8,128)(2,1)S(1)}, s16[272,128]{1,0:T(8,128)(2,1)S(1)}, u32[]{:S(2)}, u32[]{:S(2)}) collective-permute-start(s16[272,128]{1,0:T(8,128)(2,1)S(1)} %get-tuple-element.50), channel_id=1, source_target_pairs={{0,12},{1,13},{2,14},{3,15},{4,8},{5,9},{6,10},{7,11},{8,4},{9,5},... | collective-permute-start | bytes 208904 | tf_op jit(solution)/shard_map/ppermute | solution.py:310
  42.6 6.3 %collective-permute-start.13 = (s16[528,128]{1,0:T(8,128)(2,1)S(1)}, s16[528,128]{1,0:T(8,128)(2,1)S(1)}, u32[]{:S(2)}, u32[]{:S(2)}) collective-permute-start(s16[528,128]{1,0:T(8,128)(2,1)S(1)} %get-tuple-element.49), channel_id=1, source_target_pairs={{0,8},{1,9},{2,10},{3,11},{4,12},{5,13},{6,14},{7,15},{8,0},{9,1},... | collective-permute-start | bytes 405512 | tf_op jit(solution)/shard_map/ppermute | solution.py:310

commit v15 on v13

--- a/solution.py
+++ b/solution.py
@@ -140,6 +140,13 @@
     return kernel
 
 
+def split_kernel(in_ref, *out_refs):
+    at = 0
+    for ref in out_refs:
+        ref[...] = in_ref[pl.ds(at, ref.shape[0])]
+        at += ref.shape[0]
+
+
 def keep_kernel(fan, slots, count, chunks, bits):
     def kernel(lists_ref, a_ref, p_ref, *out_refs):
         find = finder(lists_ref, fan, slots)
@@ -357,10 +364,11 @@
         sent, part = second(own_kept[n], own_came[n], sizes[n], own_bits[n], after)
         parts.append(part)
         after = (sent,)
-    p_x = hold(p_x, (*after, lists_x))
-    p_xr = lax.ppermute(p_x, "row", swap)
-
-    (made, joined), came_0 = send(lists_x, (a, p_x, p_xr), (0,), other_bits[:1], True, (), 0)
+    pieces = [jax.ShapeDtypeStruct((held // 2, width, width), p.dtype)] * 2
+    pieces = call(split_kernel, pieces, (), (p_x,), (*after, lists_x))
+    p_xr = [lax.ppermute(x, "row", swap) for x in pieces]
+
+    (made, joined), came_0 = send(lists_x, (a, p_x, *p_xr), (0,), other_bits[:1], True, (), 0)
     (made,), came_1 = send(lists_x, (a, joined), (1,), other_bits[1:], False, (made,), 0)
     other_came = came_0 + came_1
     other_kept = keep(lists_x, (a, joined), other_bits, (made,), 1)

time: 48.8 us -> 48.8 us (level)
  starting transfers between devices: 21.7 us -> 22.2 us
  waiting for transfers between devices: 11 us -> 10.5 us
    ppermute x1 -> x2, starting transfers between devices: 0.07 us -> 0.57 us  [on_device(): p_xr = [lax.ppermute(x, 'row', swap) for x in pieces]]
    pallas_call x19 -> x20, Pallas kernels: 15 us -> 15.1 us  [call(): pl.pallas_call(wrapped, out_shape=out_shape, in_specs=[pl.BlockSpec(memor...]
  transfers between devices with their start and end apart: 16 -> 17, of which waited for: 6 -> 5; matrix products, arithmetic and copies ran while one was open for 0% -> 0% of each run, Pallas kernels for 29% -> 29%
where the time goes in v15:
time: 48.8 us; the launch traced here: 48.7 us
  starting transfers between devices  22.2 us (45%)
  Pallas kernels  15.1 us (31%)
  waiting for transfers between devices  10.5 us (22%)
  local copies, waits for them, and re-layouts  0.72 us (1%)
    pallas_call x20, Pallas kernels, call(): pl.pallas_call(wrapped, out_shape=out_shape, in_specs=[pl.BlockSpec(memor...  15.1 us
    ppermute x9, starting transfers between devices, exchange(): return lax.ppermute(x, 'layer', [(i, i ^ 1 << bit) for i in range(layers)])  12.1 us
    ppermute x9, waiting for transfers between devices, exchange(): return lax.ppermute(x, 'layer', [(i, i ^ 1 << bit) for i in range(layers)])  5.78 us
    ppermute x3, starting transfers between devices, cross(): return lax.ppermute(x, ('col', 'layer'), perm)  5.28 us
    ppermute x3, waiting for transfers between devices, cross(): return lax.ppermute(x, ('col', 'layer'), perm)  4.68 us
    ppermute x1, starting transfers between devices, on_device(): p_x = lax.ppermute(p, 'col', swap)  2.56 us
    ppermute x1, starting transfers between devices, on_device(): lists_x = lax.ppermute(hold(lists_far, own_kept[:1]), 'col', swap)  1.24 us
  transfers between devices with their start and end apart: 17, of which 5 were waited for; matrix products, arithmetic and copies ran while one was open for 0% of the time, Pallas kernels for 29%

profile of v15, /device:TPU:0, one launch (start us, length us, event | category | flops | bytes accessed | tf_op | source)
XLA Modules:
  0.0 48.7 jit_solution(5129881068584688973)
XLA Ops:
  0.5 2.6 %collective-permute-start.2 = (bf16[16,128,128]{2,1,0:T(8,128)(2,1)}, bf16[16,128,128]{2,1,0:T(8,128)(2,1)S(1)}, u32[]{:S(2)}, u32[]{:S(2)}) collective-permute-start(bf16[16,128,128]{2,1,0:T(8,128)(2,1)} %bitcast.16), channel_id=1, source_target_pairs={{0,8},{8,0},{1,9},{9,1},{2,10},{10,2},{3,11},{11,3},{4,12},{12,4},... | collective-permute-start | bytes 1572872 | tf_op jit(solution)/shard_map/ppermute | solution.py:350
  3.0 0.7 %copy-done.2 = s32[1,1,1,2,32,16]{4,5,3,2,1,0:T(8,128)S(1)} copy-done((s32[1,1,1,2,32,16]{4,5,3,2,1,0:T(8,128)S(1)}, s32[1,1,1,2,32,16]{4,5,3,2,1,0:T(8,128)}, u32[]{:S(2)}) %copy-start.2) | copy-done | bytes 4120
  3.9 3.2 %shard_map.49 = (s16[1040,128]{1,0:T(8,128)(2,1)S(1)}, s16[1040,128]{1,0:T(8,128)(2,1)S(1)}, bf16[32,128,128]{2,1,0:T(8,128)(2,1)S(1)}) custom-call(s32[8,128]{1,0:T(8,128)S(1)} %get-tuple-element.31.refs_0_, bf16[64,128,128]{2,1,0:T(8,128)(2,1)S(1)} %bitcast.10, bf16[16,128,128]{2,1,0:T(8,128)(2,1)S(1)} %bitcast.18, ...), custom_call_target="tpu_custom_call" | custom-call | flops 5368709120 | bytes 4730880 | tf_op jit(solution)/shard_map/pallas_call | solution.py:267
  7.1 1.7 %collective-permute-start.3 = (s16[1040,128]{1,0:T(8,128)(2,1)S(1)}, s16[1040,128]{1,0:T(8,128)(2,1)S(1)}, u32[]{:S(2)}, u32[]{:S(2)}) collective-permute-start(s16[1040,128]{1,0:T(8,128)(2,1)S(1)} %get-tuple-element.36), channel_id=1, source_target_pairs={{0,2},{1,3},{2,0},{3,1},{4,6},{5,7},{6,4},{7,5},{8,10},{9,11},{10,... | collective-permute-start | bytes 798728 | tf_op jit(solution)/shard_map/ppermute | solution.py:312
  8.8 1.5 %collective-permute-start.4 = (s16[1040,128]{1,0:T(8,128)(2,1)S(1)}, s16[1040,128]{1,0:T(8,128)(2,1)S(1)}, u32[]{:S(2)}, u32[]{:S(2)}) collective-permute-start(s16[1040,128]{1,0:T(8,128)(2,1)S(1)} %get-tuple-element.33.refs_3_), channel_id=1, source_target_pairs={{0,1},{1,0},{2,3},{3,2},{4,5},{5,4},{6,7},{7,6},{8,9},{9,8},{10,11... | collective-permute-start | bytes 798728 | tf_op jit(solution)/shard_map/ppermute | solution.py:312
  10.3 3.0 %shard_map.50 = (f32[8,128,128]{2,1,0:T(8,128)S(1)}, f32[8,128,128]{2,1,0:T(8,128)S(1)}) custom-call(s32[8,128]{1,0:T(8,128)S(1)} %get-tuple-element.31.refs_0_, bf16[64,128,128]{2,1,0:T(8,128)(2,1)S(1)} %bitcast.11, bf16[32,128,128]{2,1,0:T(8,128)(2,1)S(1)} %get-tuple-element.32.refs_2_, s16[1040,128]{1,0:T(8,128)(2,1)S(1)} %get-tuple-element.33.refs_3_), custom_call_target="tpu_custom_call" | custom-call | flops 5368709120 | bytes 4198400 | tf_op jit(solution)/shard_map/pallas_call | solution.py:267
  13.3 1.2 %collective-permute-start.1 = (s32[8,128]{1,0:T(8,128)S(1)}, s32[8,128]{1,0:T(8,128)S(1)}, u32[]{:S(2)}, u32[]{:S(2)}) collective-permute-start(s32[8,128]{1,0:T(8,128)S(1)} %shard_map.51), channel_id=1, source_target_pairs={{0,8},{8,0},{1,9},{9,1},{2,10},{10,2},{3,11},{11,3},{4,12},{12,4},... | collective-permute-start | bytes 12296 | tf_op jit(solution)/shard_map/ppermute | solution.py:361
  14.5 2.4 %collective-permute-done.4.refs_1_ = s16[1040,128]{1,0:T(8,128)(2,1)S(1)} collective-permute-done((s16[1040,128]{1,0:T(8,128)(2,1)S(1)}, s16[1040,128]{1,0:T(8,128)(2,1)S(1)}, u32[]{:S(2)}, u32[]{:S(2)}) %collective-permute-start.4) | collective-permute-done | bytes 266272 | tf_op jit(solution)/shard_map/ppermute | solution.py:312
  17.9 1.5 %collective-permute-start.9 = (s16[528,128]{1,0:T(8,128)(2,1)S(1)}, s16[528,128]{1,0:T(8,128)(2,1)S(1)}, u32[]{:S(2)}, u32[]{:S(2)}) collective-permute-start(s16[528,128]{1,0:T(8,128)(2,1)S(1)} %get-tuple-element.38.refs_1_), channel_id=1, source_target_pairs={{0,1},{1,0},{2,3},{3,2},{4,5},{5,4},{6,7},{7,6},{8,9},{9,8},{10,11... | collective-permute-start | bytes 405512 | tf_op jit(solution)/shard_map/ppermute | solution.py:312
  19.9 2.0 %shard_map.55 = (s16[1040,128]{1,0:T(8,128)(2,1)S(1)}, bf16[32,128,128]{2,1,0:T(8,128)(2,1)S(1)}) custom-call(s32[8,128]{1,0:T(8,128)S(1)} %collective-permute-done.1.refs_2_.refs_0_, bf16[64,128,128]{2,1,0:T(8,128)(2,1)S(1)} %bitcast.12, bf16[16,128,128]{2,1,0:T(8,128)(2,1)S(1)} %collective-permute-done.2.refs_0_.refs_2_, ...), custom_call_target="tpu_custom_call" | custom-call | bytes 1 | tf_op jit(solution)/shard_map/pallas_call | solution.py:267
  21.9 1.6 %collective-permute-start.7 = (s16[1040,128]{1,0:T(8,128)(2,1)S(1)}, s16[1040,128]{1,0:T(8,128)(2,1)S(1)}, u32[]{:S(2)}, u32[]{:S(2)}) collective-permute-start(s16[1040,128]{1,0:T(8,128)(2,1)S(1)} %get-tuple-element.42.refs_3_), channel_id=1, source_target_pairs={{0,2},{1,3},{2,0},{3,1},{4,6},{5,7},{6,4},{7,5},{8,10},{9,11},{10,... | collective-permute-start | bytes 798728 | tf_op jit(solution)/shard_map/ppermute | solution.py:312
  23.6 1.9 %shard_map.56.refs_3_ = s16[1040,128]{1,0:T(8,128)(2,1)S(1)} custom-call(s32[8,128]{1,0:T(8,128)S(1)} %collective-permute-done.1.refs_2_.refs_0_, bf16[64,128,128]{2,1,0:T(8,128)(2,1)S(1)} %bitcast.13, bf16[32,128,128]{2,1,0:T(8,128)(2,1)S(1)} %get-tuple-element.41.refs_2_, s16[1040,128]{1,0:T(8,128)(2,1)S(1)} %get-tuple-element.42.refs_3_), custom_call_target="tpu_custom_call" | custom-call | bytes 1 | tf_op jit(solution)/shard_map/pallas_call | solution.py:267
  25.5 0.6 %collective-permute-start.10 = (s16[1040,128]{1,0:T(8,128)(2,1)S(1)}, s16[1040,128]{1,0:T(8,128)(2,1)S(1)}, u32[]{:S(2)}, u32[]{:S(2)}) collective-permute-start(s16[1040,128]{1,0:T(8,128)(2,1)S(1)} %shard_map.56.refs_3_), channel_id=1, source_target_pairs={{0,1},{1,0},{2,3},{3,2},{4,5},{5,4},{6,7},{7,6},{8,9},{9,8},{10,11... | collective-permute-start | bytes 798728 | tf_op jit(solution)/shard_map/ppermute | solution.py:312
  26.1 3.0 %shard_map.57 = (f32[8,128,128]{2,1,0:T(8,128)S(1)}, f32[8,128,128]{2,1,0:T(8,128)S(1)}) custom-call(s32[8,128]{1,0:T(8,128)S(1)} %collective-permute-done.1.refs_2_.refs_0_, bf16[64,128,128]{2,1,0:T(8,128)(2,1)S(1)} %bitcast.14, bf16[32,128,128]{2,1,0:T(8,128)(2,1)S(1)} %get-tuple-element.41.refs_2_, s16[1040,128]{1,0:T(8,128)(2,1)S(1)} %shard_map.56.refs_3_), custom_call_target="tpu_custom_call" | custom-call | flops 5368709120 | bytes 4198400 | tf_op jit(solution)/shard_map/pallas_call | solution.py:267
  29.2 2.7 %collective-permute-start.13 = (s16[528,128]{1,0:T(8,128)(2,1)S(1)}, s16[528,128]{1,0:T(8,128)(2,1)S(1)}, u32[]{:S(2)}, u32[]{:S(2)}) collective-permute-start(s16[528,128]{1,0:T(8,128)(2,1)S(1)} %get-tuple-element.46.refs_2_), channel_id=1, source_target_pairs={{0,4},{1,5},{2,6},{3,7},{4,0},{5,1},{6,2},{7,3},{8,12},{9,13},{10,... | collective-permute-start | bytes 405512 | tf_op jit(solution)/shard_map/ppermute | solution.py:312
  32.0 1.6 %collective-permute-start.11 = (s16[528,128]{1,0:T(8,128)(2,1)S(1)}, s16[528,128]{1,0:T(8,128)(2,1)S(1)}, u32[]{:S(2)}, u32[]{:S(2)}) collective-permute-start(s16[528,128]{1,0:T(8,128)(2,1)S(1)} %get-tuple-element.49.refs_2_), channel_id=1, source_target_pairs={{0,1},{1,0},{2,3},{3,2},{4,5},{5,4},{6,7},{7,6},{8,9},{9,8},{10,11... | collective-permute-start | bytes 405512 | tf_op jit(solution)/shard_map/ppermute | solution.py:312
  34.3 3.3 %collective-permute-done.13.refs_1_ = s16[528,128]{1,0:T(8,128)(2,1)S(1)} collective-permute-done((s16[528,128]{1,0:T(8,128)(2,1)S(1)}, s16[528,128]{1,0:T(8,128)(2,1)S(1)}, u32[]{:S(2)}, u32[]{:S(2)}) %collective-permute-start.13) | collective-permute-done | bytes 135200 | tf_op jit(solution)/shard_map/ppermute | solution.py:312
  37.8 2.2 %collective-permute-start.15 = (s16[272,128]{1,0:T(8,128)(2,1)S(1)}, s16[272,128]{1,0:T(8,128)(2,1)S(1)}, u32[]{:S(2)}, u32[]{:S(2)}) collective-permute-start(s16[272,128]{1,0:T(8,128)(2,1)S(1)} %shard_map.62.refs_4_), channel_id=1, source_target_pairs={{0,12},{1,13},{2,14},{3,15},{4,8},{5,9},{6,10},{7,11},{8,4},{9,5},... | collective-permute-start | bytes 208904 | tf_op jit(solution)/shard_map/ppermute | solution.py:317
  40.1 2.4 %collective-permute-start.16 = (s16[272,128]{1,0:T(8,128)(2,1)S(1)}, s16[272,128]{1,0:T(8,128)(2,1)S(1)}, u32[]{:S(2)}, u32[]{:S(2)}) collective-permute-start(s16[272,128]{1,0:T(8,128)(2,1)S(1)} %get-tuple-element.54), channel_id=1, source_target_pairs={{0,12},{1,13},{2,14},{3,15},{4,8},{5,9},{6,10},{7,11},{8,4},{9,5},... | collective-permute-start | bytes 208904 | tf_op jit(solution)/shard_map/ppermute | solution.py:317
  42.5 0.7 %collective-permute-start.14 = (s16[528,128]{1,0:T(8,128)(2,1)S(1)}, s16[528,128]{1,0:T(8,128)(2,1)S(1)}, u32[]{:S(2)}, u32[]{:S(2)}) collective-permute-start(s16[528,128]{1,0:T(8,128)(2,1)S(1)} %get-tuple-element.53), channel_id=1, source_target_pairs={{0,8},{1,9},{2,10},{3,11},{4,12},{5,13},{6,14},{7,15},{8,0},{9,1},... | collective-permute-start | bytes 405512 | tf_op jit(solution)/shard_map/ppermute | solution.py:317
  43.2 2.5 %collective-permute-done.15.refs_1_ = s16[272,128]{1,0:T(8,128)(2,1)S(1)} collective-permute-done((s16[272,128]{1,0:T(8,128)(2,1)S(1)}, s16[272,128]{1,0:T(8,128)(2,1)S(1)}, u32[]{:S(2)}, u32[]{:S(2)}) %collective-permute-start.15) | collective-permute-done | bytes 69664 | tf_op jit(solution)/shard_map/ppermute | solution.py:317
  45.7 1.5 %collective-permute-done.16.refs_1_ = s16[272,128]{1,0:T(8,128)(2,1)S(1)} collective-permute-done((s16[272,128]{1,0:T(8,128)(2,1)S(1)}, s16[272,128]{1,0:T(8,128)(2,1)S(1)}, u32[]{:S(2)}, u32[]{:S(2)}) %collective-permute-start.16) | collective-permute-done | bytes 69664 | tf_op jit(solution)/shard_map/ppermute | solution.py:317
  47.3 0.7 %collective-permute-done.14.refs_0_ = s16[528,128]{1,0:T(8,128)(2,1)S(1)} collective-permute-done((s16[528,128]{1,0:T(8,128)(2,1)S(1)}, s16[528,128]{1,0:T(8,128)(2,1)S(1)}, u32[]{:S(2)}, u32[]{:S(2)}) %collective-permute-start.14) | collective-permute-done | bytes 135200 | tf_op jit(solution)/shard_map/ppermute | solution.py:317
  48.0 0.7 %shard_map.66 = bf16[4,128,128]{2,1,0:T(8,128)(2,1)} custom-call(s16[528,128]{1,0:T(8,128)(2,1)S(1)} %collective-permute-done.14.refs_0_, f32[2,128,128]{2,1,0:T(8,128)S(1)} %shard_map.64.refs_2_.refs_1_, f32[2,128,128]{2,1,0:T(8,128)S(1)} %shard_map.65.refs_2_), custom_call_target="tpu_custom_call" | custom-call | bytes 1 | tf_op jit(solution)/shard_map/pallas_call | solution.py:267
  (39 shorter events, 3.3 us)
Async XLA Ops:
  0.0 3.0 %copy-start = (bf16[1,1,1,64,128,128]{5,4,3,2,1,0:T(8,128)(2,1)S(1)}, bf16[1,1,1,64,128,128]{5,4,3,2,1,0:T(8,128)(2,1)}, u32[]{:S(2)}) copy-start(bf16[1,1,1,64,128,128]{5,4,3,2,1,0:T(8,128)(2,1)} %param.4) | copy-start | bytes 6291460
  0.0 3.0 %copy-start.1 = (bf16[1,1,1,16,128,128]{5,4,3,2,1,0:T(8,128)(2,1)S(1)}, bf16[1,1,1,16,128,128]{5,4,3,2,1,0:T(8,128)(2,1)}, u32[]{:S(2)}) copy-start(bf16[1,1,1,16,128,128]{5,4,3,2,1,0:T(8,128)(2,1)} %param.5) | copy-start | bytes 1572868
  0.0 3.8 %collective-permute-start = (bf16[16,128,128]{2,1,0:T(8,128)(2,1)}, bf16[16,128,128]{2,1,0:T(8,128)(2,1)S(1)}, u32[]{:S(2)}, u32[]{:S(2)}) collective-permute-start(bf16[16,128,128]{2,1,0:T(8,128)(2,1)} %bitcast.15), channel_id=1, source_target_pairs={{0,16},{16,0},{1,17},{17,1},{2,18},{18,2},{3,19},{19,3},{4,20},{20... | collective-permute-start | bytes 1572872 | tf_op jit(solution)/shard_map/ppermute | solution.py:351
  0.5 16.8 %collective-permute-start.2 = (bf16[16,128,128]{2,1,0:T(8,128)(2,1)}, bf16[16,128,128]{2,1,0:T(8,128)(2,1)S(1)}, u32[]{:S(2)}, u32[]{:S(2)}) collective-permute-start(bf16[16,128,128]{2,1,0:T(8,128)(2,1)} %bitcast.16), channel_id=1, source_target_pairs={{0,8},{8,0},{1,9},{9,1},{2,10},{10,2},{3,11},{11,3},{4,12},{12,4},... | collective-permute-start | bytes 1572872 | tf_op jit(solution)/shard_map/ppermute | solution.py:350
  3.0 0.7 %copy-start.2 = (s32[1,1,1,2,32,16]{4,5,3,2,1,0:T(8,128)S(1)}, s32[1,1,1,2,32,16]{4,5,3,2,1,0:T(8,128)}, u32[]{:S(2)}) copy-start(s32[1,1,1,2,32,16]{4,5,3,2,1,0:T(8,128)} %param.6) | copy-start | bytes 12292
  3.0 0.7 %copy-start.3 = (s32[1,1,1,2,32,16]{4,5,3,2,1,0:T(8,128)S(1)}, s32[1,1,1,2,32,16]{4,5,3,2,1,0:T(8,128)}, u32[]{:S(2)}) copy-start(s32[1,1,1,2,32,16]{4,5,3,2,1,0:T(8,128)} %param.7) | copy-start | bytes 12292
  7.1 10.0 %collective-permute-start.3 = (s16[1040,128]{1,0:T(8,128)(2,1)S(1)}, s16[1040,128]{1,0:T(8,128)(2,1)S(1)}, u32[]{:S(2)}, u32[]{:S(2)}) collective-permute-start(s16[1040,128]{1,0:T(8,128)(2,1)S(1)} %get-tuple-element.36), channel_id=1, source_target_pairs={{0,2},{1,3},{2,0},{3,1},{4,6},{5,7},{6,4},{7,5},{8,10},{9,11},{10,... | collective-permute-start | bytes 798728 | tf_op jit(solution)/shard_map/ppermute | solution.py:312
  8.8 8.1 %collective-permute-start.4 = (s16[1040,128]{1,0:T(8,128)(2,1)S(1)}, s16[1040,128]{1,0:T(8,128)(2,1)S(1)}, u32[]{:S(2)}, u32[]{:S(2)}) collective-permute-start(s16[1040,128]{1,0:T(8,128)(2,1)S(1)} %get-tuple-element.33.refs_3_), channel_id=1, source_target_pairs={{0,1},{1,0},{2,3},{3,2},{4,5},{5,4},{6,7},{7,6},{8,9},{9,8},{10,11... | collective-permute-start | bytes 798728 | tf_op jit(solution)/shard_map/ppermute | solution.py:312
  13.3 4.0 %collective-permute-start.1 = (s32[8,128]{1,0:T(8,128)S(1)}, s32[8,128]{1,0:T(8,128)S(1)}, u32[]{:S(2)}, u32[]{:S(2)}) collective-permute-start(s32[8,128]{1,0:T(8,128)S(1)} %shard_map.51), channel_id=1, source_target_pairs={{0,8},{8,0},{1,9},{9,1},{2,10},{10,2},{3,11},{11,3},{4,12},{12,4},... | collective-permute-start | bytes 12296 | tf_op jit(solution)/shard_map/ppermute | solution.py:361
  17.3 2.5 %collective-permute-start.5 = (bf16[8,128,128]{2,1,0:T(8,128)(2,1)S(1)}, bf16[8,128,128]{2,1,0:T(8,128)(2,1)S(1)}, u32[]{:S(2)}, u32[]{:S(2)}) collective-permute-start(bf16[8,128,128]{2,1,0:T(8,128)(2,1)S(1)} %get-tuple-element.39), channel_id=1, source_target_pairs={{0,16},{16,0},{1,17},{17,1},{2,18},{18,2},{3,19},{19,3},{4,20},{20... | collective-permute-start | bytes 786440 | tf_op jit(solution)/shard_map/ppermute | solution.py:369
  17.4 2.5 %collective-permute-start.6 = (bf16[8,128,128]{2,1,0:T(8,128)(2,1)S(1)}, bf16[8,128,128]{2,1,0:T(8,128)(2,1)S(1)}, u32[]{:S(2)}, u32[]{:S(2)}) collective-permute-start(bf16[8,128,128]{2,1,0:T(8,128)(2,1)S(1)} %get-tuple-element.40), channel_id=1, source_target_pairs={{0,16},{16,0},{1,17},{17,1},{2,18},{18,2},{3,19},{19,3},{4,20},{20... | collective-permute-start | bytes 786440 | tf_op jit(solution)/shard_map/ppermute | solution.py:369
  17.9 11.1 %collective-permute-start.9 = (s16[528,128]{1,0:T(8,128)(2,1)S(1)}, s16[528,128]{1,0:T(8,128)(2,1)S(1)}, u32[]{:S(2)}, u32[]{:S(2)}) collective-permute-start(s16[528,128]{1,0:T(8,128)(2,1)S(1)} %get-tuple-element.38.refs_1_), channel_id=1, source_target_pairs={{0,1},{1,0},{2,3},{3,2},{4,5},{5,4},{6,7},{7,6},{8,9},{9,8},{10,11... | collective-permute-start | bytes 405512 | tf_op jit(solution)/shard_map/ppermute | solution.py:312
  19.4 9.6 %collective-permute-start.8 = (s16[528,128]{1,0:T(8,128)(2,1)S(1)}, s16[528,128]{1,0:T(8,128)(2,1)S(1)}, u32[]{:S(2)}, u32[]{:S(2)}) collective-permute-start(s16[528,128]{1,0:T(8,128)(2,1)S(1)} %get-tuple-element.37.refs_2_), channel_id=1, source_target_pairs={{0,2},{1,3},{2,0},{3,1},{4,6},{5,7},{6,4},{7,5},{8,10},{9,11},{10,... | collective-permute-start | bytes 405512 | tf_op jit(solution)/shard_map/ppermute | solution.py:312
  21.9 9.9 %collective-permute-start.7 = (s16[1040,128]{1,0:T(8,128)(2,1)S(1)}, s16[1040,128]{1,0:T(8,128)(2,1)S(1)}, u32[]{:S(2)}, u32[]{:S(2)}) collective-permute-start(s16[1040,128]{1,0:T(8,128)(2,1)S(1)} %get-tuple-element.42.refs_3_), channel_id=1, source_target_pairs={{0,2},{1,3},{2,0},{3,1},{4,6},{5,7},{6,4},{7,5},{8,10},{9,11},{10,... | collective-permute-start | bytes 798728 | tf_op jit(solution)/shard_map/ppermute | solution.py:312
  25.5 8.1 %collective-permute-start.10 = (s16[1040,128]{1,0:T(8,128)(2,1)S(1)}, s16[1040,128]{1,0:T(8,128)(2,1)S(1)}, u32[]{:S(2)}, u32[]{:S(2)}) collective-permute-start(s16[1040,128]{1,0:T(8,128)(2,1)S(1)} %shard_map.56.refs_3_), channel_id=1, source_target_pairs={{0,1},{1,0},{2,3},{3,2},{4,5},{5,4},{6,7},{7,6},{8,9},{9,8},{10,11... | collective-permute-start | bytes 798728 | tf_op jit(solution)/shard_map/ppermute | solution.py:312
  29.2 8.4 %collective-permute-start.13 = (s16[528,128]{1,0:T(8,128)(2,1)S(1)}, s16[528,128]{1,0:T(8,128)(2,1)S(1)}, u32[]{:S(2)}, u32[]{:S(2)}) collective-permute-start(s16[528,128]{1,0:T(8,128)(2,1)S(1)} %get-tuple-element.46.refs_2_), channel_id=1, source_target_pairs={{0,4},{1,5},{2,6},{3,7},{4,0},{5,1},{6,2},{7,3},{8,12},{9,13},{10,... | collective-permute-start | bytes 405512 | tf_op jit(solution)/shard_map/ppermute | solution.py:312
  32.0 5.7 %collective-permute-start.11 = (s16[528,128]{1,0:T(8,128)(2,1)S(1)}, s16[528,128]{1,0:T(8,128)(2,1)S(1)}, u32[]{:S(2)}, u32[]{:S(2)}) collective-permute-start(s16[528,128]{1,0:T(8,128)(2,1)S(1)} %get-tuple-element.49.refs_2_), channel_id=1, source_target_pairs={{0,1},{1,0},{2,3},{3,2},{4,5},{5,4},{6,7},{7,6},{8,9},{9,8},{10,11... | collective-permute-start | bytes 405512 | tf_op jit(solution)/shard_map/ppermute | solution.py:312
  33.8 6.2 %collective-permute-start.12 = (s16[528,128]{1,0:T(8,128)(2,1)S(1)}, s16[528,128]{1,0:T(8,128)(2,1)S(1)}, u32[]{:S(2)}, u32[]{:S(2)}) collective-permute-start(s16[528,128]{1,0:T(8,128)(2,1)S(1)} %get-tuple-element.51.refs_2_), channel_id=1, source_target_pairs={{0,2},{1,3},{2,0},{3,1},{4,6},{5,7},{6,4},{7,5},{8,10},{9,11},{10,... | collective-permute-start | bytes 405512 | tf_op jit(solution)/shard_map/ppermute | solution.py:312
  37.8 7.9 %collective-permute-start.15 = (s16[272,128]{1,0:T(8,128)(2,1)S(1)}, s16[272,128]{1,0:T(8,128)(2,1)S(1)}, u32[]{:S(2)}, u32[]{:S(2)}) collective-permute-start(s16[272,128]{1,0:T(8,128)(2,1)S(1)} %shard_map.62.refs_4_), channel_id=1, source_target_pairs={{0,12},{1,13},{2,14},{3,15},{4,8},{5,9},{6,10},{7,11},{8,4},{9,5},... | collective-permute-start | bytes 208904 | tf_op jit(solution)/shard_map/ppermute | solution.py:317
  40.1 7.1 %collective-permute-start.16 = (s16[272,128]{1,0:T(8,128)(2,1)S(1)}, s16[272,128]{1,0:T(8,128)(2,1)S(1)}, u32[]{:S(2)}, u32[]{:S(2)}) collective-permute-start(s16[272,128]{1,0:T(8,128)(2,1)S(1)} %get-tuple-element.54), channel_id=1, source_target_pairs={{0,12},{1,13},{2,14},{3,15},{4,8},{5,9},{6,10},{7,11},{8,4},{9,5},... | collective-permute-start | bytes 208904 | tf_op jit(solution)/shard_map/ppermute | solution.py:317
  42.5 5.4 %collective-permute-start.14 = (s16[528,128]{1,0:T(8,128)(2,1)S(1)}, s16[528,128]{1,0:T(8,128)(2,1)S(1)}, u32[]{:S(2)}, u32[]{:S(2)}) collective-permute-start(s16[528,128]{1,0:T(8,128)(2,1)S(1)} %get-tuple-element.53), channel_id=1, source_target_pairs={{0,8},{1,9},{2,10},{3,11},{4,12},{5,13},{6,14},{7,15},{8,0},{9,1},... | collective-permute-start | bytes 405512 | tf_op jit(solution)/shard_map/ppermute | solution.py:317

commit v16 on v15

--- a/solution.py
+++ b/solution.py
@@ -336,7 +336,7 @@
         kept, came = zip(*parts)
         return call(add_kernel(sizes, rest, bit), shapes, (), (*kept, *came), after)
 
-    own_bits, other_bits = (0, 1), (1, 0)
+    own_bits, other_bits = (0, 1), (0, 1)
     sizes = [size for _, size in chunks]
     every = list(range(bits))
 

time: 48.8 us -> 50.4 us (1.033)
  waiting for transfers between devices: 10.5 us -> 13.4 us
  starting transfers between devices: 22.2 us -> 20.9 us
    ppermute x9, waiting for transfers between devices: 5.78 us -> 8.14 us  [exchange(): return lax.ppermute(x, 'layer', [(i, i ^ 1 << bit) for i in range(layers)])]
    ppermute x9, starting transfers between devices: 12.1 us -> 11 us  [exchange(): return lax.ppermute(x, 'layer', [(i, i ^ 1 << bit) for i in range(layers)])]
    ppermute x3, waiting for transfers between devices: 4.68 us -> 5.25 us  [cross(): return lax.ppermute(x, ('col', 'layer'), perm)]
  transfers between devices with their start and end apart: 17 -> 17, of which waited for: 5 -> 6; matrix products, arithmetic and copies ran while one was open for 0% -> 0% of each run, Pallas kernels for 29% -> 28%
where the time goes in v16:
time: 50.4 us; the launch traced here: 50.3 us
  starting transfers between devices  20.9 us (41%)
  Pallas kernels  15 us (30%)
  waiting for transfers between devices  13.4 us (27%)
  local copies, waits for them, and re-layouts  0.72 us (1%)
    pallas_call x20, Pallas kernels, call(): pl.pallas_call(wrapped, out_shape=out_shape, in_specs=[pl.BlockSpec(memor...  15 us
    ppermute x9, starting transfers between devices, exchange(): return lax.ppermute(x, 'layer', [(i, i ^ 1 << bit) for i in range(layers)])  11 us
    ppermute x9, waiting for transfers between devices, exchange(): return lax.ppermute(x, 'layer', [(i, i ^ 1 << bit) for i in range(layers)])  8.14 us
    ppermute x3, waiting for transfers between devices, cross(): return lax.ppermute(x, ('col', 'layer'), perm)  5.25 us
    ppermute x3, starting transfers between devices, cross(): return lax.ppermute(x, ('col', 'layer'), perm)  5.01 us
    ppermute x1, starting transfers between devices, on_device(): p_x = lax.ppermute(p, 'col', swap)  2.56 us
    ppermute x1, starting transfers between devices, on_device(): lists_x = lax.ppermute(hold(lists_far, own_kept[:1]), 'col', swap)  1.24 us
  transfers between devices with their start and end apart: 17, of which 6 were waited for; matrix products, arithmetic and copies ran while one was open for 0% of the time, Pallas kernels for 28%

profile of v16, /device:TPU:0, one launch (start us, length us, event | category | flops | bytes accessed | tf_op | source)
XLA Modules:
  0.0 50.3 jit_solution(17716224041781082944)
XLA Ops:
  0.5 2.6 %collective-permute-start.2 = (bf16[16,128,128]{2,1,0:T(8,128)(2,1)}, bf16[16,128,128]{2,1,0:T(8,128)(2,1)S(1)}, u32[]{:S(2)}, u32[]{:S(2)}) collective-permute-start(bf16[16,128,128]{2,1,0:T(8,128)(2,1)} %bitcast.16), channel_id=1, source_target_pairs={{0,8},{8,0},{1,9},{9,1},{2,10},{10,2},{3,11},{11,3},{4,12},{12,4},... | collective-permute-start | bytes 1572872 | tf_op jit(solution)/shard_map/ppermute | solution.py:350
  3.0 0.7 %copy-done.2 = s32[1,1,1,2,32,16]{4,5,3,2,1,0:T(8,128)S(1)} copy-done((s32[1,1,1,2,32,16]{4,5,3,2,1,0:T(8,128)S(1)}, s32[1,1,1,2,32,16]{4,5,3,2,1,0:T(8,128)}, u32[]{:S(2)}) %copy-start.2) | copy-done | bytes 4120
  3.9 3.2 %shard_map.49 = (s16[1040,128]{1,0:T(8,128)(2,1)S(1)}, s16[1040,128]{1,0:T(8,128)(2,1)S(1)}, bf16[32,128,128]{2,1,0:T(8,128)(2,1)S(1)}) custom-call(s32[8,128]{1,0:T(8,128)S(1)} %get-tuple-element.31.refs_0_, bf16[64,128,128]{2,1,0:T(8,128)(2,1)S(1)} %bitcast.10, bf16[16,128,128]{2,1,0:T(8,128)(2,1)S(1)} %bitcast.18, ...), custom_call_target="tpu_custom_call" | custom-call | flops 5368709120 | bytes 4730880 | tf_op jit(solution)/shard_map/pallas_call | solution.py:267
  7.1 1.7 %collective-permute-start.3 = (s16[1040,128]{1,0:T(8,128)(2,1)S(1)}, s16[1040,128]{1,0:T(8,128)(2,1)S(1)}, u32[]{:S(2)}, u32[]{:S(2)}) collective-permute-start(s16[1040,128]{1,0:T(8,128)(2,1)S(1)} %get-tuple-element.36), channel_id=1, source_target_pairs={{0,2},{1,3},{2,0},{3,1},{4,6},{5,7},{6,4},{7,5},{8,10},{9,11},{10,... | collective-permute-start | bytes 798728 | tf_op jit(solution)/shard_map/ppermute | solution.py:312
  8.8 1.5 %collective-permute-start.4 = (s16[1040,128]{1,0:T(8,128)(2,1)S(1)}, s16[1040,128]{1,0:T(8,128)(2,1)S(1)}, u32[]{:S(2)}, u32[]{:S(2)}) collective-permute-start(s16[1040,128]{1,0:T(8,128)(2,1)S(1)} %get-tuple-element.33.refs_3_), channel_id=1, source_target_pairs={{0,1},{1,0},{2,3},{3,2},{4,5},{5,4},{6,7},{7,6},{8,9},{9,8},{10,11... | collective-permute-start | bytes 798728 | tf_op jit(solution)/shard_map/ppermute | solution.py:312
  10.3 3.0 %shard_map.50 = (f32[8,128,128]{2,1,0:T(8,128)S(1)}, f32[8,128,128]{2,1,0:T(8,128)S(1)}) custom-call(s32[8,128]{1,0:T(8,128)S(1)} %get-tuple-element.31.refs_0_, bf16[64,128,128]{2,1,0:T(8,128)(2,1)S(1)} %bitcast.11, bf16[32,128,128]{2,1,0:T(8,128)(2,1)S(1)} %get-tuple-element.32.refs_2_, s16[1040,128]{1,0:T(8,128)(2,1)S(1)} %get-tuple-element.33.refs_3_), custom_call_target="tpu_custom_call" | custom-call | flops 5368709120 | bytes 4198400 | tf_op jit(solution)/shard_map/pallas_call | solution.py:267
  13.3 1.2 %collective-permute-start.1 = (s32[8,128]{1,0:T(8,128)S(1)}, s32[8,128]{1,0:T(8,128)S(1)}, u32[]{:S(2)}, u32[]{:S(2)}) collective-permute-start(s32[8,128]{1,0:T(8,128)S(1)} %shard_map.51), channel_id=1, source_target_pairs={{0,8},{8,0},{1,9},{9,1},{2,10},{10,2},{3,11},{11,3},{4,12},{12,4},... | collective-permute-start | bytes 12296 | tf_op jit(solution)/shard_map/ppermute | solution.py:361
  14.5 2.4 %collective-permute-done.4.refs_1_ = s16[1040,128]{1,0:T(8,128)(2,1)S(1)} collective-permute-done((s16[1040,128]{1,0:T(8,128)(2,1)S(1)}, s16[1040,128]{1,0:T(8,128)(2,1)S(1)}, u32[]{:S(2)}, u32[]{:S(2)}) %collective-permute-start.4) | collective-permute-done | bytes 266272 | tf_op jit(solution)/shard_map/ppermute | solution.py:312
  17.9 1.5 %collective-permute-start.9 = (s16[528,128]{1,0:T(8,128)(2,1)S(1)}, s16[528,128]{1,0:T(8,128)(2,1)S(1)}, u32[]{:S(2)}, u32[]{:S(2)}) collective-permute-start(s16[528,128]{1,0:T(8,128)(2,1)S(1)} %get-tuple-element.38.refs_1_), channel_id=1, source_target_pairs={{0,1},{1,0},{2,3},{3,2},{4,5},{5,4},{6,7},{7,6},{8,9},{9,8},{10,11... | collective-permute-start | bytes 405512 | tf_op jit(solution)/shard_map/ppermute | solution.py:312
  19.9 2.0 %shard_map.55 = (s16[1040,128]{1,0:T(8,128)(2,1)S(1)}, bf16[32,128,128]{2,1,0:T(8,128)(2,1)S(1)}) custom-call(s32[8,128]{1,0:T(8,128)S(1)} %collective-permute-done.1.refs_2_.refs_0_, bf16[64,128,128]{2,1,0:T(8,128)(2,1)S(1)} %bitcast.12, bf16[16,128,128]{2,1,0:T(8,128)(2,1)S(1)} %collective-permute-done.2.refs_0_.refs_2_, ...), custom_call_target="tpu_custom_call" | custom-call | bytes 1 | tf_op jit(solution)/shard_map/pallas_call | solution.py:267
  21.9 1.0 %collective-permute-start.7 = (s16[1040,128]{1,0:T(8,128)(2,1)S(1)}, s16[1040,128]{1,0:T(8,128)(2,1)S(1)}, u32[]{:S(2)}, u32[]{:S(2)}) collective-permute-start(s16[1040,128]{1,0:T(8,128)(2,1)S(1)} %get-tuple-element.42.refs_3_), channel_id=1, source_target_pairs={{0,1},{1,0},{2,3},{3,2},{4,5},{5,4},{6,7},{7,6},{8,9},{9,8},{10,11... | collective-permute-start | bytes 798728 | tf_op jit(solution)/shard_map/ppermute | solution.py:312
  22.9 1.9 %shard_map.56.refs_3_ = s16[1040,128]{1,0:T(8,128)(2,1)S(1)} custom-call(s32[8,128]{1,0:T(8,128)S(1)} %collective-permute-done.1.refs_2_.refs_0_, bf16[64,128,128]{2,1,0:T(8,128)(2,1)S(1)} %bitcast.13, bf16[32,128,128]{2,1,0:T(8,128)(2,1)S(1)} %get-tuple-element.41.refs_2_, s16[1040,128]{1,0:T(8,128)(2,1)S(1)} %get-tuple-element.42.refs_3_), custom_call_target="tpu_custom_call" | custom-call | bytes 1 | tf_op jit(solution)/shard_map/pallas_call | solution.py:267
  24.8 1.2 %collective-permute-start.10 = (s16[1040,128]{1,0:T(8,128)(2,1)S(1)}, s16[1040,128]{1,0:T(8,128)(2,1)S(1)}, u32[]{:S(2)}, u32[]{:S(2)}) collective-permute-start(s16[1040,128]{1,0:T(8,128)(2,1)S(1)} %shard_map.56.refs_3_), channel_id=1, source_target_pairs={{0,2},{1,3},{2,0},{3,1},{4,6},{5,7},{6,4},{7,5},{8,10},{9,11},{10,... | collective-permute-start | bytes 798728 | tf_op jit(solution)/shard_map/ppermute | solution.py:312
  26.0 3.0 %shard_map.57 = (f32[8,128,128]{2,1,0:T(8,128)S(1)}, f32[8,128,128]{2,1,0:T(8,128)S(1)}) custom-call(s32[8,128]{1,0:T(8,128)S(1)} %collective-permute-done.1.refs_2_.refs_0_, bf16[64,128,128]{2,1,0:T(8,128)(2,1)S(1)} %bitcast.14, bf16[32,128,128]{2,1,0:T(8,128)(2,1)S(1)} %get-tuple-element.41.refs_2_, s16[1040,128]{1,0:T(8,128)(2,1)S(1)} %shard_map.56.refs_3_), custom_call_target="tpu_custom_call" | custom-call | flops 5368709120 | bytes 4198400 | tf_op jit(solution)/shard_map/pallas_call | solution.py:267
  29.2 2.7 %collective-permute-start.13 = (s16[528,128]{1,0:T(8,128)(2,1)S(1)}, s16[528,128]{1,0:T(8,128)(2,1)S(1)}, u32[]{:S(2)}, u32[]{:S(2)}) collective-permute-start(s16[528,128]{1,0:T(8,128)(2,1)S(1)} %get-tuple-element.46.refs_2_), channel_id=1, source_target_pairs={{0,4},{1,5},{2,6},{3,7},{4,0},{5,1},{6,2},{7,3},{8,12},{9,13},{10,... | collective-permute-start | bytes 405512 | tf_op jit(solution)/shard_map/ppermute | solution.py:312
  32.0 0.9 %collective-permute-start.11 = (s16[528,128]{1,0:T(8,128)(2,1)S(1)}, s16[528,128]{1,0:T(8,128)(2,1)S(1)}, u32[]{:S(2)}, u32[]{:S(2)}) collective-permute-start(s16[528,128]{1,0:T(8,128)(2,1)S(1)} %get-tuple-element.49.refs_2_), channel_id=1, source_target_pairs={{0,2},{1,3},{2,0},{3,1},{4,6},{5,7},{6,4},{7,5},{8,10},{9,11},{10,... | collective-permute-start | bytes 405512 | tf_op jit(solution)/shard_map/ppermute | solution.py:312
  33.0 4.1 %collective-permute-done.10.refs_1_ = s16[1040,128]{1,0:T(8,128)(2,1)S(1)} collective-permute-done((s16[1040,128]{1,0:T(8,128)(2,1)S(1)}, s16[1040,128]{1,0:T(8,128)(2,1)S(1)}, u32[]{:S(2)}, u32[]{:S(2)}) %collective-permute-start.10) | collective-permute-done | bytes 266272 | tf_op jit(solution)/shard_map/ppermute | solution.py:312
  37.4 1.5 %collective-permute-done.11.refs_1_.refs_2_ = s16[528,128]{1,0:T(8,128)(2,1)S(1)} collective-permute-done((s16[528,128]{1,0:T(8,128)(2,1)S(1)}, s16[528,128]{1,0:T(8,128)(2,1)S(1)}, u32[]{:S(2)}, u32[]{:S(2)}) %collective-permute-start.11) | collective-permute-done | bytes 135200 | tf_op jit(solution)/shard_map/ppermute | solution.py:312
  38.9 3.3 %collective-permute-start.15 = (s16[272,128]{1,0:T(8,128)(2,1)S(1)}, s16[272,128]{1,0:T(8,128)(2,1)S(1)}, u32[]{:S(2)}, u32[]{:S(2)}) collective-permute-start(s16[272,128]{1,0:T(8,128)(2,1)S(1)} %shard_map.62.refs_4_), channel_id=1, source_target_pairs={{0,12},{1,13},{2,14},{3,15},{4,8},{5,9},{6,10},{7,11},{8,4},{9,5},... | collective-permute-start | bytes 208904 | tf_op jit(solution)/shard_map/ppermute | solution.py:317
  42.5 0.6 %collective-permute-start.16 = (s16[272,128]{1,0:T(8,128)(2,1)S(1)}, s16[272,128]{1,0:T(8,128)(2,1)S(1)}, u32[]{:S(2)}, u32[]{:S(2)}) collective-permute-start(s16[272,128]{1,0:T(8,128)(2,1)S(1)} %get-tuple-element.54), channel_id=1, source_target_pairs={{0,12},{1,13},{2,14},{3,15},{4,8},{5,9},{6,10},{7,11},{8,4},{9,5},... | collective-permute-start | bytes 208904 | tf_op jit(solution)/shard_map/ppermute | solution.py:317
  43.0 1.2 %collective-permute-start.14 = (s16[528,128]{1,0:T(8,128)(2,1)S(1)}, s16[528,128]{1,0:T(8,128)(2,1)S(1)}, u32[]{:S(2)}, u32[]{:S(2)}) collective-permute-start(s16[528,128]{1,0:T(8,128)(2,1)S(1)} %get-tuple-element.53), channel_id=1, source_target_pairs={{0,8},{1,9},{2,10},{3,11},{4,12},{5,13},{6,14},{7,15},{8,0},{9,1},... | collective-permute-start | bytes 405512 | tf_op jit(solution)/shard_map/ppermute | solution.py:317
  44.2 2.8 %collective-permute-done.15.refs_1_ = s16[272,128]{1,0:T(8,128)(2,1)S(1)} collective-permute-done((s16[272,128]{1,0:T(8,128)(2,1)S(1)}, s16[272,128]{1,0:T(8,128)(2,1)S(1)}, u32[]{:S(2)}, u32[]{:S(2)}) %collective-permute-start.15) | collective-permute-done | bytes 69664 | tf_op jit(solution)/shard_map/ppermute | solution.py:317
  47.0 2.5 %collective-permute-done.16.refs_1_ = s16[272,128]{1,0:T(8,128)(2,1)S(1)} collective-permute-done((s16[272,128]{1,0:T(8,128)(2,1)S(1)}, s16[272,128]{1,0:T(8,128)(2,1)S(1)}, u32[]{:S(2)}, u32[]{:S(2)}) %collective-permute-start.16) | collective-permute-done | bytes 69664 | tf_op jit(solution)/shard_map/ppermute | solution.py:317
  49.6 0.7 %shard_map.66 = bf16[4,128,128]{2,1,0:T(8,128)(2,1)} custom-call(s16[528,128]{1,0:T(8,128)(2,1)S(1)} %collective-permute-done.14.refs_0_, f32[2,128,128]{2,1,0:T(8,128)S(1)} %shard_map.64.refs_2_.refs_1_, f32[2,128,128]{2,1,0:T(8,128)S(1)} %shard_map.65.refs_2_), custom_call_target="tpu_custom_call" | custom-call | bytes 1 | tf_op jit(solution)/shard_map/pallas_call | solution.py:267
  (39 shorter events, 3.0 us)
Async XLA Ops:
  0.0 3.0 %copy-start = (bf16[1,1,1,64,128,128]{5,4,3,2,1,0:T(8,128)(2,1)S(1)}, bf16[1,1,1,64,128,128]{5,4,3,2,1,0:T(8,128)(2,1)}, u32[]{:S(2)}) copy-start(bf16[1,1,1,64,128,128]{5,4,3,2,1,0:T(8,128)(2,1)} %param.4) | copy-start | bytes 6291460
  0.0 3.0 %copy-start.1 = (bf16[1,1,1,16,128,128]{5,4,3,2,1,0:T(8,128)(2,1)S(1)}, bf16[1,1,1,16,128,128]{5,4,3,2,1,0:T(8,128)(2,1)}, u32[]{:S(2)}) copy-start(bf16[1,1,1,16,128,128]{5,4,3,2,1,0:T(8,128)(2,1)} %param.5) | copy-start | bytes 1572868
  0.0 3.8 %collective-permute-start = (bf16[16,128,128]{2,1,0:T(8,128)(2,1)}, bf16[16,128,128]{2,1,0:T(8,128)(2,1)S(1)}, u32[]{:S(2)}, u32[]{:S(2)}) collective-permute-start(bf16[16,128,128]{2,1,0:T(8,128)(2,1)} %bitcast.15), channel_id=1, source_target_pairs={{0,16},{16,0},{1,17},{17,1},{2,18},{18,2},{3,19},{19,3},{4,20},{20... | collective-permute-start | bytes 1572872 | tf_op jit(solution)/shard_map/ppermute | solution.py:351
  0.5 16.8 %collective-permute-start.2 = (bf16[16,128,128]{2,1,0:T(8,128)(2,1)}, bf16[16,128,128]{2,1,0:T(8,128)(2,1)S(1)}, u32[]{:S(2)}, u32[]{:S(2)}) collective-permute-start(bf16[16,128,128]{2,1,0:T(8,128)(2,1)} %bitcast.16), channel_id=1, source_target_pairs={{0,8},{8,0},{1,9},{9,1},{2,10},{10,2},{3,11},{11,3},{4,12},{12,4},... | collective-permute-start | bytes 1572872 | tf_op jit(solution)/shard_map/ppermute | solution.py:350
  3.0 0.7 %copy-start.2 = (s32[1,1,1,2,32,16]{4,5,3,2,1,0:T(8,128)S(1)}, s32[1,1,1,2,32,16]{4,5,3,2,1,0:T(8,128)}, u32[]{:S(2)}) copy-start(s32[1,1,1,2,32,16]{4,5,3,2,1,0:T(8,128)} %param.6) | copy-start | bytes 12292
  3.0 0.7 %copy-start.3 = (s32[1,1,1,2,32,16]{4,5,3,2,1,0:T(8,128)S(1)}, s32[1,1,1,2,32,16]{4,5,3,2,1,0:T(8,128)}, u32[]{:S(2)}) copy-start(s32[1,1,1,2,32,16]{4,5,3,2,1,0:T(8,128)} %param.7) | copy-start | bytes 12292
  7.1 10.0 %collective-permute-start.3 = (s16[1040,128]{1,0:T(8,128)(2,1)S(1)}, s16[1040,128]{1,0:T(8,128)(2,1)S(1)}, u32[]{:S(2)}, u32[]{:S(2)}) collective-permute-start(s16[1040,128]{1,0:T(8,128)(2,1)S(1)} %get-tuple-element.36), channel_id=1, source_target_pairs={{0,2},{1,3},{2,0},{3,1},{4,6},{5,7},{6,4},{7,5},{8,10},{9,11},{10,... | collective-permute-start | bytes 798728 | tf_op jit(solution)/shard_map/ppermute | solution.py:312
  8.8 8.1 %collective-permute-start.4 = (s16[1040,128]{1,0:T(8,128)(2,1)S(1)}, s16[1040,128]{1,0:T(8,128)(2,1)S(1)}, u32[]{:S(2)}, u32[]{:S(2)}) collective-permute-start(s16[1040,128]{1,0:T(8,128)(2,1)S(1)} %get-tuple-element.33.refs_3_), channel_id=1, source_target_pairs={{0,1},{1,0},{2,3},{3,2},{4,5},{5,4},{6,7},{7,6},{8,9},{9,8},{10,11... | collective-permute-start | bytes 798728 | tf_op jit(solution)/shard_map/ppermute | solution.py:312
  13.3 4.0 %collective-permute-start.1 = (s32[8,128]{1,0:T(8,128)S(1)}, s32[8,128]{1,0:T(8,128)S(1)}, u32[]{:S(2)}, u32[]{:S(2)}) collective-permute-start(s32[8,128]{1,0:T(8,128)S(1)} %shard_map.51), channel_id=1, source_target_pairs={{0,8},{8,0},{1,9},{9,1},{2,10},{10,2},{3,11},{11,3},{4,12},{12,4},... | collective-permute-start | bytes 12296 | tf_op jit(solution)/shard_map/ppermute | solution.py:361
  17.3 2.5 %collective-permute-start.5 = (bf16[8,128,128]{2,1,0:T(8,128)(2,1)S(1)}, bf16[8,128,128]{2,1,0:T(8,128)(2,1)S(1)}, u32[]{:S(2)}, u32[]{:S(2)}) collective-permute-start(bf16[8,128,128]{2,1,0:T(8,128)(2,1)S(1)} %get-tuple-element.39), channel_id=1, source_target_pairs={{0,16},{16,0},{1,17},{17,1},{2,18},{18,2},{3,19},{19,3},{4,20},{20... | collective-permute-start | bytes 786440 | tf_op jit(solution)/shard_map/ppermute | solution.py:369
  17.4 2.5 %collective-permute-start.6 = (bf16[8,128,128]{2,1,0:T(8,128)(2,1)S(1)}, bf16[8,128,128]{2,1,0:T(8,128)(2,1)S(1)}, u32[]{:S(2)}, u32[]{:S(2)}) collective-permute-start(bf16[8,128,128]{2,1,0:T(8,128)(2,1)S(1)} %get-tuple-element.40), channel_id=1, source_target_pairs={{0,16},{16,0},{1,17},{17,1},{2,18},{18,2},{3,19},{19,3},{4,20},{20... | collective-permute-start | bytes 786440 | tf_op jit(solution)/shard_map/ppermute | solution.py:369
  17.9 11.1 %collective-permute-start.9 = (s16[528,128]{1,0:T(8,128)(2,1)S(1)}, s16[528,128]{1,0:T(8,128)(2,1)S(1)}, u32[]{:S(2)}, u32[]{:S(2)}) collective-permute-start(s16[528,128]{1,0:T(8,128)(2,1)S(1)} %get-tuple-element.38.refs_1_), channel_id=1, source_target_pairs={{0,1},{1,0},{2,3},{3,2},{4,5},{5,4},{6,7},{7,6},{8,9},{9,8},{10,11... | collective-permute-start | bytes 405512 | tf_op jit(solution)/shard_map/ppermute | solution.py:312
  19.4 9.6 %collective-permute-start.8 = (s16[528,128]{1,0:T(8,128)(2,1)S(1)}, s16[528,128]{1,0:T(8,128)(2,1)S(1)}, u32[]{:S(2)}, u32[]{:S(2)}) collective-permute-start(s16[528,128]{1,0:T(8,128)(2,1)S(1)} %get-tuple-element.37.refs_2_), channel_id=1, source_target_pairs={{0,2},{1,3},{2,0},{3,1},{4,6},{5,7},{6,4},{7,5},{8,10},{9,11},{10,... | collective-permute-start | bytes 405512 | tf_op jit(solution)/shard_map/ppermute | solution.py:312
  21.9 9.9 %collective-permute-start.7 = (s16[1040,128]{1,0:T(8,128)(2,1)S(1)}, s16[1040,128]{1,0:T(8,128)(2,1)S(1)}, u32[]{:S(2)}, u32[]{:S(2)}) collective-permute-start(s16[1040,128]{1,0:T(8,128)(2,1)S(1)} %get-tuple-element.42.refs_3_), channel_id=1, source_target_pairs={{0,1},{1,0},{2,3},{3,2},{4,5},{5,4},{6,7},{7,6},{8,9},{9,8},{10,11... | collective-permute-start | bytes 798728 | tf_op jit(solution)/shard_map/ppermute | solution.py:312
  24.8 12.2 %collective-permute-start.10 = (s16[1040,128]{1,0:T(8,128)(2,1)S(1)}, s16[1040,128]{1,0:T(8,128)(2,1)S(1)}, u32[]{:S(2)}, u32[]{:S(2)}) collective-permute-start(s16[1040,128]{1,0:T(8,128)(2,1)S(1)} %shard_map.56.refs_3_), channel_id=1, source_target_pairs={{0,2},{1,3},{2,0},{3,1},{4,6},{5,7},{6,4},{7,5},{8,10},{9,11},{10,... | collective-permute-start | bytes 798728 | tf_op jit(solution)/shard_map/ppermute | solution.py:312
  29.2 8.1 %collective-permute-start.13 = (s16[528,128]{1,0:T(8,128)(2,1)S(1)}, s16[528,128]{1,0:T(8,128)(2,1)S(1)}, u32[]{:S(2)}, u32[]{:S(2)}) collective-permute-start(s16[528,128]{1,0:T(8,128)(2,1)S(1)} %get-tuple-element.46.refs_2_), channel_id=1, source_target_pairs={{0,4},{1,5},{2,6},{3,7},{4,0},{5,1},{6,2},{7,3},{8,12},{9,13},{10,... | collective-permute-start | bytes 405512 | tf_op jit(solution)/shard_map/ppermute | solution.py:312
  32.0 6.8 %collective-permute-start.11 = (s16[528,128]{1,0:T(8,128)(2,1)S(1)}, s16[528,128]{1,0:T(8,128)(2,1)S(1)}, u32[]{:S(2)}, u32[]{:S(2)}) collective-permute-start(s16[528,128]{1,0:T(8,128)(2,1)S(1)} %get-tuple-element.49.refs_2_), channel_id=1, source_target_pairs={{0,2},{1,3},{2,0},{3,1},{4,6},{5,7},{6,4},{7,5},{8,10},{9,11},{10,... | collective-permute-start | bytes 405512 | tf_op jit(solution)/shard_map/ppermute | solution.py:312
  37.3 5.1 %collective-permute-start.12 = (s16[528,128]{1,0:T(8,128)(2,1)S(1)}, s16[528,128]{1,0:T(8,128)(2,1)S(1)}, u32[]{:S(2)}, u32[]{:S(2)}) collective-permute-start(s16[528,128]{1,0:T(8,128)(2,1)S(1)} %get-tuple-element.51.refs_2_), channel_id=1, source_target_pairs={{0,1},{1,0},{2,3},{3,2},{4,5},{5,4},{6,7},{7,6},{8,9},{9,8},{10,11... | collective-permute-start | bytes 405512 | tf_op jit(solution)/shard_map/ppermute | solution.py:312
  38.9 8.1 %collective-permute-start.15 = (s16[272,128]{1,0:T(8,128)(2,1)S(1)}, s16[272,128]{1,0:T(8,128)(2,1)S(1)}, u32[]{:S(2)}, u32[]{:S(2)}) collective-permute-start(s16[272,128]{1,0:T(8,128)(2,1)S(1)} %shard_map.62.refs_4_), channel_id=1, source_target_pairs={{0,12},{1,13},{2,14},{3,15},{4,8},{5,9},{6,10},{7,11},{8,4},{9,5},... | collective-permute-start | bytes 208904 | tf_op jit(solution)/shard_map/ppermute | solution.py:317
  42.5 7.0 %collective-permute-start.16 = (s16[272,128]{1,0:T(8,128)(2,1)S(1)}, s16[272,128]{1,0:T(8,128)(2,1)S(1)}, u32[]{:S(2)}, u32[]{:S(2)}) collective-permute-start(s16[272,128]{1,0:T(8,128)(2,1)S(1)} %get-tuple-element.54), channel_id=1, source_target_pairs={{0,12},{1,13},{2,14},{3,15},{4,8},{5,9},{6,10},{7,11},{8,4},{9,5},... | collective-permute-start | bytes 208904 | tf_op jit(solution)/shard_map/ppermute | solution.py:317
  43.0 6.5 %collective-permute-start.14 = (s16[528,128]{1,0:T(8,128)(2,1)S(1)}, s16[528,128]{1,0:T(8,128)(2,1)S(1)}, u32[]{:S(2)}, u32[]{:S(2)}) collective-permute-start(s16[528,128]{1,0:T(8,128)(2,1)S(1)} %get-tuple-element.53), channel_id=1, source_target_pairs={{0,8},{1,9},{2,10},{3,11},{4,12},{5,13},{6,14},{7,15},{8,0},{9,1},... | collective-permute-start | bytes 405512 | tf_op jit(solution)/shard_map/ppermute | solution.py:317

commit v17 on v15

--- a/solution.py
+++ b/solution.py
@@ -165,28 +165,17 @@
     return kernel
 
 
-def cross_kernel(sizes, bit, whose):
-    def kernel(*refs):
-        n = len(sizes)
-        kept_refs, in_refs, out_refs = refs[:n], refs[n : 2 * n], refs[2 * n :]
-        width = out_refs[0].shape[-1]
+def cross_kernel(size, bit):
+    def kernel(kept_ref, in_ref, far_ref, near_ref):
+        width = far_ref.shape[-1]
         mine = own_bit(bit)
-        heads = [get_head(ref, ref.shape[0] // width) for ref in in_refs]
-
-        def put(out_ref, side, chosen):
-            count = out_ref.shape[0] // width
-            head, slot = new_head(count, width), 0
-            for c in chosen:
-                for i in range(sizes[c]):
-                    at = side * sizes[c] + i
-                    tile = kept_refs[c][at] + get_tile(in_refs[c], at, heads[c])
-                    head = put_tile(out_ref, slot, tile, head)
-                    slot += 1
+        head_in = get_head(in_ref, in_ref.shape[0] // width)
+        for out_ref, side in ((far_ref, 1 - mine), (near_ref, mine)):
+            head = new_head(size, width)
+            for i in range(size):
+                at = side * size + i
+                head = put_tile(out_ref, i, kept_ref[at] + get_tile(in_ref, at, head_in), head)
             put_head(out_ref, head)
-
-        put(out_refs[0], 1 - mine, [whose])
-        if len(out_refs) > 1:
-            put(out_refs[1], mine, range(n))
 
     return kernel
 
@@ -236,24 +225,23 @@
         out_ref[i] = kept_ref[i] + get_tile(in_ref, i, head)
 
 
-def early_kernel(first):
-    def kernel(own_ref, far_ref, out_ref):
-        size = out_ref.shape[0]
-        head = get_head(far_ref, size)
-        for i in range(size):
-            out_ref[i] = own_ref[first + i] + get_tile(far_ref, i, head)
-
-    return kernel
-
-
-def last_kernel(near_ref, *refs):
-    early_refs, out_ref = refs[:-1], refs[-1]
-    count = out_ref.shape[0]
-    head, at = get_head(near_ref, count), 0
-    for ref in early_refs:
-        for i in range(ref.shape[0]):
-            out_ref[at] = (ref[i] + get_tile(near_ref, at, head)).astype(out_ref.dtype)
-            at += 1
+def chunk_sums(own_ref, first, far_ref, near_ref, size):
+    heads = [get_head(ref, size) for ref in (far_ref, near_ref)]
+    for i in range(size):
+        yield own_ref[first + i] + get_tile(far_ref, i, heads[0]) + get_tile(near_ref, i, heads[1])
+
+
+def early_kernel(own_ref, far_ref, near_ref, out_ref):
+    size = out_ref.shape[0]
+    for i, total in enumerate(chunk_sums(own_ref, 0, far_ref, near_ref, size)):
+        out_ref[i] = total
+
+
+def last_kernel(early_ref, own_ref, far_ref, near_ref, out_ref):
+    first = early_ref.shape[0]
+    out_ref[pl.ds(0, first)] = early_ref[...].astype(out_ref.dtype)
+    for i, total in enumerate(chunk_sums(own_ref, first, far_ref, near_ref, out_ref.shape[0] - first)):
+        out_ref[first + i] = total.astype(out_ref.dtype)
 
 
 def call(kernel, out_shape, smem, vmem, after=(), scratch=(), flops=0):
@@ -396,18 +384,13 @@
     own = call(sum_kernel, floats(count), (), own, after)
     moved, top, after = [], rest[0], (own,)
     for n in range(2):
-        shapes = [message(sizes[n], width)] + [message(count, width)] * n
-        used, used_sizes = ([streams[0]], sizes[:1]) if n == 0 else (streams, sizes)
-        kept, came = zip(*used)
-        sent = call(cross_kernel(used_sizes, top, n), shapes, (), (*kept, *came), after)
-        after = (sent[0],)
-        moved.append(cross(sent[0], top))
-    near = cross(sent[1], None)
-    early = []
-    for n, (first, size) in enumerate(chunks):
-        early.append(call(early_kernel(first), floats(size), (), (own, moved[n]), early[-1:], (), 10**9))
+        shapes = [message(sizes[n], width)] * 2
+        far, near = call(cross_kernel(sizes[n], top), shapes, (), streams[n], after)
+        after = (far,)
+        moved.append((cross(far, top), cross(near, None)))
+    early = call(early_kernel, floats(sizes[0]), (), (own, *moved[0]), (), (), 10**9)
     result = jax.ShapeDtypeStruct((count, width, width), jnp.bfloat16)
-    return call(last_kernel, result, (), (near, *early))[None, None]
+    return call(last_kernel, result, (), (early, own, *moved[1]))[None, None]
 
 
 def solution(mesh):

time: 48.8 us -> 48.9 us (level)
  starting transfers between devices: 22.2 us -> 22.9 us
  waiting for transfers between devices: 10.5 us -> 9.8 us
    ppermute x3 -> x4, starting transfers between devices: 5.28 us -> 5.99 us  [cross(): return lax.ppermute(x, ('col', 'layer'), perm)]
    ppermute x3 -> x4, waiting for transfers between devices: 4.68 us -> 4.01 us  [cross(): return lax.ppermute(x, ('col', 'layer'), perm)]
    pallas_call x20 -> x19, Pallas kernels: 15.1 us -> 15.1 us  [call(): pl.pallas_call(wrapped, out_shape=out_shape, in_specs=[pl.BlockSpec(memor...]
  transfers between devices with their start and end apart: 17 -> 18, of which waited for: 5 -> 4; matrix products, arithmetic and copies ran while one was open for 0% -> 0% of each run, Pallas kernels for 29% -> 29%
where the time goes in v17:
time: 48.9 us; the launch traced here: 48.7 us
  starting transfers between devices  22.9 us (47%)
  Pallas kernels  15.1 us (31%)
  waiting for transfers between devices  9.8 us (20%)
  local copies, waits for them, and re-layouts  0.72 us (1%)
    pallas_call x19, Pallas kernels, call(): pl.pallas_call(wrapped, out_shape=out_shape, in_specs=[pl.BlockSpec(memor...  15.1 us
    ppermute x9, starting transfers between devices, exchange(): return lax.ppermute(x, 'layer', [(i, i ^ 1 << bit) for i in range(layers)])  12.1 us
    ppermute x4, starting transfers between devices, cross(): return lax.ppermute(x, ('col', 'layer'), perm)  5.99 us
    ppermute x9, waiting for transfers between devices, exchange(): return lax.ppermute(x, 'layer', [(i, i ^ 1 << bit) for i in range(layers)])  5.78 us
    ppermute x4, waiting for transfers between devices, cross(): return lax.ppermute(x, ('col', 'layer'), perm)  4.01 us
    ppermute x1, starting transfers between devices, on_device(): p_x = lax.ppermute(p, 'col', swap)  2.56 us
    ppermute x1, starting transfers between devices, on_device(): lists_x = lax.ppermute(hold(lists_far, own_kept[:1]), 'col', swap)  1.24 us
  transfers between devices with their start and end apart: 18, of which 4 were waited for; matrix products, arithmetic and copies ran while one was open for 0% of the time, Pallas kernels for 29%

profile of v17, /device:TPU:0, one launch (start us, length us, event | category | flops | bytes accessed | tf_op | source)
XLA Modules:
  0.0 48.7 jit_solution(11475664845959294379)
XLA Ops:
  0.5 2.6 %collective-permute-start.6 = (bf16[16,128,128]{2,1,0:T(8,128)(2,1)}, bf16[16,128,128]{2,1,0:T(8,128)(2,1)S(1)}, u32[]{:S(2)}, u32[]{:S(2)}) collective-permute-start(bf16[16,128,128]{2,1,0:T(8,128)(2,1)} %bitcast.16), channel_id=1, source_target_pairs={{0,8},{8,0},{1,9},{9,1},{2,10},{10,2},{3,11},{11,3},{4,12},{12,4},... | collective-permute-start | bytes 1572872 | tf_op jit(solution)/shard_map/ppermute | solution.py:338
  3.0 0.7 %copy-done.2 = s32[1,1,1,2,32,16]{4,5,3,2,1,0:T(8,128)S(1)} copy-done((s32[1,1,1,2,32,16]{4,5,3,2,1,0:T(8,128)S(1)}, s32[1,1,1,2,32,16]{4,5,3,2,1,0:T(8,128)}, u32[]{:S(2)}) %copy-start.2) | copy-done | bytes 4120
  3.9 3.2 %shard_map.49 = (s16[1040,128]{1,0:T(8,128)(2,1)S(1)}, s16[1040,128]{1,0:T(8,128)(2,1)S(1)}, bf16[32,128,128]{2,1,0:T(8,128)(2,1)S(1)}) custom-call(s32[8,128]{1,0:T(8,128)S(1)} %get-tuple-element.32.refs_0_, bf16[64,128,128]{2,1,0:T(8,128)(2,1)S(1)} %bitcast.10, bf16[16,128,128]{2,1,0:T(8,128)(2,1)S(1)} %bitcast.18, ...), custom_call_target="tpu_custom_call" | custom-call | flops 5368709120 | bytes 4730880 | tf_op jit(solution)/shard_map/pallas_call | solution.py:255
  7.1 1.7 %collective-permute-start.2 = (s16[1040,128]{1,0:T(8,128)(2,1)S(1)}, s16[1040,128]{1,0:T(8,128)(2,1)S(1)}, u32[]{:S(2)}, u32[]{:S(2)}) collective-permute-start(s16[1040,128]{1,0:T(8,128)(2,1)S(1)} %get-tuple-element.38), channel_id=1, source_target_pairs={{0,2},{1,3},{2,0},{3,1},{4,6},{5,7},{6,4},{7,5},{8,10},{9,11},{10,... | collective-permute-start | bytes 798728 | tf_op jit(solution)/shard_map/ppermute | solution.py:300
  8.8 1.5 %collective-permute-start.1 = (s16[1040,128]{1,0:T(8,128)(2,1)S(1)}, s16[1040,128]{1,0:T(8,128)(2,1)S(1)}, u32[]{:S(2)}, u32[]{:S(2)}) collective-permute-start(s16[1040,128]{1,0:T(8,128)(2,1)S(1)} %get-tuple-element.34.refs_3_), channel_id=1, source_target_pairs={{0,1},{1,0},{2,3},{3,2},{4,5},{5,4},{6,7},{7,6},{8,9},{9,8},{10,11... | collective-permute-start | bytes 798728 | tf_op jit(solution)/shard_map/ppermute | solution.py:300
  10.3 3.0 %shard_map.50 = (f32[8,128,128]{2,1,0:T(8,128)S(1)}, f32[8,128,128]{2,1,0:T(8,128)S(1)}) custom-call(s32[8,128]{1,0:T(8,128)S(1)} %get-tuple-element.32.refs_0_, bf16[64,128,128]{2,1,0:T(8,128)(2,1)S(1)} %bitcast.11, bf16[32,128,128]{2,1,0:T(8,128)(2,1)S(1)} %get-tuple-element.33.refs_2_, s16[1040,128]{1,0:T(8,128)(2,1)S(1)} %get-tuple-element.34.refs_3_), custom_call_target="tpu_custom_call" | custom-call | flops 5368709120 | bytes 4198400 | tf_op jit(solution)/shard_map/pallas_call | solution.py:255
  13.3 1.2 %collective-permute-start.5 = (s32[8,128]{1,0:T(8,128)S(1)}, s32[8,128]{1,0:T(8,128)S(1)}, u32[]{:S(2)}, u32[]{:S(2)}) collective-permute-start(s32[8,128]{1,0:T(8,128)S(1)} %shard_map.53), channel_id=1, source_target_pairs={{0,8},{8,0},{1,9},{9,1},{2,10},{10,2},{3,11},{11,3},{4,12},{12,4},... | collective-permute-start | bytes 12296 | tf_op jit(solution)/shard_map/ppermute | solution.py:349
  14.5 2.4 %collective-permute-done.1.refs_1_ = s16[1040,128]{1,0:T(8,128)(2,1)S(1)} collective-permute-done((s16[1040,128]{1,0:T(8,128)(2,1)S(1)}, s16[1040,128]{1,0:T(8,128)(2,1)S(1)}, u32[]{:S(2)}, u32[]{:S(2)}) %collective-permute-start.1) | collective-permute-done | bytes 266272 | tf_op jit(solution)/shard_map/ppermute | solution.py:300
  17.9 1.5 %collective-permute-start.4 = (s16[528,128]{1,0:T(8,128)(2,1)S(1)}, s16[528,128]{1,0:T(8,128)(2,1)S(1)}, u32[]{:S(2)}, u32[]{:S(2)}) collective-permute-start(s16[528,128]{1,0:T(8,128)(2,1)S(1)} %get-tuple-element.41.refs_1_), channel_id=1, source_target_pairs={{0,1},{1,0},{2,3},{3,2},{4,5},{5,4},{6,7},{7,6},{8,9},{9,8},{10,11... | collective-permute-start | bytes 405512 | tf_op jit(solution)/shard_map/ppermute | solution.py:300
  19.9 2.0 %shard_map.55 = (s16[1040,128]{1,0:T(8,128)(2,1)S(1)}, bf16[32,128,128]{2,1,0:T(8,128)(2,1)S(1)}) custom-call(s32[8,128]{1,0:T(8,128)S(1)} %collective-permute-done.5.refs_2_.refs_0_, bf16[64,128,128]{2,1,0:T(8,128)(2,1)S(1)} %bitcast.12, bf16[16,128,128]{2,1,0:T(8,128)(2,1)S(1)} %collective-permute-done.6.refs_0_.refs_2_, ...), custom_call_target="tpu_custom_call" | custom-call | bytes 1 | tf_op jit(solution)/shard_map/pallas_call | solution.py:255
  21.9 1.6 %collective-permute-start.11 = (s16[1040,128]{1,0:T(8,128)(2,1)S(1)}, s16[1040,128]{1,0:T(8,128)(2,1)S(1)}, u32[]{:S(2)}, u32[]{:S(2)}) collective-permute-start(s16[1040,128]{1,0:T(8,128)(2,1)S(1)} %get-tuple-element.46.refs_3_), channel_id=1, source_target_pairs={{0,2},{1,3},{2,0},{3,1},{4,6},{5,7},{6,4},{7,5},{8,10},{9,11},{10,... | collective-permute-start | bytes 798728 | tf_op jit(solution)/shard_map/ppermute | solution.py:300
  23.6 1.9 %shard_map.56.refs_3_ = s16[1040,128]{1,0:T(8,128)(2,1)S(1)} custom-call(s32[8,128]{1,0:T(8,128)S(1)} %collective-permute-done.5.refs_2_.refs_0_, bf16[64,128,128]{2,1,0:T(8,128)(2,1)S(1)} %bitcast.13, bf16[32,128,128]{2,1,0:T(8,128)(2,1)S(1)} %get-tuple-element.45.refs_2_, s16[1040,128]{1,0:T(8,128)(2,1)S(1)} %get-tuple-element.46.refs_3_), custom_call_target="tpu_custom_call" | custom-call | bytes 1 | tf_op jit(solution)/shard_map/pallas_call | solution.py:255
  25.5 0.6 %collective-permute-start.10 = (s16[1040,128]{1,0:T(8,128)(2,1)S(1)}, s16[1040,128]{1,0:T(8,128)(2,1)S(1)}, u32[]{:S(2)}, u32[]{:S(2)}) collective-permute-start(s16[1040,128]{1,0:T(8,128)(2,1)S(1)} %shard_map.56.refs_3_), channel_id=1, source_target_pairs={{0,1},{1,0},{2,3},{3,2},{4,5},{5,4},{6,7},{7,6},{8,9},{9,8},{10,11... | collective-permute-start | bytes 798728 | tf_op jit(solution)/shard_map/ppermute | solution.py:300
  26.1 3.0 %shard_map.57 = (f32[8,128,128]{2,1,0:T(8,128)S(1)}, f32[8,128,128]{2,1,0:T(8,128)S(1)}) custom-call(s32[8,128]{1,0:T(8,128)S(1)} %collective-permute-done.5.refs_2_.refs_0_, bf16[64,128,128]{2,1,0:T(8,128)(2,1)S(1)} %bitcast.14, bf16[32,128,128]{2,1,0:T(8,128)(2,1)S(1)} %get-tuple-element.45.refs_2_, s16[1040,128]{1,0:T(8,128)(2,1)S(1)} %shard_map.56.refs_3_), custom_call_target="tpu_custom_call" | custom-call | flops 5368709120 | bytes 4198400 | tf_op jit(solution)/shard_map/pallas_call | solution.py:255
  29.2 2.7 %collective-permute-start.9 = (s16[528,128]{1,0:T(8,128)(2,1)S(1)}, s16[528,128]{1,0:T(8,128)(2,1)S(1)}, u32[]{:S(2)}, u32[]{:S(2)}) collective-permute-start(s16[528,128]{1,0:T(8,128)(2,1)S(1)} %get-tuple-element.49.refs_2_), channel_id=1, source_target_pairs={{0,4},{1,5},{2,6},{3,7},{4,0},{5,1},{6,2},{7,3},{8,12},{9,13},{10,... | collective-permute-start | bytes 405512 | tf_op jit(solution)/shard_map/ppermute | solution.py:300
  32.0 1.6 %collective-permute-start.12 = (s16[528,128]{1,0:T(8,128)(2,1)S(1)}, s16[528,128]{1,0:T(8,128)(2,1)S(1)}, u32[]{:S(2)}, u32[]{:S(2)}) collective-permute-start(s16[528,128]{1,0:T(8,128)(2,1)S(1)} %get-tuple-element.51.refs_2_), channel_id=1, source_target_pairs={{0,1},{1,0},{2,3},{3,2},{4,5},{5,4},{6,7},{7,6},{8,9},{9,8},{10,11... | collective-permute-start | bytes 405512 | tf_op jit(solution)/shard_map/ppermute | solution.py:300
  34.3 3.3 %collective-permute-done.9.refs_1_ = s16[528,128]{1,0:T(8,128)(2,1)S(1)} collective-permute-done((s16[528,128]{1,0:T(8,128)(2,1)S(1)}, s16[528,128]{1,0:T(8,128)(2,1)S(1)}, u32[]{:S(2)}, u32[]{:S(2)}) %collective-permute-start.9) | collective-permute-done | bytes 135200 | tf_op jit(solution)/shard_map/ppermute | solution.py:300
  37.8 1.4 %collective-permute-start.14 = (s16[272,128]{1,0:T(8,128)(2,1)S(1)}, s16[272,128]{1,0:T(8,128)(2,1)S(1)}, u32[]{:S(2)}, u32[]{:S(2)}) collective-permute-start(s16[272,128]{1,0:T(8,128)(2,1)S(1)} %get-tuple-element.55), channel_id=1, source_target_pairs={{0,8},{1,9},{2,10},{3,11},{4,12},{5,13},{6,14},{7,15},{8,0},{9,1},... | collective-permute-start | bytes 208904 | tf_op jit(solution)/shard_map/ppermute | solution.py:305
  39.2 1.7 %collective-permute-start.13 = (s16[272,128]{1,0:T(8,128)(2,1)S(1)}, s16[272,128]{1,0:T(8,128)(2,1)S(1)}, u32[]{:S(2)}, u32[]{:S(2)}) collective-permute-start(s16[272,128]{1,0:T(8,128)(2,1)S(1)} %get-tuple-element.54.refs_2_), channel_id=1, source_target_pairs={{0,12},{1,13},{2,14},{3,15},{4,8},{5,9},{6,10},{7,11},{8,4},{9,5},... | collective-permute-start | bytes 208904 | tf_op jit(solution)/shard_map/ppermute | solution.py:305
  41.1 2.2 %collective-permute-start.16 = (s16[272,128]{1,0:T(8,128)(2,1)S(1)}, s16[272,128]{1,0:T(8,128)(2,1)S(1)}, u32[]{:S(2)}, u32[]{:S(2)}) collective-permute-start(s16[272,128]{1,0:T(8,128)(2,1)S(1)} %get-tuple-element.57), channel_id=1, source_target_pairs={{0,12},{1,13},{2,14},{3,15},{4,8},{5,9},{6,10},{7,11},{8,4},{9,5},... | collective-permute-start | bytes 208904 | tf_op jit(solution)/shard_map/ppermute | solution.py:305
  43.2 0.7 %collective-permute-start.17 = (s16[272,128]{1,0:T(8,128)(2,1)S(1)}, s16[272,128]{1,0:T(8,128)(2,1)S(1)}, u32[]{:S(2)}, u32[]{:S(2)}) collective-permute-start(s16[272,128]{1,0:T(8,128)(2,1)S(1)} %get-tuple-element.58), channel_id=1, source_target_pairs={{0,8},{1,9},{2,10},{3,11},{4,12},{5,13},{6,14},{7,15},{8,0},{9,1},... | collective-permute-start | bytes 208904 | tf_op jit(solution)/shard_map/ppermute | solution.py:305
  43.9 2.4 %collective-permute-done.13.refs_1_ = s16[272,128]{1,0:T(8,128)(2,1)S(1)} collective-permute-done((s16[272,128]{1,0:T(8,128)(2,1)S(1)}, s16[272,128]{1,0:T(8,128)(2,1)S(1)}, u32[]{:S(2)}, u32[]{:S(2)}) %collective-permute-start.13) | collective-permute-done | bytes 69664 | tf_op jit(solution)/shard_map/ppermute | solution.py:305
  46.3 1.7 %collective-permute-done.16.refs_2_ = s16[272,128]{1,0:T(8,128)(2,1)S(1)} collective-permute-done((s16[272,128]{1,0:T(8,128)(2,1)S(1)}, s16[272,128]{1,0:T(8,128)(2,1)S(1)}, u32[]{:S(2)}, u32[]{:S(2)}) %collective-permute-start.16) | collective-permute-done | bytes 69664 | tf_op jit(solution)/shard_map/ppermute | solution.py:305
  48.0 0.7 %shard_map.65 = bf16[4,128,128]{2,1,0:T(8,128)(2,1)} custom-call(f32[2,128,128]{2,1,0:T(8,128)S(1)} %shard_map.63.refs_0_, f32[4,128,128]{2,1,0:T(8,128)S(1)} %shard_map.61.refs_2_.refs_0_.refs_1_, s16[272,128]{1,0:T(8,128)(2,1)S(1)} %collective-permute-done.16.refs_2_, s16[272,128]{1,0:T(8,128)(2,1)S(1)} %collective-permute-done.17.refs_3_), custom_call_target="tpu_custom_call" | custom-call | bytes 1 | tf_op jit(solution)/shard_map/pallas_call | solution.py:255
  (40 shorter events, 3.3 us)
Async XLA Ops:
  0.0 3.0 %copy-start = (bf16[1,1,1,64,128,128]{5,4,3,2,1,0:T(8,128)(2,1)S(1)}, bf16[1,1,1,64,128,128]{5,4,3,2,1,0:T(8,128)(2,1)}, u32[]{:S(2)}) copy-start(bf16[1,1,1,64,128,128]{5,4,3,2,1,0:T(8,128)(2,1)} %param.4) | copy-start | bytes 6291460
  0.0 3.0 %copy-start.1 = (bf16[1,1,1,16,128,128]{5,4,3,2,1,0:T(8,128)(2,1)S(1)}, bf16[1,1,1,16,128,128]{5,4,3,2,1,0:T(8,128)(2,1)}, u32[]{:S(2)}) copy-start(bf16[1,1,1,16,128,128]{5,4,3,2,1,0:T(8,128)(2,1)} %param.5) | copy-start | bytes 1572868
  0.0 3.8 %collective-permute-start = (bf16[16,128,128]{2,1,0:T(8,128)(2,1)}, bf16[16,128,128]{2,1,0:T(8,128)(2,1)S(1)}, u32[]{:S(2)}, u32[]{:S(2)}) collective-permute-start(bf16[16,128,128]{2,1,0:T(8,128)(2,1)} %bitcast.15), channel_id=1, source_target_pairs={{0,16},{16,0},{1,17},{17,1},{2,18},{18,2},{3,19},{19,3},{4,20},{20... | collective-permute-start | bytes 1572872 | tf_op jit(solution)/shard_map/ppermute | solution.py:339
  0.5 16.8 %collective-permute-start.6 = (bf16[16,128,128]{2,1,0:T(8,128)(2,1)}, bf16[16,128,128]{2,1,0:T(8,128)(2,1)S(1)}, u32[]{:S(2)}, u32[]{:S(2)}) collective-permute-start(bf16[16,128,128]{2,1,0:T(8,128)(2,1)} %bitcast.16), channel_id=1, source_target_pairs={{0,8},{8,0},{1,9},{9,1},{2,10},{10,2},{3,11},{11,3},{4,12},{12,4},... | collective-permute-start | bytes 1572872 | tf_op jit(solution)/shard_map/ppermute | solution.py:338
  3.0 0.7 %copy-start.2 = (s32[1,1,1,2,32,16]{4,5,3,2,1,0:T(8,128)S(1)}, s32[1,1,1,2,32,16]{4,5,3,2,1,0:T(8,128)}, u32[]{:S(2)}) copy-start(s32[1,1,1,2,32,16]{4,5,3,2,1,0:T(8,128)} %param.6) | copy-start | bytes 12292
  3.0 0.7 %copy-start.3 = (s32[1,1,1,2,32,16]{4,5,3,2,1,0:T(8,128)S(1)}, s32[1,1,1,2,32,16]{4,5,3,2,1,0:T(8,128)}, u32[]{:S(2)}) copy-start(s32[1,1,1,2,32,16]{4,5,3,2,1,0:T(8,128)} %param.7) | copy-start | bytes 12292
  7.1 10.0 %collective-permute-start.2 = (s16[1040,128]{1,0:T(8,128)(2,1)S(1)}, s16[1040,128]{1,0:T(8,128)(2,1)S(1)}, u32[]{:S(2)}, u32[]{:S(2)}) collective-permute-start(s16[1040,128]{1,0:T(8,128)(2,1)S(1)} %get-tuple-element.38), channel_id=1, source_target_pairs={{0,2},{1,3},{2,0},{3,1},{4,6},{5,7},{6,4},{7,5},{8,10},{9,11},{10,... | collective-permute-start | bytes 798728 | tf_op jit(solution)/shard_map/ppermute | solution.py:300
  8.8 8.1 %collective-permute-start.1 = (s16[1040,128]{1,0:T(8,128)(2,1)S(1)}, s16[1040,128]{1,0:T(8,128)(2,1)S(1)}, u32[]{:S(2)}, u32[]{:S(2)}) collective-permute-start(s16[1040,128]{1,0:T(8,128)(2,1)S(1)} %get-tuple-element.34.refs_3_), channel_id=1, source_target_pairs={{0,1},{1,0},{2,3},{3,2},{4,5},{5,4},{6,7},{7,6},{8,9},{9,8},{10,11... | collective-permute-start | bytes 798728 | tf_op jit(solution)/shard_map/ppermute | solution.py:300
  13.3 4.0 %collective-permute-start.5 = (s32[8,128]{1,0:T(8,128)S(1)}, s32[8,128]{1,0:T(8,128)S(1)}, u32[]{:S(2)}, u32[]{:S(2)}) collective-permute-start(s32[8,128]{1,0:T(8,128)S(1)} %shard_map.53), channel_id=1, source_target_pairs={{0,8},{8,0},{1,9},{9,1},{2,10},{10,2},{3,11},{11,3},{4,12},{12,4},... | collective-permute-start | bytes 12296 | tf_op jit(solution)/shard_map/ppermute | solution.py:349
  17.3 2.5 %collective-permute-start.7 = (bf16[8,128,128]{2,1,0:T(8,128)(2,1)S(1)}, bf16[8,128,128]{2,1,0:T(8,128)(2,1)S(1)}, u32[]{:S(2)}, u32[]{:S(2)}) collective-permute-start(bf16[8,128,128]{2,1,0:T(8,128)(2,1)S(1)} %get-tuple-element.43), channel_id=1, source_target_pairs={{0,16},{16,0},{1,17},{17,1},{2,18},{18,2},{3,19},{19,3},{4,20},{20... | collective-permute-start | bytes 786440 | tf_op jit(solution)/shard_map/ppermute | solution.py:357
  17.4 2.5 %collective-permute-start.8 = (bf16[8,128,128]{2,1,0:T(8,128)(2,1)S(1)}, bf16[8,128,128]{2,1,0:T(8,128)(2,1)S(1)}, u32[]{:S(2)}, u32[]{:S(2)}) collective-permute-start(bf16[8,128,128]{2,1,0:T(8,128)(2,1)S(1)} %get-tuple-element.44), channel_id=1, source_target_pairs={{0,16},{16,0},{1,17},{17,1},{2,18},{18,2},{3,19},{19,3},{4,20},{20... | collective-permute-start | bytes 786440 | tf_op jit(solution)/shard_map/ppermute | solution.py:357
  17.9 11.1 %collective-permute-start.4 = (s16[528,128]{1,0:T(8,128)(2,1)S(1)}, s16[528,128]{1,0:T(8,128)(2,1)S(1)}, u32[]{:S(2)}, u32[]{:S(2)}) collective-permute-start(s16[528,128]{1,0:T(8,128)(2,1)S(1)} %get-tuple-element.41.refs_1_), channel_id=1, source_target_pairs={{0,1},{1,0},{2,3},{3,2},{4,5},{5,4},{6,7},{7,6},{8,9},{9,8},{10,11... | collective-permute-start | bytes 405512 | tf_op jit(solution)/shard_map/ppermute | solution.py:300
  19.4 9.6 %collective-permute-start.3 = (s16[528,128]{1,0:T(8,128)(2,1)S(1)}, s16[528,128]{1,0:T(8,128)(2,1)S(1)}, u32[]{:S(2)}, u32[]{:S(2)}) collective-permute-start(s16[528,128]{1,0:T(8,128)(2,1)S(1)} %get-tuple-element.39.refs_2_), channel_id=1, source_target_pairs={{0,2},{1,3},{2,0},{3,1},{4,6},{5,7},{6,4},{7,5},{8,10},{9,11},{10,... | collective-permute-start | bytes 405512 | tf_op jit(solution)/shard_map/ppermute | solution.py:300
  21.9 9.9 %collective-permute-start.11 = (s16[1040,128]{1,0:T(8,128)(2,1)S(1)}, s16[1040,128]{1,0:T(8,128)(2,1)S(1)}, u32[]{:S(2)}, u32[]{:S(2)}) collective-permute-start(s16[1040,128]{1,0:T(8,128)(2,1)S(1)} %get-tuple-element.46.refs_3_), channel_id=1, source_target_pairs={{0,2},{1,3},{2,0},{3,1},{4,6},{5,7},{6,4},{7,5},{8,10},{9,11},{10,... | collective-permute-start | bytes 798728 | tf_op jit(solution)/shard_map/ppermute | solution.py:300
  25.5 8.1 %collective-permute-start.10 = (s16[1040,128]{1,0:T(8,128)(2,1)S(1)}, s16[1040,128]{1,0:T(8,128)(2,1)S(1)}, u32[]{:S(2)}, u32[]{:S(2)}) collective-permute-start(s16[1040,128]{1,0:T(8,128)(2,1)S(1)} %shard_map.56.refs_3_), channel_id=1, source_target_pairs={{0,1},{1,0},{2,3},{3,2},{4,5},{5,4},{6,7},{7,6},{8,9},{9,8},{10,11... | collective-permute-start | bytes 798728 | tf_op jit(solution)/shard_map/ppermute | solution.py:300
  29.2 8.4 %collective-permute-start.9 = (s16[528,128]{1,0:T(8,128)(2,1)S(1)}, s16[528,128]{1,0:T(8,128)(2,1)S(1)}, u32[]{:S(2)}, u32[]{:S(2)}) collective-permute-start(s16[528,128]{1,0:T(8,128)(2,1)S(1)} %get-tuple-element.49.refs_2_), channel_id=1, source_target_pairs={{0,4},{1,5},{2,6},{3,7},{4,0},{5,1},{6,2},{7,3},{8,12},{9,13},{10,... | collective-permute-start | bytes 405512 | tf_op jit(solution)/shard_map/ppermute | solution.py:300
  32.0 5.7 %collective-permute-start.12 = (s16[528,128]{1,0:T(8,128)(2,1)S(1)}, s16[528,128]{1,0:T(8,128)(2,1)S(1)}, u32[]{:S(2)}, u32[]{:S(2)}) collective-permute-start(s16[528,128]{1,0:T(8,128)(2,1)S(1)} %get-tuple-element.51.refs_2_), channel_id=1, source_target_pairs={{0,1},{1,0},{2,3},{3,2},{4,5},{5,4},{6,7},{7,6},{8,9},{9,8},{10,11... | collective-permute-start | bytes 405512 | tf_op jit(solution)/shard_map/ppermute | solution.py:300
  33.8 7.2 %collective-permute-start.15 = (s16[528,128]{1,0:T(8,128)(2,1)S(1)}, s16[528,128]{1,0:T(8,128)(2,1)S(1)}, u32[]{:S(2)}, u32[]{:S(2)}) collective-permute-start(s16[528,128]{1,0:T(8,128)(2,1)S(1)} %get-tuple-element.52.refs_2_), channel_id=1, source_target_pairs={{0,2},{1,3},{2,0},{3,1},{4,6},{5,7},{6,4},{7,5},{8,10},{9,11},{10,... | collective-permute-start | bytes 405512 | tf_op jit(solution)/shard_map/ppermute | solution.py:300
  37.8 6.1 %collective-permute-start.14 = (s16[272,128]{1,0:T(8,128)(2,1)S(1)}, s16[272,128]{1,0:T(8,128)(2,1)S(1)}, u32[]{:S(2)}, u32[]{:S(2)}) collective-permute-start(s16[272,128]{1,0:T(8,128)(2,1)S(1)} %get-tuple-element.55), channel_id=1, source_target_pairs={{0,8},{1,9},{2,10},{3,11},{4,12},{5,13},{6,14},{7,15},{8,0},{9,1},... | collective-permute-start | bytes 208904 | tf_op jit(solution)/shard_map/ppermute | solution.py:305
  39.2 7.1 %collective-permute-start.13 = (s16[272,128]{1,0:T(8,128)(2,1)S(1)}, s16[272,128]{1,0:T(8,128)(2,1)S(1)}, u32[]{:S(2)}, u32[]{:S(2)}) collective-permute-start(s16[272,128]{1,0:T(8,128)(2,1)S(1)} %get-tuple-element.54.refs_2_), channel_id=1, source_target_pairs={{0,12},{1,13},{2,14},{3,15},{4,8},{5,9},{6,10},{7,11},{8,4},{9,5},... | collective-permute-start | bytes 208904 | tf_op jit(solution)/shard_map/ppermute | solution.py:305
  41.1 6.9 %collective-permute-start.16 = (s16[272,128]{1,0:T(8,128)(2,1)S(1)}, s16[272,128]{1,0:T(8,128)(2,1)S(1)}, u32[]{:S(2)}, u32[]{:S(2)}) collective-permute-start(s16[272,128]{1,0:T(8,128)(2,1)S(1)} %get-tuple-element.57), channel_id=1, source_target_pairs={{0,12},{1,13},{2,14},{3,15},{4,8},{5,9},{6,10},{7,11},{8,4},{9,5},... | collective-permute-start | bytes 208904 | tf_op jit(solution)/shard_map/ppermute | solution.py:305
  43.2 4.8 %collective-permute-start.17 = (s16[272,128]{1,0:T(8,128)(2,1)S(1)}, s16[272,128]{1,0:T(8,128)(2,1)S(1)}, u32[]{:S(2)}, u32[]{:S(2)}) collective-permute-start(s16[272,128]{1,0:T(8,128)(2,1)S(1)} %get-tuple-element.58), channel_id=1, source_target_pairs={{0,8},{1,9},{2,10},{3,11},{4,12},{5,13},{6,14},{7,15},{8,0},{9,1},... | collective-permute-start | bytes 208904 | tf_op jit(solution)/shard_map/ppermute | solution.py:305

commit v18 on v15

--- a/solution.py
+++ b/solution.py
@@ -363,12 +363,13 @@
     for n in range(2):
         sent, part = second(own_kept[n], own_came[n], sizes[n], own_bits[n], after)
         parts.append(part)
-        after = (sent,)
+        late, after = sent, (sent,)
     pieces = [jax.ShapeDtypeStruct((held // 2, width, width), p.dtype)] * 2
     pieces = call(split_kernel, pieces, (), (p_x,), (*after, lists_x))
     p_xr = [lax.ppermute(x, "row", swap) for x in pieces]
 
     (made, joined), came_0 = send(lists_x, (a, p_x, *p_xr), (0,), other_bits[:1], True, (), 0)
+    parts[1] = (parts[1][0], exchange(hold(late, (made,)), 1 - own_bits[1]))
     (made,), came_1 = send(lists_x, (a, joined), (1,), other_bits[1:], False, (made,), 0)
     other_came = came_0 + came_1
     other_kept = keep(lists_x, (a, joined), other_bits, (made,), 1)

time: 48.8 us -> 49.9 us (1.023)
  starting transfers between devices: 22.2 us -> 22.8 us
    ppermute x2, waiting for transfers between devices: 0.01 us -> 0.95 us  [on_device(): p_xr = [lax.ppermute(x, 'row', swap) for x in pieces]]
    ppermute x9, waiting for transfers between devices: 5.78 us -> 4.88 us  [exchange(): return lax.ppermute(x, 'layer', [(i, i ^ 1 << bit) for i in range(layers)])]
    ppermute x3, starting transfers between devices: 5.28 us -> 5.86 us  [cross(): return lax.ppermute(x, ('col', 'layer'), perm)]
  transfers between devices with their start and end apart: 17 -> 17, of which waited for: 5 -> 7; matrix products, arithmetic and copies ran while one was open for 0% -> 0% of each run, Pallas kernels for 29% -> 29%
where the time goes in v18:
time: 49.9 us; the launch traced here: 49.7 us
  starting transfers between devices  22.8 us (46%)
  Pallas kernels  15.2 us (30%)
  waiting for transfers between devices  10.8 us (22%)
  local copies, waits for them, and re-layouts  0.72 us (1%)
    pallas_call x20, Pallas kernels, call(): pl.pallas_call(wrapped, out_shape=out_shape, in_specs=[pl.BlockSpec(memor...  15.2 us
    ppermute x9, starting transfers between devices, exchange(): return lax.ppermute(x, 'layer', [(i, i ^ 1 << bit) for i in range(layers)])  12.1 us
    ppermute x3, starting transfers between devices, cross(): return lax.ppermute(x, ('col', 'layer'), perm)  5.86 us
    ppermute x3, waiting for transfers between devices, cross(): return lax.ppermute(x, ('col', 'layer'), perm)  4.93 us
    ppermute x9, waiting for transfers between devices, exchange(): return lax.ppermute(x, 'layer', [(i, i ^ 1 << bit) for i in range(layers)])  4.88 us
    ppermute x1, starting transfers between devices, on_device(): p_x = lax.ppermute(p, 'col', swap)  2.56 us
    ppermute x1, starting transfers between devices, on_device(): lists_x = lax.ppermute(hold(lists_far, own_kept[:1]), 'col', swap)  1.24 us
  transfers between devices with their start and end apart: 17, of which 7 were waited for; matrix products, arithmetic and copies ran while one was open for 0% of the time, Pallas kernels for 29%

profile of v18, /device:TPU:0, one launch (start us, length us, event | category | flops | bytes accessed | tf_op | source)
XLA Modules:
  0.0 49.7 jit_solution(4947828362093331078)
XLA Ops:
  0.5 2.6 %collective-permute-start.2 = (bf16[16,128,128]{2,1,0:T(8,128)(2,1)}, bf16[16,128,128]{2,1,0:T(8,128)(2,1)S(1)}, u32[]{:S(2)}, u32[]{:S(2)}) collective-permute-start(bf16[16,128,128]{2,1,0:T(8,128)(2,1)} %bitcast.16), channel_id=1, source_target_pairs={{0,8},{8,0},{1,9},{9,1},{2,10},{10,2},{3,11},{11,3},{4,12},{12,4},... | collective-permute-start | bytes 1572872 | tf_op jit(solution)/shard_map/ppermute | solution.py:350
  3.0 0.7 %copy-done.2 = s32[1,1,1,2,32,16]{4,5,3,2,1,0:T(8,128)S(1)} copy-done((s32[1,1,1,2,32,16]{4,5,3,2,1,0:T(8,128)S(1)}, s32[1,1,1,2,32,16]{4,5,3,2,1,0:T(8,128)}, u32[]{:S(2)}) %copy-start.2) | copy-done | bytes 4120
  3.9 3.3 %shard_map.49 = (s16[1040,128]{1,0:T(8,128)(2,1)S(1)}, s16[1040,128]{1,0:T(8,128)(2,1)S(1)}, bf16[32,128,128]{2,1,0:T(8,128)(2,1)S(1)}) custom-call(s32[8,128]{1,0:T(8,128)S(1)} %get-tuple-element.31.refs_0_, bf16[64,128,128]{2,1,0:T(8,128)(2,1)S(1)} %bitcast.10, bf16[16,128,128]{2,1,0:T(8,128)(2,1)S(1)} %bitcast.18, ...), custom_call_target="tpu_custom_call" | custom-call | flops 5368709120 | bytes 4730880 | tf_op jit(solution)/shard_map/pallas_call | solution.py:267
  7.2 1.7 %collective-permute-start.3 = (s16[1040,128]{1,0:T(8,128)(2,1)S(1)}, s16[1040,128]{1,0:T(8,128)(2,1)S(1)}, u32[]{:S(2)}, u32[]{:S(2)}) collective-permute-start(s16[1040,128]{1,0:T(8,128)(2,1)S(1)} %get-tuple-element.36), channel_id=1, source_target_pairs={{0,2},{1,3},{2,0},{3,1},{4,6},{5,7},{6,4},{7,5},{8,10},{9,11},{10,... | collective-permute-start | bytes 798728 | tf_op jit(solution)/shard_map/ppermute | solution.py:312
  8.8 1.5 %collective-permute-start.4 = (s16[1040,128]{1,0:T(8,128)(2,1)S(1)}, s16[1040,128]{1,0:T(8,128)(2,1)S(1)}, u32[]{:S(2)}, u32[]{:S(2)}) collective-permute-start(s16[1040,128]{1,0:T(8,128)(2,1)S(1)} %get-tuple-element.33.refs_3_), channel_id=1, source_target_pairs={{0,1},{1,0},{2,3},{3,2},{4,5},{5,4},{6,7},{7,6},{8,9},{9,8},{10,11... | collective-permute-start | bytes 798728 | tf_op jit(solution)/shard_map/ppermute | solution.py:312
  10.4 3.1 %shard_map.50 = (f32[8,128,128]{2,1,0:T(8,128)S(1)}, f32[8,128,128]{2,1,0:T(8,128)S(1)}) custom-call(s32[8,128]{1,0:T(8,128)S(1)} %get-tuple-element.31.refs_0_, bf16[64,128,128]{2,1,0:T(8,128)(2,1)S(1)} %bitcast.11, bf16[32,128,128]{2,1,0:T(8,128)(2,1)S(1)} %get-tuple-element.32.refs_2_, s16[1040,128]{1,0:T(8,128)(2,1)S(1)} %get-tuple-element.33.refs_3_), custom_call_target="tpu_custom_call" | custom-call | flops 5368709120 | bytes 4198400 | tf_op jit(solution)/shard_map/pallas_call | solution.py:267
  13.4 1.2 %collective-permute-start.1 = (s32[8,128]{1,0:T(8,128)S(1)}, s32[8,128]{1,0:T(8,128)S(1)}, u32[]{:S(2)}, u32[]{:S(2)}) collective-permute-start(s32[8,128]{1,0:T(8,128)S(1)} %shard_map.51), channel_id=1, source_target_pairs={{0,8},{8,0},{1,9},{9,1},{2,10},{10,2},{3,11},{11,3},{4,12},{12,4},... | collective-permute-start | bytes 12296 | tf_op jit(solution)/shard_map/ppermute | solution.py:361
  14.7 2.3 %collective-permute-done.4.refs_1_ = s16[1040,128]{1,0:T(8,128)(2,1)S(1)} collective-permute-done((s16[1040,128]{1,0:T(8,128)(2,1)S(1)}, s16[1040,128]{1,0:T(8,128)(2,1)S(1)}, u32[]{:S(2)}, u32[]{:S(2)}) %collective-permute-start.4) | collective-permute-done | bytes 266272 | tf_op jit(solution)/shard_map/ppermute | solution.py:312
  18.4 0.6 %collective-permute-done.5.refs_3_ = bf16[8,128,128]{2,1,0:T(8,128)(2,1)S(1)} collective-permute-done((bf16[8,128,128]{2,1,0:T(8,128)(2,1)S(1)}, bf16[8,128,128]{2,1,0:T(8,128)(2,1)S(1)}, u32[]{:S(2)}, u32[]{:S(2)}) %collective-permute-start.5) | collective-permute-done | bytes 262176 | tf_op jit(solution)/shard_map/ppermute | solution.py:369
  19.4 2.0 %shard_map.55 = (s16[1040,128]{1,0:T(8,128)(2,1)S(1)}, bf16[32,128,128]{2,1,0:T(8,128)(2,1)S(1)}) custom-call(s32[8,128]{1,0:T(8,128)S(1)} %collective-permute-done.1.refs_2_.refs_0_, bf16[64,128,128]{2,1,0:T(8,128)(2,1)S(1)} %bitcast.12, bf16[16,128,128]{2,1,0:T(8,128)(2,1)S(1)} %collective-permute-done.2.refs_0_.refs_2_, ...), custom_call_target="tpu_custom_call" | custom-call | bytes 1 | tf_op jit(solution)/shard_map/pallas_call | solution.py:267
  21.4 0.7 %collective-permute-start.7 = (s16[1040,128]{1,0:T(8,128)(2,1)S(1)}, s16[1040,128]{1,0:T(8,128)(2,1)S(1)}, u32[]{:S(2)}, u32[]{:S(2)}) collective-permute-start(s16[1040,128]{1,0:T(8,128)(2,1)S(1)} %get-tuple-element.42.refs_3_.refs_1_), channel_id=1, source_target_pairs={{0,2},{1,3},{2,0},{3,1},{4,6},{5,7},{6,4},{7,5},{8,10},{9,11},{10,... | collective-permute-start | bytes 798728 | tf_op jit(solution)/shard_map/ppermute | solution.py:312
  22.1 1.5 %collective-permute-start.9 = (s16[528,128]{1,0:T(8,128)(2,1)S(1)}, s16[528,128]{1,0:T(8,128)(2,1)S(1)}, u32[]{:S(2)}, u32[]{:S(2)}) collective-permute-start(s16[528,128]{1,0:T(8,128)(2,1)S(1)} %shard_map.58), channel_id=1, source_target_pairs={{0,1},{1,0},{2,3},{3,2},{4,5},{5,4},{6,7},{7,6},{8,9},{9,8},{10,11... | collective-permute-start | bytes 405512 | tf_op jit(solution)/shard_map/ppermute | solution.py:312
  23.6 1.9 %shard_map.56.refs_3_ = s16[1040,128]{1,0:T(8,128)(2,1)S(1)} custom-call(s32[8,128]{1,0:T(8,128)S(1)} %collective-permute-done.1.refs_2_.refs_0_, bf16[64,128,128]{2,1,0:T(8,128)(2,1)S(1)} %bitcast.13, bf16[32,128,128]{2,1,0:T(8,128)(2,1)S(1)} %get-tuple-element.41.refs_2_, s16[1040,128]{1,0:T(8,128)(2,1)S(1)} %get-tuple-element.42.refs_3_.refs_1_), custom_call_target="tpu_custom_call" | custom-call | bytes 1 | tf_op jit(solution)/shard_map/pallas_call | solution.py:267
  26.1 3.0 %shard_map.57 = (f32[8,128,128]{2,1,0:T(8,128)S(1)}, f32[8,128,128]{2,1,0:T(8,128)S(1)}) custom-call(s32[8,128]{1,0:T(8,128)S(1)} %collective-permute-done.1.refs_2_.refs_0_, bf16[64,128,128]{2,1,0:T(8,128)(2,1)S(1)} %bitcast.14, bf16[32,128,128]{2,1,0:T(8,128)(2,1)S(1)} %get-tuple-element.41.refs_2_, s16[1040,128]{1,0:T(8,128)(2,1)S(1)} %shard_map.56.refs_3_), custom_call_target="tpu_custom_call" | custom-call | flops 5368709120 | bytes 4198400 | tf_op jit(solution)/shard_map/pallas_call | solution.py:267
  29.3 2.7 %collective-permute-start.13 = (s16[528,128]{1,0:T(8,128)(2,1)S(1)}, s16[528,128]{1,0:T(8,128)(2,1)S(1)}, u32[]{:S(2)}, u32[]{:S(2)}) collective-permute-start(s16[528,128]{1,0:T(8,128)(2,1)S(1)} %get-tuple-element.46.refs_2_), channel_id=1, source_target_pairs={{0,4},{1,5},{2,6},{3,7},{4,0},{5,1},{6,2},{7,3},{8,12},{9,13},{10,... | collective-permute-start | bytes 405512 | tf_op jit(solution)/shard_map/ppermute | solution.py:312
  32.1 1.6 %collective-permute-start.11 = (s16[528,128]{1,0:T(8,128)(2,1)S(1)}, s16[528,128]{1,0:T(8,128)(2,1)S(1)}, u32[]{:S(2)}, u32[]{:S(2)}) collective-permute-start(s16[528,128]{1,0:T(8,128)(2,1)S(1)} %get-tuple-element.49.refs_2_), channel_id=1, source_target_pairs={{0,1},{1,0},{2,3},{3,2},{4,5},{5,4},{6,7},{7,6},{8,9},{9,8},{10,11... | collective-permute-start | bytes 405512 | tf_op jit(solution)/shard_map/ppermute | solution.py:312
  33.8 1.5 %collective-permute-start.12 = (s16[528,128]{1,0:T(8,128)(2,1)S(1)}, s16[528,128]{1,0:T(8,128)(2,1)S(1)}, u32[]{:S(2)}, u32[]{:S(2)}) collective-permute-start(s16[528,128]{1,0:T(8,128)(2,1)S(1)} %get-tuple-element.51.refs_2_), channel_id=1, source_target_pairs={{0,2},{1,3},{2,0},{3,1},{4,6},{5,7},{6,4},{7,5},{8,10},{9,11},{10,... | collective-permute-start | bytes 405512 | tf_op jit(solution)/shard_map/ppermute | solution.py:312
  35.3 2.5 %collective-permute-done.13.refs_1_ = s16[528,128]{1,0:T(8,128)(2,1)S(1)} collective-permute-done((s16[528,128]{1,0:T(8,128)(2,1)S(1)}, s16[528,128]{1,0:T(8,128)(2,1)S(1)}, u32[]{:S(2)}, u32[]{:S(2)}) %collective-permute-start.13) | collective-permute-done | bytes 135200 | tf_op jit(solution)/shard_map/ppermute | solution.py:312
  38.0 2.0 %collective-permute-start.15 = (s16[272,128]{1,0:T(8,128)(2,1)S(1)}, s16[272,128]{1,0:T(8,128)(2,1)S(1)}, u32[]{:S(2)}, u32[]{:S(2)}) collective-permute-start(s16[272,128]{1,0:T(8,128)(2,1)S(1)} %shard_map.63.refs_4_), channel_id=1, source_target_pairs={{0,12},{1,13},{2,14},{3,15},{4,8},{5,9},{6,10},{7,11},{8,4},{9,5},... | collective-permute-start | bytes 208904 | tf_op jit(solution)/shard_map/ppermute | solution.py:317
  40.1 3.4 %collective-permute-start.16 = (s16[272,128]{1,0:T(8,128)(2,1)S(1)}, s16[272,128]{1,0:T(8,128)(2,1)S(1)}, u32[]{:S(2)}, u32[]{:S(2)}) collective-permute-start(s16[272,128]{1,0:T(8,128)(2,1)S(1)} %get-tuple-element.54), channel_id=1, source_target_pairs={{0,12},{1,13},{2,14},{3,15},{4,8},{5,9},{6,10},{7,11},{8,4},{9,5},... | collective-permute-start | bytes 208904 | tf_op jit(solution)/shard_map/ppermute | solution.py:317
  44.0 2.0 %collective-permute-done.15.refs_1_ = s16[272,128]{1,0:T(8,128)(2,1)S(1)} collective-permute-done((s16[272,128]{1,0:T(8,128)(2,1)S(1)}, s16[272,128]{1,0:T(8,128)(2,1)S(1)}, u32[]{:S(2)}, u32[]{:S(2)}) %collective-permute-start.15) | collective-permute-done | bytes 69664 | tf_op jit(solution)/shard_map/ppermute | solution.py:317
  46.1 1.5 %collective-permute-done.16.refs_1_ = s16[272,128]{1,0:T(8,128)(2,1)S(1)} collective-permute-done((s16[272,128]{1,0:T(8,128)(2,1)S(1)}, s16[272,128]{1,0:T(8,128)(2,1)S(1)}, u32[]{:S(2)}, u32[]{:S(2)}) %collective-permute-start.16) | collective-permute-done | bytes 69664 | tf_op jit(solution)/shard_map/ppermute | solution.py:317
  47.6 1.5 %collective-permute-done.14.refs_0_ = s16[528,128]{1,0:T(8,128)(2,1)S(1)} collective-permute-done((s16[528,128]{1,0:T(8,128)(2,1)S(1)}, s16[528,128]{1,0:T(8,128)(2,1)S(1)}, u32[]{:S(2)}, u32[]{:S(2)}) %collective-permute-start.14) | collective-permute-done | bytes 135200 | tf_op jit(solution)/shard_map/ppermute | solution.py:317
  49.0 0.7 %shard_map.67 = bf16[4,128,128]{2,1,0:T(8,128)(2,1)} custom-call(s16[528,128]{1,0:T(8,128)(2,1)S(1)} %collective-permute-done.14.refs_0_, f32[2,128,128]{2,1,0:T(8,128)S(1)} %shard_map.65.refs_2_.refs_1_, f32[2,128,128]{2,1,0:T(8,128)S(1)} %shard_map.66.refs_2_), custom_call_target="tpu_custom_call" | custom-call | bytes 1 | tf_op jit(solution)/shard_map/pallas_call | solution.py:267
  (40 shorter events, 4.2 us)
Async XLA Ops:
  0.0 3.0 %copy-start = (bf16[1,1,1,64,128,128]{5,4,3,2,1,0:T(8,128)(2,1)S(1)}, bf16[1,1,1,64,128,128]{5,4,3,2,1,0:T(8,128)(2,1)}, u32[]{:S(2)}) copy-start(bf16[1,1,1,64,128,128]{5,4,3,2,1,0:T(8,128)(2,1)} %param.4) | copy-start | bytes 6291460
  0.0 3.0 %copy-start.1 = (bf16[1,1,1,16,128,128]{5,4,3,2,1,0:T(8,128)(2,1)S(1)}, bf16[1,1,1,16,128,128]{5,4,3,2,1,0:T(8,128)(2,1)}, u32[]{:S(2)}) copy-start(bf16[1,1,1,16,128,128]{5,4,3,2,1,0:T(8,128)(2,1)} %param.5) | copy-start | bytes 1572868
  0.0 3.8 %collective-permute-start = (bf16[16,128,128]{2,1,0:T(8,128)(2,1)}, bf16[16,128,128]{2,1,0:T(8,128)(2,1)S(1)}, u32[]{:S(2)}, u32[]{:S(2)}) collective-permute-start(bf16[16,128,128]{2,1,0:T(8,128)(2,1)} %bitcast.15), channel_id=1, source_target_pairs={{0,16},{16,0},{1,17},{17,1},{2,18},{18,2},{3,19},{19,3},{4,20},{20... | collective-permute-start | bytes 1572872 | tf_op jit(solution)/shard_map/ppermute | solution.py:351
  0.5 16.9 %collective-permute-start.2 = (bf16[16,128,128]{2,1,0:T(8,128)(2,1)}, bf16[16,128,128]{2,1,0:T(8,128)(2,1)S(1)}, u32[]{:S(2)}, u32[]{:S(2)}) collective-permute-start(bf16[16,128,128]{2,1,0:T(8,128)(2,1)} %bitcast.16), channel_id=1, source_target_pairs={{0,8},{8,0},{1,9},{9,1},{2,10},{10,2},{3,11},{11,3},{4,12},{12,4},... | collective-permute-start | bytes 1572872 | tf_op jit(solution)/shard_map/ppermute | solution.py:350
  3.0 0.7 %copy-start.2 = (s32[1,1,1,2,32,16]{4,5,3,2,1,0:T(8,128)S(1)}, s32[1,1,1,2,32,16]{4,5,3,2,1,0:T(8,128)}, u32[]{:S(2)}) copy-start(s32[1,1,1,2,32,16]{4,5,3,2,1,0:T(8,128)} %param.6) | copy-start | bytes 12292
  3.0 0.7 %copy-start.3 = (s32[1,1,1,2,32,16]{4,5,3,2,1,0:T(8,128)S(1)}, s32[1,1,1,2,32,16]{4,5,3,2,1,0:T(8,128)}, u32[]{:S(2)}) copy-start(s32[1,1,1,2,32,16]{4,5,3,2,1,0:T(8,128)} %param.7) | copy-start | bytes 12292
  7.2 10.0 %collective-permute-start.3 = (s16[1040,128]{1,0:T(8,128)(2,1)S(1)}, s16[1040,128]{1,0:T(8,128)(2,1)S(1)}, u32[]{:S(2)}, u32[]{:S(2)}) collective-permute-start(s16[1040,128]{1,0:T(8,128)(2,1)S(1)} %get-tuple-element.36), channel_id=1, source_target_pairs={{0,2},{1,3},{2,0},{3,1},{4,6},{5,7},{6,4},{7,5},{8,10},{9,11},{10,... | collective-permute-start | bytes 798728 | tf_op jit(solution)/shard_map/ppermute | solution.py:312
  8.8 8.1 %collective-permute-start.4 = (s16[1040,128]{1,0:T(8,128)(2,1)S(1)}, s16[1040,128]{1,0:T(8,128)(2,1)S(1)}, u32[]{:S(2)}, u32[]{:S(2)}) collective-permute-start(s16[1040,128]{1,0:T(8,128)(2,1)S(1)} %get-tuple-element.33.refs_3_), channel_id=1, source_target_pairs={{0,1},{1,0},{2,3},{3,2},{4,5},{5,4},{6,7},{7,6},{8,9},{9,8},{10,11... | collective-permute-start | bytes 798728 | tf_op jit(solution)/shard_map/ppermute | solution.py:312
  13.4 3.9 %collective-permute-start.1 = (s32[8,128]{1,0:T(8,128)S(1)}, s32[8,128]{1,0:T(8,128)S(1)}, u32[]{:S(2)}, u32[]{:S(2)}) collective-permute-start(s32[8,128]{1,0:T(8,128)S(1)} %shard_map.51), channel_id=1, source_target_pairs={{0,8},{8,0},{1,9},{9,1},{2,10},{10,2},{3,11},{11,3},{4,12},{12,4},... | collective-permute-start | bytes 12296 | tf_op jit(solution)/shard_map/ppermute | solution.py:361
  17.4 1.6 %collective-permute-start.5 = (bf16[8,128,128]{2,1,0:T(8,128)(2,1)S(1)}, bf16[8,128,128]{2,1,0:T(8,128)(2,1)S(1)}, u32[]{:S(2)}, u32[]{:S(2)}) collective-permute-start(bf16[8,128,128]{2,1,0:T(8,128)(2,1)S(1)} %get-tuple-element.39), channel_id=1, source_target_pairs={{0,16},{16,0},{1,17},{17,1},{2,18},{18,2},{3,19},{19,3},{4,20},{20... | collective-permute-start | bytes 786440 | tf_op jit(solution)/shard_map/ppermute | solution.py:369
  17.5 1.9 %collective-permute-start.6 = (bf16[8,128,128]{2,1,0:T(8,128)(2,1)S(1)}, bf16[8,128,128]{2,1,0:T(8,128)(2,1)S(1)}, u32[]{:S(2)}, u32[]{:S(2)}) collective-permute-start(bf16[8,128,128]{2,1,0:T(8,128)(2,1)S(1)} %get-tuple-element.40), channel_id=1, source_target_pairs={{0,16},{16,0},{1,17},{17,1},{2,18},{18,2},{3,19},{19,3},{4,20},{20... | collective-permute-start | bytes 786440 | tf_op jit(solution)/shard_map/ppermute | solution.py:369
  18.0 11.1 %collective-permute-start.8 = (s16[528,128]{1,0:T(8,128)(2,1)S(1)}, s16[528,128]{1,0:T(8,128)(2,1)S(1)}, u32[]{:S(2)}, u32[]{:S(2)}) collective-permute-start(s16[528,128]{1,0:T(8,128)(2,1)S(1)} %get-tuple-element.37.refs_2_), channel_id=1, source_target_pairs={{0,2},{1,3},{2,0},{3,1},{4,6},{5,7},{6,4},{7,5},{8,10},{9,11},{10,... | collective-permute-start | bytes 405512 | tf_op jit(solution)/shard_map/ppermute | solution.py:312
  21.4 10.5 %collective-permute-start.7 = (s16[1040,128]{1,0:T(8,128)(2,1)S(1)}, s16[1040,128]{1,0:T(8,128)(2,1)S(1)}, u32[]{:S(2)}, u32[]{:S(2)}) collective-permute-start(s16[1040,128]{1,0:T(8,128)(2,1)S(1)} %get-tuple-element.42.refs_3_.refs_1_), channel_id=1, source_target_pairs={{0,2},{1,3},{2,0},{3,1},{4,6},{5,7},{6,4},{7,5},{8,10},{9,11},{10,... | collective-permute-start | bytes 798728 | tf_op jit(solution)/shard_map/ppermute | solution.py:312
  22.1 7.0 %collective-permute-start.9 = (s16[528,128]{1,0:T(8,128)(2,1)S(1)}, s16[528,128]{1,0:T(8,128)(2,1)S(1)}, u32[]{:S(2)}, u32[]{:S(2)}) collective-permute-start(s16[528,128]{1,0:T(8,128)(2,1)S(1)} %shard_map.58), channel_id=1, source_target_pairs={{0,1},{1,0},{2,3},{3,2},{4,5},{5,4},{6,7},{7,6},{8,9},{9,8},{10,11... | collective-permute-start | bytes 405512 | tf_op jit(solution)/shard_map/ppermute | solution.py:312
  25.6 8.1 %collective-permute-start.10 = (s16[1040,128]{1,0:T(8,128)(2,1)S(1)}, s16[1040,128]{1,0:T(8,128)(2,1)S(1)}, u32[]{:S(2)}, u32[]{:S(2)}) collective-permute-start(s16[1040,128]{1,0:T(8,128)(2,1)S(1)} %shard_map.56.refs_3_), channel_id=1, source_target_pairs={{0,1},{1,0},{2,3},{3,2},{4,5},{5,4},{6,7},{7,6},{8,9},{9,8},{10,11... | collective-permute-start | bytes 798728 | tf_op jit(solution)/shard_map/ppermute | solution.py:312
  29.3 8.6 %collective-permute-start.13 = (s16[528,128]{1,0:T(8,128)(2,1)S(1)}, s16[528,128]{1,0:T(8,128)(2,1)S(1)}, u32[]{:S(2)}, u32[]{:S(2)}) collective-permute-start(s16[528,128]{1,0:T(8,128)(2,1)S(1)} %get-tuple-element.46.refs_2_), channel_id=1, source_target_pairs={{0,4},{1,5},{2,6},{3,7},{4,0},{5,1},{6,2},{7,3},{8,12},{9,13},{10,... | collective-permute-start | bytes 405512 | tf_op jit(solution)/shard_map/ppermute | solution.py:312
  32.1 5.8 %collective-permute-start.11 = (s16[528,128]{1,0:T(8,128)(2,1)S(1)}, s16[528,128]{1,0:T(8,128)(2,1)S(1)}, u32[]{:S(2)}, u32[]{:S(2)}) collective-permute-start(s16[528,128]{1,0:T(8,128)(2,1)S(1)} %get-tuple-element.49.refs_2_), channel_id=1, source_target_pairs={{0,1},{1,0},{2,3},{3,2},{4,5},{5,4},{6,7},{7,6},{8,9},{9,8},{10,11... | collective-permute-start | bytes 405512 | tf_op jit(solution)/shard_map/ppermute | solution.py:312
  33.8 6.1 %collective-permute-start.12 = (s16[528,128]{1,0:T(8,128)(2,1)S(1)}, s16[528,128]{1,0:T(8,128)(2,1)S(1)}, u32[]{:S(2)}, u32[]{:S(2)}) collective-permute-start(s16[528,128]{1,0:T(8,128)(2,1)S(1)} %get-tuple-element.51.refs_2_), channel_id=1, source_target_pairs={{0,2},{1,3},{2,0},{3,1},{4,6},{5,7},{6,4},{7,5},{8,10},{9,11},{10,... | collective-permute-start | bytes 405512 | tf_op jit(solution)/shard_map/ppermute | solution.py:312
  38.0 8.0 %collective-permute-start.15 = (s16[272,128]{1,0:T(8,128)(2,1)S(1)}, s16[272,128]{1,0:T(8,128)(2,1)S(1)}, u32[]{:S(2)}, u32[]{:S(2)}) collective-permute-start(s16[272,128]{1,0:T(8,128)(2,1)S(1)} %shard_map.63.refs_4_), channel_id=1, source_target_pairs={{0,12},{1,13},{2,14},{3,15},{4,8},{5,9},{6,10},{7,11},{8,4},{9,5},... | collective-permute-start | bytes 208904 | tf_op jit(solution)/shard_map/ppermute | solution.py:317
  40.1 7.4 %collective-permute-start.16 = (s16[272,128]{1,0:T(8,128)(2,1)S(1)}, s16[272,128]{1,0:T(8,128)(2,1)S(1)}, u32[]{:S(2)}, u32[]{:S(2)}) collective-permute-start(s16[272,128]{1,0:T(8,128)(2,1)S(1)} %get-tuple-element.54), channel_id=1, source_target_pairs={{0,12},{1,13},{2,14},{3,15},{4,8},{5,9},{6,10},{7,11},{8,4},{9,5},... | collective-permute-start | bytes 208904 | tf_op jit(solution)/shard_map/ppermute | solution.py:317
  43.5 5.5 %collective-permute-start.14 = (s16[528,128]{1,0:T(8,128)(2,1)S(1)}, s16[528,128]{1,0:T(8,128)(2,1)S(1)}, u32[]{:S(2)}, u32[]{:S(2)}) collective-permute-start(s16[528,128]{1,0:T(8,128)(2,1)S(1)} %get-tuple-element.53), channel_id=1, source_target_pairs={{0,8},{1,9},{2,10},{3,11},{4,12},{5,13},{6,14},{7,15},{8,0},{9,1},... | collective-permute-start | bytes 405512 | tf_op jit(solution)/shard_map/ppermute | solution.py:317
